TPU v7x, 32 devices: a whole 2x2x4 slice. The times are simulated.
32 devices in a mesh: frm: 16 (over z, y, x), sp: 2 (over core).
Axes of the slice: x: 2, y: 2, z: 4, core: 2. Of those that a mesh axis runs over, the one named last changes fastest.
Arguments:
- tokens: bfloat16 [64, 256, 1024], P('frm', 'sp'), may hold values from -6 to 6
- out_cotangent: bfloat16 [64, 256, 1024], P('frm', 'sp'), may hold values from -6 to 6
- level_embed: bfloat16 [64, 1024], P(('frm', 'sp')), may hold values from -6 to 6
- ada_weight: bfloat16 [1024, 6144], replicated, may hold values from -0.1875 to 0.1875
- ada_bias: bfloat16 [6144], replicated, may hold values from -2 to 2
- qkv_weight: bfloat16 [1024, 3072], replicated, may hold values from -0.1875 to 0.1875
- qkv_bias: bfloat16 [3072], replicated, may hold values from -2 to 2
- proj_weight: bfloat16 [1024, 1024], replicated, may hold values from -1.5 to 1.5
- proj_bias: bfloat16 [1024], replicated, may hold values from -2 to 2
- up_weight: bfloat16 [1024, 4096], replicated, may hold values from -0.1875 to 0.1875
- up_bias: bfloat16 [4096], replicated, may hold values from -2 to 2
- down_weight: bfloat16 [4096, 1024], replicated, may hold values from -0.09375 to 0.09375
- down_bias: bfloat16 [1024], replicated, may hold values from -2 to 2
- context_count: int32 [4], replicated, may hold values from 1 to 15, as said below
- frame_level: int32 [4, 16], replicated, may hold values from 0 to 63, as said below
- slot_time: int32 [64], replicated, may hold values from 0 to 15, as said below
Outputs:
- block_out: bfloat16 [64, 256, 1024], P('frm', 'sp')
- tokens_grad: bfloat16 [64, 256, 1024], P('frm', 'sp')
- ada_weight_grad: float32 [1024, 6144], P(('frm', 'sp'))
- ada_bias_grad: float32 [6144], P(('frm', 'sp'))
- qkv_weight_grad: float32 [1024, 3072], P(('frm', 'sp'))
- qkv_bias_grad: float32 [3072], P(('frm', 'sp'))
- proj_weight_grad: float32 [1024, 1024], P(('frm', 'sp'))
- proj_bias_grad: float32 [1024], P(('frm', 'sp'))
- up_weight_grad: float32 [1024, 4096], P(('frm', 'sp'))
- up_bias_grad: float32 [4096], P(('frm', 'sp'))
- down_weight_grad: float32 [4096, 1024], P(('frm', 'sp'))
- down_bias_grad: float32 [1024], P(('frm', 'sp'))
Inputs may be any that keep to these rules, and one draw needn't show every extreme that they name: `context_count`: every clip has at least one context frame and at least one noisy frame. frame_level[c, t] is 0 exactly for t < context_count[c] and at least 1 otherwise. `slot_time`: slots c * 16 to (c + 1) * 16 - 1 hold the frames of clip c, each time 0 to 15 once.
All inputs are finite; a program needn't handle non-finite values.
Results may differ from a plain program's by a relative error of at most 0.014.
The roundings to bfloat16 on the way count: a program that leaves them out, or rounds other values in their place, can miss the bound.
Values may be sent and summed in bfloat16 or wider, within the bound.
No kernel may reach another device: no remote copies, remote signals or barrier semaphores. Data moves between devices by JAX's collectives and lax.ppermute only.
A program may use at most 512 MiB of HBM per device.

v0:
```python
from functools import partial
import math

import jax
import jax.numpy as jnp
from jax import lax
from jax.sharding import PartitionSpec as P

HEADS = 16
HDIM = 64
FRAMES = 16
GRID = 16


norm_eps = 1e-06
masked_out = -1e30


def from_partner(value, axis, stride):
    mask = 2**stride
    pairs = [(source, source ^ mask) for source in range(lax.axis_size(axis))]
    return lax.ppermute(value, axis, pairs)


def layer_norm(values_in):
    centre = values_in - jnp.mean(values_in, axis=-1, keepdims=True)
    inv_scale = lax.rsqrt(jnp.mean(centre * centre, axis=-1, keepdims=True) + norm_eps)
    return (centre * inv_scale, inv_scale)


def norm_back(grad_in, normed, inv_scale):
    mean_grad = jnp.mean(grad_in, axis=-1, keepdims=True)
    mean_mix = jnp.mean(grad_in * normed, axis=-1, keepdims=True)
    return inv_scale * (grad_in - mean_grad - normed * mean_mix)


def frequencies(span_dims):
    pair_ids = jnp.arange(span_dims // 2, dtype=jnp.float32)
    return jnp.exp(pair_ids * (-2.0 * math.log(10000.0) / span_dims))


def rotary_angles(tok_times, tok_rows, tok_cols, head_dim):
    first_span = head_dim // 4
    second_span = 3 * head_dim // 8
    return (
        tok_times[:, None] * frequencies(first_span)[None, :],
        tok_rows[:, None] * frequencies(second_span)[None, :],
        tok_cols[:, None] * frequencies(second_span)[None, :],
    )


def rotate(values_in, angle_set, direction):
    pieces = []
    offset = 0
    for angle_row in angle_set:
        half_span = angle_row.shape[1]
        lead_part = values_in[..., offset : offset + half_span]
        tail_part = values_in[..., offset + half_span : offset + 2 * half_span]
        cosine = jnp.cos(angle_row)[:, None, :]
        sine_term = direction * jnp.sin(angle_row)[:, None, :]
        pieces.append(lead_part * cosine - tail_part * sine_term)
        pieces.append(tail_part * cosine + lead_part * sine_term)
        offset = offset + 2 * half_span
    return jnp.concatenate(pieces, axis=-1)


def inner_rows(left_op, right_op):
    return lax.dot_general(
        left_op, right_op, (((0,), (0,)), ((), ())), preferred_element_type=jnp.float32
    )


def outer_cols(left_op, right_op):
    return lax.dot_general(
        left_op, right_op, (((1,), (1,)), ((), ())), preferred_element_type=jnp.float32
    )


def body(
    tokens,
    out_cotangent,
    level_embed,
    ada_weight,
    ada_bias,
    qkv_weight,
    qkv_bias,
    proj_weight,
    proj_bias,
    up_weight,
    up_bias,
    down_weight,
    down_bias,
    context_count,
    frame_level,
    slot_time,
):
    frames_here, patch_here, model_width = tokens.shape
    rows_here = frames_here * patch_here
    score_scale = 1.0 / math.sqrt(HDIM)
    frame_index = lax.axis_index("frm")
    patch_index = lax.axis_index("sp")
    first_slot = frame_index * frames_here
    clip_id = first_slot // FRAMES
    my_times = lax.dynamic_slice_in_dim(slot_time, first_slot, frames_here)
    clip_times = lax.dynamic_slice_in_dim(slot_time, clip_id * FRAMES, FRAMES)
    clip_levels = lax.dynamic_index_in_dim(frame_level, clip_id, 0, keepdims=False)
    my_levels = jnp.take(clip_levels, my_times)
    clip_context = lax.dynamic_index_in_dim(context_count, clip_id, 0, keepdims=False)
    embed_act = jax.nn.silu(level_embed.astype(jnp.float32)).astype(jnp.bfloat16)
    local_mod = (
        jnp.dot(embed_act, ada_weight, preferred_element_type=jnp.float32)
        + ada_bias.astype(jnp.float32)
    ).astype(jnp.bfloat16)
    mod_table = lax.all_gather(local_mod, ("frm", "sp"), axis=0, tiled=True)
    level_count = mod_table.shape[0]
    level_pick = my_levels[:, None] == jnp.arange(level_count, dtype=jnp.int32)[None, :]
    frame_mod = jnp.dot(
        level_pick.astype(jnp.bfloat16), mod_table, preferred_element_type=jnp.float32
    )
    mod_parts = [
        frame_mod[:, None, part_no * model_width : (part_no + 1) * model_width]
        for part_no in range(6)
    ]
    shift_one, scale_one, gate_one, shift_two, scale_two, gate_two = mod_parts
    inputs = tokens.astype(jnp.float32)
    normed_one, rscale_one = layer_norm(inputs)
    hidden_one = (
        (normed_one * (1.0 + scale_one) + shift_one)
        .astype(jnp.bfloat16)
        .reshape(rows_here, model_width)
    )
    projected = jnp.dot(
        hidden_one, qkv_weight, preferred_element_type=jnp.float32
    ) + qkv_bias.astype(jnp.float32)
    patch_ids = patch_index * patch_here + jnp.arange(patch_here, dtype=jnp.int32)
    tok_times = jnp.repeat(my_times, patch_here).astype(jnp.float32)
    tok_rows = jnp.tile(patch_ids // GRID, frames_here).astype(jnp.float32)
    tok_cols = jnp.tile(patch_ids % GRID, frames_here).astype(jnp.float32)
    angle_set = rotary_angles(tok_times, tok_rows, tok_cols, HDIM)
    split_shape = (rows_here, HEADS, HDIM)
    queries = rotate(projected[:, :model_width].reshape(split_shape), angle_set, 1.0).astype(
        jnp.bfloat16
    )
    keys_own = rotate(
        projected[:, model_width : 2 * model_width].reshape(split_shape), angle_set, 1.0
    ).astype(jnp.bfloat16)
    values_own = projected[:, 2 * model_width :].astype(jnp.bfloat16)
    keyval_own = jnp.stack(
        [
            keys_own.reshape(frames_here, patch_here, model_width),
            values_own.reshape(frames_here, patch_here, model_width),
        ]
    )
    bit_count = (FRAMES // frames_here).bit_length() - 1
    stacked = lax.all_gather(keyval_own, "sp", axis=2, tiled=True)
    for bit_pos in range(bit_count):
        peer_part = from_partner(stacked, "frm", bit_pos)
        widen_is_upper = frame_index >> bit_pos & 1 == 1
        stacked = jnp.concatenate(
            [
                jnp.where(widen_is_upper, peer_part, stacked),
                jnp.where(widen_is_upper, stacked, peer_part),
            ],
            axis=1,
        )
    key_frames = stacked.shape[1]
    key_patches = stacked.shape[2]
    key_count = key_frames * key_patches
    key_heads = stacked[0].reshape(key_count, HEADS, HDIM).transpose(1, 0, 2)
    value_heads = stacked[1].reshape(key_count, HEADS, HDIM).transpose(1, 0, 2)
    query_heads = queries.transpose(1, 0, 2)
    time_ok = (clip_times[None, :] <= my_times[:, None]) | (clip_times[None, :] < clip_context)
    visible = jnp.broadcast_to(
        time_ok[:, None, :, None], (frames_here, patch_here, key_frames, key_patches)
    ).reshape(rows_here, key_count)

    def head_scores(query_one, key_one):
        scores = jnp.dot(query_one, key_one.T, preferred_element_type=jnp.float32) * score_scale
        return jnp.where(visible, scores, masked_out)

    def head_forward(operands):
        query_one, key_one, value_one = operands
        scores = head_scores(query_one, key_one)
        row_top = jnp.max(scores, axis=1, keepdims=True)
        log_total = row_top + jnp.log(jnp.sum(jnp.exp(scores - row_top), axis=1, keepdims=True))
        probs_low = jnp.exp(scores - log_total).astype(jnp.bfloat16)
        return (jnp.dot(probs_low, value_one, preferred_element_type=jnp.float32), log_total)

    attended, log_totals = lax.map(head_forward, (query_heads, key_heads, value_heads))
    attn_low = attended.transpose(1, 0, 2).reshape(rows_here, model_width).astype(jnp.bfloat16)
    attn_proj = (
        jnp.dot(attn_low, proj_weight, preferred_element_type=jnp.float32)
        + proj_bias.astype(jnp.float32)
    ).reshape(frames_here, patch_here, model_width)
    after_attn = inputs + gate_one * attn_proj
    normed_two, rscale_two = layer_norm(after_attn)
    hidden_two = (
        (normed_two * (1.0 + scale_two) + shift_two)
        .astype(jnp.bfloat16)
        .reshape(rows_here, model_width)
    )
    pre_act = jnp.dot(hidden_two, up_weight, preferred_element_type=jnp.float32) + up_bias.astype(
        jnp.float32
    )
    gelu_value, gelu_back = jax.vjp(partial(jax.nn.gelu, approximate=True), pre_act)
    activated = gelu_value.astype(jnp.bfloat16)
    branch_out = (
        jnp.dot(activated, down_weight, preferred_element_type=jnp.float32)
        + down_bias.astype(jnp.float32)
    ).reshape(frames_here, patch_here, model_width)
    block_out = (after_attn + gate_two * branch_out).astype(jnp.bfloat16)
    grad_out = out_cotangent.astype(jnp.float32)
    grad_gate_two = jnp.sum(grad_out * branch_out, axis=1)
    grad_branch = (gate_two * grad_out).astype(jnp.bfloat16).reshape(rows_here, model_width)
    down_w_grad = inner_rows(activated, grad_branch)
    down_b_grad = jnp.sum(grad_branch.astype(jnp.float32), axis=0)
    grad_act = outer_cols(grad_branch, down_weight)
    grad_pre = gelu_back(grad_act)[0].astype(jnp.bfloat16)
    up_w_grad = inner_rows(hidden_two, grad_pre)
    up_b_grad = jnp.sum(grad_pre.astype(jnp.float32), axis=0)
    grad_hidden_two = outer_cols(grad_pre, up_weight).reshape(frames_here, patch_here, model_width)
    grad_shift_two = jnp.sum(grad_hidden_two, axis=1)
    grad_scale_two = jnp.sum(grad_hidden_two * normed_two, axis=1)
    grad_after = grad_out + norm_back(grad_hidden_two * (1.0 + scale_two), normed_two, rscale_two)
    grad_gate_one = jnp.sum(grad_after * attn_proj, axis=1)
    grad_proj = (gate_one * grad_after).astype(jnp.bfloat16).reshape(rows_here, model_width)
    proj_w_grad = inner_rows(attn_low, grad_proj)
    proj_b_grad = jnp.sum(grad_proj.astype(jnp.float32), axis=0)
    grad_attended = outer_cols(grad_proj, proj_weight).astype(jnp.bfloat16)
    grad_att_heads = grad_attended.reshape(rows_here, HEADS, HDIM).transpose(1, 0, 2)

    def head_backward(operands):
        query_one, key_one, value_one, grad_one, log_total = operands
        scores = head_scores(query_one, key_one)
        probs = jnp.exp(scores - log_total)
        probs_low = probs.astype(jnp.bfloat16)
        grad_probs = jnp.dot(grad_one, value_one.T, preferred_element_type=jnp.float32)
        value_grad = inner_rows(probs_low, grad_one)
        row_mix = jnp.sum(probs * grad_probs, axis=1, keepdims=True)
        grad_scores = (probs * (grad_probs - row_mix)).astype(jnp.bfloat16)
        query_grad = jnp.dot(grad_scores, key_one, preferred_element_type=jnp.float32) * score_scale
        key_grad = inner_rows(grad_scores, query_one) * score_scale
        return (query_grad, key_grad, value_grad)

    query_grads, key_grads, value_grads = lax.map(
        head_backward, (query_heads, key_heads, value_heads, grad_att_heads, log_totals)
    )
    clip_grads = jnp.stack(
        [
            key_grads.transpose(1, 0, 2).reshape(key_frames, key_patches, model_width),
            value_grads.transpose(1, 0, 2).reshape(key_frames, key_patches, model_width),
        ]
    )
    stacked = clip_grads
    for bit_pos in reversed(range(bit_count)):
        half_size = stacked.shape[1] // 2
        lower_half = stacked[:, :half_size]
        upper_half = stacked[:, half_size:]
        is_upper = frame_index >> bit_pos & 1 == 1
        keep_part = jnp.where(is_upper, upper_half, lower_half)
        send_part = jnp.where(is_upper, lower_half, upper_half)
        stacked = keep_part + from_partner(send_part.astype(jnp.bfloat16), "frm", bit_pos).astype(
            send_part.dtype
        )
    own_grads = lax.psum_scatter(
        stacked.astype(jnp.bfloat16), "sp", scatter_dimension=2, tiled=True
    ).astype(jnp.float32)
    key_grad_own = rotate(own_grads[0].reshape(split_shape), angle_set, -1.0).reshape(
        rows_here, model_width
    )
    value_grad_own = own_grads[1].reshape(rows_here, model_width)
    query_grad_own = rotate(query_grads.transpose(1, 0, 2), angle_set, -1.0).reshape(
        rows_here, model_width
    )
    grad_projected = jnp.concatenate([query_grad_own, key_grad_own, value_grad_own], axis=1).astype(
        jnp.bfloat16
    )
    qkv_w_grad = inner_rows(hidden_one, grad_projected)
    qkv_b_grad = jnp.sum(grad_projected.astype(jnp.float32), axis=0)
    grad_hidden_one = outer_cols(grad_projected, qkv_weight).reshape(
        frames_here, patch_here, model_width
    )
    grad_shift_one = jnp.sum(grad_hidden_one, axis=1)
    grad_scale_one = jnp.sum(grad_hidden_one * normed_one, axis=1)
    tokens_grad = (
        grad_after + norm_back(grad_hidden_one * (1.0 + scale_one), normed_one, rscale_one)
    ).astype(jnp.bfloat16)
    frame_mod_grad = jnp.concatenate(
        [
            grad_shift_one,
            grad_scale_one,
            grad_gate_one,
            grad_shift_two,
            grad_scale_two,
            grad_gate_two,
        ],
        axis=1,
    )
    table_terms = lax.dot_general(
        level_pick.astype(jnp.float32),
        frame_mod_grad,
        (((0,), (0,)), ((), ())),
        precision=lax.Precision.HIGHEST,
        preferred_element_type=jnp.float32,
    )
    level_grad = lax.psum_scatter(
        table_terms, ("frm", "sp"), scatter_dimension=0, tiled=True
    ).astype(jnp.bfloat16)
    ada_w_grad = inner_rows(embed_act, level_grad)
    ada_b_grad = jnp.sum(level_grad.astype(jnp.float32), axis=0)
    summed = (
        lax.psum_scatter(ada_w_grad, ("frm", "sp"), scatter_dimension=0, tiled=True),
        lax.psum_scatter(ada_b_grad, ("frm", "sp"), scatter_dimension=0, tiled=True),
        lax.psum_scatter(qkv_w_grad, ("frm", "sp"), scatter_dimension=0, tiled=True),
        lax.psum_scatter(qkv_b_grad, ("frm", "sp"), scatter_dimension=0, tiled=True),
        lax.psum_scatter(proj_w_grad, ("frm", "sp"), scatter_dimension=0, tiled=True),
        lax.psum_scatter(proj_b_grad, ("frm", "sp"), scatter_dimension=0, tiled=True),
        lax.psum_scatter(up_w_grad, ("frm", "sp"), scatter_dimension=0, tiled=True),
        lax.psum_scatter(up_b_grad, ("frm", "sp"), scatter_dimension=0, tiled=True),
        lax.psum_scatter(down_w_grad, ("frm", "sp"), scatter_dimension=0, tiled=True),
        lax.psum_scatter(down_b_grad, ("frm", "sp"), scatter_dimension=0, tiled=True),
    )
    return (
        block_out,
        tokens_grad,
        summed[0],
        summed[1],
        summed[2],
        summed[3],
        summed[4],
        summed[5],
        summed[6],
        summed[7],
        summed[8],
        summed[9],
    )


def solution(mesh):
    return jax.shard_map(
        body,
        mesh=mesh,
        in_specs=(
            P("frm", "sp", None),
            P("frm", "sp", None),
            P(("frm", "sp"), None),
            P(),
            P(),
            P(),
            P(),
            P(),
            P(),
            P(),
            P(),
            P(),
            P(),
            P(),
            P(),
            P(),
        ),
        out_specs=(
            P("frm", "sp", None),
            P("frm", "sp", None),
            P(("frm", "sp"), None),
            P(("frm", "sp")),
            P(("frm", "sp"), None),
            P(("frm", "sp")),
            P(("frm", "sp"), None),
            P(("frm", "sp")),
            P(("frm", "sp"), None),
            P(("frm", "sp")),
            P(("frm", "sp"), None),
            P(("frm", "sp")),
        ),
        check_vma=False,
    )
```

profile of v0, /device:TPU:0, one launch (start us, length us, event | category | flops | bytes accessed | tf_op | source)
XLA Modules:
  0.0 2938.0 jit_solution(14423301681476718976)
XLA Ops:
  20.5 48.1 %all-gather = bf16[32,2,6144]{2,1,0:T(2,128)(2,1)} all-gather(bf16[1,2,6144]{2,1,0:T(2,128)(2,1)S(1)} %fusion.51), channel_id=1, replica_groups=mesh['frm'=16,'sp'=2] {'frm','sp'}, dimensions={0}, use_global_device_ids=true | all-gather | bytes 811008 | tf_op jit(solution)/shard_map/all_gather | solution.py:114
  101.8 14.0 concatenate.30
  122.7 8.9 all-gather.3.cloned.1.call-done
  133.4 91.3 %collective-permute-done = bf16[2,4,256,1024]{2,1,3,0:T(4,128)(2,1)} collective-permute-done((bf16[2,4,256,1024]{2,1,3,0:T(4,128)(2,1)}, bf16[2,4,256,1024]{2,1,3,0:T(4,128)(2,1)}, u32[]{:S(2)}, u32[]{:S(2)}) %collective-permute-start) | collective-permute-done | bytes 4194336 | tf_op jit(solution)/shard_map/ppermute | solution.py:22
  242.0 14.0 concatenate.29
  261.9 155.2 %collective-permute-done.1 = bf16[2,8,256,1024]{2,1,3,0:T(8,128)(2,1)} collective-permute-done((bf16[2,8,256,1024]{2,1,3,0:T(8,128)(2,1)}, bf16[2,8,256,1024]{2,1,3,0:T(8,128)(2,1)}, u32[]{:S(2)}, u32[]{:S(2)}) %collective-permute-start.1) | collective-permute-done | bytes 8388640 | tf_op jit(solution)/shard_map/ppermute | solution.py:22
  417.1 9.0 broadcast_select_fusion
  432.3 13.5 reshape_squeeze.17
  445.7 15.6 copy.64
  461.3 13.5 reshape_squeeze.16
  474.8 15.6 copy.63
  490.3 169.6 %while.30 = (s32[]{:T(128)}, bf16[16,512,64]{1,2,0:T(8,128)(2,1)}, f32[16,512,1]{1,2,0:T(1,128)}, bf16[16,512,64]{2,1,0:T(8,128)(2,1)}, bf16[16,4096,64]{2,1,0:T...) while((s32[]{:T(128)}, bf16[16,512,64]{1,2,0:T(8,128)(2,1)}, ...), condition=%wide.region_5.6_spmd.clone.clone, body=%wide.region_2.5_spmd.clone.sunk.clone | while | flops 551550464 | bytes 35934360 | solution.py:189
  664.9 15.6 fusion.94
  686.1 12.9 convert_reduce_fusion
  699.0 9.1 fusion.70
  717.0 530.2 %while.31 = (s32[]{:T(128)}, f32[16,512,64]{1,2,0:T(8,128)}, f32[16,4096,64]{1,2,0:T(8,128)}, f32[16,4096,64]{1,2,0:T(8,128)}, bf16[16,512,64]{2,1,0:T(8,128)(2,...) while((s32[]{:T(128)}, f32[16,512,64]{1,2,0:T(8,128)}, ...), condition=%wide.region_12.13_spmd.clone.clone, body=%wide.region_10.12_spmd.clone.sunk.clone | while | flops 1361346048 | bytes 110640328 | solution.py:245
  722.4 8.4 multiply_reduce_fusion.6
  730.8 7.9 multiply_convert_fusion.8
  755.6 8.4 multiply_reduce_fusion.6
  788.7 8.4 multiply_reduce_fusion.6
  797.1 7.9 multiply_convert_fusion.8
  821.8 8.4 multiply_reduce_fusion.6
  830.2 7.9 multiply_convert_fusion.8
  855.0 8.4 multiply_reduce_fusion.6
  863.4 7.9 multiply_convert_fusion.8
  888.2 8.4 multiply_reduce_fusion.6
  921.3 8.4 multiply_reduce_fusion.6
  929.7 7.9 multiply_convert_fusion.8
  954.4 8.4 multiply_reduce_fusion.6
  962.8 7.9 multiply_convert_fusion.8
  987.7 8.4 multiply_reduce_fusion.6
  1020.8 8.4 multiply_reduce_fusion.6
  1029.2 7.9 multiply_convert_fusion.8
  1053.9 8.4 multiply_reduce_fusion.6
  1062.3 7.9 multiply_convert_fusion.8
  1087.0 8.4 multiply_reduce_fusion.6
  1120.1 8.4 multiply_reduce_fusion.6
  1128.5 7.9 multiply_convert_fusion.8
  1153.2 8.4 multiply_reduce_fusion.6
  1161.6 7.9 multiply_convert_fusion.8
  1186.4 8.4 multiply_reduce_fusion.6
  1219.5 8.4 multiply_reduce_fusion.6
  1247.1 11.4 copy.78
  1258.5 11.0 copy.77
  1281.8 11.2 select_convert_fusion
  1294.9 179.2 %collective-permute-done.2 = bf16[2,8,256,1024]{2,1,3,0:T(8,128)(2,1)S(1)} collective-permute-done((bf16[2,8,256,1024]{2,1,3,0:T(8,128)(2,1)S(1)}, bf16[2,8,256,1024]{2,1,3,0:T(8,128)(2,1)S(1)}, u32[]{:S(2)}, u32[]{:S(2)}) %collective-permute-start.2) | collective-permute-done | bytes 8388640 | tf_op jit(solution)/shard_map/ppermute | solution.py:22
  1474.1 11.6 convert_add_fusion
  1490.5 88.4 %collective-permute-done.3 = bf16[2,4,256,1024]{2,1,3,0:T(4,128)(2,1)S(1)} collective-permute-done((bf16[2,4,256,1024]{2,1,3,0:T(4,128)(2,1)S(1)}, bf16[2,4,256,1024]{2,1,3,0:T(4,128)(2,1)S(1)}, u32[]{:S(2)}, u32[]{:S(2)}) %collective-permute-start.3) | collective-permute-done | bytes 4194336 | tf_op jit(solution)/shard_map/ppermute | solution.py:22
  1583.3 89.0 %copy.70 = bf16[2,4,256,1024]{1,3,0,2:T(8,128)(2,1)} copy(bf16[2,4,256,1024]{2,1,3,0:T(4,128)(2,1)} %add_convert_fusion) | data formatting | bytes 8388608
  1672.3 295.8 %reshape.530 = bf16[256,8192]{1,0:T(8,128)(2,1)} reshape(bf16[256,2,1024,4]{3,2,1,0:T(8,128)(2,1)} %bitcast.48) | data formatting | bytes 8388608
  1971.7 15.4 fusion.86
  1988.3 10.3 fusion.96
  2001.5 147.4 %reshape.531 = bf16[128,2,1024,4]{3,2,1,0:T(8,128)(2,1)} reshape(bf16[128,8192]{1,0:T(8,128)(2,1)} %reduce-scatter.19.cloned.1.call-done) | data formatting | bytes 4194304
  2148.9 56.6 %slice_convert_fusion = (f32[1,4,128,1024]{1,3,0,2:T(8,128)}, bf16[1,4,128,1024]{1,3,0,2:T(8,128)(2,1)}) fusion(bf16[2,4,128,1024]{1,3,0,2:T(8,128)(2,1)} %bitcast.49), kind=kLoop, calls=%fused_computation.53 | loop fusion | flops 524288 | bytes 5242880 | tf_op jit(solution)/shard_map/reshape;squeeze | solution.py:268
  2205.6 36.9 %copy.80 = f32[1,4,128,1024]{2,1,3,0:T(4,128)} copy(f32[1,4,128,1024]{1,3,0,2:T(8,128)} %get-tuple-element.262) | data formatting | bytes 4194304
  2244.5 30.3 %copy.74 = bf16[1,4,128,1024]{2,1,3,0:T(4,128)(2,1)S(1)} copy(bf16[1,4,128,1024]{1,3,0,2:T(8,128)(2,1)} %get-tuple-element.263) | data formatting | bytes 2097152
  2279.4 9.7 concatenate.34
  2296.8 11.0 fusion.84
  2319.2 80.3 %all-reduce.8 = bf16[64,6144]{1,0:T(8,128)(2,1)} all-reduce(f32[64,6144]{1,0:T(8,128)S(1)} %fusion.75), channel_id=3, replica_groups=mesh['frm'=16,'sp'=2] {'frm','sp'}, use_global_device_ids=true, to_apply=%region_22.23.clone | all-reduce | flops 393216 | bytes 2359296
  2399.6 11.3 fusion.81
  2414.2 42.9 %all-reduce.6 = (f32[6144]{0:T(1024)S(1)}, f32[3072]{0:T(1024)S(1)}, f32[1024]{0:T(1024)S(1)}, f32[4096]{0:T(1024)S(1)}, f32[1024]{0:T(1024)S(1)}) all-reduce(f32[6144]{0:T(1024)S(1)} %convert_reduce_fusion.5, f32[3072]{0:T(1024)S(1)} %convert_reduce_fusion.1, ...), channel_id=5, replica_groups=mesh['frm'=16,'sp'=2] {'frm','sp'}, use_global_device_ids=true, to_apply=%region_25.26.clone | all-reduce | flops 15360 | bytes 122880
  2460.1 54.0 %reduce-scatter.15.cloned.1.call-done = f32[32,4096]{1,0:T(8,128)} async-done(((f32[1024,4096]{1,0:T(8,128)}), f32[32,4096]{1,0:T(8,128)}) %reduce-scatter.15.cloned.1.call-update) | async-done | bytes 524304 | tf_op jit(solution)/shard_map/reduce_scatter | solution.py:318
  2514.1 165.3 %reduce-scatter.11.cloned.1.call-done = f32[32,3072]{1,0:T(8,128)} async-done(((f32[1024,3072]{1,0:T(8,128)}), f32[32,3072]{1,0:T(8,128)}) %reduce-scatter.11.cloned.1.call-update) | async-done | bytes 393232 | tf_op jit(solution)/shard_map/reduce_scatter | solution.py:314
  2679.4 251.5 %reduce-scatter.9.cloned.1.call-done = f32[32,6144]{1,0:T(8,128)} async-done(((f32[1024,6144]{1,0:T(8,128)}), f32[32,6144]{1,0:T(8,128)}) %reduce-scatter.9.cloned.1.call-update) | async-done | bytes 786448 | tf_op jit(solution)/shard_map/reduce_scatter | solution.py:312
  (502 shorter events, 651.6 us)
Async XLA Ops:
  7.2 652.7 %copy-start = (bf16[1024,1024]{1,0:T(8,128)(2,1)S(1)}, bf16[1024,1024]{1,0:T(8,128)(2,1)}, u32[]{:S(2)}) copy-start(bf16[1024,1024]{1,0:T(8,128)(2,1)} %param.27) | copy-start | bytes 6291460
  7.2 124.5 %all-gather.3.cloned.1.call-start = ((), (), s32[]{:S(2)}) async-start(), calls=%async_computation.6 | async-start | bytes 6291456 | tf_op jit(solution)/shard_map/all_gather | solution.py:155
  9.6 64.0 %copy-start.42 = (f32[4,128]{1,0:T(4,128)}, f32[4,128]{1,0:T(4,128)S(1)}, u32[]{:S(2)}) copy-start(f32[4,128]{1,0:T(4,128)S(1)} %broadcast_multiply_fusion.6) | copy-start | bytes 6148
  11.3 62.4 %copy-start.44 = (f32[4,128]{1,0:T(4,128)}, f32[4,128]{1,0:T(4,128)S(1)}, u32[]{:S(2)}) copy-start(f32[4,128]{1,0:T(4,128)S(1)} %add_rsqrt_fusion.1) | copy-start | bytes 6148
  12.6 58.9 %copy-start.54 = (s32[4]{0:T(128)}, s32[4]{0:T(128)S(1)}, u32[]{:S(2)}) copy-start(s32[4]{0:T(128)S(1)} %and_select_fusion.2) | copy-start | bytes 52
  14.0 59.6 %copy-start.5 = (bf16[4,128,1024]{2,1,0:T(8,128)(2,1)S(1)}, bf16[4,128,1024]{2,1,0:T(8,128)(2,1)}, u32[]{:S(2)}) copy-start(bf16[4,128,1024]{2,1,0:T(8,128)(2,1)} %param.20) | copy-start | bytes 3145732
  73.6 9.8 copy-start.34
  77.5 5.9 copy-start.21
  96.9 142.3 %copy-start.24 = (f32[512,12]{0,1:T(8,128)}, f32[512,12]{0,1:T(8,128)S(1)}, u32[]{:S(2)}) copy-start(f32[512,12]{0,1:T(8,128)S(1)} %get-tuple-element.319) | copy-start | bytes 73732
  96.9 142.3 %copy-start.26 = (f32[512,12]{0,1:T(8,128)}, f32[512,12]{0,1:T(8,128)S(1)}, u32[]{:S(2)}) copy-start(f32[512,12]{0,1:T(8,128)S(1)} %get-tuple-element.327) | copy-start | bytes 73732
  122.4 1879.1 %reduce-scatter.19.cloned.1.call-start = ((), (), s32[]{:S(2)}) async-start(), calls=%async_computation.12 | async-start | bytes 6291456
  131.7 93.1 %collective-permute-start = (bf16[2,4,256,1024]{2,1,3,0:T(4,128)(2,1)}, bf16[2,4,256,1024]{2,1,3,0:T(4,128)(2,1)}, u32[]{:S(2)}, u32[]{:S(2)}) collective-permute-start(bf16[2,4,256,1024]{2,1,3,0:T(4,128)(2,1)} %all-gather.3.cloned.1.call-done), channel_id=1, source_target_pairs={{0,2},{2,0},{4,6},{6,4},{8,10},{10,8},{12,14},{14,12},{16,18},{18,... | collective-permute-start | bytes 12582920 | tf_op jit(solution)/shard_map/ppermute | solution.py:22
  228.5 6.4 copy-start.3
  228.5 6.4 copy-start.4
  228.6 8.2 copy-start.59
  228.6 8.7 copy-start.56
  228.6 9.3 copy-start.57
  228.6 9.9 copy-start.52
  235.0 182.1 %collective-permute-start.1 = (bf16[2,8,256,1024]{2,1,3,0:T(8,128)(2,1)}, bf16[2,8,256,1024]{2,1,3,0:T(8,128)(2,1)}, u32[]{:S(2)}, u32[]{:S(2)}) collective-permute-start(bf16[2,8,256,1024]{2,1,3,0:T(8,128)(2,1)} %pad_maximum_fusion.1), channel_id=1, source_target_pairs={{0,4},{2,6},{4,0},{6,2},{8,12},{10,14},{12,8},{14,10},{16,20},{18,... | collective-permute-start | bytes 25165832 | tf_op jit(solution)/shard_map/ppermute | solution.py:22
  490.3 169.6 %copy-start.37 = (f32[1024]{0:T(1024)S(1)}, f32[1024]{0:T(1024)}, u32[]{:S(2)}) copy-start(f32[1024]{0:T(1024)} %convert_element_type.179) | copy-start | bytes 12292
  490.3 172.1 %copy-start.36 = (f32[4,1024]{1,0:T(4,128)S(1)}, f32[4,1024]{1,0:T(4,128)}, u32[]{:S(2)}) copy-start(f32[4,1024]{1,0:T(4,128)} %get-tuple-element.313) | copy-start | bytes 49156
  662.4 18.0 copy-start.7
  662.5 18.0 slice-start
  664.9 15.6 copy-start.48
  664.9 15.6 copy-start.53
  664.9 15.6 slice-start.1
  680.5 5.5 copy-start.60
  699.0 9.1 copy-start.15
  722.4 8.4 copy-start.2
  755.6 8.4 copy-start.2
  788.7 8.4 copy-start.2
  821.8 8.4 copy-start.2
  855.0 8.4 copy-start.2
  888.1 8.4 copy-start.2
  921.3 8.4 copy-start.2
  954.4 8.4 copy-start.2
  987.7 8.4 copy-start.2
  1020.8 8.4 copy-start.2
  1053.9 8.4 copy-start.2
  1086.9 8.4 copy-start.2
  1120.1 8.4 copy-start.2
  1153.2 8.4 copy-start.2
  1186.3 8.4 copy-start.2
  1219.5 8.4 copy-start.2
  1293.1 181.0 %collective-permute-start.2 = (bf16[2,8,256,1024]{2,1,3,0:T(8,128)(2,1)S(1)}, bf16[2,8,256,1024]{2,1,3,0:T(8,128)(2,1)S(1)}, u32[]{:S(2)}, u32[]{:S(2)}) collective-permute-start(bf16[2,8,256,1024]{2,1,3,0:T(8,128)(2,1)S(1)} %select_convert_fusion), channel_id=1, source_target_pairs={{0,4},{2,6},{4,0},{6,2},{8,12},{10,14},{12,8},{14,10},{16,20},{18,... | collective-permute-start | bytes 25165832 | tf_op jit(solution)/shard_map/ppermute | solution.py:22
  1488.7 90.2 %collective-permute-start.3 = (bf16[2,4,256,1024]{2,1,3,0:T(4,128)(2,1)S(1)}, bf16[2,4,256,1024]{2,1,3,0:T(4,128)(2,1)S(1)}, u32[]{:S(2)}, u32[]{:S(2)}) collective-permute-start(bf16[2,4,256,1024]{2,1,3,0:T(4,128)(2,1)S(1)} %select_convert_fusion.1), channel_id=1, source_target_pairs={{0,2},{2,0},{4,6},{6,4},{8,10},{10,8},{12,14},{14,12},{16,18},{18,... | collective-permute-start | bytes 12582920 | tf_op jit(solution)/shard_map/ppermute | solution.py:22
  1672.3 295.9 %copy-start.10 = (bf16[16,512,64]{1,2,0:T(8,128)(2,1)S(1)}, bf16[16,512,64]{1,2,0:T(8,128)(2,1)}, u32[]{:S(2)}) copy-start(bf16[16,512,64]{1,2,0:T(8,128)(2,1)} %get-tuple-element.104) | copy-start | bytes 3145732
  1672.3 295.9 %copy-start.20 = (bf16[4,128,1024]{2,1,0:T(8,128)(2,1)S(1)}, bf16[4,128,1024]{2,1,0:T(8,128)(2,1)}, u32[]{:S(2)}) copy-start(bf16[4,128,1024]{2,1,0:T(8,128)(2,1)} %copy-done.19) | copy-start | bytes 3145732
  1968.1 492.0 %reduce-scatter.13.cloned.1.call-start = ((), (), s32[]{:S(2)}) async-start(), calls=%async_computation.9 | async-start | bytes 4325376 | tf_op jit(solution)/shard_map/reduce_scatter | solution.py:316
  1971.4 488.7 %reduce-scatter.17.cloned.1.call-start = ((), (), s32[]{:S(2)}) async-start(), calls=%async_computation.11 | async-start | bytes 17301504 | tf_op jit(solution)/shard_map/reduce_scatter | solution.py:320
  1987.1 527.0 %reduce-scatter.15.cloned.1.call-start = ((), (), s32[]{:S(2)}) async-start(), calls=%async_computation.10 | async-start | bytes 17301504 | tf_op jit(solution)/shard_map/reduce_scatter | solution.py:318
  1998.7 680.7 %reduce-scatter.11.cloned.1.call-start = ((), (), s32[]{:S(2)}) async-start(), calls=%async_computation.8 | async-start | bytes 12976128 | tf_op jit(solution)/shard_map/reduce_scatter | solution.py:314
  2244.5 31.5 %copy-start.33 = (f32[512,8]{0,1:T(8,128)S(1)}, f32[512,8]{0,1:T(8,128)}, u32[]{:S(2)}) copy-start(f32[512,8]{0,1:T(8,128)} %copy-done.32) | copy-start | bytes 49156
  2276.0 20.7 copy-start.12
  2289.2 18.7 copy-start.13
  2296.8 11.0 copy-start.14
  2307.8 7.5 copy-start.6
  2307.8 7.5 copy-start.43
  2307.8 7.5 copy-start.45
  2307.8 623.1 %reduce-scatter.9.cloned.1.call-start = ((), (), s32[]{:S(2)}) async-start(), calls=%async_computation.7 | async-start | bytes 25952256 | tf_op jit(solution)/shard_map/reduce_scatter | solution.py:312
  2308.5 7.8 copy-start.8
  2308.5 7.8 copy-start.9
  2316.3 83.2 %copy-start.46 = (bf16[2,1024]{1,0:T(2,128)(2,1)S(1)}, bf16[2,1024]{1,0:T(2,128)(2,1)}, u32[]{:S(2)}) copy-start(bf16[2,1024]{1,0:T(2,128)(2,1)} %param.22) | copy-start | bytes 12292
  2410.9 520.0 %copy-start.1 = (bf16[1024,1024]{1,0:T(8,128)(2,1)S(1)}, bf16[1024,1024]{1,0:T(8,128)(2,1)}, u32[]{:S(2)}) copy-start(bf16[1024,1024]{1,0:T(8,128)(2,1)} %param.27) | copy-start | bytes 6291460
  (25 other events, 64.7 us)
Sparse Core Ops, SparseCore 0:
  122.6 9.0 all-gather.2
  1968.2 13.1 reduce-scatter.18
  1984.4 142.3 reduce-scatter.12
  2129.6 178.5 reduce-scatter.16
  2311.0 203.0 reduce-scatter.14
  2521.6 157.7 reduce-scatter.10
  2686.4 244.4 reduce-scatter.8
where the time goes:
time: 2960 us; the launch traced here: 2940 us
  waiting for transfers between devices  994 us (34%)
  local copies, waits for them, and re-layouts  862 us (29%)
  matrix products  580 us (20%)
  other arithmetic  306 us (10%)
  blocking collectives  171 us (6%)
    unnamed x147, local copies, waits for them, and re-layouts  674 us
    ppermute x4, waiting for transfers between devices, from_partner(): return lax.ppermute(value, axis, pairs)  514 us
    reduce_scatter x1, waiting for transfers between devices, body(): lax.psum_scatter(ada_w_grad, ('frm', 'sp'), scatter_dimension=0, tiled=True)  252 us
    dot_general x32, matrix products, head_scores(): jnp.dot(query_one, key_one.T, preferred_element_type=jnp.float32)  184 us
    dot_general x37, matrix products, inner_rows(): lax.dot_general(left_op, right_op, (((0,), (0,)), ((), ())), preferred_el...  180 us
    reduce_scatter x1, waiting for transfers between devices, body(): lax.psum_scatter(qkv_w_grad, ('frm', 'sp'), scatter_dimension=0, tiled=True)  165 us
    convert_element_type x16, other arithmetic, head_backward(): grad_scores = (probs * (grad_probs - row_mix)).astype(jnp.bfloat16)  127 us
    unnamed x2, blocking collectives  123 us
  transfers between devices with their start and end apart: 11, of which 8 were waited for; matrix products, arithmetic and copies ran while one was open for 13% of the time, Pallas kernels for 0%

commit v1 on v0

v1 whole, which is shorter than its diff:
```python
import functools
import math

import jax
import jax.numpy as jnp
import numpy as np
from jax import lax
from jax.experimental import pallas as pl
from jax.experimental.pallas import tpu as pltpu
from jax.sharding import PartitionSpec as P

HEADS = 16
HDIM = 64
FRAMES = 16
GRID = 16
LANES = 128
MIB = 2**20

norm_eps = 1e-06
masked_out = -1e30
score_scale = 0.125

f32 = jnp.float32
bf16 = jnp.bfloat16
NN = (((1,), (0,)), ((), ()))
NT = (((1,), (1,)), ((), ()))
TN = (((0,), (0,)), ((), ()))
AXES = ("frm", "sp")
VMEM = pltpu.VMEM


def dot(left_op, right_op, dims=NN):
    return lax.dot_general(left_op, right_op, dims, preferred_element_type=f32)


def exchange(value, groups):
    return lax.all_to_all(value, AXES, 0, 0, axis_index_groups=groups)


def to_everyone(value, devices):
    return exchange(
        jnp.broadcast_to(value[None], (devices,) + value.shape), [list(range(devices))]
    )


def rotary_lanes():
    lane = np.arange(LANES) % HDIM
    start = np.where(lane < 16, 0, np.where(lane < 40, 16, 40))
    half = np.where(lane < 16, 8, 12)
    offset = lane - start
    freq = np.exp((offset % half).astype(np.float32) * np.float32(-math.log(10000.0)) / half)
    sign = np.where(offset < half, -1.0, 1.0)
    return (
        freq.astype(np.float32),
        sign.astype(np.float32),
        (lane < 16),
        (lane >= 16) & (lane < 40),
    )


def rotate_lanes(value, cosine, sine):
    lane = lax.broadcasted_iota(jnp.int32, value.shape, 1) % HDIM
    near_first = pltpu.roll(value, LANES - 8, 1)
    near_second = pltpu.roll(value, 8, 1)
    far_first = pltpu.roll(value, LANES - 12, 1)
    far_second = pltpu.roll(value, 12, 1)
    in_first = (lane < 28) | ((lane >= 40) & (lane < 52))
    far = jnp.where(in_first, far_first, far_second)
    near = jnp.where(lane < 8, near_first, near_second)
    partner = jnp.where(lane < 16, near, far)
    return value * cosine + partner * sine


def keyval_kernel(tok_ref, shift_ref, scale_ref, wk_ref, wv_ref, bk_ref, bv_ref,
                  cos_ref, sin_ref, hid_ref, kv_ref):
    frames, patches, _ = tok_ref.shape
    cols = wk_ref.shape[1]

    @pl.when(pl.program_id(0) == 0)
    def _():
        for f in range(frames):
            x = tok_ref[f].astype(f32)
            centre = x - jnp.mean(x, axis=1, keepdims=True)
            inv = lax.rsqrt(jnp.mean(centre * centre, axis=1, keepdims=True) + norm_eps)
            hid = centre * inv * (1.0 + scale_ref[f : f + 1, :]) + shift_ref[f : f + 1, :]
            hid_ref[f * patches : (f + 1) * patches, :] = hid.astype(bf16)

    keys = dot(hid_ref[...], wk_ref[...]) + bk_ref[...]
    vals = (dot(hid_ref[...], wv_ref[...]) + bv_ref[...]).astype(bf16)
    for p in range(cols // LANES):
        lanes = slice(p * LANES, (p + 1) * LANES)
        kv_ref[p, 0] = rotate_lanes(keys[:, lanes], cos_ref[...], sin_ref[...]).astype(bf16)
        kv_ref[p, 1] = vals[:, lanes]


def query_kernel(hid_ref, wq_ref, bq_ref, cos_ref, sin_ref, q_ref):
    query = dot(hid_ref[...], wq_ref[...]) + bq_ref[...]
    for p in range(wq_ref.shape[1] // LANES):
        lanes = slice(p * LANES, (p + 1) * LANES)
        q_ref[p] = rotate_lanes(query[:, lanes], cos_ref[...], sin_ref[...]).astype(bf16)


def whole(shape):
    return pl.BlockSpec(shape, lambda *_: (0,) * len(shape))


def project(tokens, shift_one, scale_one, qkv_weight, qkv_bias, cosine, sine, cols=512):
    frames, patches, width = tokens.shape
    rows = frames * patches
    pairs = width // LANES
    steps, some = width // cols, cols // LANES

    def column(part):
        return lambda c: (0, part * steps + c)

    hidden, keyvals = pl.pallas_call(
        keyval_kernel,
        out_shape=[
            jax.ShapeDtypeStruct((rows, width), bf16),
            jax.ShapeDtypeStruct((pairs, 2, rows, LANES), bf16),
        ],
        grid=(steps,),
        in_specs=[
            whole(tokens.shape),
            whole(shift_one.shape),
            whole(scale_one.shape),
            pl.BlockSpec((width, cols), column(1)),
            pl.BlockSpec((width, cols), column(2)),
            pl.BlockSpec((1, cols), column(1)),
            pl.BlockSpec((1, cols), column(2)),
            whole((rows, LANES)),
            whole((rows, LANES)),
        ],
        out_specs=[
            whole((rows, width)),
            pl.BlockSpec((some, 2, rows, LANES), lambda c: (c, 0, 0, 0)),
        ],
        compiler_params=pltpu.CompilerParams(vmem_limit_bytes=40 * MIB),
        cost_estimate=pl.CostEstimate(
            flops=4 * rows * width * width, bytes_accessed=8 * MIB, transcendentals=0
        ),
        name="project_keyval",
    )(tokens, shift_one, scale_one, qkv_weight, qkv_weight, qkv_bias, qkv_bias, cosine, sine)
    queries = pl.pallas_call(
        query_kernel,
        out_shape=jax.ShapeDtypeStruct((pairs, rows, LANES), bf16),
        grid=(steps,),
        in_specs=[
            whole((rows, width)),
            pl.BlockSpec((width, cols), column(0)),
            pl.BlockSpec((1, cols), column(0)),
            whole((rows, LANES)),
            whole((rows, LANES)),
        ],
        out_specs=pl.BlockSpec((some, rows, LANES), lambda c: (c, 0, 0)),
        compiler_params=pltpu.CompilerParams(vmem_limit_bytes=40 * MIB),
        cost_estimate=pl.CostEstimate(
            flops=2 * rows * width * width, bytes_accessed=4 * MIB, transcendentals=0
        ),
        name="project_query",
    )(hidden, qkv_weight, qkv_bias, cosine, sine)
    return hidden, keyvals, queries


def key_extra(first_frame, rows, patches):
    row = lax.broadcasted_iota(jnp.int32, (rows, LANES), 0)
    lane = lax.broadcasted_iota(jnp.int32, (rows, LANES), 1)
    hit = (lane == first_frame + row // patches) | ((lane >= FRAMES) & (lane < FRAMES + 3))
    return jnp.where(hit, 1.0, 0.0).astype(bf16)


def split_three(column):
    high = column.astype(bf16).astype(f32)
    rest = column - high
    mid = rest.astype(bf16).astype(f32)
    return high, mid, rest - mid


def attend_kernel(part, rows_part, patches, joined, chunk, q_ref, vis_ref, kv_ref, o_ref, ext_ref,
                  key_all, val_all):
    blocks, rows, _ = q_ref.shape
    frames, frames_part = rows // patches, rows_part // patches
    for b in range(blocks):
        here = slice(b * rows, (b + 1) * rows)
        key_all[here, :LANES] = kv_ref[b, 0]
        key_all[here, LANES:] = key_extra((b // 2) * frames, rows, patches)
        val_all[here, :LANES] = kv_ref[b, 1]
        val_all[here, LANES:] = jnp.full((rows, LANES), 1.0, bf16)
    tile = joined * rows_part
    lane = lax.broadcasted_iota(jnp.int32, (tile, LANES), 1)
    mine_rows = slice(part * rows_part, (part + 1) * rows_part)

    def step(t, carry):
        query = jnp.concatenate([q_ref[t * joined + i, mine_rows, :] for i in range(joined)], axis=0)
        query = query * score_scale
        seen = jnp.concatenate(
            [
                jnp.broadcast_to(
                    vis_ref[pl.ds((t * joined + i) * frames + part * frames_part + f, 1), :],
                    (patches, LANES),
                )
                for i in range(joined)
                for f in range(frames_part)
            ],
            axis=0,
        )
        outs, ext_heads = [], []
        for h in range(2):
            mine = jnp.where((lane >= HDIM) == (h == 1), query, jnp.zeros_like(query))
            query_ext = jnp.concatenate([mine.astype(bf16), seen.astype(bf16)], axis=1)
            top = None
            for c in range(blocks * rows // chunk):
                keys_here = slice(c * chunk, (c + 1) * chunk)
                scores = dot(query_ext, key_all[keys_here, :], NT)
                chunk_top = jnp.max(scores, axis=1, keepdims=True)
                new_top = chunk_top if top is None else jnp.maximum(top, chunk_top)
                some = dot(jnp.exp(scores - new_top).astype(bf16), val_all[keys_here, :])
                total = some if top is None else total * jnp.exp(top - new_top) + some
                top = new_top
            weight_sum = total[:, LANES : LANES + 1]
            outs.append(total[:, :LANES] / weight_sum)
            high, mid, low = split_three(-(top + jnp.log(weight_sum)))
            ext = jnp.where(lane == FRAMES, high, seen)
            ext = jnp.where(lane == FRAMES + 1, mid, ext)
            ext_heads.append(jnp.where(lane == FRAMES + 2, low, ext).astype(bf16))
        out = jnp.where(lane < HDIM, outs[0], outs[1]).astype(bf16)
        for i in range(joined):
            here = slice(i * rows_part, (i + 1) * rows_part)
            o_ref[t * joined + i] = out[here, :]
            for h in range(2):
                ext_ref[h, t * joined + i] = ext_heads[h][here, :]
        return carry

    lax.fori_loop(0, blocks // joined, step, 0)


def attend(queries, visible, keyvals, patches, part, parts, tile=512, chunk=1024):
    blocks, rows, _ = queries.shape
    rows_part = rows // parts
    keys = blocks * rows
    return pl.pallas_call(
        functools.partial(attend_kernel, part, rows_part, patches, tile // rows_part, chunk),
        out_shape=[
            jax.ShapeDtypeStruct((blocks, rows_part, LANES), bf16),
            jax.ShapeDtypeStruct((2, blocks, rows_part, LANES), bf16),
        ],
        in_specs=[pl.BlockSpec(memory_space=VMEM)] * 3,
        out_specs=[pl.BlockSpec(memory_space=VMEM)] * 2,
        scratch_shapes=[VMEM((keys, 2 * LANES), bf16), VMEM((keys, 2 * LANES), bf16)],
        compiler_params=pltpu.CompilerParams(vmem_limit_bytes=48 * MIB),
        cost_estimate=pl.CostEstimate(
            flops=8 * blocks * rows_part * keys * 2 * LANES,
            bytes_accessed=4 * MIB,
            transcendentals=0,
        ),
        name="attend",
    )(queries, visible, keyvals)


def attend_back_kernel(parts, part, patches, chunk, carried, last, *refs):
    at = 0

    def take(count):
        nonlocal at
        found = refs[at : at + count]
        at += count
        return found

    (q_ref, kv_ref, do_ref) = take(3)
    ext_refs, o_refs = take(parts), take(parts)
    ctime_ref, stime_ref, cpatch_ref, spatch_ref = take(4)
    carry_ref = take(1)[0] if carried else None
    (dkv_ref, dq_ref) = take(2)
    q_all, do_all, key_all, val_all, key_turned, dq_turned = refs[at:]
    blocks, rows, _ = q_ref.shape
    rows_part = rows // parts
    frames, frames_part = rows // patches, rows_part // patches
    queries = blocks * rows
    lane = lax.broadcasted_iota(jnp.int32, (rows_part, LANES), 1)
    for b in range(blocks):
        for i in range(parts):
            here = slice(b * rows + i * rows_part, b * rows + (i + 1) * rows_part)
            there = slice(i * rows_part, (i + 1) * rows_part)
            query = q_ref[b, there, :] * score_scale
            grad = do_ref[b, there, :]
            mixed = grad.astype(f32) * o_refs[i][b].astype(f32)
            for h in range(2):
                mine = (lane >= HDIM) == (h == 1)
                q_all[h, here, :LANES] = jnp.where(mine, query, jnp.zeros_like(query)).astype(bf16)
                q_all[h, here, LANES:] = ext_refs[i][h, b]
                do_all[h, here, :LANES] = jnp.where(mine, grad, jnp.zeros_like(grad))
                row_mix = jnp.sum(jnp.where(mine, mixed, 0.0), axis=1, keepdims=True)
                high, mid, low = split_three(-row_mix)
                ext = jnp.where(lane == 1, mid, jnp.where(lane == 2, low, 0.0))
                do_all[h, here, LANES:] = jnp.where(lane == 0, high, ext).astype(bf16)
    if carried:
        dq_turned[...] = carry_ref[...]
    else:
        dq_turned[...] = jnp.zeros_like(dq_turned)
    key_rows = slice(part * rows_part, (part + 1) * rows_part)
    for b in range(blocks):
        here = slice(b * rows_part, (b + 1) * rows_part)
        keys = kv_ref[b, 0, key_rows, :]
        key_all[here, :LANES] = keys
        key_all[here, LANES:] = key_extra((b // 2) * frames + part * frames_part, rows_part, patches)
        val_all[here, :LANES] = kv_ref[b, 1, key_rows, :]
        val_all[here, LANES:] = jnp.where(lane < 3, 1.0, 0.0).astype(bf16)
        key_turned[b] = keys.astype(f32).T.astype(bf16)

    def back(value, row, half):
        cosine = ctime_ref[pl.ds(row, 1), :] + cpatch_ref[half]
        sine = stime_ref[pl.ds(row, 1), :] + spatch_ref[half]
        return rotate_lanes(value, cosine, -sine).astype(bf16)

    def step(t, carry):
        here = pl.ds(pl.multiple_of(t * rows_part, rows_part), rows_part)
        key_tile = key_all[here, :]
        val_tile = val_all[here, :]
        turned = key_turned[t]
        dk = jnp.zeros((rows_part, LANES), f32)
        dv = jnp.zeros((rows_part, LANES), f32)
        for c in range(queries // chunk):
            span = slice(c * chunk, (c + 1) * chunk)
            for h in range(2):
                query = q_all[h, span, :]
                grad = do_all[h, span, :]
                probs = jnp.exp(dot(key_tile, query, NT))
                dv = dv + dot(probs.astype(bf16), grad[:, :LANES])
                grad_scores = (probs * dot(val_tile, grad, NT)).astype(bf16)
                dk = dk + dot(grad_scores, query[:, :LANES])
                head = slice(HDIM * h, HDIM * (h + 1))
                dq_turned[head, span] += dot(turned[head, :], grad_scores)
        for f in range(frames_part):
            rows_here = slice(f * patches, (f + 1) * patches)
            row = t * frames + part * frames_part + f
            dkv_ref[t, 0, rows_here, :] = back(dk[rows_here, :], row, t % 2)
        dkv_ref[t, 1] = dv.astype(bf16)
        return carry

    lax.fori_loop(0, blocks, step, 0)

    if last:
        for b in range(blocks):
            for f in range(frames):
                there = slice(b * rows + f * patches, b * rows + (f + 1) * patches)
                turned_back = back(dq_turned[:, there].T * score_scale, b * frames + f, b % 2)
                dq_ref[b, f * patches : (f + 1) * patches, :] = turned_back
    else:
        dq_ref[...] = dq_turned[...]


def attend_back(queries, keyvals, grads, exts, outs, rotary, carry, part, last, patches, chunk=1024):
    parts = len(exts)
    blocks, rows, _ = queries.shape
    rows_part = rows // parts
    total = blocks * rows
    carried = carry is not None
    operands = [queries, keyvals, grads, *exts, *outs, *rotary] + ([carry] if carried else [])
    dq_shape = jax.ShapeDtypeStruct((LANES, total), f32)
    if last:
        dq_shape = jax.ShapeDtypeStruct((blocks, rows, LANES), bf16)
    return pl.pallas_call(
        functools.partial(attend_back_kernel, parts, part, patches, chunk, carried, last),
        out_shape=[jax.ShapeDtypeStruct((blocks, 2, rows_part, LANES), bf16), dq_shape],
        in_specs=[pl.BlockSpec(memory_space=VMEM)] * len(operands),
        out_specs=[pl.BlockSpec(memory_space=VMEM)] * 2,
        scratch_shapes=[
            VMEM((2, total, 2 * LANES), bf16),
            VMEM((2, total, 2 * LANES), bf16),
            VMEM((blocks * rows_part, 2 * LANES), bf16),
            VMEM((blocks * rows_part, 2 * LANES), bf16),
            VMEM((blocks, LANES, rows_part), bf16),
            VMEM((LANES, total), f32),
        ],
        compiler_params=pltpu.CompilerParams(vmem_limit_bytes=56 * MIB),
        cost_estimate=pl.CostEstimate(
            flops=20 * total * blocks * rows_part * 2 * LANES,
            bytes_accessed=8 * MIB,
            transcendentals=0,
        ),
        name="attend_back",
    )(*operands)


def feed_kernel(hid_ref, grad_ref, up_ref, bias_ref, down_ref,
                branch_ref, back_ref, biasgrad_ref, joined_ref,
                hid_turned, up_slots, down_slots, up_sems, down_sems):
    step, steps = pl.program_id(0), pl.num_programs(0)
    width, cols = up_ref.shape
    devices, _, share, _ = joined_ref.shape
    quarters = down_slots.shape[2]
    dests = down_slots.shape[1]
    up_parts = width // cols
    slot = step % 2

    def copies(at):
        across = pl.ds(pl.multiple_of((at % up_parts) * cols, cols), cols)
        up_copy = pltpu.make_async_copy(
            up_slots.at[at % 2], joined_ref.at[:, at // up_parts, :, across], up_sems.at[at % 2]
        )
        down_copy = pltpu.make_async_copy(
            down_slots.at[at % 2],
            joined_ref.at[pl.ds(at * dests, dests), quarters : 2 * quarters],
            down_sems.at[at % 2],
        )
        return up_copy, down_copy

    @pl.when(step == 0)
    def _():
        hid_turned[...] = hid_ref[...].T

    pre = dot(hid_ref[...], up_ref[...]) + bias_ref[...]
    square = pre * pre
    bend = jnp.tanh(0.7978845608 * (pre + 0.044715 * pre * square))
    act = (0.5 * pre * (1.0 + bend)).astype(bf16)
    slope = 0.5 * (1.0 + bend) + 0.5 * pre * (1.0 - bend * bend) * (
        0.7978845608 * (1.0 + 3.0 * 0.044715 * square)
    )
    branch = dot(act, down_ref[...])
    pre_grad = (slope * dot(grad_ref[...], down_ref[...], NT)).astype(bf16)
    biasgrad_ref[...] = jnp.sum(pre_grad.astype(f32), axis=0, keepdims=True)
    back = dot(pre_grad, up_ref[...], NT)

    @pl.when(step == 0)
    def _():
        branch_ref[...] = branch
        back_ref[...] = back

    @pl.when(step > 0)
    def _():
        branch_ref[...] += branch
        back_ref[...] += back

    @pl.when(step >= 2)
    def _():
        for copy in copies(step - 2):
            copy.wait()

    up_grad = dot(hid_turned[...], pre_grad).astype(bf16)
    up_slots[slot] = up_grad.reshape(devices, share, cols)
    down_grad = dot(act.T, grad_ref[...]).astype(bf16)
    down_slots[slot] = down_grad.reshape(dests, quarters, share, width)
    for copy in copies(step):
        copy.start()

    @pl.when(step == steps - 1)
    def _():
        for at in (steps - 2, steps - 1):
            for copy in copies(at):
                copy.wait()


def feed_forward(hidden, grad, up_weight, up_bias, down_weight, devices, cols=512):
    rows, width = hidden.shape
    inner = up_weight.shape[1]
    share, quarters = width // devices, inner // width
    dests = cols * devices // inner
    return pl.pallas_call(
        feed_kernel,
        out_shape=[
            jax.ShapeDtypeStruct((rows, width), f32),
            jax.ShapeDtypeStruct((rows, width), f32),
            jax.ShapeDtypeStruct((1, inner), f32),
            jax.ShapeDtypeStruct((devices, 2 * quarters + 1, share, width), bf16),
        ],
        grid=(inner // cols,),
        in_specs=[
            whole((rows, width)),
            whole((rows, width)),
            pl.BlockSpec((width, cols), lambda c: (0, c)),
            pl.BlockSpec((1, cols), lambda c: (0, c)),
            pl.BlockSpec((cols, width), lambda c: (c, 0)),
        ],
        out_specs=[
            whole((rows, width)),
            whole((rows, width)),
            pl.BlockSpec((1, cols), lambda c: (0, c)),
            pl.BlockSpec(memory_space=pl.ANY),
        ],
        scratch_shapes=[
            VMEM((width, rows), bf16),
            VMEM((2, devices, share, cols), bf16),
            VMEM((2, dests, quarters, share, width), bf16),
            pltpu.SemaphoreType.DMA((2,)),
            pltpu.SemaphoreType.DMA((2,)),
        ],
        compiler_params=pltpu.CompilerParams(vmem_limit_bytes=56 * MIB),
        cost_estimate=pl.CostEstimate(
            flops=12 * rows * width * inner, bytes_accessed=36 * MIB, transcendentals=0
        ),
        name="feed_forward",
    )(hidden, grad, up_weight, up_bias, down_weight)


def proj_grad_kernel(attn_ref, grad_ref, _, joined_ref):
    devices, _, share, width = joined_ref.shape
    joined_ref[...] = dot(attn_ref[...].T, grad_ref[...]).astype(bf16).reshape(
        devices, 1, share, width
    )


def proj_weight_grad(attn_low, grad_proj, joined, steps=2):
    rows, width = attn_low.shape
    devices, entries, share, _ = joined.shape
    return pl.pallas_call(
        proj_grad_kernel,
        out_shape=jax.ShapeDtypeStruct(joined.shape, joined.dtype),
        grid=(steps,),
        in_specs=[
            pl.BlockSpec((rows, width // steps), lambda c: (0, c)),
            whole((rows, width)),
            pl.BlockSpec(memory_space=pl.ANY),
        ],
        out_specs=pl.BlockSpec(
            (devices // steps, 1, share, width), lambda c: (c, entries - 1, 0, 0)
        ),
        input_output_aliases={2: 0},
        compiler_params=pltpu.CompilerParams(vmem_limit_bytes=40 * MIB),
        cost_estimate=pl.CostEstimate(
            flops=2 * rows * width * width, bytes_accessed=4 * MIB, transcendentals=0
        ),
        name="proj_weight_grad",
    )(attn_low, grad_proj, joined)


def layer_norm(values_in):
    centre = values_in - jnp.mean(values_in, axis=-1, keepdims=True)
    inv_scale = lax.rsqrt(jnp.mean(centre * centre, axis=-1, keepdims=True) + norm_eps)
    return (centre * inv_scale, inv_scale)


def norm_back(grad_in, normed, inv_scale):
    mean_grad = jnp.mean(grad_in, axis=-1, keepdims=True)
    mean_mix = jnp.mean(grad_in * normed, axis=-1, keepdims=True)
    return inv_scale * (grad_in - mean_grad - normed * mean_mix)


def body(
    tokens,
    out_cotangent,
    level_embed,
    ada_weight,
    ada_bias,
    qkv_weight,
    qkv_bias,
    proj_weight,
    proj_bias,
    up_weight,
    up_bias,
    down_weight,
    down_bias,
    context_count,
    frame_level,
    slot_time,
):
    frames, patches, width = tokens.shape
    rows = frames * patches
    inner = up_weight.shape[1]
    frm_count, sp_count = lax.axis_size("frm"), lax.axis_size("sp")
    devices = frm_count * sp_count
    group = FRAMES // frames * sp_count
    clips = devices // group
    frm, sp = lax.axis_index("frm"), lax.axis_index("sp")
    me = frm * sp_count + sp
    clip = me // group
    clip_groups = [list(range(first, first + group)) for first in range(0, devices, group)]
    everyone = [list(range(devices))]
    halves = 2
    share = width // devices
    per_dest = inner // devices

    levels_here = level_embed.shape[0]
    embed_all = to_everyone(level_embed, devices).reshape(devices * levels_here, width)

    clip_times = lax.dynamic_slice_in_dim(slot_time, clip * FRAMES, FRAMES)
    clip_levels = lax.dynamic_index_in_dim(frame_level, clip, 0, keepdims=False)
    context = lax.dynamic_index_in_dim(context_count, clip, 0, keepdims=False)
    seen = (clip_times[None, :] <= clip_times[:, None]) | (clip_times[None, :] < context)
    visible = jnp.pad(
        jnp.where(seen, 0.0, masked_out).astype(f32), ((0, 0), (0, LANES - FRAMES))
    )

    def by_blocks(table):
        table = table.reshape(FRAMES // frames, 1, frames, LANES)
        return jnp.broadcast_to(table, (FRAMES // frames, sp_count, frames, LANES)).reshape(
            group * frames, LANES
        )

    visible = by_blocks(visible)
    freq, sign, time_lane, row_lane = rotary_lanes()
    angle_time = clip_times.astype(f32)[:, None] * freq[None, :]
    ctime = by_blocks(jnp.where(time_lane[None, :], jnp.cos(angle_time), 0.0))
    stime = by_blocks(jnp.where(time_lane[None, :], jnp.sin(angle_time) * sign[None, :], 0.0))
    patch_ids = jnp.arange(sp_count * patches, dtype=jnp.int32).reshape(sp_count, patches)
    place = jnp.where(
        row_lane[None, None, :], (patch_ids // GRID)[..., None], (patch_ids % GRID)[..., None]
    )
    angle_patch = place.astype(f32) * freq[None, None, :]
    cpatch = jnp.where(time_lane, 0.0, jnp.cos(angle_patch))
    spatch = jnp.where(time_lane, 0.0, jnp.sin(angle_patch) * sign)
    rotary = [ctime, stime, cpatch, spatch]

    def my_table(time_part, patch_part):
        mine = lax.dynamic_slice_in_dim(time_part, me % group * frames, frames)
        half = lax.dynamic_index_in_dim(patch_part, sp, 0, keepdims=False)
        return (mine[:, None, :] + half[None]).reshape(rows, LANES)

    cosine, sine = my_table(ctime, cpatch), my_table(stime, spatch)

    my_times = lax.dynamic_slice_in_dim(slot_time, frm * frames, frames)
    my_levels = jnp.take(clip_levels, my_times)
    embed_act = jax.nn.silu(embed_all.astype(f32)).astype(bf16)
    level_ids = jnp.arange(devices * levels_here, dtype=jnp.int32)
    pick = (my_levels[:, None] == level_ids[None, :]).astype(bf16)
    my_embed = dot(pick, embed_act).astype(bf16)
    frame_mod = dot(my_embed, ada_weight) + ada_bias.astype(f32)
    frame_mod = lax.reduce_precision(frame_mod, 8, 7)
    mod_parts = [frame_mod[:, i * width : (i + 1) * width] for i in range(6)]
    shift_one, scale_one = mod_parts[0], mod_parts[1]
    gate_one, shift_two, scale_two, gate_two = [part[:, None, :] for part in mod_parts[2:]]

    hidden_one, keyval_parts, query_parts = project(
        tokens, shift_one, scale_one, qkv_weight, qkv_bias.astype(f32)[None, :], cosine, sine
    )
    keyvals = exchange(keyval_parts, clip_groups)
    queries = exchange(query_parts, clip_groups)
    outs, exts, attended = [], [], []
    for part in range(halves):
        out, ext = attend(queries, visible, keyvals, patches, part, halves)
        outs.append(out)
        exts.append(ext)
        attended.append(exchange(out, clip_groups))

    hidden_own, _ = lax.optimization_barrier((hidden_one, queries))
    hidden_clip = lax.all_gather(hidden_own, AXES, axis_index_groups=clip_groups).reshape(
        group * rows, width
    )

    attn_low = jnp.concatenate(
        [part.transpose(1, 0, 2).reshape(rows // halves, width) for part in attended], axis=0
    )
    attn_proj = (dot(attn_low, proj_weight) + proj_bias.astype(f32)).reshape(
        frames, patches, width
    )
    inputs = tokens.astype(f32)
    after_attn = inputs + gate_one * attn_proj
    normed_two, rscale_two = layer_norm(after_attn)
    hidden_two = (
        (normed_two * (1.0 + scale_two) + shift_two).astype(bf16).reshape(rows, width)
    )
    grad_out = out_cotangent.astype(f32)
    grad_branch = (gate_two * grad_out).astype(bf16).reshape(rows, width)
    branch, grad_hidden_two, up_b_grad, joined = feed_forward(
        hidden_two, grad_branch, up_weight, up_bias.astype(f32)[None, :], down_weight, devices
    )

    grad_hidden_two = grad_hidden_two.reshape(frames, patches, width)
    grad_after = grad_out + norm_back(grad_hidden_two * (1.0 + scale_two), normed_two, rscale_two)
    grad_proj = (gate_one * grad_after).astype(bf16).reshape(rows, width)
    grad_parts = dot(grad_proj, proj_weight, NT).astype(bf16)
    grad_parts = grad_parts.reshape(rows, group, LANES).transpose(1, 0, 2)
    grads = exchange(grad_parts, clip_groups)

    joined = proj_weight_grad(attn_low, grad_proj, joined)
    summed = lax.psum_scatter(joined, AXES, scatter_dimension=0, tiled=True)[0].astype(f32)
    quarters = inner // width
    up_w_out = jnp.concatenate([summed[i] for i in range(quarters)], axis=1)
    down_w_out = summed[quarters : 2 * quarters].reshape(per_dest, width)
    proj_w_out = summed[2 * quarters]

    branch_out = (branch + down_bias.astype(f32)).reshape(frames, patches, width)
    block_out = (after_attn + gate_two * branch_out).astype(bf16)
    early_sums = jnp.concatenate(
        [
            jnp.sum(grad_after * attn_proj, axis=1),
            jnp.sum(grad_hidden_two, axis=1),
            jnp.sum(grad_hidden_two * normed_two, axis=1),
            jnp.sum(grad_out * branch_out, axis=1),
        ],
        axis=1,
    )

    def share_out(slot_sums, biases):
        high = biases.astype(bf16)
        low = (biases - high.astype(f32)).astype(bf16)
        sums = slot_sums.astype(bf16).reshape(1, -1)
        sums = jnp.broadcast_to(sums, (devices, sums.shape[1]))
        got = exchange(jnp.concatenate([sums, high, low], axis=1), everyone).astype(f32)
        count = slot_sums.size
        extra = jnp.sum(got[:, count:], axis=0)
        size = biases.shape[1]
        return (
            got[:, :count].reshape(devices * frames, -1).astype(bf16),
            extra[:size] + extra[size:],
        )

    early_biases = jnp.concatenate(
        [
            up_b_grad.reshape(devices, per_dest),
            jnp.sum(grad_proj.astype(f32), axis=0).reshape(devices, share),
            jnp.sum(grad_branch.astype(f32), axis=0).reshape(devices, share),
        ],
        axis=1,
    )
    early_slots, early_bias_out = share_out(early_sums, early_biases)
    up_b_out = early_bias_out[:per_dest]
    proj_b_out = early_bias_out[per_dest : per_dest + share]
    down_b_out = early_bias_out[per_dest + share :]
    slot_ids = (jnp.arange(devices * frames, dtype=jnp.int32) // (sp_count * frames)) * frames
    slot_ids = slot_ids + jnp.arange(devices * frames, dtype=jnp.int32) % frames
    slot_levels = frame_level[slot_ids // FRAMES, slot_time[slot_ids]]
    member_of = (level_ids[:, None] == slot_levels[None, :]).astype(bf16)
    my_columns = lax.dynamic_slice_in_dim(embed_act, me * share, share, axis=1)

    def level_out(slots):
        level_grad = dot(member_of, slots).astype(bf16)
        return dot(my_columns, level_grad, TN), jnp.sum(level_grad.astype(f32), axis=0)

    early_w, early_b = level_out(early_slots)

    carry = None
    own_keyvals, grad_keyvals = [], []
    for part in range(halves):
        some, carry = attend_back(
            queries, keyvals, grads, exts, outs, rotary, carry, part, part == halves - 1, patches
        )
        grad_keyvals.append(some)
        own_keyvals.append(exchange(some, clip_groups))
    grad_queries = carry
    own_queries = exchange(grad_queries, clip_groups)

    grad_keyval = jnp.concatenate(grad_keyvals, axis=2)
    grad_heads = jnp.concatenate(
        [grad_queries, grad_keyval[:, 0], grad_keyval[:, 1]], axis=2
    ).reshape(group * rows, 3 * LANES)
    qkv_part = dot(hidden_clip, grad_heads, TN).astype(bf16)
    qkv_got = exchange(qkv_part.reshape(devices, share, 3 * LANES), everyone)
    qkv_w_out = (
        jnp.sum(qkv_got.reshape(clips, group, share, 3 * LANES).astype(f32), axis=0)
        .reshape(group, share, 3, LANES)
        .transpose(1, 2, 0, 3)
        .reshape(share, 3 * width)
    )

    def to_rows(value):
        return value.transpose(1, 0, 2).reshape(value.shape[1], width)

    grad_rows = jnp.concatenate(
        [
            to_rows(own_queries),
            jnp.concatenate([to_rows(part[:, 0]) for part in own_keyvals], axis=0),
            jnp.concatenate([to_rows(part[:, 1]) for part in own_keyvals], axis=0),
        ],
        axis=1,
    )
    grad_hidden_one = dot(grad_rows, qkv_weight, NT).reshape(frames, patches, width)
    normed_one, rscale_one = layer_norm(inputs)
    late_sums = jnp.concatenate(
        [jnp.sum(grad_hidden_one, axis=1), jnp.sum(grad_hidden_one * normed_one, axis=1)], axis=1
    )
    tokens_grad = (
        grad_after
        + norm_back(grad_hidden_one * (1.0 + scale_one[:, None, :]), normed_one, rscale_one)
    ).astype(bf16)
    late_slots, qkv_b_out = share_out(
        late_sums, jnp.sum(grad_rows.astype(f32), axis=0).reshape(devices, 3 * share)
    )
    late_w, late_b = level_out(late_slots)
    ada_w_out = jnp.concatenate([late_w, early_w], axis=1)
    ada_b_all = jnp.concatenate([late_b, early_b])
    ada_share = ada_b_all.shape[0] // devices
    ada_b_out = lax.dynamic_slice_in_dim(ada_b_all, me * ada_share, ada_share)
    return (
        block_out,
        tokens_grad,
        ada_w_out,
        ada_b_out,
        qkv_w_out,
        qkv_b_out,
        proj_w_out,
        proj_b_out,
        up_w_out,
        up_b_out,
        down_w_out,
        down_b_out,
    )


def solution(mesh):
    tokens_spec = P("frm", "sp", None)
    rows_spec = P(AXES, None)
    vector_spec = P(AXES)
    return jax.shard_map(
        body,
        mesh=mesh,
        in_specs=(tokens_spec, tokens_spec, rows_spec) + (P(),) * 13,
        out_specs=(tokens_spec, tokens_spec) + (rows_spec, vector_spec) * 5,
        check_vma=False,
    )
```

time: 2960 us -> 590 us (0.20)
  waiting for transfers between devices: 994 us -> 86.4 us
  local copies, waits for them, and re-layouts: 862 us -> 66.1 us
  matrix products: 580 us -> 31.1 us
  other arithmetic: 306 us -> 47.5 us
  Pallas kernels: 0 us -> 213 us
  blocking collectives: 171 us -> 84.5 us
    unnamed x147 -> x107, local copies, waits for them, and re-layouts: 674 us -> 35.8 us
    dot_general x128 -> x9, matrix products: 580 us -> 31.1 us  [dot(): return lax.dot_general(left_op, right_op, dims, preferred_element_type=f32)]
    ppermute x4 -> x0, waiting for transfers between devices: 514 us -> none  [from_partner(): return lax.ppermute(value, axis, pairs)]
    reduce_scatter x5 -> x1, waiting for transfers between devices: 471 us -> 0.01 us  [body(): lax.psum_scatter(joined, AXES, scatter_dimension=0, tiled=True)[0]]
    pallas_call x0 -> x8, Pallas kernels: none -> 213 us  [the longest x2 112 us: attend_back(): pl.pallas_call(functools.partial(attend_back_kernel, parts, part, patches...]
    convert_element_type x27 -> x10, other arithmetic: 150 us -> 4.55 us  [the longest x1 1.64 us: body(): (normed_two * (1.0 + scale_two) + shift_two).astype(bf16)]
    unnamed x2 -> x0, blocking collectives: 123 us -> none
    all_to_all x0 -> x8, waiting for transfers between devices: none -> 86.4 us  [exchange(): return lax.all_to_all(value, AXES, 0, 0, axis_index_groups=groups)]
  transfers between devices with their start and end apart: 11 -> 10, of which waited for: 8 -> 6; matrix products, arithmetic and copies ran while one was open for 13% -> 19% of each run, Pallas kernels for 0% -> 35%
where the time goes in v1:
time: 590 us; the launch traced here: 582 us
  Pallas kernels  213 us (36%)
  waiting for transfers between devices  86.4 us (15%)
  blocking collectives  84.5 us (14%)
  local copies, waits for them, and re-layouts  66.1 us (11%)
  other arithmetic  47.5 us (8%)
  starting transfers between devices  36.4 us (6%)
  matrix products  31.1 us (5%)
  between operations  16.8 us (3%)
    pallas_call x2, Pallas kernels, attend_back(): pl.pallas_call(functools.partial(attend_back_kernel, parts, part, patches...  112 us
    all_to_all x8, waiting for transfers between devices, exchange(): return lax.all_to_all(value, AXES, 0, 0, axis_index_groups=groups)  86.4 us
    all_to_all x4, blocking collectives, exchange(): return lax.all_to_all(value, AXES, 0, 0, axis_index_groups=groups)  84.5 us
    pallas_call x2, Pallas kernels, attend(): pl.pallas_call(functools.partial(attend_kernel, part, rows_part, patches,...  49.9 us
    pallas_call x1, Pallas kernels, feed_forward(): pl.pallas_call(feed_kernel, out_shape=[jax.ShapeDtypeStruct((rows, width)...  39.8 us
    all_to_all x8, starting transfers between devices, exchange(): return lax.all_to_all(value, AXES, 0, 0, axis_index_groups=groups)  36.1 us
    unnamed x107, local copies, waits for them, and re-layouts  35.8 us
    dot_general x9, matrix products, dot(): return lax.dot_general(left_op, right_op, dims, preferred_element_type=f32)  31.1 us
  transfers between devices with their start and end apart: 10, of which 6 were waited for; matrix products, arithmetic and copies ran while one was open for 19% of the time, Pallas kernels for 35%

profile of v1, /device:TPU:0, one launch (start us, length us, event | category | flops | bytes accessed | tf_op | source)
XLA Modules:
  0.0 581.7 jit_solution(16286634050374573533)
XLA Ops:
  8.0 1.6 broadcast_in_dim.148
  9.6 7.3 %all-to-all-start = ((bf16[32,2,1024]{2,1,0:T(2,128)(2,1)}), bf16[32,2,1024]{2,1,0:T(2,128)(2,1)S(1)}, u32[]{:S(2)}, u32[]{:S(2)}) async-start(bf16[32,2,1024]{2,1,0:T(2,128)(2,1)} %broadcast_in_dim.148), calls=%async_computation | async-start | bytes 262144 | tf_op jit(solution)/shard_map/all_to_all | solution.py:37
  22.2 1.9 broadcast_compare_fusion.1
  25.0 1.5 multiply_select_fusion
  26.6 1.3 convert_element_type.148
  29.5 7.2 %fusion = f32[4,6144]{1,0:T(4,128)} fusion(bf16[1024,6144]{1,0:T(8,128)(2,1)} %param.27, bf16[64,1024]{1,0:T(8,128)(2,1)S(1)} %multiply_convert_fusion.1, f32[6144]{0:T(1024)} %convert_element_type.148, s32[4]{0:T(128)} %and_select_fusion.5), kind=kOutput, calls=%fused_computation.4 | convolution fusion | flops 50909440 | bytes 12836880 | tf_op jit(solution)/shard_map/dot_general | solution.py:33
  36.7 1.4 broadcast_add_fusion.3
  38.2 2.8 copy-done.2
  41.9 4.6 project_keyval.1
  47.5 1.3 copy-done.11
  48.8 2.8 copy-done.3
  53.8 3.6 project_query.1
  57.4 19.2 %all_to_all.68.q_ref.refs_0_ = bf16[8,512,128]{2,1,0:T(8,128)(2,1)} all-to-all(bf16[8,512,128]{2,1,0:T(8,128)(2,1)S(1)} %project_query.1), channel_id=1, replica_groups={{0,1,2,3,4,5,6,7},{8,9,10,11,12,13,14,15},{16,17,18,19,20,21,22,23},{24..., dimensions={0} | all-to-all | bytes 2097152 | tf_op jit(solution)/shard_map/all_to_all | solution.py:37
  76.7 4.7 all-to-all-start.2
  82.3 36.9 %all-to-all-done.2.kv_ref.refs_1_ = bf16[8,2,512,128]{3,2,1,0:T(8,128)(2,1)} async-done(((bf16[8,2,512,128]{3,2,1,0:T(8,128)(2,1)}), bf16[8,2,512,128]{3,2,1,0:T(8,128)(2,1)}, u32[]{:S(2)}, u32[]{:S(2)}) %all-to-all-start.2) | async-done | bytes 2097184 | tf_op jit(solution)/shard_map/all_to_all | solution.py:37
  120.5 24.9 %attend.2 = (bf16[8,256,128]{2,1,0:T(8,128)(2,1)S(1)}, bf16[2,8,256,128]{3,2,1,0:T(8,128)(2,1)S(1)}) custom-call(bf16[8,512,128]{2,1,0:T(8,128)(2,1)S(1)} %copy-done.12, f32[32,128]{1,0:T(8,128)S(1)} %bitcast.157, bf16[8,2,512,128]{3,2,1,0:T(8,128)(2,1)} %all-to-all-done.2.kv_ref.refs_1_), custom_call_target="tpu_custom_call" | custom-call | flops 17179869184 | bytes 4194304 | tf_op jit(solution)/shard_map/attend/pallas_call | solution.py:241
  147.2 4.4 all-to-all-start.3
  152.8 24.9 %attend.3 = (bf16[8,256,128]{2,1,0:T(8,128)(2,1)S(1)}, bf16[2,8,256,128]{3,2,1,0:T(8,128)(2,1)S(1)}) custom-call(bf16[8,512,128]{2,1,0:T(8,128)(2,1)S(1)} %copy-done.13, f32[32,128]{1,0:T(8,128)S(1)} %bitcast.158, bf16[8,2,512,128]{3,2,1,0:T(8,128)(2,1)} %all-to-all-done.2.kv_ref.refs_1_), custom_call_target="tpu_custom_call" | custom-call | flops 17179869184 | bytes 4194304 | tf_op jit(solution)/shard_map/attend/pallas_call | solution.py:241
  179.5 4.2 all-to-all-start.4
  184.0 3.1 convert_reduce_fusion.2
  187.1 1.9 bitcast_dynamic-update-slice_fusion.1
  189.0 4.5 all-to-all-done.4
  193.5 1.9 bitcast_dynamic-update-slice_fusion.attn_ref
  195.5 2.5 convolution_add_fusion.1
  200.0 1.6 add_convert_fusion.1
  201.6 39.8 %feed_forward.1 = (f32[512,1024]{1,0:T(8,128)}, f32[512,1024]{1,0:T(8,128)}, f32[1,4096]{1,0:T(1,128)}, bf16[32,9,32,1024]{3,2,1,0:T(8,128)(2,1)}) custom-call(bf16[512,1024]{1,0:T(8,128)(2,1)} %bitcast.185, bf16[512,1024]{1,0:T(8,128)(2,1)} %bitcast.184, bf16[1024,4096]{1,0:T(8,128)(2,1)} %up_ref.1, f32[1,4096]{1,0:T(1,128)} %bitcast.199, ...), custom_call_target="tpu_custom_call" | custom-call | flops 25769803776 | bytes 37748736 | tf_op jit(solution)/shard_map/feed_forward/pallas_call | solution.py:458
  241.5 1.9 fusion.22
  243.4 2.1 fusion.20
  246.4 2.4 convert_reduce_fusion.3
  248.8 2.6 proj_weight_grad.1
  251.4 2.3 convolution_convert_fusion.2
  253.7 1.5 copy.82
  255.8 19.0 %all_to_all.69.refs_2_ = bf16[8,512,128]{2,1,0:T(8,128)(2,1)} all-to-all(bf16[8,512,128]{2,1,0:T(8,128)(2,1)S(1)} %bitcast.169), channel_id=1, replica_groups={{0,1,2,3,4,5,6,7},{8,9,10,11,12,13,14,15},{16,17,18,19,20,21,22,23},{24..., dimensions={0} | all-to-all | bytes 2097152 | tf_op jit(solution)/shard_map/all_to_all | solution.py:37
  274.8 55.0 %attend_back.2 = (bf16[8,2,256,128]{3,2,1,0:T(8,128)(2,1)}, f32[128,4096]{1,0:T(8,128)}) custom-call(bf16[8,512,128]{2,1,0:T(8,128)(2,1)} %all_to_all.68.q_ref.refs_0_, bf16[8,2,512,128]{3,2,1,0:T(8,128)(2,1)} %all-to-all-done.2.kv_ref.refs_1_, bf16[8,512,128]{2,1,0:T(8,128)(2,1)} %all_to_all.69.refs_2_, bf16[2,8,256,128]{3,2,1,0:T(8,128)(2,1)} %copy-done.16, ...), custom_call_target="tpu_custom_call" | custom-call | flops 42949672960 | bytes 8388608 | tf_op jit(solution)/shard_map/attend_back/pallas_call | solution.py:362
  329.8 57.4 %attend_back.3 = (bf16[8,2,256,128]{3,2,1,0:T(8,128)(2,1)}, bf16[8,512,128]{2,1,0:T(8,128)(2,1)}) custom-call(bf16[8,512,128]{2,1,0:T(8,128)(2,1)} %all_to_all.68.q_ref.refs_0_, bf16[8,2,512,128]{3,2,1,0:T(8,128)(2,1)} %all-to-all-done.2.kv_ref.refs_1_, bf16[8,512,128]{2,1,0:T(8,128)(2,1)} %all_to_all.69.refs_2_, bf16[2,8,256,128]{3,2,1,0:T(8,128)(2,1)} %copy-done.16, ...), custom_call_target="tpu_custom_call" | custom-call | flops 42949672960 | bytes 8388608 | tf_op jit(solution)/shard_map/attend_back/pallas_call | solution.py:362
  387.2 26.5 %all_to_all.70 = bf16[8,2,256,128]{3,2,1,0:T(8,128)(2,1)S(1)} all-to-all(bf16[8,2,256,128]{3,2,1,0:T(8,128)(2,1)} %get-tuple-element.38), channel_id=1, replica_groups={{0,1,2,3,4,5,6,7},{8,9,10,11,12,13,14,15},{16,17,18,19,20,21,22,23},{24..., dimensions={0} | all-to-all | bytes 2097152 | tf_op jit(solution)/shard_map/all_to_all | solution.py:37
  413.7 19.8 %all_to_all.71 = bf16[8,2,256,128]{3,2,1,0:T(8,128)(2,1)S(1)} all-to-all(bf16[8,2,256,128]{3,2,1,0:T(8,128)(2,1)S(1)} %copy-done.24), channel_id=1, replica_groups={{0,1,2,3,4,5,6,7},{8,9,10,11,12,13,14,15},{16,17,18,19,20,21,22,23},{24..., dimensions={0} | all-to-all | bytes 2097152 | tf_op jit(solution)/shard_map/all_to_all | solution.py:37
  433.5 3.8 all-to-all-start.6
  438.6 1.2 copy.88
  440.9 1.3 copy.87
  442.2 2.1 copy.86
  445.3 7.4 %all-to-all-done.6 = bf16[8,512,128]{2,1,0:T(8,128)(2,1)S(1)} async-done(((bf16[8,512,128]{2,1,0:T(8,128)(2,1)}), bf16[8,512,128]{2,1,0:T(8,128)(2,1)S(1)}, u32[]{:S(2)}, u32[]{:S(2)}) %all-to-all-start.6) | async-done | bytes 1048608 | tf_op jit(solution)/shard_map/all_to_all | solution.py:37
  453.2 6.7 %fusion.21 = (f32[512]{0:T(512)S(1)}, f32[512,1024]{1,0:T(8,128)S(1)}) fusion(f32[4,1024]{1,0:T(4,128)S(1)} %copy-done.34, bf16[1024,3072]{1,0:T(8,128)(2,1)} %wq_ref.1, bf16[256,1024]{0,1:T(8,128)(2,1)S(1)} %bitcast.175, bf16[256,1024]{0,1:T(8,128)(2,1)S(1)} %bitcast.177, bf16[256,1024]{0,1:T(8,128)(2,1)} %bitcast.179, bf16[256,1024]{0,1:T(8,128)(2,1)} %bitcast.181, ...), kind=kOutput, calls=%fused_computation.36 | convolution fusion | flops 3238002176 | bytes 11552768 | tf_op jit(solution)/shard_map/dot_general | solution.py:33
  462.0 9.5 %convert_reduce_fusion = f32[3072]{0:T(1024)S(1)} fusion(bf16[256,1024]{0,1:T(8,128)(2,1)S(1)} %bitcast.176, bf16[256,1024]{0,1:T(8,128)(2,1)S(1)} %bitcast.178, bf16[256,1024]{0,1:T(8,128)(2,1)S(1)} %bitcast.180, bf16[256,1024]{0,1:T(8,128)(2,1)S(1)} %bitcast.182, bf16[512,1024]{0,1:T(8,128)(2,1)S(1)} %bitcast.167), kind=kLoop, calls=%fused_computation.5 | loop fusion | flops 17298432 | bytes 3158016 | tf_op jit(solution)/shard_map/reduce_sum | solution.py:766
  474.5 5.1 all-to-all-start.9
  479.7 4.8 multiply_reduce_fusion
  485.0 1.5 reduce.4
  486.5 1.9 reshape.579
  488.4 7.0 %all-to-all-done.9 = bf16[32,2,4192]{2,1,0:T(2,128)(2,1)S(1)} async-done(((bf16[32,2,4192]{2,1,0:T(2,128)(2,1)}), bf16[32,2,4192]{2,1,0:T(2,128)(2,1)S(1)}, u32[]{:S(2)}, u32[]{:S(2)}) %all-to-all-start.9) | async-done | bytes 536608 | tf_op jit(solution)/shard_map/all_to_all | solution.py:37
  495.4 3.1 all-to-all-start.10
  498.6 1.3 gather_fusion.1
  500.0 1.5 gather_fusion.2
  501.5 1.3 constant_dynamic-update-slice_fusion.1
  502.8 1.4 constant_dynamic-update-slice_fusion
  504.2 1.5 slice_bitcast_fusion.1
  505.7 3.9 reshape.582
  512.0 13.4 %all-to-all-done.10 = bf16[32,2,8384]{2,1,0:T(2,128)(2,1)S(1)} async-done(((bf16[32,2,8384]{2,1,0:T(2,128)(2,1)}), bf16[32,2,8384]{2,1,0:T(2,128)(2,1)S(1)}, u32[]{:S(2)}, u32[]{:S(2)}) %all-to-all-start.10) | async-done | bytes 1073184 | tf_op jit(solution)/shard_map/all_to_all | solution.py:37
  525.5 3.9 reshape.580
  529.3 1.7 copy.111
  532.1 1.9 convert_element_type.175
  534.6 9.9 %bitcast_convert_fusion = bf16[1024,384]{1,0:T(8,128)(2,1)} fusion(bf16[8,512,1024]{2,1,0:T(8,128)(2,1)} %bitcast.200, bf16[8,512,128]{2,1,0:T(8,128)(2,1)} %get-tuple-element.62, bf16[8,512,128]{2,1,0:T(8,128)(2,1)} %get-tuple-element.61, bf16[8,512,128]{2,1,0:T(8,128)(2,1)} %get-tuple-element.36), kind=kOutput, calls=%fused_computation.53 | convolution fusion | flops 3231055872 | bytes 12320768 | tf_op jit(solution)/shard_map/dot_general | solution.py:33
  544.5 3.6 all-to-all-start.11
  551.7 17.1 %all-to-all-done.11 = bf16[32,32,384]{2,1,0:T(8,128)(2,1)S(1)} async-done(((bf16[32,32,384]{2,1,0:T(8,128)(2,1)}), bf16[32,32,384]{2,1,0:T(8,128)(2,1)S(1)}, u32[]{:S(2)}, u32[]{:S(2)}) %all-to-all-start.11) | async-done | bytes 786464 | tf_op jit(solution)/shard_map/all_to_all | solution.py:37
  570.1 1.3 convert_element_type.182
  (187 shorter events, 43.5 us)
Async XLA Ops:
  8.0 187.4 %copy-start = (bf16[1024,1024]{1,0:T(8,128)(2,1)S(1)}, bf16[1024,1024]{1,0:T(8,128)(2,1)}, u32[]{:S(2)}) copy-start(bf16[1024,1024]{1,0:T(8,128)(2,1)} %param.31) | copy-start | bytes 6291460
  9.6 19.8 %all-to-all-start = ((bf16[32,2,1024]{2,1,0:T(2,128)(2,1)}), bf16[32,2,1024]{2,1,0:T(2,128)(2,1)S(1)}, u32[]{:S(2)}, u32[]{:S(2)}) async-start(bf16[32,2,1024]{2,1,0:T(2,128)(2,1)} %broadcast_in_dim.148), calls=%async_computation | async-start | bytes 262144 | tf_op jit(solution)/shard_map/all_to_all | solution.py:37
  16.9 517.8 %all-gather.3.cloned.1.call-start = ((), (), s32[]{:S(2)}) async-start(), calls=%async_computation.14 | async-start | bytes 9437184 | tf_op jit(solution)/shard_map/all_gather | solution.py:635
  26.5 2.9 copy-start.32
  26.5 2.9 copy-start.33
  26.5 2.1 copy-start.41
  26.5 2.1 copy-start.42
  29.5 7.2 %copy-start.30 = (bf16[64,1024]{1,0:T(8,128)(2,1)}, bf16[64,1024]{1,0:T(8,128)(2,1)S(1)}, u32[]{:S(2)}) copy-start(bf16[64,1024]{1,0:T(8,128)(2,1)S(1)} %multiply_convert_fusion.1) | copy-start | bytes 393220
  29.5 8.6 %copy-start.4 = (bf16[4,128,1024]{2,1,0:T(8,128)(2,1)S(1)}, bf16[4,128,1024]{2,1,0:T(8,128)(2,1)}, u32[]{:S(2)}) copy-start(bf16[4,128,1024]{2,1,0:T(8,128)(2,1)} %tok_ref.1) | copy-start | bytes 3145732
  38.2 2.8 copy-start.2
  41.0 0.9 copy-start.9
  46.5 1.0 copy-start.6
  47.5 1.3 copy-start.11
  48.8 2.8 copy-start.3
  51.6 1.2 copy-start.7
  52.8 0.9 copy-start.10
  76.7 4.7 copy-start.45
  76.7 4.7 copy-start.44
  76.7 5.3 copy-start.46
  76.7 5.3 copy-start.47
  76.7 42.5 %all-to-all-start.2 = ((bf16[8,2,512,128]{3,2,1,0:T(8,128)(2,1)}), bf16[8,2,512,128]{3,2,1,0:T(8,128)(2,1)}, u32[]{:S(2)}, u32[]{:S(2)}) async-start(bf16[8,2,512,128]{3,2,1,0:T(8,128)(2,1)} %copy-done.11), calls=%async_computation.2 | async-start | bytes 4194304 | tf_op jit(solution)/shard_map/all_to_all | solution.py:37
  82.3 115.6 %copy-start.39 = (f32[4,128]{1,0:T(4,128)}, f32[4,128]{1,0:T(4,128)S(1)}, u32[]{:S(2)}) copy-start(f32[4,128]{1,0:T(4,128)S(1)} %broadcast_multiply_fusion.1) | copy-start | bytes 6148
  119.2 1.2 copy-start.12
  145.4 0.8 copy-start.14
  146.2 1.0 copy-start.16
  147.2 32.3 %all-to-all-start.3 = ((bf16[8,256,128]{2,1,0:T(8,128)(2,1)}), bf16[8,256,128]{2,1,0:T(8,128)(2,1)}, u32[]{:S(2)}, u32[]{:S(2)}) async-start(bf16[8,256,128]{2,1,0:T(8,128)(2,1)} %copy-done.14), calls=%async_computation.3 | async-start | bytes 1048576 | tf_op jit(solution)/shard_map/all_to_all | solution.py:37
  151.6 1.2 copy-start.13
  152.8 31.2 %copy-start.35 = (f32[4,1024]{1,0:T(4,128)S(1)}, f32[4,1024]{1,0:T(4,128)}, u32[]{:S(2)}) copy-start(f32[4,1024]{1,0:T(4,128)} %get-tuple-element.79) | copy-start | bytes 49156
  177.7 0.8 copy-start.15
  178.5 1.0 copy-start.17
  179.5 14.0 %all-to-all-start.4 = ((bf16[8,256,128]{2,1,0:T(8,128)(2,1)}), bf16[8,256,128]{2,1,0:T(8,128)(2,1)}, u32[]{:S(2)}, u32[]{:S(2)}) async-start(bf16[8,256,128]{2,1,0:T(8,128)(2,1)} %copy-done.15), calls=%async_computation.4 | async-start | bytes 1048576 | tf_op jit(solution)/shard_map/all_to_all | solution.py:37
  183.7 386.4 %reduce-scatter.2.cloned.1.call-start = ((), (), s32[]{:S(2)}) async-start(), calls=%async_computation.13 | async-start | bytes 19464192 | tf_op jit(solution)/shard_map/reduce_scatter | solution.py:665
  195.5 2.5 copy-start.36
  198.0 1.3 copy-start.23
  199.3 0.7 copy-start.31
  199.3 0.7 copy-start.37
  241.5 1.9 copy-start.22
  243.4 2.2 copy-start.20
  246.4 2.4 copy-start.8
  387.2 26.5 %copy-start.24 = (bf16[8,2,256,128]{3,2,1,0:T(8,128)(2,1)S(1)}, bf16[8,2,256,128]{3,2,1,0:T(8,128)(2,1)}, u32[]{:S(2)}) copy-start(bf16[8,2,256,128]{3,2,1,0:T(8,128)(2,1)} %get-tuple-element.37) | copy-start | bytes 3145732
  413.7 23.6 %copy-start.43 = (f32[1024]{0:T(1024)S(1)}, f32[1024]{0:T(1024)}, u32[]{:S(2)}) copy-start(f32[1024]{0:T(1024)} %get-tuple-element.53) | copy-start | bytes 12292
  413.7 23.7 %copy-start.38 = (f32[1,4096]{1,0:T(1,128)S(1)}, f32[1,4096]{1,0:T(1,128)}, u32[]{:S(2)}) copy-start(f32[1,4096]{1,0:T(1,128)} %get-tuple-element.39) | copy-start | bytes 49156
  433.5 19.2 %all-to-all-start.6 = ((bf16[8,512,128]{2,1,0:T(8,128)(2,1)}), bf16[8,512,128]{2,1,0:T(8,128)(2,1)S(1)}, u32[]{:S(2)}, u32[]{:S(2)}) async-start(bf16[8,512,128]{2,1,0:T(8,128)(2,1)} %get-tuple-element.36), calls=%async_computation.6 | async-start | bytes 2097152 | tf_op jit(solution)/shard_map/all_to_all | solution.py:37
  440.9 3.4 copy-start.29
  442.2 11.0 %copy-start.34 = (f32[4,1024]{1,0:T(4,128)S(1)}, f32[4,1024]{1,0:T(4,128)}, u32[]{:S(2)}) copy-start(f32[4,1024]{1,0:T(4,128)} %get-tuple-element.76) | copy-start | bytes 49156
  453.2 6.8 %copy-start.5 = (bf16[4,128,1024]{2,1,0:T(8,128)(2,1)S(1)}, bf16[4,128,1024]{2,1,0:T(8,128)(2,1)}, u32[]{:S(2)}) copy-start(bf16[4,128,1024]{2,1,0:T(8,128)(2,1)} %tok_ref.1) | copy-start | bytes 3145732
  453.2 6.8 %copy-start.40 = (f32[4,128]{1,0:T(4,128)S(1)}, f32[4,128]{1,0:T(4,128)}, u32[]{:S(2)}) copy-start(f32[4,128]{1,0:T(4,128)} %copy-done.39) | copy-start | bytes 6148
  460.0 1.4 copy-start.21
  460.0 1.5 copy-start.27
  460.0 2.0 copy-start.28
  474.5 20.9 %all-to-all-start.9 = ((bf16[32,2,4192]{2,1,0:T(2,128)(2,1)}), bf16[32,2,4192]{2,1,0:T(2,128)(2,1)S(1)}, u32[]{:S(2)}, u32[]{:S(2)}) async-start(bf16[32,2,4192]{2,1,0:T(2,128)(2,1)} %reshape.581), calls=%async_computation.9 | async-start | bytes 1081344 | tf_op jit(solution)/shard_map/all_to_all | solution.py:37
  486.5 12.1 %copy-start.18 = (s32[64]{0:T(128)S(1)}, s32[64]{0:T(128)}, u32[]{:S(2)}) copy-start(s32[64]{0:T(128)} %param.39) | copy-start | bytes 772
  486.5 13.5 %copy-start.19 = (s32[4,16]{1,0:T(4,128)S(1)}, s32[4,16]{1,0:T(4,128)}, u32[]{:S(2)}) copy-start(s32[4,16]{1,0:T(4,128)} %param.38) | copy-start | bytes 772
  495.4 6.1 %copy-start.25 = (bf16[32,2,4192]{2,1,0:T(2,128)(2,1)}, bf16[32,2,4192]{2,1,0:T(2,128)(2,1)S(1)}, u32[]{:S(2)}) copy-start(bf16[32,2,4192]{2,1,0:T(2,128)(2,1)S(1)} %all-to-all-done.9) | copy-start | bytes 1609732
  495.4 30.1 %all-to-all-start.10 = ((bf16[32,2,8384]{2,1,0:T(2,128)(2,1)}), bf16[32,2,8384]{2,1,0:T(2,128)(2,1)S(1)}, u32[]{:S(2)}, u32[]{:S(2)}) async-start(bf16[32,2,8384]{2,1,0:T(2,128)(2,1)} %reshape.579), calls=%async_computation.10 | async-start | bytes 2162688 | tf_op jit(solution)/shard_map/all_to_all | solution.py:37
  544.5 24.2 %all-to-all-start.11 = ((bf16[32,32,384]{2,1,0:T(8,128)(2,1)}), bf16[32,32,384]{2,1,0:T(8,128)(2,1)S(1)}, u32[]{:S(2)}, u32[]{:S(2)}) async-start(bf16[32,32,384]{2,1,0:T(8,128)(2,1)} %bitcast.51), calls=%async_computation.11 | async-start | bytes 1572864 | tf_op jit(solution)/shard_map/all_to_all | solution.py:37
  570.1 2.9 copy-start.26
  570.1 3.7 copy-start.1
Sparse Core Ops, SparseCore 0:
  76.8 73.5 all-gather.2
Sparse Core Ops, SparseCore 1:
  251.5 216.8 reduce-scatter.1

commit v2 on v1

--- a/solution.py
+++ b/solution.py
@@ -71,40 +71,38 @@
     return value * cosine + partner * sine
 
 
-def keyval_kernel(tok_ref, shift_ref, scale_ref, wk_ref, wv_ref, bk_ref, bv_ref,
-                  cos_ref, sin_ref, hid_ref, kv_ref):
+def project_kernel(tok_ref, shift_ref, scale_ref, wq_ref, wk_ref, wv_ref, bq_ref, bk_ref, bv_ref,
+                   cos_ref, sin_ref, turned_ref, out_ref, hid_all):
     frames, patches, _ = tok_ref.shape
-    cols = wk_ref.shape[1]
 
     @pl.when(pl.program_id(0) == 0)
     def _():
         for f in range(frames):
+            here = slice(f * patches, (f + 1) * patches)
             x = tok_ref[f].astype(f32)
             centre = x - jnp.mean(x, axis=1, keepdims=True)
             inv = lax.rsqrt(jnp.mean(centre * centre, axis=1, keepdims=True) + norm_eps)
             hid = centre * inv * (1.0 + scale_ref[f : f + 1, :]) + shift_ref[f : f + 1, :]
-            hid_ref[f * patches : (f + 1) * patches, :] = hid.astype(bf16)
-
-    keys = dot(hid_ref[...], wk_ref[...]) + bk_ref[...]
-    vals = (dot(hid_ref[...], wv_ref[...]) + bv_ref[...]).astype(bf16)
-    for p in range(cols // LANES):
-        lanes = slice(p * LANES, (p + 1) * LANES)
-        kv_ref[p, 0] = rotate_lanes(keys[:, lanes], cos_ref[...], sin_ref[...]).astype(bf16)
-        kv_ref[p, 1] = vals[:, lanes]
-
-
-def query_kernel(hid_ref, wq_ref, bq_ref, cos_ref, sin_ref, q_ref):
-    query = dot(hid_ref[...], wq_ref[...]) + bq_ref[...]
+            hid = hid.astype(bf16)
+            hid_all[here, :] = hid
+            turned_ref[:, here] = hid.T
+
+    hid = hid_all[...]
+    query = dot(hid, wq_ref[...]) + bq_ref[...]
+    keys = dot(hid, wk_ref[...]) + bk_ref[...]
+    vals = (dot(hid, wv_ref[...]) + bv_ref[...]).astype(bf16)
     for p in range(wq_ref.shape[1] // LANES):
         lanes = slice(p * LANES, (p + 1) * LANES)
-        q_ref[p] = rotate_lanes(query[:, lanes], cos_ref[...], sin_ref[...]).astype(bf16)
+        out_ref[p, 0] = rotate_lanes(query[:, lanes], cos_ref[...], sin_ref[...]).astype(bf16)
+        out_ref[p, 1] = rotate_lanes(keys[:, lanes], cos_ref[...], sin_ref[...]).astype(bf16)
+        out_ref[p, 2] = vals[:, lanes]
 
 
 def whole(shape):
     return pl.BlockSpec(shape, lambda *_: (0,) * len(shape))
 
 
-def project(tokens, shift_one, scale_one, qkv_weight, qkv_bias, cosine, sine, cols=512):
+def project(tokens, shift_one, scale_one, qkv_weight, qkv_bias, cosine, sine, cols=256):
     frames, patches, width = tokens.shape
     rows = frames * patches
     pairs = width // LANES
@@ -113,53 +111,28 @@
     def column(part):
         return lambda c: (0, part * steps + c)
 
-    hidden, keyvals = pl.pallas_call(
-        keyval_kernel,
+    return pl.pallas_call(
+        project_kernel,
         out_shape=[
-            jax.ShapeDtypeStruct((rows, width), bf16),
-            jax.ShapeDtypeStruct((pairs, 2, rows, LANES), bf16),
+            jax.ShapeDtypeStruct((width, rows), bf16),
+            jax.ShapeDtypeStruct((pairs, 3, rows, LANES), bf16),
         ],
         grid=(steps,),
-        in_specs=[
-            whole(tokens.shape),
-            whole(shift_one.shape),
-            whole(scale_one.shape),
-            pl.BlockSpec((width, cols), column(1)),
-            pl.BlockSpec((width, cols), column(2)),
-            pl.BlockSpec((1, cols), column(1)),
-            pl.BlockSpec((1, cols), column(2)),
-            whole((rows, LANES)),
-            whole((rows, LANES)),
-        ],
+        in_specs=[whole(tokens.shape), whole(shift_one.shape), whole(scale_one.shape)]
+        + [pl.BlockSpec((width, cols), column(part)) for part in range(3)]
+        + [pl.BlockSpec((1, cols), column(part)) for part in range(3)]
+        + [whole((rows, LANES)), whole((rows, LANES))],
         out_specs=[
-            whole((rows, width)),
-            pl.BlockSpec((some, 2, rows, LANES), lambda c: (c, 0, 0, 0)),
-        ],
+            whole((width, rows)),
+            pl.BlockSpec((some, 3, rows, LANES), lambda c: (c, 0, 0, 0)),
+        ],
+        scratch_shapes=[VMEM((rows, width), bf16)],
         compiler_params=pltpu.CompilerParams(vmem_limit_bytes=40 * MIB),
         cost_estimate=pl.CostEstimate(
-            flops=4 * rows * width * width, bytes_accessed=8 * MIB, transcendentals=0
+            flops=6 * rows * width * width, bytes_accessed=10 * MIB, transcendentals=0
         ),
-        name="project_keyval",
-    )(tokens, shift_one, scale_one, qkv_weight, qkv_weight, qkv_bias, qkv_bias, cosine, sine)
-    queries = pl.pallas_call(
-        query_kernel,
-        out_shape=jax.ShapeDtypeStruct((pairs, rows, LANES), bf16),
-        grid=(steps,),
-        in_specs=[
-            whole((rows, width)),
-            pl.BlockSpec((width, cols), column(0)),
-            pl.BlockSpec((1, cols), column(0)),
-            whole((rows, LANES)),
-            whole((rows, LANES)),
-        ],
-        out_specs=pl.BlockSpec((some, rows, LANES), lambda c: (c, 0, 0)),
-        compiler_params=pltpu.CompilerParams(vmem_limit_bytes=40 * MIB),
-        cost_estimate=pl.CostEstimate(
-            flops=2 * rows * width * width, bytes_accessed=4 * MIB, transcendentals=0
-        ),
-        name="project_query",
-    )(hidden, qkv_weight, qkv_bias, cosine, sine)
-    return hidden, keyvals, queries
+        name="project",
+    )(tokens, shift_one, scale_one, *[qkv_weight] * 3, *[qkv_bias] * 3, cosine, sine)
 
 
 def key_extra(first_frame, rows, patches):
@@ -176,22 +149,24 @@
     return high, mid, rest - mid
 
 
-def attend_kernel(part, rows_part, patches, joined, chunk, q_ref, vis_ref, kv_ref, o_ref, ext_ref,
+def attend_kernel(part, rows_part, patches, joined, chunk, qkv_ref, vis_ref, o_ref, ext_ref,
                   key_all, val_all):
-    blocks, rows, _ = q_ref.shape
+    blocks, _, rows, _ = qkv_ref.shape
     frames, frames_part = rows // patches, rows_part // patches
     for b in range(blocks):
         here = slice(b * rows, (b + 1) * rows)
-        key_all[here, :LANES] = kv_ref[b, 0]
+        key_all[here, :LANES] = qkv_ref[b, 1]
         key_all[here, LANES:] = key_extra((b // 2) * frames, rows, patches)
-        val_all[here, :LANES] = kv_ref[b, 1]
+        val_all[here, :LANES] = qkv_ref[b, 2]
         val_all[here, LANES:] = jnp.full((rows, LANES), 1.0, bf16)
     tile = joined * rows_part
     lane = lax.broadcasted_iota(jnp.int32, (tile, LANES), 1)
     mine_rows = slice(part * rows_part, (part + 1) * rows_part)
 
     def step(t, carry):
-        query = jnp.concatenate([q_ref[t * joined + i, mine_rows, :] for i in range(joined)], axis=0)
+        query = jnp.concatenate(
+            [qkv_ref[t * joined + i, 0, mine_rows, :] for i in range(joined)], axis=0
+        )
         query = query * score_scale
         seen = jnp.concatenate(
             [
@@ -234,8 +209,8 @@
     lax.fori_loop(0, blocks // joined, step, 0)
 
 
-def attend(queries, visible, keyvals, patches, part, parts, tile=512, chunk=1024):
-    blocks, rows, _ = queries.shape
+def attend(heads, visible, patches, part, parts, tile=512, chunk=1024):
+    blocks, _, rows, _ = heads.shape
     rows_part = rows // parts
     keys = blocks * rows
     return pl.pallas_call(
@@ -244,7 +219,7 @@
             jax.ShapeDtypeStruct((blocks, rows_part, LANES), bf16),
             jax.ShapeDtypeStruct((2, blocks, rows_part, LANES), bf16),
         ],
-        in_specs=[pl.BlockSpec(memory_space=VMEM)] * 3,
+        in_specs=[pl.BlockSpec(memory_space=VMEM)] * 2,
         out_specs=[pl.BlockSpec(memory_space=VMEM)] * 2,
         scratch_shapes=[VMEM((keys, 2 * LANES), bf16), VMEM((keys, 2 * LANES), bf16)],
         compiler_params=pltpu.CompilerParams(vmem_limit_bytes=48 * MIB),
@@ -254,7 +229,7 @@
             transcendentals=0,
         ),
         name="attend",
-    )(queries, visible, keyvals)
+    )(heads, visible)
 
 
 def attend_back_kernel(parts, part, patches, chunk, carried, last, *refs):
@@ -266,13 +241,16 @@
         at += count
         return found
 
-    (q_ref, kv_ref, do_ref) = take(3)
+    (qkv_ref, do_ref) = take(2)
     ext_refs, o_refs = take(parts), take(parts)
     ctime_ref, stime_ref, cpatch_ref, spatch_ref = take(4)
     carry_ref = take(1)[0] if carried else None
-    (dkv_ref, dq_ref) = take(2)
+    if last:
+        (grads_ref,) = take(1)
+    else:
+        grads_ref, carry_out = take(2)
     q_all, do_all, key_all, val_all, key_turned, dq_turned = refs[at:]
-    blocks, rows, _ = q_ref.shape
+    blocks, _, rows, _ = qkv_ref.shape
     rows_part = rows // parts
     frames, frames_part = rows // patches, rows_part // patches
     queries = blocks * rows
@@ -281,7 +259,7 @@
         for i in range(parts):
             here = slice(b * rows + i * rows_part, b * rows + (i + 1) * rows_part)
             there = slice(i * rows_part, (i + 1) * rows_part)
-            query = q_ref[b, there, :] * score_scale
+            query = qkv_ref[b, 0, there, :] * score_scale
             grad = do_ref[b, there, :]
             mixed = grad.astype(f32) * o_refs[i][b].astype(f32)
             for h in range(2):
@@ -300,12 +278,14 @@
     key_rows = slice(part * rows_part, (part + 1) * rows_part)
     for b in range(blocks):
         here = slice(b * rows_part, (b + 1) * rows_part)
-        keys = kv_ref[b, 0, key_rows, :]
+        keys = qkv_ref[b, 1, key_rows, :]
         key_all[here, :LANES] = keys
         key_all[here, LANES:] = key_extra((b // 2) * frames + part * frames_part, rows_part, patches)
-        val_all[here, :LANES] = kv_ref[b, 1, key_rows, :]
+        val_all[here, :LANES] = qkv_ref[b, 2, key_rows, :]
         val_all[here, LANES:] = jnp.where(lane < 3, 1.0, 0.0).astype(bf16)
         key_turned[b] = keys.astype(f32).T.astype(bf16)
+
+    first = rows if last else 0
 
     def back(value, row, half):
         cosine = ctime_ref[pl.ds(row, 1), :] + cpatch_ref[half]
@@ -333,8 +313,9 @@
         for f in range(frames_part):
             rows_here = slice(f * patches, (f + 1) * patches)
             row = t * frames + part * frames_part + f
-            dkv_ref[t, 0, rows_here, :] = back(dk[rows_here, :], row, t % 2)
-        dkv_ref[t, 1] = dv.astype(bf16)
+            keys_here = slice(first + f * patches, first + (f + 1) * patches)
+            grads_ref[t, keys_here, :] = back(dk[rows_here, :], row, t % 2)
+        grads_ref[t, first + rows_part : first + 2 * rows_part, :] = dv.astype(bf16)
         return carry
 
     lax.fori_loop(0, blocks, step, 0)
@@ -344,26 +325,27 @@
             for f in range(frames):
                 there = slice(b * rows + f * patches, b * rows + (f + 1) * patches)
                 turned_back = back(dq_turned[:, there].T * score_scale, b * frames + f, b % 2)
-                dq_ref[b, f * patches : (f + 1) * patches, :] = turned_back
+                grads_ref[b, f * patches : (f + 1) * patches, :] = turned_back
     else:
-        dq_ref[...] = dq_turned[...]
-
-
-def attend_back(queries, keyvals, grads, exts, outs, rotary, carry, part, last, patches, chunk=1024):
+        carry_out[...] = dq_turned[...]
+
+
+def attend_back(heads, grads, exts, outs, rotary, carry, part, last, patches, chunk=1024):
     parts = len(exts)
-    blocks, rows, _ = queries.shape
+    blocks, _, rows, _ = heads.shape
     rows_part = rows // parts
     total = blocks * rows
     carried = carry is not None
-    operands = [queries, keyvals, grads, *exts, *outs, *rotary] + ([carry] if carried else [])
-    dq_shape = jax.ShapeDtypeStruct((LANES, total), f32)
-    if last:
-        dq_shape = jax.ShapeDtypeStruct((blocks, rows, LANES), bf16)
+    operands = [heads, grads, *exts, *outs, *rotary] + ([carry] if carried else [])
+    kept = 2 * rows_part + (rows if last else 0)
+    out_shape = [jax.ShapeDtypeStruct((blocks, kept, LANES), bf16)]
+    if not last:
+        out_shape.append(jax.ShapeDtypeStruct((LANES, total), f32))
     return pl.pallas_call(
         functools.partial(attend_back_kernel, parts, part, patches, chunk, carried, last),
-        out_shape=[jax.ShapeDtypeStruct((blocks, 2, rows_part, LANES), bf16), dq_shape],
+        out_shape=out_shape,
         in_specs=[pl.BlockSpec(memory_space=VMEM)] * len(operands),
-        out_specs=[pl.BlockSpec(memory_space=VMEM)] * 2,
+        out_specs=[pl.BlockSpec(memory_space=VMEM)] * len(out_shape),
         scratch_shapes=[
             VMEM((2, total, 2 * LANES), bf16),
             VMEM((2, total, 2 * LANES), bf16),
@@ -523,16 +505,283 @@
     )(attn_low, grad_proj, joined)
 
 
-def layer_norm(values_in):
-    centre = values_in - jnp.mean(values_in, axis=-1, keepdims=True)
-    inv_scale = lax.rsqrt(jnp.mean(centre * centre, axis=-1, keepdims=True) + norm_eps)
-    return (centre * inv_scale, inv_scale)
-
-
-def norm_back(grad_in, normed, inv_scale):
-    mean_grad = jnp.mean(grad_in, axis=-1, keepdims=True)
-    mean_mix = jnp.mean(grad_in * normed, axis=-1, keepdims=True)
-    return inv_scale * (grad_in - mean_grad - normed * mean_mix)
+def merge_kernel(*refs):
+    parts = len(refs) - 13
+    att_refs = refs[:parts]
+    (weight_ref, bias_ref, tok_ref, cot_ref, gate_one_ref, shift_ref, scale_ref, gate_two_ref,
+     low_ref, proj_ref, after_ref, hid_ref, grad_ref) = refs[parts:]
+    frames, patches, width = tok_ref.shape
+    pairs, rows_part, _ = att_refs[0].shape
+    for i, att_ref in enumerate(att_refs):
+        low = jnp.concatenate([att_ref[p] for p in range(pairs)], axis=1)
+        there = slice(i * rows_part, (i + 1) * rows_part)
+        low_ref[there, :] = low
+        proj = dot(low, weight_ref[...]) + bias_ref[...]
+        proj_ref[there, :] = proj
+        for j in range(rows_part // patches):
+            f = i * (rows_part // patches) + j
+            here = slice(f * patches, (f + 1) * patches)
+            row = slice(f, f + 1)
+            after = tok_ref[f].astype(f32) + gate_one_ref[row, :] * proj[
+                j * patches : (j + 1) * patches, :
+            ]
+            after_ref[here, :] = after
+            centre = after - jnp.mean(after, axis=1, keepdims=True)
+            inv = lax.rsqrt(jnp.mean(centre * centre, axis=1, keepdims=True) + norm_eps)
+            hid = centre * inv * (1.0 + scale_ref[row, :]) + shift_ref[row, :]
+            hid_ref[here, :] = hid.astype(bf16)
+            grad_ref[here, :] = (gate_two_ref[row, :] * cot_ref[f].astype(f32)).astype(bf16)
+
+
+def merge_heads(attended, proj_weight, proj_bias, tokens, cotangent, mods):
+    frames, patches, width = tokens.shape
+    rows = frames * patches
+    operands = [*attended, proj_weight, proj_bias, tokens, cotangent, *mods]
+    return pl.pallas_call(
+        merge_kernel,
+        out_shape=[
+            jax.ShapeDtypeStruct((rows, width), bf16),
+            jax.ShapeDtypeStruct((rows, width), f32),
+            jax.ShapeDtypeStruct((rows, width), f32),
+            jax.ShapeDtypeStruct((rows, width), bf16),
+            jax.ShapeDtypeStruct((rows, width), bf16),
+        ],
+        in_specs=[pl.BlockSpec(memory_space=VMEM)] * len(operands),
+        out_specs=[pl.BlockSpec(memory_space=VMEM)] * 5,
+        compiler_params=pltpu.CompilerParams(vmem_limit_bytes=48 * MIB),
+        cost_estimate=pl.CostEstimate(
+            flops=2 * rows * width * width, bytes_accessed=16 * MIB, transcendentals=0
+        ),
+        name="merge_heads",
+    )(*operands)
+
+
+def unmerge_kernel(branch_ref, back_ref, after_ref, proj_ref, cot_ref, gate_one_ref, scale_ref,
+                   gate_two_ref, weight_ref, bias_ref,
+                   out_ref, grad_ref, gproj_ref, parts_ref, sums_ref, biases_ref):
+    frames, patches, width = cot_ref.shape
+    pairs = parts_ref.shape[0]
+    proj_sum = jnp.zeros((1, width), f32)
+    down_sum = jnp.zeros((1, width), f32)
+
+    def column_sum(value):
+        return jnp.sum(value, axis=0, keepdims=True)
+
+    for f in range(frames):
+        here = slice(f * patches, (f + 1) * patches)
+        row = slice(f, f + 1)
+        cot = cot_ref[f].astype(f32)
+        after = after_ref[here, :]
+        branch = branch_ref[here, :] + bias_ref[...]
+        out_ref[f] = (after + gate_two_ref[row, :] * branch).astype(bf16)
+        sums_ref[3 * frames + f : 3 * frames + f + 1, :] = column_sum(cot * branch)
+        down_sum += column_sum((gate_two_ref[row, :] * cot).astype(bf16).astype(f32))
+        centre = after - jnp.mean(after, axis=1, keepdims=True)
+        inv = lax.rsqrt(jnp.mean(centre * centre, axis=1, keepdims=True) + norm_eps)
+        normed = centre * inv
+        back = back_ref[here, :]
+        sums_ref[frames + f : frames + f + 1, :] = column_sum(back)
+        sums_ref[2 * frames + f : 2 * frames + f + 1, :] = column_sum(back * normed)
+        scaled = back * (1.0 + scale_ref[row, :])
+        mean_grad = jnp.mean(scaled, axis=1, keepdims=True)
+        mean_mix = jnp.mean(scaled * normed, axis=1, keepdims=True)
+        grad = cot + inv * (scaled - mean_grad - normed * mean_mix)
+        grad_ref[here, :] = grad
+        sums_ref[f : f + 1, :] = column_sum(grad * proj_ref[here, :])
+        gproj = (gate_one_ref[row, :] * grad).astype(bf16)
+        gproj_ref[here, :] = gproj
+        proj_sum += column_sum(gproj.astype(f32))
+    biases_ref[0:1, :] = proj_sum
+    biases_ref[1:2, :] = down_sum
+    step = 2 * patches
+    for i in range(frames * patches // step):
+        here = slice(i * step, (i + 1) * step)
+        part = dot(gproj_ref[here, :], weight_ref[...], NT).astype(bf16)
+        for p in range(pairs):
+            parts_ref[p, here, :] = part[:, p * LANES : (p + 1) * LANES]
+
+
+def unmerge_heads(branch, back, after, proj, cotangent, gate_one, scale_two, gate_two,
+                  proj_weight, down_bias):
+    frames, patches, width = cotangent.shape
+    rows = frames * patches
+    operands = [branch, back, after, proj, cotangent, gate_one, scale_two, gate_two, proj_weight,
+                down_bias]
+    return pl.pallas_call(
+        unmerge_kernel,
+        out_shape=[
+            jax.ShapeDtypeStruct((frames, patches, width), bf16),
+            jax.ShapeDtypeStruct((rows, width), f32),
+            jax.ShapeDtypeStruct((rows, width), bf16),
+            jax.ShapeDtypeStruct((width // LANES, rows, LANES), bf16),
+            jax.ShapeDtypeStruct((4 * frames, width), f32),
+            jax.ShapeDtypeStruct((2, width), f32),
+        ],
+        in_specs=[pl.BlockSpec(memory_space=VMEM)] * len(operands),
+        out_specs=[pl.BlockSpec(memory_space=VMEM)] * 6,
+        compiler_params=pltpu.CompilerParams(vmem_limit_bytes=56 * MIB),
+        cost_estimate=pl.CostEstimate(
+            flops=2 * rows * width * width, bytes_accessed=20 * MIB, transcendentals=0
+        ),
+        name="unmerge_heads",
+    )(*operands)
+
+
+def heads_grad_kernel(hid_ref, first_ref, last_ref, out_ref, total):
+    rows = hid_ref.shape[2]
+    rows_part = first_ref.shape[1] // 2
+    grad = jnp.concatenate(
+        [
+            last_ref[0, :rows, :],
+            jnp.concatenate(
+                [first_ref[0, :rows_part, :], last_ref[0, rows : rows + rows_part, :]], axis=0
+            ),
+            jnp.concatenate([first_ref[0, rows_part:, :], last_ref[0, rows + rows_part :, :]], axis=0),
+        ],
+        axis=1,
+    )
+    some = dot(hid_ref[0], grad)
+
+    @pl.when(pl.program_id(0) == 0)
+    def _():
+        total[...] = some
+
+    @pl.when(pl.program_id(0) > 0)
+    def _():
+        total[...] += some
+
+    @pl.when(pl.program_id(0) == pl.num_programs(0) - 1)
+    def _():
+        out_ref[...] = total[...].astype(bf16)
+
+
+def heads_grad(hidden_clip, first, last):
+    blocks, width, rows = hidden_clip.shape
+    return pl.pallas_call(
+        heads_grad_kernel,
+        out_shape=jax.ShapeDtypeStruct((width, 3 * LANES), bf16),
+        grid=(blocks,),
+        in_specs=[
+            pl.BlockSpec((1, width, rows), lambda b: (b, 0, 0)),
+            pl.BlockSpec((1,) + first.shape[1:], lambda b: (b, 0, 0)),
+            pl.BlockSpec((1,) + last.shape[1:], lambda b: (b, 0, 0)),
+        ],
+        out_specs=whole((width, 3 * LANES)),
+        scratch_shapes=[VMEM((width, 3 * LANES), f32)],
+        compiler_params=pltpu.CompilerParams(vmem_limit_bytes=40 * MIB),
+        cost_estimate=pl.CostEstimate(
+            flops=6 * blocks * rows * width * LANES, bytes_accessed=12 * MIB, transcendentals=0
+        ),
+        name="heads_grad",
+    )(hidden_clip, first, last)
+
+
+def finish_kernel(first_ref, last_ref, wq_ref, wk_ref, wv_ref, tok_ref, scale_ref, after_ref,
+                  out_ref, sums_ref, bq_ref, bk_ref, bv_ref, total):
+    frames, patches, width = tok_ref.shape
+    rows = frames * patches
+    rows_part = first_ref.shape[1] // 2
+    step = pl.program_id(0)
+    query, keys, vals = [], [], []
+    for p in range(first_ref.shape[0]):
+        query.append(last_ref[p, :rows, :])
+        keys.append(
+            jnp.concatenate(
+                [first_ref[p, :rows_part, :], last_ref[p, rows : rows + rows_part, :]], axis=0
+            )
+        )
+        vals.append(
+            jnp.concatenate([first_ref[p, rows_part:, :], last_ref[p, rows + rows_part :, :]], axis=0)
+        )
+    some = None
+    for grads, weight_ref, bias_ref in (
+        (query, wq_ref, bq_ref), (keys, wk_ref, bk_ref), (vals, wv_ref, bv_ref)
+    ):
+        grads = jnp.concatenate(grads, axis=1)
+        bias_ref[...] = jnp.sum(grads.astype(f32), axis=0, keepdims=True)
+        term = dot(grads, weight_ref[...], NT)
+        some = term if some is None else some + term
+
+    @pl.when(step == 0)
+    def _():
+        total[...] = some
+
+    @pl.when(step > 0)
+    def _():
+        total[...] += some
+
+    @pl.when(step == pl.num_programs(0) - 1)
+    def _():
+        for f in range(frames):
+            here = slice(f * patches, (f + 1) * patches)
+            x = tok_ref[f].astype(f32)
+            centre = x - jnp.mean(x, axis=1, keepdims=True)
+            inv = lax.rsqrt(jnp.mean(centre * centre, axis=1, keepdims=True) + norm_eps)
+            normed = centre * inv
+            back = total[here, :]
+            sums_ref[f : f + 1, :] = jnp.sum(back, axis=0, keepdims=True)
+            sums_ref[frames + f : frames + f + 1, :] = jnp.sum(back * normed, axis=0, keepdims=True)
+            scaled = back * (1.0 + scale_ref[f : f + 1, :])
+            mean_grad = jnp.mean(scaled, axis=1, keepdims=True)
+            mean_mix = jnp.mean(scaled * normed, axis=1, keepdims=True)
+            grad = after_ref[here, :] + inv * (scaled - mean_grad - normed * mean_mix)
+            out_ref[f] = grad.astype(bf16)
+
+
+def finish(first, last, qkv_weight, tokens, scale_one, grad_after, cols=256):
+    frames, patches, width = tokens.shape
+    rows = frames * patches
+    steps, some = width // cols, cols // LANES
+
+    def column(part):
+        return lambda c: (0, part * steps + c)
+
+    return pl.pallas_call(
+        finish_kernel,
+        out_shape=[
+            jax.ShapeDtypeStruct((frames, patches, width), bf16),
+            jax.ShapeDtypeStruct((2 * frames, width), f32),
+        ]
+        + [jax.ShapeDtypeStruct((1, width), f32)] * 3,
+        grid=(steps,),
+        in_specs=[
+            pl.BlockSpec((some,) + first.shape[1:], lambda c: (c, 0, 0)),
+            pl.BlockSpec((some,) + last.shape[1:], lambda c: (c, 0, 0)),
+        ]
+        + [pl.BlockSpec((width, cols), column(part)) for part in range(3)]
+        + [whole(tokens.shape), whole(scale_one.shape), whole((rows, width))],
+        out_specs=[whole((frames, patches, width)), whole((2 * frames, width))]
+        + [pl.BlockSpec((1, cols), lambda c: (0, c))] * 3,
+        scratch_shapes=[VMEM((rows, width), f32)],
+        compiler_params=pltpu.CompilerParams(vmem_limit_bytes=48 * MIB),
+        cost_estimate=pl.CostEstimate(
+            flops=6 * rows * width * width, bytes_accessed=16 * MIB, transcendentals=0
+        ),
+        name="finish",
+    )(first, last, *[qkv_weight] * 3, tokens, scale_one, grad_after)
+
+
+def lay_rows_kernel(group, got_ref, out_ref):
+    clips = got_ref.shape[0] // group
+    width = out_ref.shape[1] // 3
+    for p in range(group):
+        total = got_ref[p].astype(f32)
+        for c in range(1, clips):
+            total = total + got_ref[c * group + p].astype(f32)
+        for part in range(3):
+            at = part * width + p * LANES
+            out_ref[:, at : at + LANES] = total[:, part * LANES : (part + 1) * LANES]
+
+
+def lay_rows(got, group):
+    share, triple = got.shape[1:]
+    return pl.pallas_call(
+        functools.partial(lay_rows_kernel, group),
+        out_shape=jax.ShapeDtypeStruct((share, group * triple), f32),
+        in_specs=[pl.BlockSpec(memory_space=VMEM)],
+        out_specs=pl.BlockSpec(memory_space=VMEM),
+        name="lay_rows",
+    )(got)
 
 
 def body(
@@ -615,50 +864,47 @@
     my_embed = dot(pick, embed_act).astype(bf16)
     frame_mod = dot(my_embed, ada_weight) + ada_bias.astype(f32)
     frame_mod = lax.reduce_precision(frame_mod, 8, 7)
-    mod_parts = [frame_mod[:, i * width : (i + 1) * width] for i in range(6)]
-    shift_one, scale_one = mod_parts[0], mod_parts[1]
-    gate_one, shift_two, scale_two, gate_two = [part[:, None, :] for part in mod_parts[2:]]
-
-    hidden_one, keyval_parts, query_parts = project(
+    shift_one, scale_one, gate_one, shift_two, scale_two, gate_two = [
+        frame_mod[:, i * width : (i + 1) * width] for i in range(6)
+    ]
+
+    hidden_turned, head_parts = project(
         tokens, shift_one, scale_one, qkv_weight, qkv_bias.astype(f32)[None, :], cosine, sine
     )
-    keyvals = exchange(keyval_parts, clip_groups)
-    queries = exchange(query_parts, clip_groups)
+    heads = exchange(head_parts, clip_groups)
     outs, exts, attended = [], [], []
     for part in range(halves):
-        out, ext = attend(queries, visible, keyvals, patches, part, halves)
+        out, ext = attend(heads, visible, patches, part, halves)
         outs.append(out)
         exts.append(ext)
         attended.append(exchange(out, clip_groups))
 
-    hidden_own, _ = lax.optimization_barrier((hidden_one, queries))
-    hidden_clip = lax.all_gather(hidden_own, AXES, axis_index_groups=clip_groups).reshape(
-        group * rows, width
-    )
-
-    attn_low = jnp.concatenate(
-        [part.transpose(1, 0, 2).reshape(rows // halves, width) for part in attended], axis=0
-    )
-    attn_proj = (dot(attn_low, proj_weight) + proj_bias.astype(f32)).reshape(
-        frames, patches, width
-    )
-    inputs = tokens.astype(f32)
-    after_attn = inputs + gate_one * attn_proj
-    normed_two, rscale_two = layer_norm(after_attn)
-    hidden_two = (
-        (normed_two * (1.0 + scale_two) + shift_two).astype(bf16).reshape(rows, width)
-    )
-    grad_out = out_cotangent.astype(f32)
-    grad_branch = (gate_two * grad_out).astype(bf16).reshape(rows, width)
+    hidden_turned, _ = lax.optimization_barrier((hidden_turned, heads))
+    hidden_clip = lax.all_gather(hidden_turned, AXES, axis_index_groups=clip_groups)
+
+    attn_low, attn_proj, after_attn, hidden_two, grad_branch = merge_heads(
+        attended,
+        proj_weight,
+        proj_bias.astype(f32)[None, :],
+        tokens,
+        out_cotangent,
+        (gate_one, shift_two, scale_two, gate_two),
+    )
     branch, grad_hidden_two, up_b_grad, joined = feed_forward(
         hidden_two, grad_branch, up_weight, up_bias.astype(f32)[None, :], down_weight, devices
     )
-
-    grad_hidden_two = grad_hidden_two.reshape(frames, patches, width)
-    grad_after = grad_out + norm_back(grad_hidden_two * (1.0 + scale_two), normed_two, rscale_two)
-    grad_proj = (gate_one * grad_after).astype(bf16).reshape(rows, width)
-    grad_parts = dot(grad_proj, proj_weight, NT).astype(bf16)
-    grad_parts = grad_parts.reshape(rows, group, LANES).transpose(1, 0, 2)
+    block_out, grad_after, grad_proj, grad_parts, early_sums, early_biases = unmerge_heads(
+        branch,
+        grad_hidden_two,
+        after_attn,
+        attn_proj,
+        out_cotangent,
+        gate_one,
+        scale_two,
+        gate_two,
+        proj_weight,
+        down_bias.astype(f32)[None, :],
+    )
     grads = exchange(grad_parts, clip_groups)
 
     joined = proj_weight_grad(attn_low, grad_proj, joined)
@@ -668,104 +914,76 @@
     down_w_out = summed[quarters : 2 * quarters].reshape(per_dest, width)
     proj_w_out = summed[2 * quarters]
 
-    branch_out = (branch + down_bias.astype(f32)).reshape(frames, patches, width)
-    block_out = (after_attn + gate_two * branch_out).astype(bf16)
-    early_sums = jnp.concatenate(
-        [
-            jnp.sum(grad_after * attn_proj, axis=1),
-            jnp.sum(grad_hidden_two, axis=1),
-            jnp.sum(grad_hidden_two * normed_two, axis=1),
-            jnp.sum(grad_out * branch_out, axis=1),
-        ],
-        axis=1,
-    )
-
-    def share_out(slot_sums, biases):
+    def slot_parts(slot_sums, biases):
+        kinds = slot_sums.shape[0] // frames
+        sums = slot_sums.reshape(kinds, frames, width).transpose(1, 0, 2).reshape(frames, -1)
+        sums = jnp.broadcast_to(sums.astype(bf16)[None], (devices, frames, kinds * width))
         high = biases.astype(bf16)
         low = (biases - high.astype(f32)).astype(bf16)
-        sums = slot_sums.astype(bf16).reshape(1, -1)
-        sums = jnp.broadcast_to(sums, (devices, sums.shape[1]))
-        got = exchange(jnp.concatenate([sums, high, low], axis=1), everyone).astype(f32)
-        count = slot_sums.size
-        extra = jnp.sum(got[:, count:], axis=0)
-        size = biases.shape[1]
-        return (
-            got[:, :count].reshape(devices * frames, -1).astype(bf16),
-            extra[:size] + extra[size:],
-        )
-
-    early_biases = jnp.concatenate(
-        [
-            up_b_grad.reshape(devices, per_dest),
-            jnp.sum(grad_proj.astype(f32), axis=0).reshape(devices, share),
-            jnp.sum(grad_branch.astype(f32), axis=0).reshape(devices, share),
-        ],
-        axis=1,
-    )
-    early_slots, early_bias_out = share_out(early_sums, early_biases)
-    up_b_out = early_bias_out[:per_dest]
-    proj_b_out = early_bias_out[per_dest : per_dest + share]
-    down_b_out = early_bias_out[per_dest + share :]
+        both = jnp.concatenate([high, low], axis=1).reshape(devices, frames, -1)
+        lanes = -(-both.shape[2] // LANES) * LANES
+        both = jnp.pad(both, ((0, 0), (0, 0), (0, lanes - both.shape[2])))
+        return jnp.concatenate([sums, both], axis=2)
+
+    def bias_share(got, count, size):
+        extra = jnp.sum(got[:, :, count:].astype(f32), axis=0)
+        extra = extra[:, : 2 * size // frames].reshape(-1)
+        return extra[:size] + extra[size:]
+
     slot_ids = (jnp.arange(devices * frames, dtype=jnp.int32) // (sp_count * frames)) * frames
     slot_ids = slot_ids + jnp.arange(devices * frames, dtype=jnp.int32) % frames
     slot_levels = frame_level[slot_ids // FRAMES, slot_time[slot_ids]]
     member_of = (level_ids[:, None] == slot_levels[None, :]).astype(bf16)
     my_columns = lax.dynamic_slice_in_dim(embed_act, me * share, share, axis=1)
 
-    def level_out(slots):
+    def level_out(got, count):
+        slots = got[:, :, :count].reshape(devices * frames, count)
         level_grad = dot(member_of, slots).astype(bf16)
         return dot(my_columns, level_grad, TN), jnp.sum(level_grad.astype(f32), axis=0)
 
-    early_w, early_b = level_out(early_slots)
-
-    carry = None
-    own_keyvals, grad_keyvals = [], []
-    for part in range(halves):
-        some, carry = attend_back(
-            queries, keyvals, grads, exts, outs, rotary, carry, part, part == halves - 1, patches
-        )
-        grad_keyvals.append(some)
-        own_keyvals.append(exchange(some, clip_groups))
-    grad_queries = carry
-    own_queries = exchange(grad_queries, clip_groups)
-
-    grad_keyval = jnp.concatenate(grad_keyvals, axis=2)
-    grad_heads = jnp.concatenate(
-        [grad_queries, grad_keyval[:, 0], grad_keyval[:, 1]], axis=2
-    ).reshape(group * rows, 3 * LANES)
-    qkv_part = dot(hidden_clip, grad_heads, TN).astype(bf16)
+    early_parts = slot_parts(
+        early_sums,
+        jnp.concatenate(
+            [
+                up_b_grad.reshape(devices, per_dest),
+                early_biases[0].reshape(devices, share),
+                early_biases[1].reshape(devices, share),
+            ],
+            axis=1,
+        ),
+    )
+    early_parts, _ = lax.optimization_barrier((early_parts, grads))
+    early_got = exchange(early_parts, everyone)
+
+    first_grads, carry = attend_back(
+        heads, grads, exts, outs, rotary, None, 0, False, patches
+    )
+    carry, early_got = lax.optimization_barrier((carry, early_got))
+    own_first = exchange(first_grads, clip_groups)
+    (last_grads,) = attend_back(heads, grads, exts, outs, rotary, carry, 1, True, patches)
+    last_parts, own_first = lax.optimization_barrier((last_grads, own_first))
+    own_last = exchange(last_parts, clip_groups)
+
+    early_w, early_b = level_out(early_got, 4 * width)
+    early_bias_out = bias_share(early_got, 4 * width, per_dest + 2 * share)
+    up_b_out = early_bias_out[:per_dest]
+    proj_b_out = early_bias_out[per_dest : per_dest + share]
+    down_b_out = early_bias_out[per_dest + share :]
+
+    qkv_part = heads_grad(hidden_clip, first_grads, last_grads)
+    qkv_part, own_last = lax.optimization_barrier((qkv_part, own_last))
     qkv_got = exchange(qkv_part.reshape(devices, share, 3 * LANES), everyone)
-    qkv_w_out = (
-        jnp.sum(qkv_got.reshape(clips, group, share, 3 * LANES).astype(f32), axis=0)
-        .reshape(group, share, 3, LANES)
-        .transpose(1, 2, 0, 3)
-        .reshape(share, 3 * width)
-    )
-
-    def to_rows(value):
-        return value.transpose(1, 0, 2).reshape(value.shape[1], width)
-
-    grad_rows = jnp.concatenate(
-        [
-            to_rows(own_queries),
-            jnp.concatenate([to_rows(part[:, 0]) for part in own_keyvals], axis=0),
-            jnp.concatenate([to_rows(part[:, 1]) for part in own_keyvals], axis=0),
-        ],
-        axis=1,
-    )
-    grad_hidden_one = dot(grad_rows, qkv_weight, NT).reshape(frames, patches, width)
-    normed_one, rscale_one = layer_norm(inputs)
-    late_sums = jnp.concatenate(
-        [jnp.sum(grad_hidden_one, axis=1), jnp.sum(grad_hidden_one * normed_one, axis=1)], axis=1
-    )
-    tokens_grad = (
-        grad_after
-        + norm_back(grad_hidden_one * (1.0 + scale_one[:, None, :]), normed_one, rscale_one)
-    ).astype(bf16)
-    late_slots, qkv_b_out = share_out(
-        late_sums, jnp.sum(grad_rows.astype(f32), axis=0).reshape(devices, 3 * share)
-    )
-    late_w, late_b = level_out(late_slots)
+    qkv_w_out = lay_rows(qkv_got, group)
+
+    tokens_grad, late_sums, *late_biases = finish(
+        own_first, own_last, qkv_weight, tokens, scale_one, grad_after
+    )
+    late_parts = slot_parts(
+        late_sums, jnp.concatenate(late_biases, axis=1).reshape(devices, 3 * share)
+    )
+    late_got = exchange(late_parts, everyone)
+    late_w, late_b = level_out(late_got, 2 * width)
+    qkv_b_out = bias_share(late_got, 2 * width, 3 * share)
     ada_w_out = jnp.concatenate([late_w, early_w], axis=1)
     ada_b_all = jnp.concatenate([late_b, early_b])
     ada_share = ada_b_all.shape[0] // devices

time: 590 us -> 480 us (0.81)
  blocking collectives: 84.5 us -> 42.2 us
  Pallas kernels: 213 us -> 248 us
  local copies, waits for them, and re-layouts: 66.1 us -> 31.1 us
  other arithmetic: 47.5 us -> 15.4 us
  matrix products: 31.1 us -> 8.36 us
  waiting for transfers between devices: 86.4 us -> 73.1 us
    all_to_all x4 -> x1, blocking collectives: 84.5 us -> 42.2 us  [exchange(): return lax.all_to_all(value, AXES, 0, 0, axis_index_groups=groups)]
    pallas_call x2 -> x6, Pallas kernels: 8.22 us -> 44 us  [the longest x1 10.6 us: finish(): pl.pallas_call(finish_kernel, out_shape=[jax.ShapeDtypeStruct((frames, pa...]
    reduce_sum x14 -> x2, other arithmetic: 27 us -> 0.8 us  [bias_share(): extra = jnp.sum(got[:, :, count:].astype(f32), axis=0)]
    dot_general x9 -> x5, matrix products: 31.1 us -> 8.36 us  [dot(): return lax.dot_general(left_op, right_op, dims, preferred_element_type=f32)]
    unnamed x107 -> x70, local copies, waits for them, and re-layouts: 35.8 us -> 18.1 us
    all_to_all x8 -> x9, waiting for transfers between devices: 86.4 us -> 73.1 us  [exchange(): return lax.all_to_all(value, AXES, 0, 0, axis_index_groups=groups)]
    transpose x8 -> x0, local copies, waits for them, and re-layouts: 8.49 us -> none  [the longest x7 8.26 us: to_rows(): return value.transpose(1, 0, 2).reshape(value.shape[1], width)]
    all_to_all x8 -> x9, starting transfers between devices: 36.1 us -> 39.6 us  [exchange(): return lax.all_to_all(value, AXES, 0, 0, axis_index_groups=groups)]
  transfers between devices with their start and end apart: 10 -> 11, of which waited for: 6 -> 5; matrix products, arithmetic and copies ran while one was open for 19% -> 5% of each run, Pallas kernels for 35% -> 50%
where the time goes in v2:
time: 480 us; the launch traced here: 474 us
  Pallas kernels  248 us (52%)
  waiting for transfers between devices  73.1 us (15%)
  blocking collectives  42.2 us (9%)
  starting transfers between devices  39.9 us (8%)
  local copies, waits for them, and re-layouts  31.1 us (6%)
  between operations  16.5 us (3%)
  other arithmetic  15.4 us (3%)
  matrix products  8.36 us (2%)
    pallas_call x2, Pallas kernels, attend_back(): pl.pallas_call(functools.partial(attend_back_kernel, parts, part, patches...  113 us
    all_to_all x9, waiting for transfers between devices, exchange(): return lax.all_to_all(value, AXES, 0, 0, axis_index_groups=groups)  73.1 us
    pallas_call x2, Pallas kernels, attend(): pl.pallas_call(functools.partial(attend_kernel, part, rows_part, patches,...  48.3 us
    all_to_all x1, blocking collectives, exchange(): return lax.all_to_all(value, AXES, 0, 0, axis_index_groups=groups)  42.2 us
    pallas_call x1, Pallas kernels, feed_forward(): pl.pallas_call(feed_kernel, out_shape=[jax.ShapeDtypeStruct((rows, width)...  39.8 us
    all_to_all x9, starting transfers between devices, exchange(): return lax.all_to_all(value, AXES, 0, 0, axis_index_groups=groups)  39.6 us
    unnamed x70, local copies, waits for them, and re-layouts  18.1 us
    pallas_call x1, Pallas kernels, finish(): pl.pallas_call(finish_kernel, out_shape=[jax.ShapeDtypeStruct((frames, pa...  10.6 us
  transfers between devices with their start and end apart: 11, of which 5 were waited for; matrix products, arithmetic and copies ran while one was open for 5% of the time, Pallas kernels for 50%

profile of v2, /device:TPU:0, one launch (start us, length us, event | category | flops | bytes accessed | tf_op | source)
XLA Modules:
  0.0 474.1 jit_solution(6035344558828429666)
XLA Ops:
  8.0 1.4 broadcast_in_dim.145
  9.4 7.3 %all-to-all-start = ((bf16[32,2,1024]{2,1,0:T(2,128)(2,1)}), bf16[32,2,1024]{2,1,0:T(2,128)(2,1)S(1)}, u32[]{:S(2)}, u32[]{:S(2)}) async-start(bf16[32,2,1024]{2,1,0:T(2,128)(2,1)} %broadcast_in_dim.145), calls=%async_computation | async-start | bytes 262144 | tf_op jit(solution)/shard_map/all_to_all | solution.py:37
  16.9 0.7 compare_select_fusion.2
  17.6 0.6 gather_fusion
  18.3 0.7 and_select_fusion.5
  19.0 1.2 dynamic_slice.40
  20.2 1.4 broadcast_compare_fusion.1
  21.7 0.8 fusion.15
  22.5 1.5 multiply_select_fusion
  24.2 0.7 convert_element_type.117
  24.9 0.7 broadcast_in_dim.173
  25.8 5.8 %fusion = f32[4,6144]{1,0:T(4,128)S(1)} fusion(bf16[1024,6144]{1,0:T(8,128)(2,1)} %param.27, bf16[64,1024]{1,0:T(8,128)(2,1)S(1)} %multiply_convert_fusion, f32[6144]{0:T(1024)S(1)} %convert_element_type.117, s32[4]{0:T(128)S(1)} %and_select_fusion.5), kind=kOutput, calls=%fused_computation.4 | convolution fusion | flops 50909440 | bytes 12836880 | tf_op jit(solution)/shard_map/dot_general | solution.py:33
  31.7 2.8 copy-done.1
  34.5 8.7 %project.1 = (bf16[1024,512]{1,0:T(8,128)(2,1)}, bf16[8,3,512,128]{3,2,1,0:T(8,128)(2,1)S(1)}) custom-call(bf16[4,128,1024]{2,1,0:T(8,128)(2,1)S(1)} %copy-done.2, f32[4,1024]{1,0:T(4,128)S(1)} %get-tuple-element.102.shift_ref, f32[4,1024]{1,0:T(4,128)S(1)} %get-tuple-element.101.scale_ref, bf16[1024,3072]{1,0:T(8,128)(2,1)S(1)} %copy-done.1, ...), custom_call_target="tpu_custom_call" | custom-call | flops 3221225472 | bytes 10485760 | tf_op jit(solution)/shard_map/project/pallas_call | solution.py:114
  43.2 42.2 %all_to_all.50.qkv_ref.refs_0_ = bf16[8,3,512,128]{3,2,1,0:T(8,128)(2,1)} all-to-all(bf16[8,3,512,128]{3,2,1,0:T(8,128)(2,1)S(1)} %get-tuple-element.48), channel_id=1, replica_groups={{0,1,2,3,4,5,6,7},{8,9,10,11,12,13,14,15},{16,17,18,19,20,21,22,23},{24..., dimensions={0} | all-to-all | bytes 6291456 | tf_op jit(solution)/shard_map/all_to_all | solution.py:37
  85.5 1.9 copy-done.6
  87.4 24.2 %attend.2 = (bf16[8,256,128]{2,1,0:T(8,128)(2,1)}, bf16[2,8,256,128]{3,2,1,0:T(8,128)(2,1)S(1)}) custom-call(bf16[8,3,512,128]{3,2,1,0:T(8,128)(2,1)S(1)} %copy-done.6, f32[32,128]{1,0:T(8,128)S(1)} %bitcast.58), custom_call_target="tpu_custom_call" | custom-call | flops 17179869184 | bytes 4194304 | tf_op jit(solution)/shard_map/attend/pallas_call | solution.py:216
  111.5 1.0 copy-done.16
  112.5 3.7 all-to-all-start.2
  116.2 1.9 copy-done.7
  118.1 24.2 %attend.3 = (bf16[8,256,128]{2,1,0:T(8,128)(2,1)}, bf16[2,8,256,128]{3,2,1,0:T(8,128)(2,1)S(1)}) custom-call(bf16[8,3,512,128]{3,2,1,0:T(8,128)(2,1)S(1)} %copy-done.7, f32[32,128]{1,0:T(8,128)S(1)} %bitcast.59), custom_call_target="tpu_custom_call" | custom-call | flops 17179869184 | bytes 4194304 | tf_op jit(solution)/shard_map/attend/pallas_call | solution.py:216
  142.3 1.0 copy-done.17
  143.3 4.2 all-to-all-start.3
  147.8 0.6 broadcast_in_dim.175
  149.0 8.2 %all-to-all-done.3.refs_1_ = bf16[8,256,128]{2,1,0:T(8,128)(2,1)S(1)} async-done(((bf16[8,256,128]{2,1,0:T(8,128)(2,1)}), bf16[8,256,128]{2,1,0:T(8,128)(2,1)S(1)}, u32[]{:S(2)}, u32[]{:S(2)}) %all-to-all-start.3) | async-done | bytes 524320 | tf_op jit(solution)/shard_map/all_to_all | solution.py:37
  157.3 5.7 %merge_heads.1 = (bf16[512,1024]{1,0:T(8,128)(2,1)S(1)}, f32[512,1024]{1,0:T(8,128)}, f32[512,1024]{1,0:T(8,128)}, bf16[512,1024]{1,0:T(8,128)(2,1)S(1)}, bf16[512,1024]{1,0:T(8,128)(2,1)S(1)}) custom-call(bf16[8,256,128]{2,1,0:T(8,128)(2,1)S(1)} %all-to-all-done.2.refs_0_, bf16[8,256,128]{2,1,0:T(8,128)(2,1)S(1)} %all-to-all-done.3.refs_1_, ...), custom_call_target="tpu_custom_call" | custom-call | flops 1073741824 | bytes 16777216 | tf_op jit(solution)/shard_map/merge_heads/pallas_call | solution.py:540
  162.9 1.0 copy-done.14
  163.9 1.0 copy-done.15
  164.8 39.8 %feed_forward.1 = (f32[512,1024]{1,0:T(8,128)}, f32[512,1024]{1,0:T(8,128)}, f32[1,4096]{1,0:T(1,128)}, bf16[32,9,32,1024]{3,2,1,0:T(8,128)(2,1)}) custom-call(bf16[512,1024]{1,0:T(8,128)(2,1)} %copy-done.14, bf16[512,1024]{1,0:T(8,128)(2,1)} %copy-done.15, bf16[1024,4096]{1,0:T(8,128)(2,1)} %up_ref.1, f32[1,4096]{1,0:T(1,128)} %bitcast.72, ...), custom_call_target="tpu_custom_call" | custom-call | flops 25769803776 | bytes 37748736 | tf_op jit(solution)/shard_map/feed_forward/pallas_call | solution.py:440
  204.6 9.2 %unmerge_heads.1 = (bf16[4,128,1024]{2,1,0:T(8,128)(2,1)}, f32[512,1024]{1,0:T(8,128)}, bf16[512,1024]{1,0:T(8,128)(2,1)}, bf16[8,512,128]{2,1,0:T(8,128)(2,1)}, f32[16,1024]{1,0:T(8,128)}, /*index=5*/f32[2,1024]{1,0:T(2,128)}) custom-call(f32[512,1024]{1,0:T(8,128)} %get-tuple-element.53.branch_ref, f32[512,1024]{1,0:T(8,128)} %get-tuple-element.54.back_ref, ...), custom_call_target="tpu_custom_call" | custom-call | flops 1073741824 | bytes 20971520 | tf_op jit(solution)/shard_map/unmerge_heads/pallas_call | solution.py:610
  213.8 1.2 copy-done.8
  215.0 2.7 proj_weight_grad.1
  217.8 3.7 all-to-all-start.4
  222.5 1.5 pad_maximum_fusion
  224.0 12.9 %all-to-all-done.4.refs_1_ = bf16[8,512,128]{2,1,0:T(8,128)(2,1)S(1)} async-done(((bf16[8,512,128]{2,1,0:T(8,128)(2,1)}), bf16[8,512,128]{2,1,0:T(8,128)(2,1)S(1)}, u32[]{:S(2)}, u32[]{:S(2)}) %all-to-all-start.4) | async-done | bytes 1048608 | tf_op jit(solution)/shard_map/all_to_all | solution.py:37
  236.8 4.2 all-to-all-start.5
  241.0 54.8 %attend_back.2 = (bf16[8,512,128]{2,1,0:T(8,128)(2,1)}, f32[128,4096]{1,0:T(8,128)}) custom-call(bf16[8,3,512,128]{3,2,1,0:T(8,128)(2,1)} %all_to_all.50.qkv_ref.refs_0_, bf16[8,512,128]{2,1,0:T(8,128)(2,1)} %copy-done.23, bf16[2,8,256,128]{3,2,1,0:T(8,128)(2,1)} %copy-done.16, bf16[2,8,256,128]{3,2,1,0:T(8,128)(2,1)} %copy-done.17, ...), custom_call_target="tpu_custom_call" | custom-call | flops 42949672960 | bytes 8388608 | tf_op jit(solution)/shard_map/attend_back/pallas_call | solution.py:344
  295.9 4.4 all-to-all-start.6
  300.3 58.0 %attend_back.3.last_ref = bf16[8,1024,128]{2,1,0:T(8,128)(2,1)} custom-call(bf16[8,3,512,128]{3,2,1,0:T(8,128)(2,1)} %all_to_all.50.qkv_ref.refs_0_, bf16[8,512,128]{2,1,0:T(8,128)(2,1)} %copy-done.23, bf16[2,8,256,128]{3,2,1,0:T(8,128)(2,1)} %copy-done.16, bf16[2,8,256,128]{3,2,1,0:T(8,128)(2,1)} %copy-done.17, ...), custom_call_target="tpu_custom_call" | custom-call | flops 42949672960 | bytes 8388608 | tf_op jit(solution)/shard_map/attend_back/pallas_call | solution.py:344
  358.3 4.7 all-to-all-start.7
  363.1 1.2 gather_fusion.1
  364.4 4.2 copy-done.3
  368.6 1.2 copy-done.5
  369.8 7.9 %heads_grad.1 = bf16[1024,384]{1,0:T(8,128)(2,1)} custom-call(bf16[8,1024,512]{2,1,0:T(8,128)(2,1)S(1)} %bitcast.51, bf16[8,512,128]{2,1,0:T(8,128)(2,1)S(1)} %copy-done.5, bf16[8,1024,128]{2,1,0:T(8,128)(2,1)S(1)} %copy-done.4), custom_call_target="tpu_custom_call" | custom-call | flops 3221225472 | bytes 12582912 | tf_op jit(solution)/shard_map/heads_grad/pallas_call | solution.py:660
  377.7 20.4 %all-to-all-done.7.last_ref = bf16[8,1024,128]{2,1,0:T(8,128)(2,1)} async-done(((bf16[8,1024,128]{2,1,0:T(8,128)(2,1)}), bf16[8,1024,128]{2,1,0:T(8,128)(2,1)}, u32[]{:S(2)}, u32[]{:S(2)}) %all-to-all-start.7) | async-done | bytes 2097184 | tf_op jit(solution)/shard_map/all_to_all | solution.py:37
  398.1 10.6 %finish.1 = (bf16[4,128,1024]{2,1,0:T(8,128)(2,1)}, f32[8,1024]{1,0:T(8,128)S(1)}, f32[1,1024]{1,0:T(1,128)S(1)}, f32[1,1024]{1,0:T(1,128)S(1)}, f32[1,1024]{1,0:T(1,128)S(1)}) custom-call(bf16[8,512,128]{2,1,0:T(8,128)(2,1)} %all-to-all-done.6.first_ref, bf16[8,1024,128]{2,1,0:T(8,128)(2,1)} %all-to-all-done.7.last_ref, bf16[1024,3072]{1,0:T(8,128)(2,1)} %wv_ref.3, ...), custom_call_target="tpu_custom_call" | custom-call | flops 3221225472 | bytes 16777216 | tf_op jit(solution)/shard_map/finish/pallas_call | solution.py:739
  409.3 1.1 pad_maximum_fusion.2
  410.3 4.2 all-to-all-start.8
  414.5 1.5 gather_fusion.2
  416.1 1.1 copy.48
  418.0 0.8 convert_reduce_fusion.2
  420.2 1.0 fusion.9
  421.3 14.7 %all-to-all-done.8 = bf16[32,4,2176]{2,1,0:T(4,128)(2,1)S(1)} async-done(((bf16[32,4,2176]{2,1,0:T(4,128)(2,1)}), bf16[32,4,2176]{2,1,0:T(4,128)(2,1)S(1)}, u32[]{:S(2)}, u32[]{:S(2)}) %all-to-all-start.8) | async-done | bytes 557088 | tf_op jit(solution)/shard_map/all_to_all | solution.py:37
  436.0 3.2 all-to-all-start.9
  440.6 0.7 fusion.18
  441.2 1.0 fusion.11
  442.2 0.9 pad_maximum_fusion.1
  443.1 16.7 %all-to-all-done.9.got_ref = bf16[32,32,384]{2,1,0:T(8,128)(2,1)S(1)} async-done(((bf16[32,32,384]{2,1,0:T(8,128)(2,1)}), bf16[32,32,384]{2,1,0:T(8,128)(2,1)S(1)}, u32[]{:S(2)}, u32[]{:S(2)}) %all-to-all-start.9) | async-done | bytes 786464 | tf_op jit(solution)/shard_map/all_to_all | solution.py:37
  459.9 0.9 copy-done.21
  460.8 2.0 lay_rows.1
  462.8 1.3 convert_element_type.139
  464.0 0.7 slice_bitcast_fusion.3
  464.7 0.8 pad_maximum_fusion.3
  465.6 0.8 slice.136
  (124 shorter events, 6.4 us)
Async XLA Ops:
  8.0 9.6 %copy-start = (s32[4,16]{1,0:T(4,128)S(1)}, s32[4,16]{1,0:T(4,128)}, u32[]{:S(2)}) copy-start(s32[4,16]{1,0:T(4,128)} %param.38) | copy-start | bytes 772
  9.4 16.2 %all-to-all-start = ((bf16[32,2,1024]{2,1,0:T(2,128)(2,1)}), bf16[32,2,1024]{2,1,0:T(2,128)(2,1)S(1)}, u32[]{:S(2)}, u32[]{:S(2)}) async-start(bf16[32,2,1024]{2,1,0:T(2,128)(2,1)} %broadcast_in_dim.145), calls=%async_computation | async-start | bytes 262144 | tf_op jit(solution)/shard_map/all_to_all | solution.py:37
  16.7 347.6 %all-gather.3.cloned.1.call-start = ((), (), s32[]{:S(2)}) async-start(), calls=%async_computation.12 | async-start | bytes 9437184 | tf_op jit(solution)/shard_map/all_gather | solution.py:883
  24.0 7.6 %copy-start.25 = (f32[2,128,128]{2,1,0:T(8,128)}, f32[2,128,128]{2,1,0:T(8,128)S(1)}, u32[]{:S(2)}) copy-start(f32[2,128,128]{2,1,0:T(8,128)S(1)} %get-tuple-element.103.refs_9_) | copy-start | bytes 393220
  24.0 7.6 %copy-start.26 = (f32[2,128,128]{2,1,0:T(8,128)}, f32[2,128,128]{2,1,0:T(8,128)S(1)}, u32[]{:S(2)}) copy-start(f32[2,128,128]{2,1,0:T(8,128)S(1)} %get-tuple-element.104.refs_8_) | copy-start | bytes 393220
  24.1 7.5 %copy-start.28 = (f32[4,2,4,128]{3,2,1,0:T(4,128)}, f32[4,2,4,128]{3,2,1,0:T(4,128)S(1)}, u32[]{:S(2)}) copy-start(f32[4,2,4,128]{3,2,1,0:T(4,128)S(1)} %broadcast_in_dim.160) | copy-start | bytes 49156
  24.1 7.5 %copy-start.29 = (f32[4,2,4,128]{3,2,1,0:T(4,128)}, f32[4,2,4,128]{3,2,1,0:T(4,128)S(1)}, u32[]{:S(2)}) copy-start(f32[4,2,4,128]{3,2,1,0:T(4,128)S(1)} %broadcast_in_dim.151) | copy-start | bytes 49156
  25.8 5.9 %copy-start.24 = (bf16[64,1024]{1,0:T(8,128)(2,1)}, bf16[64,1024]{1,0:T(8,128)(2,1)S(1)}, u32[]{:S(2)}) copy-start(bf16[64,1024]{1,0:T(8,128)(2,1)S(1)} %multiply_convert_fusion) | copy-start | bytes 393220
  25.8 5.9 %copy-start.2 = (bf16[4,128,1024]{2,1,0:T(8,128)(2,1)S(1)}, bf16[4,128,1024]{2,1,0:T(8,128)(2,1)}, u32[]{:S(2)}) copy-start(bf16[4,128,1024]{2,1,0:T(8,128)(2,1)} %tok_ref.3) | copy-start | bytes 3145732
  31.7 11.5 %copy-start.12 = (f32[4,1024]{1,0:T(4,128)}, f32[4,1024]{1,0:T(4,128)S(1)}, u32[]{:S(2)}) copy-start(f32[4,1024]{1,0:T(4,128)S(1)} %get-tuple-element.101.scale_ref) | copy-start | bytes 49156
  31.7 125.6 %copy-start.9 = (f32[4,1024]{1,0:T(4,128)}, f32[4,1024]{1,0:T(4,128)S(1)}, u32[]{:S(2)}) copy-start(f32[4,1024]{1,0:T(4,128)S(1)} %get-tuple-element.97.refs_9_.gate_two_ref) | copy-start | bytes 49156
  31.7 125.6 %copy-start.10 = (f32[4,1024]{1,0:T(4,128)}, f32[4,1024]{1,0:T(4,128)S(1)}, u32[]{:S(2)}) copy-start(f32[4,1024]{1,0:T(4,128)S(1)} %get-tuple-element.98.refs_8_.scale_ref) | copy-start | bytes 49156
  31.7 125.6 %copy-start.11 = (f32[4,1024]{1,0:T(4,128)}, f32[4,1024]{1,0:T(4,128)S(1)}, u32[]{:S(2)}) copy-start(f32[4,1024]{1,0:T(4,128)S(1)} %get-tuple-element.100.refs_6_.gate_one_ref) | copy-start | bytes 49156
  31.7 2.8 copy-start.1
  85.5 1.9 copy-start.6
  111.5 1.0 copy-start.16
  112.5 30.8 %all-to-all-start.2 = ((bf16[8,256,128]{2,1,0:T(8,128)(2,1)}), bf16[8,256,128]{2,1,0:T(8,128)(2,1)S(1)}, u32[]{:S(2)}, u32[]{:S(2)}) async-start(bf16[8,256,128]{2,1,0:T(8,128)(2,1)} %get-tuple-element.49.refs_4_), calls=%async_computation.2 | async-start | bytes 1048576 | tf_op jit(solution)/shard_map/all_to_all | solution.py:37
  116.2 1.9 copy-start.7
  118.1 29.7 %copy-start.33 = (bf16[1024]{0:T(1024)(128)(2,1)S(1)}, bf16[1024]{0:T(1024)(128)(2,1)}, u32[]{:S(2)}) copy-start(bf16[1024]{0:T(1024)(128)(2,1)} %param.32) | copy-start | bytes 6148
  118.1 29.7 %copy-start.31 = (bf16[4096]{0:T(1024)(128)(2,1)S(1)}, bf16[4096]{0:T(1024)(128)(2,1)}, u32[]{:S(2)}) copy-start(bf16[4096]{0:T(1024)(128)(2,1)} %param.34) | copy-start | bytes 24580
  118.1 30.3 %copy-start.34 = (bf16[1024]{0:T(1024)(128)(2,1)S(1)}, bf16[1024]{0:T(1024)(128)(2,1)}, u32[]{:S(2)}) copy-start(bf16[1024]{0:T(1024)(128)(2,1)} %param.36) | copy-start | bytes 6148
  142.3 1.0 copy-start.17
  143.3 14.0 %all-to-all-start.3 = ((bf16[8,256,128]{2,1,0:T(8,128)(2,1)}), bf16[8,256,128]{2,1,0:T(8,128)(2,1)S(1)}, u32[]{:S(2)}, u32[]{:S(2)}) async-start(bf16[8,256,128]{2,1,0:T(8,128)(2,1)} %get-tuple-element.50.refs_5_), calls=%async_computation.3 | async-start | bytes 1048576 | tf_op jit(solution)/shard_map/all_to_all | solution.py:37
  147.5 315.3 %reduce-scatter.2.cloned.1.call-start = ((), (), s32[]{:S(2)}) async-start(), calls=%async_computation.11 | async-start | bytes 19464192 | tf_op jit(solution)/shard_map/reduce_scatter | solution.py:911
  162.9 1.0 copy-start.14
  163.9 1.0 copy-start.15
  213.8 1.2 copy-start.8
  217.8 3.7 copy-start.32
  217.8 3.9 copy-start.30
  217.8 4.1 copy-start.27
  217.8 19.0 %all-to-all-start.4 = ((bf16[8,512,128]{2,1,0:T(8,128)(2,1)}), bf16[8,512,128]{2,1,0:T(8,128)(2,1)S(1)}, u32[]{:S(2)}, u32[]{:S(2)}) async-start(bf16[8,512,128]{2,1,0:T(8,128)(2,1)} %get-tuple-element.58), calls=%async_computation.4 | async-start | bytes 2097152 | tf_op jit(solution)/shard_map/all_to_all | solution.py:37
  236.8 4.2 copy-start.23
  236.8 59.0 %all-to-all-start.5 = ((bf16[32,4,4224]{2,1,0:T(4,128)(2,1)}), bf16[32,4,4224]{2,1,0:T(4,128)(2,1)S(1)}, u32[]{:S(2)}, u32[]{:S(2)}) async-start(bf16[32,4,4224]{2,1,0:T(4,128)(2,1)} %pad_maximum_fusion), calls=%async_computation.5 | async-start | bytes 2162688 | tf_op jit(solution)/shard_map/all_to_all | solution.py:37
  295.9 4.4 copy-start.19
  295.9 62.5 %all-to-all-start.6 = ((bf16[8,512,128]{2,1,0:T(8,128)(2,1)}), bf16[8,512,128]{2,1,0:T(8,128)(2,1)}, u32[]{:S(2)}, u32[]{:S(2)}) async-start(bf16[8,512,128]{2,1,0:T(8,128)(2,1)} %get-tuple-element.67.first_ref), calls=%async_computation.6 | async-start | bytes 2097152 | tf_op jit(solution)/shard_map/all_to_all | solution.py:37
  358.3 4.8 %copy-start.18 = (s32[64]{0:T(128)S(1)}, s32[64]{0:T(128)}, u32[]{:S(2)}) copy-start(s32[64]{0:T(128)} %param.39) | copy-start | bytes 772
  358.3 6.0 %copy-start.4 = (bf16[8,1024,128]{2,1,0:T(8,128)(2,1)S(1)}, bf16[8,1024,128]{2,1,0:T(8,128)(2,1)}, u32[]{:S(2)}) copy-start(bf16[8,1024,128]{2,1,0:T(8,128)(2,1)} %attend_back.3.last_ref) | copy-start | bytes 6291460
  358.3 39.8 %all-to-all-start.7 = ((bf16[8,1024,128]{2,1,0:T(8,128)(2,1)}), bf16[8,1024,128]{2,1,0:T(8,128)(2,1)}, u32[]{:S(2)}, u32[]{:S(2)}) async-start(bf16[8,1024,128]{2,1,0:T(8,128)(2,1)} %attend_back.3.last_ref), calls=%async_computation.7 | async-start | bytes 4194304 | tf_op jit(solution)/shard_map/all_to_all | solution.py:37
  364.4 4.2 copy-start.3
  368.6 1.2 copy-start.5
  369.8 28.3 %copy-start.13 = (f32[4,1024]{1,0:T(4,128)S(1)}, f32[4,1024]{1,0:T(4,128)}, u32[]{:S(2)}) copy-start(f32[4,1024]{1,0:T(4,128)} %copy-done.12) | copy-start | bytes 49156
  410.3 5.7 %copy-start.20 = (bf16[32,4,4224]{2,1,0:T(4,128)(2,1)S(1)}, bf16[32,4,4224]{2,1,0:T(4,128)(2,1)}, u32[]{:S(2)}) copy-start(bf16[32,4,4224]{2,1,0:T(4,128)(2,1)} %copy-done.19) | copy-start | bytes 3244036
  410.3 25.7 %all-to-all-start.8 = ((bf16[32,4,2176]{2,1,0:T(4,128)(2,1)}), bf16[32,4,2176]{2,1,0:T(4,128)(2,1)S(1)}, u32[]{:S(2)}, u32[]{:S(2)}) async-start(bf16[32,4,2176]{2,1,0:T(4,128)(2,1)} %pad_maximum_fusion.2), calls=%async_computation.8 | async-start | bytes 1114112 | tf_op jit(solution)/shard_map/all_to_all | solution.py:37
  416.1 1.6 slice-start
  436.0 23.9 %all-to-all-start.9 = ((bf16[32,32,384]{2,1,0:T(8,128)(2,1)}), bf16[32,32,384]{2,1,0:T(8,128)(2,1)S(1)}, u32[]{:S(2)}, u32[]{:S(2)}) async-start(bf16[32,32,384]{2,1,0:T(8,128)(2,1)} %bitcast.23), calls=%async_computation.9 | async-start | bytes 1572864 | tf_op jit(solution)/shard_map/all_to_all | solution.py:37
  459.9 0.9 copy-start.21
  462.8 2.8 copy-start.22
Sparse Core Ops, SparseCore 0:
  85.5 59.1 all-gather.2
Sparse Core Ops, SparseCore 1:
  217.8 227.4 reduce-scatter.1

commit v3 on v2

v3 whole, which is shorter than its diff:
```python
import functools
import math

import jax
import jax.numpy as jnp
import numpy as np
from jax import lax
from jax.experimental import pallas as pl
from jax.experimental.pallas import tpu as pltpu
from jax.sharding import PartitionSpec as P

HEADS = 16
HDIM = 64
FRAMES = 16
GRID = 16
LANES = 128
MIB = 2**20

norm_eps = 1e-06
masked_out = -1e30
score_scale = 0.125

f32 = jnp.float32
bf16 = jnp.bfloat16
NN = (((1,), (0,)), ((), ()))
NT = (((1,), (1,)), ((), ()))
TN = (((0,), (0,)), ((), ()))
AXES = ("frm", "sp")
VMEM = pltpu.VMEM


def dot(left_op, right_op, dims=NN):
    return lax.dot_general(left_op, right_op, dims, preferred_element_type=f32)


def exchange(value, groups):
    return lax.all_to_all(value, AXES, 0, 0, axis_index_groups=groups)


def to_everyone(value, devices):
    return exchange(
        jnp.broadcast_to(value[None], (devices,) + value.shape), [list(range(devices))]
    )


def rotary_lanes():
    lane = np.arange(LANES) % HDIM
    start = np.where(lane < 16, 0, np.where(lane < 40, 16, 40))
    half = np.where(lane < 16, 8, 12)
    offset = lane - start
    freq = np.exp((offset % half).astype(np.float32) * np.float32(-math.log(10000.0)) / half)
    sign = np.where(offset < half, -1.0, 1.0)
    return (
        freq.astype(np.float32),
        sign.astype(np.float32),
        (lane < 16),
        (lane >= 16) & (lane < 40),
    )


def rotate_lanes(value, cosine, sine):
    lane = lax.broadcasted_iota(jnp.int32, value.shape, 1) % HDIM
    near_first = pltpu.roll(value, LANES - 8, 1)
    near_second = pltpu.roll(value, 8, 1)
    far_first = pltpu.roll(value, LANES - 12, 1)
    far_second = pltpu.roll(value, 12, 1)
    in_first = (lane < 28) | ((lane >= 40) & (lane < 52))
    far = jnp.where(in_first, far_first, far_second)
    near = jnp.where(lane < 8, near_first, near_second)
    partner = jnp.where(lane < 16, near, far)
    return value * cosine + partner * sine


def project_kernel(tok_ref, shift_ref, scale_ref, wq_ref, wk_ref, wv_ref, bq_ref, bk_ref, bv_ref,
                   cos_ref, sin_ref, turned_ref, out_ref, hid_all):
    frames, patches, _ = tok_ref.shape

    @pl.when(pl.program_id(0) == 0)
    def _():
        for f in range(frames):
            here = slice(f * patches, (f + 1) * patches)
            x = tok_ref[f].astype(f32)
            centre = x - jnp.mean(x, axis=1, keepdims=True)
            inv = lax.rsqrt(jnp.mean(centre * centre, axis=1, keepdims=True) + norm_eps)
            hid = centre * inv * (1.0 + scale_ref[f : f + 1, :]) + shift_ref[f : f + 1, :]
            hid = hid.astype(bf16)
            hid_all[here, :] = hid
            turned_ref[:, here] = hid.T

    hid = hid_all[...]
    query = dot(hid, wq_ref[...]) + bq_ref[...]
    keys = dot(hid, wk_ref[...]) + bk_ref[...]
    vals = (dot(hid, wv_ref[...]) + bv_ref[...]).astype(bf16)
    for p in range(wq_ref.shape[1] // LANES):
        lanes = slice(p * LANES, (p + 1) * LANES)
        out_ref[p, 0] = rotate_lanes(query[:, lanes], cos_ref[...], sin_ref[...]).astype(bf16)
        out_ref[p, 1] = rotate_lanes(keys[:, lanes], cos_ref[...], sin_ref[...]).astype(bf16)
        out_ref[p, 2] = vals[:, lanes]


def whole(shape):
    return pl.BlockSpec(shape, lambda *_: (0,) * len(shape))


def project(tokens, shift_one, scale_one, qkv_weight, qkv_bias, cosine, sine, cols=256):
    frames, patches, width = tokens.shape
    rows = frames * patches
    pairs = width // LANES
    steps, some = width // cols, cols // LANES

    def column(part):
        return lambda c: (0, part * steps + c)

    return pl.pallas_call(
        project_kernel,
        out_shape=[
            jax.ShapeDtypeStruct((width, rows), bf16),
            jax.ShapeDtypeStruct((pairs, 3, rows, LANES), bf16),
        ],
        grid=(steps,),
        in_specs=[whole(tokens.shape), whole(shift_one.shape), whole(scale_one.shape)]
        + [pl.BlockSpec((width, cols), column(part)) for part in range(3)]
        + [pl.BlockSpec((1, cols), column(part)) for part in range(3)]
        + [whole((rows, LANES)), whole((rows, LANES))],
        out_specs=[
            whole((width, rows)),
            pl.BlockSpec((some, 3, rows, LANES), lambda c: (c, 0, 0, 0)),
        ],
        scratch_shapes=[VMEM((rows, width), bf16)],
        compiler_params=pltpu.CompilerParams(vmem_limit_bytes=40 * MIB),
        cost_estimate=pl.CostEstimate(
            flops=6 * rows * width * width, bytes_accessed=10 * MIB, transcendentals=0
        ),
        name="project",
    )(tokens, shift_one, scale_one, *[qkv_weight] * 3, *[qkv_bias] * 3, cosine, sine)


def key_extra(first_frame, rows, patches):
    row = lax.broadcasted_iota(jnp.int32, (rows, LANES), 0)
    lane = lax.broadcasted_iota(jnp.int32, (rows, LANES), 1)
    hit = (lane == first_frame + row // patches) | ((lane >= FRAMES) & (lane < FRAMES + 3))
    return jnp.where(hit, 1.0, 0.0).astype(bf16)


def split_three(column):
    high = column.astype(bf16).astype(f32)
    rest = column - high
    mid = rest.astype(bf16).astype(f32)
    return high, mid, rest - mid


def attend_kernel(part, rows_part, patches, joined, joined_keys, qkv_ref, vis_ref, o_ref, ext_ref):
    blocks, _, rows, _ = qkv_ref.shape
    frames, frames_part = rows // patches, rows_part // patches
    tile, chunk = joined * rows_part, joined_keys * rows
    lane = lax.broadcasted_iota(jnp.int32, (tile, LANES), 1)
    mine_rows = slice(part * rows_part, (part + 1) * rows_part)
    ones = jnp.full((chunk, LANES), 1.0, bf16)

    def step(t, carry):
        query = jnp.concatenate(
            [qkv_ref[t * joined + i, 0, mine_rows, :] for i in range(joined)], axis=0
        )
        query = query * score_scale
        seen = jnp.concatenate(
            [
                jnp.broadcast_to(
                    vis_ref[pl.ds((t * joined + i) * frames + part * frames_part + f, 1), :],
                    (patches, LANES),
                )
                for i in range(joined)
                for f in range(frames_part)
            ],
            axis=0,
        )
        outs, ext_heads = [], []
        for h in range(2):
            mine = jnp.where((lane >= HDIM) == (h == 1), query, jnp.zeros_like(query))
            query_ext = jnp.concatenate([mine.astype(bf16), seen.astype(bf16)], axis=1)
            top = None
            for c in range(0, blocks, joined_keys):
                some_blocks = range(c, c + joined_keys)
                keys = jnp.concatenate(
                    [
                        jnp.concatenate(
                            [qkv_ref[b, 1], key_extra((b // 2) * frames, rows, patches)], axis=1
                        )
                        for b in some_blocks
                    ],
                    axis=0,
                )
                vals = jnp.concatenate([qkv_ref[b, 2] for b in some_blocks], axis=0)
                vals = jnp.concatenate([vals, ones], axis=1)
                scores = dot(query_ext, keys, NT)
                chunk_top = jnp.max(scores, axis=1, keepdims=True)
                new_top = chunk_top if top is None else jnp.maximum(top, chunk_top)
                some = dot(jnp.exp(scores - new_top).astype(bf16), vals)
                total = some if top is None else total * jnp.exp(top - new_top) + some
                top = new_top
            weight_sum = total[:, LANES : LANES + 1]
            outs.append(total[:, :LANES] / weight_sum)
            high, mid, low = split_three(-(top + jnp.log(weight_sum)))
            ext = jnp.where(lane == FRAMES, high, seen)
            ext = jnp.where(lane == FRAMES + 1, mid, ext)
            ext_heads.append(jnp.where(lane == FRAMES + 2, low, ext).astype(bf16))
        out = jnp.where(lane < HDIM, outs[0], outs[1]).astype(bf16)
        for i in range(joined):
            here = slice(i * rows_part, (i + 1) * rows_part)
            o_ref[t * joined + i] = out[here, :]
            for h in range(2):
                ext_ref[h, t * joined + i] = ext_heads[h][here, :]
        return carry

    lax.fori_loop(0, blocks // joined, step, 0)


def attend(heads, visible, patches, part, parts, tile=1024, chunk=1024):
    blocks, _, rows, _ = heads.shape
    rows_part = rows // parts
    keys = blocks * rows
    return pl.pallas_call(
        functools.partial(
            attend_kernel, part, rows_part, patches, tile // rows_part, chunk // rows
        ),
        out_shape=[
            jax.ShapeDtypeStruct((blocks, rows_part, LANES), bf16),
            jax.ShapeDtypeStruct((2, blocks, rows_part, LANES), bf16),
        ],
        in_specs=[pl.BlockSpec(memory_space=VMEM)] * 2,
        out_specs=[pl.BlockSpec(memory_space=VMEM)] * 2,
        compiler_params=pltpu.CompilerParams(vmem_limit_bytes=48 * MIB),
        cost_estimate=pl.CostEstimate(
            flops=8 * blocks * rows_part * keys * 2 * LANES,
            bytes_accessed=4 * MIB,
            transcendentals=0,
        ),
        name="attend",
    )(heads, visible)


def attend_back_kernel(parts, part, patches, joined, together, carried, last, *refs):
    at = 0

    def take(count):
        nonlocal at
        found = refs[at : at + count]
        at += count
        return found

    (qkv_ref, do_ref) = take(2)
    ext_refs, o_refs = take(parts), take(parts)
    ctime_ref, stime_ref, cpatch_ref, spatch_ref = take(4)
    if carried:
        carry_ref, mix_ref = take(2)
    if last:
        (grads_ref,) = take(1)
    else:
        grads_ref, carry_out, mix_ref = take(3)
    (dq_turned,) = refs[at:]
    blocks, _, rows, _ = qkv_ref.shape
    rows_part = rows // parts
    frames, frames_part = rows // patches, rows_part // patches
    lane = lax.broadcasted_iota(jnp.int32, (rows_part, LANES), 1)
    if carried:
        dq_turned[...] = carry_ref[...]
    else:
        dq_turned[...] = jnp.zeros_like(dq_turned)
        for b in range(blocks):
            for i in range(parts):
                there = slice(i * rows_part, (i + 1) * rows_part)
                mixed = do_ref[b, there, :].astype(f32) * o_refs[i][b].astype(f32)
                for h in range(2):
                    mine = jnp.where((lane >= HDIM) == (h == 1), mixed, 0.0)
                    high, mid, low = split_three(-jnp.sum(mine, axis=1, keepdims=True))
                    ext = jnp.where(lane == 1, mid, jnp.where(lane == 2, low, 0.0))
                    mix_ref[h, b, there, :] = jnp.where(lane == 0, high, ext).astype(bf16)
    key_rows = slice(part * rows_part, (part + 1) * rows_part)
    key_lane = lax.broadcasted_iota(jnp.int32, (together * rows_part, LANES), 1)
    mix_keys = jnp.where(key_lane < 3, 1.0, 0.0).astype(bf16)

    def back(value, row, half):
        cosine = ctime_ref[pl.ds(row, 1), :] + cpatch_ref[half]
        sine = stime_ref[pl.ds(row, 1), :] + spatch_ref[half]
        return rotate_lanes(value, cosine, -sine).astype(bf16)

    first = rows if last else 0

    def step(t, carry):
        key_blocks = [t * together + i for i in range(together)]
        keys = jnp.concatenate([qkv_ref[b, 1, key_rows, :] for b in key_blocks], axis=0)
        keys = keys * score_scale
        vals = jnp.concatenate([qkv_ref[b, 2, key_rows, :] for b in key_blocks], axis=0)
        turned = keys.astype(f32).T.astype(bf16)
        extra = jnp.concatenate(
            [
                key_extra((b // 2) * frames + part * frames_part, rows_part, patches)
                for b in key_blocks
            ],
            axis=0,
        )
        key_tiles, val_tiles = [], []
        for h in range(2):
            mine = (key_lane >= HDIM) == (h == 1)
            none = jnp.zeros_like(keys)
            key_tiles.append(
                jnp.concatenate([jnp.where(mine, keys, none).astype(bf16), extra], axis=1)
            )
            val_tiles.append(jnp.concatenate([jnp.where(mine, vals, none), mix_keys], axis=1))
        dk = [jnp.zeros((together * rows_part, LANES), f32)] * 2
        dv = [jnp.zeros((together * rows_part, LANES), f32)] * 2
        for c in range(0, blocks, joined):
            some = range(c, c + joined)
            span = slice(c * rows, (c + joined) * rows)
            query = jnp.concatenate([qkv_ref[b, 0] for b in some], axis=0)
            grad = jnp.concatenate([do_ref[b] for b in some], axis=0)
            for h in range(2):
                ext = jnp.concatenate([ext_refs[i][h, b] for b in some for i in range(parts)], axis=0)
                mix = jnp.concatenate([mix_ref[h, b] for b in some], axis=0)
                probs = jnp.exp(dot(key_tiles[h], jnp.concatenate([query, ext], axis=1), NT))
                dv[h] = dv[h] + dot(probs.astype(bf16), grad)
                moved = dot(val_tiles[h], jnp.concatenate([grad, mix], axis=1), NT)
                grad_scores = (probs * moved).astype(bf16)
                dk[h] = dk[h] + dot(grad_scores, query)
                head = slice(HDIM * h, HDIM * (h + 1))
                dq_turned[head, span] += dot(turned[head, :], grad_scores)
        dk = jnp.where(key_lane < HDIM, dk[0], dk[1]) * score_scale
        dv = jnp.where(key_lane < HDIM, dv[0], dv[1]).astype(bf16)
        for i, b in enumerate(key_blocks):
            for f in range(frames_part):
                rows_here = slice(i * rows_part + f * patches, i * rows_part + (f + 1) * patches)
                row = b * frames + part * frames_part + f
                keys_here = slice(first + f * patches, first + (f + 1) * patches)
                grads_ref[b, keys_here, :] = back(dk[rows_here, :], row, b % 2)
            grads_ref[b, first + rows_part : first + 2 * rows_part, :] = dv[
                i * rows_part : (i + 1) * rows_part, :
            ]
        return carry

    lax.fori_loop(0, blocks // together, step, 0)

    if last:
        for b in range(blocks):
            for f in range(frames):
                there = slice(b * rows + f * patches, b * rows + (f + 1) * patches)
                turned_back = back(dq_turned[:, there].T, b * frames + f, b % 2)
                grads_ref[b, f * patches : (f + 1) * patches, :] = turned_back
    else:
        carry_out[...] = dq_turned[...]


def attend_back(heads, grads, exts, outs, rotary, carry, part, last, patches, chunk=2048, together=2):
    parts = len(exts)
    blocks, _, rows, _ = heads.shape
    rows_part = rows // parts
    total = blocks * rows
    operands = [heads, grads, *exts, *outs, *rotary, *(carry or ())]
    kept = 2 * rows_part + (rows if last else 0)
    out_shape = [jax.ShapeDtypeStruct((blocks, kept, LANES), bf16)]
    if not last:
        out_shape.append(jax.ShapeDtypeStruct((LANES, total), f32))
        out_shape.append(jax.ShapeDtypeStruct((2, blocks, rows, LANES), bf16))
    return pl.pallas_call(
        functools.partial(
            attend_back_kernel, parts, part, patches, chunk // rows, together, carry is not None, last
        ),
        out_shape=out_shape,
        in_specs=[pl.BlockSpec(memory_space=VMEM)] * len(operands),
        out_specs=[pl.BlockSpec(memory_space=VMEM)] * len(out_shape),
        scratch_shapes=[VMEM((LANES, total), f32)],
        compiler_params=pltpu.CompilerParams(vmem_limit_bytes=56 * MIB),
        cost_estimate=pl.CostEstimate(
            flops=20 * total * blocks * rows_part * 2 * LANES,
            bytes_accessed=8 * MIB,
            transcendentals=0,
        ),
        name="attend_back",
    )(*operands)


def act_grad_kernel(cot_ref, gate_ref, down_ref, grad_ref, out_ref):
    frames, patches, _ = cot_ref.shape

    @pl.when(pl.program_id(0) == 0)
    def _():
        for f in range(frames):
            grad = gate_ref[f : f + 1, :] * cot_ref[f].astype(f32)
            grad_ref[f * patches : (f + 1) * patches, :] = grad.astype(bf16)

    out_ref[...] = dot(grad_ref[...], down_ref[...], NT)


def act_grad(cotangent, gate_two, down_weight, cols=512):
    frames, patches, width = cotangent.shape
    rows, inner = frames * patches, down_weight.shape[0]
    return pl.pallas_call(
        act_grad_kernel,
        out_shape=[
            jax.ShapeDtypeStruct((rows, width), bf16),
            jax.ShapeDtypeStruct((rows, inner), f32),
        ],
        grid=(inner // cols,),
        in_specs=[
            whole(cotangent.shape),
            whole(gate_two.shape),
            pl.BlockSpec((cols, width), lambda c: (c, 0)),
        ],
        out_specs=[whole((rows, width)), pl.BlockSpec((rows, cols), lambda c: (0, c))],
        compiler_params=pltpu.CompilerParams(vmem_limit_bytes=40 * MIB),
        cost_estimate=pl.CostEstimate(
            flops=2 * rows * width * inner, bytes_accessed=18 * MIB, transcendentals=0
        ),
        name="act_grad",
    )(cotangent, gate_two, down_weight)


def feed_kernel(hid_ref, grad_ref, actgrad_ref, up_ref, bias_ref, down_ref,
                branch_ref, back_ref, biasgrad_ref, joined_ref,
                hid_turned, up_slots, down_slots, up_sems, down_sems):
    step, steps = pl.program_id(0), pl.num_programs(0)
    width, cols = up_ref.shape
    group, clips, _, share, _ = joined_ref.shape
    some_clips, quarters = down_slots.shape[2:4]
    up_parts = width // cols
    slot = step % 2

    def copies(at):
        across = pl.ds(pl.multiple_of((at % up_parts) * cols, cols), cols)
        up_copy = pltpu.make_async_copy(
            up_slots.at[at % 2], joined_ref.at[:, :, at // up_parts, :, across], up_sems.at[at % 2]
        )
        down_copy = pltpu.make_async_copy(
            down_slots.at[at % 2],
            joined_ref.at[:, pl.ds(at * some_clips, some_clips), quarters : 2 * quarters],
            down_sems.at[at % 2],
        )
        return up_copy, down_copy

    @pl.when(step == 0)
    def _():
        hid_turned[...] = hid_ref[...].T

    @pl.when(step >= 2)
    def _():
        for copy in copies(step - 2):
            copy.wait()

    pre = dot(hid_ref[...], up_ref[...]) + bias_ref[...]
    square = pre * pre
    bend = jnp.tanh(pre * (0.7978845608 + (0.7978845608 * 0.044715) * square))
    half = 0.5 * (1.0 + bend)
    act = (pre * half).astype(bf16)
    slope = half + (0.5 * pre) * (1.0 - bend * bend) * (
        0.7978845608 + (0.7978845608 * 3.0 * 0.044715) * square
    )
    pre_grad = (slope * actgrad_ref[...]).astype(bf16)
    biasgrad_ref[...] = jnp.sum(pre_grad.astype(f32), axis=0, keepdims=True)
    branch = dot(act, down_ref[...])
    back = dot(pre_grad, up_ref[...], NT)
    up_grad = dot(hid_turned[...], pre_grad).astype(bf16)
    up_grad = up_grad.reshape(clips, group, share, cols)
    for c in range(clips):
        up_slots[slot, :, c] = up_grad[c]
    down_grad = dot(act.T, grad_ref[...]).astype(bf16)
    down_grad = down_grad.reshape(some_clips, group, quarters, share, width)
    for c in range(some_clips):
        down_slots[slot, :, c] = down_grad[c]

    @pl.when(step == 0)
    def _():
        branch_ref[...] = branch
        back_ref[...] = back

    @pl.when(step > 0)
    def _():
        branch_ref[...] += branch
        back_ref[...] += back

    for copy in copies(step):
        copy.start()

    @pl.when(step == steps - 1)
    def _():
        for at in (steps - 2, steps - 1):
            for copy in copies(at):
                copy.wait()


def feed_forward(hidden, grad, grad_act, up_weight, up_bias, down_weight, group, clips, cols=1024):
    rows, width = hidden.shape
    inner = up_weight.shape[1]
    share, quarters = width // (group * clips), inner // width
    some_clips = cols * clips // inner
    return pl.pallas_call(
        feed_kernel,
        out_shape=[
            jax.ShapeDtypeStruct((rows, width), f32),
            jax.ShapeDtypeStruct((rows, width), f32),
            jax.ShapeDtypeStruct((1, inner), f32),
            jax.ShapeDtypeStruct((group, clips, 2 * quarters + 1, share, width), bf16),
        ],
        grid=(inner // cols,),
        in_specs=[
            whole((rows, width)),
            whole((rows, width)),
            pl.BlockSpec((rows, cols), lambda c: (0, c)),
            pl.BlockSpec((width, cols), lambda c: (0, c)),
            pl.BlockSpec((1, cols), lambda c: (0, c)),
            pl.BlockSpec((cols, width), lambda c: (c, 0)),
        ],
        out_specs=[
            whole((rows, width)),
            whole((rows, width)),
            pl.BlockSpec((1, cols), lambda c: (0, c)),
            pl.BlockSpec(memory_space=pl.ANY),
        ],
        scratch_shapes=[
            VMEM((width, rows), bf16),
            VMEM((2, group, clips, share, cols), bf16),
            VMEM((2, group, some_clips, quarters, share, width), bf16),
            pltpu.SemaphoreType.DMA((2,)),
            pltpu.SemaphoreType.DMA((2,)),
        ],
        compiler_params=pltpu.CompilerParams(vmem_limit_bytes=58 * MIB),
        cost_estimate=pl.CostEstimate(
            flops=10 * rows * width * inner, bytes_accessed=44 * MIB, transcendentals=0
        ),
        name="feed_forward",
    )(hidden, grad, grad_act, up_weight, up_bias, down_weight)


def proj_grad_kernel(attn_ref, grad_ref, _, joined_ref):
    group, clips, _, share, width = joined_ref.shape
    grad = dot(attn_ref[...].T, grad_ref[...]).astype(bf16).reshape(clips, group, share, width)
    for c in range(clips):
        joined_ref[:, c, 0] = grad[c]


def proj_weight_grad(attn_low, grad_proj, joined):
    rows, width = attn_low.shape
    group, clips, entries, share, _ = joined.shape
    return pl.pallas_call(
        proj_grad_kernel,
        out_shape=jax.ShapeDtypeStruct(joined.shape, joined.dtype),
        grid=(1,),
        in_specs=[
            whole((rows, width)),
            whole((rows, width)),
            pl.BlockSpec(memory_space=pl.ANY),
        ],
        out_specs=pl.BlockSpec((group, clips, 1, share, width), lambda c: (0, 0, entries - 1, 0, 0)),
        input_output_aliases={2: 0},
        compiler_params=pltpu.CompilerParams(vmem_limit_bytes=40 * MIB),
        cost_estimate=pl.CostEstimate(
            flops=2 * rows * width * width, bytes_accessed=4 * MIB, transcendentals=0
        ),
        name="proj_weight_grad",
    )(attn_low, grad_proj, joined)


def merge_kernel(*refs):
    parts = len(refs) - 10
    att_refs = refs[:parts]
    (weight_ref, bias_ref, tok_ref, gate_one_ref, shift_ref, scale_ref,
     low_ref, proj_ref, after_ref, hid_ref) = refs[parts:]
    frames, patches, width = tok_ref.shape
    pairs, rows_part, _ = att_refs[0].shape
    for i, att_ref in enumerate(att_refs):
        low = jnp.concatenate([att_ref[p] for p in range(pairs)], axis=1)
        there = slice(i * rows_part, (i + 1) * rows_part)
        low_ref[there, :] = low
        proj = dot(low, weight_ref[...]) + bias_ref[...]
        proj_ref[there, :] = proj
        for j in range(rows_part // patches):
            f = i * (rows_part // patches) + j
            here = slice(f * patches, (f + 1) * patches)
            row = slice(f, f + 1)
            after = tok_ref[f].astype(f32) + gate_one_ref[row, :] * proj[
                j * patches : (j + 1) * patches, :
            ]
            after_ref[here, :] = after
            centre = after - jnp.mean(after, axis=1, keepdims=True)
            inv = lax.rsqrt(jnp.mean(centre * centre, axis=1, keepdims=True) + norm_eps)
            hid = centre * inv * (1.0 + scale_ref[row, :]) + shift_ref[row, :]
            hid_ref[here, :] = hid.astype(bf16)


def merge_heads(attended, proj_weight, proj_bias, tokens, mods):
    frames, patches, width = tokens.shape
    rows = frames * patches
    operands = [*attended, proj_weight, proj_bias, tokens, *mods]
    return pl.pallas_call(
        merge_kernel,
        out_shape=[
            jax.ShapeDtypeStruct((rows, width), bf16),
            jax.ShapeDtypeStruct((rows, width), f32),
            jax.ShapeDtypeStruct((rows, width), f32),
            jax.ShapeDtypeStruct((rows, width), bf16),
        ],
        in_specs=[pl.BlockSpec(memory_space=VMEM)] * len(operands),
        out_specs=[pl.BlockSpec(memory_space=VMEM)] * 4,
        compiler_params=pltpu.CompilerParams(vmem_limit_bytes=48 * MIB),
        cost_estimate=pl.CostEstimate(
            flops=2 * rows * width * width, bytes_accessed=16 * MIB, transcendentals=0
        ),
        name="merge_heads",
    )(*operands)


def column_sum(value):
    return jnp.sum(value, axis=0, keepdims=True)


def unmerge_kernel(back_ref, after_ref, cot_ref, gate_one_ref, scale_ref, weight_ref,
                   grad_ref, gproj_ref, parts_ref):
    frames, patches, width = cot_ref.shape
    for f in range(frames):
        here = slice(f * patches, (f + 1) * patches)
        row = slice(f, f + 1)
        after = after_ref[here, :]
        centre = after - jnp.mean(after, axis=1, keepdims=True)
        inv = lax.rsqrt(jnp.mean(centre * centre, axis=1, keepdims=True) + norm_eps)
        normed = centre * inv
        scaled = back_ref[here, :] * (1.0 + scale_ref[row, :])
        mean_grad = jnp.mean(scaled, axis=1, keepdims=True)
        mean_mix = jnp.mean(scaled * normed, axis=1, keepdims=True)
        grad = cot_ref[f].astype(f32) + inv * (scaled - mean_grad - normed * mean_mix)
        grad_ref[here, :] = grad
        gproj_ref[here, :] = (gate_one_ref[row, :] * grad).astype(bf16)
    step = 2 * patches
    for i in range(frames * patches // step):
        here = slice(i * step, (i + 1) * step)
        part = dot(gproj_ref[here, :], weight_ref[...], NT).astype(bf16)
        for p in range(parts_ref.shape[0]):
            parts_ref[p, here, :] = part[:, p * LANES : (p + 1) * LANES]


def unmerge_heads(back, after, cotangent, gate_one, scale_two, proj_weight):
    frames, patches, width = cotangent.shape
    rows = frames * patches
    operands = [back, after, cotangent, gate_one, scale_two, proj_weight]
    return pl.pallas_call(
        unmerge_kernel,
        out_shape=[
            jax.ShapeDtypeStruct((rows, width), f32),
            jax.ShapeDtypeStruct((rows, width), bf16),
            jax.ShapeDtypeStruct((width // LANES, rows, LANES), bf16),
        ],
        in_specs=[pl.BlockSpec(memory_space=VMEM)] * len(operands),
        out_specs=[pl.BlockSpec(memory_space=VMEM)] * 3,
        compiler_params=pltpu.CompilerParams(vmem_limit_bytes=48 * MIB),
        cost_estimate=pl.CostEstimate(
            flops=2 * rows * width * width, bytes_accessed=12 * MIB, transcendentals=0
        ),
        name="unmerge_heads",
    )(*operands)


def side_kernel(branch_ref, back_ref, after_ref, proj_ref, cot_ref, gate_two_ref, bias_ref,
                grad_ref, gproj_ref, gbranch_ref, out_ref, sums_ref, biases_ref):
    frames, patches, width = cot_ref.shape
    proj_sum = jnp.zeros((1, width), f32)
    down_sum = jnp.zeros((1, width), f32)
    for f in range(frames):
        here = slice(f * patches, (f + 1) * patches)
        cot = cot_ref[f].astype(f32)
        after = after_ref[here, :]
        branch = branch_ref[here, :] + bias_ref[...]
        out_ref[f] = (after + gate_two_ref[f : f + 1, :] * branch).astype(bf16)
        centre = after - jnp.mean(after, axis=1, keepdims=True)
        inv = lax.rsqrt(jnp.mean(centre * centre, axis=1, keepdims=True) + norm_eps)
        back = back_ref[here, :]
        for kind, term in enumerate(
            (grad_ref[here, :] * proj_ref[here, :], back, back * (centre * inv), cot * branch)
        ):
            sums_ref[kind * frames + f : kind * frames + f + 1, :] = column_sum(term)
        down_sum += column_sum(gbranch_ref[here, :].astype(f32))
        proj_sum += column_sum(gproj_ref[here, :].astype(f32))
    biases_ref[0:1, :] = proj_sum
    biases_ref[1:2, :] = down_sum


def side_sums(branch, back, after, proj, cotangent, gate_two, down_bias, grad_after, grad_proj,
              grad_branch):
    frames, patches, width = cotangent.shape
    operands = [branch, back, after, proj, cotangent, gate_two, down_bias, grad_after, grad_proj,
                grad_branch]
    return pl.pallas_call(
        side_kernel,
        out_shape=[
            jax.ShapeDtypeStruct((frames, patches, width), bf16),
            jax.ShapeDtypeStruct((4 * frames, width), f32),
            jax.ShapeDtypeStruct((2, width), f32),
        ],
        in_specs=[pl.BlockSpec(memory_space=VMEM)] * len(operands),
        out_specs=[pl.BlockSpec(memory_space=VMEM)] * 3,
        compiler_params=pltpu.CompilerParams(vmem_limit_bytes=48 * MIB),
        cost_estimate=pl.CostEstimate(flops=0, bytes_accessed=16 * MIB, transcendentals=0),
        name="side_sums",
    )(*operands)


def heads_grad_kernel(hid_ref, first_ref, last_ref, out_ref, bias_ref, total):
    rows = hid_ref.shape[2]
    rows_part = first_ref.shape[1] // 2
    grad = jnp.concatenate(
        [
            last_ref[0, :rows, :],
            jnp.concatenate(
                [first_ref[0, :rows_part, :], last_ref[0, rows : rows + rows_part, :]], axis=0
            ),
            jnp.concatenate([first_ref[0, rows_part:, :], last_ref[0, rows + rows_part :, :]], axis=0),
        ],
        axis=1,
    )
    some = dot(hid_ref[0], grad)
    some_bias = column_sum(grad.astype(f32))

    @pl.when(pl.program_id(0) == 0)
    def _():
        total[...] = some
        bias_ref[...] = some_bias

    @pl.when(pl.program_id(0) > 0)
    def _():
        total[...] += some
        bias_ref[...] += some_bias

    @pl.when(pl.program_id(0) == pl.num_programs(0) - 1)
    def _():
        devices, triple, _ = out_ref.shape
        share = triple // 3
        for k in range(3):
            part = total[:, k * LANES : (k + 1) * LANES].astype(bf16)
            out_ref[:, k * share : (k + 1) * share, :] = part.reshape(devices, share, LANES)


def heads_grad(hidden_clip, first, last, devices):
    blocks, width, rows = hidden_clip.shape
    shape = (devices, 3 * width // devices, LANES)
    return pl.pallas_call(
        heads_grad_kernel,
        out_shape=[
            jax.ShapeDtypeStruct(shape, bf16),
            jax.ShapeDtypeStruct((1, 3 * LANES), f32),
        ],
        grid=(blocks,),
        in_specs=[
            pl.BlockSpec((1, width, rows), lambda b: (b, 0, 0)),
            pl.BlockSpec((1,) + first.shape[1:], lambda b: (b, 0, 0)),
            pl.BlockSpec((1,) + last.shape[1:], lambda b: (b, 0, 0)),
        ],
        out_specs=[whole(shape), whole((1, 3 * LANES))],
        scratch_shapes=[VMEM((width, 3 * LANES), f32)],
        compiler_params=pltpu.CompilerParams(vmem_limit_bytes=40 * MIB),
        cost_estimate=pl.CostEstimate(
            flops=6 * blocks * rows * width * LANES, bytes_accessed=12 * MIB, transcendentals=0
        ),
        name="heads_grad",
    )(hidden_clip, first, last)


def finish_kernel(first_ref, last_ref, wq_ref, wk_ref, wv_ref, tok_ref, scale_ref, after_ref,
                  part_ref, partbias_ref, out_ref, send_ref, total):
    frames, patches, width = tok_ref.shape
    rows = frames * patches
    rows_part = first_ref.shape[1] // 2
    step = pl.program_id(0)
    query, keys, vals = [], [], []
    for p in range(first_ref.shape[0]):
        query.append(last_ref[p, :rows, :])
        keys.append(
            jnp.concatenate(
                [first_ref[p, :rows_part, :], last_ref[p, rows : rows + rows_part, :]], axis=0
            )
        )
        vals.append(
            jnp.concatenate([first_ref[p, rows_part:, :], last_ref[p, rows + rows_part :, :]], axis=0)
        )
    some = None
    for grads, weight_ref in ((query, wq_ref), (keys, wk_ref), (vals, wv_ref)):
        term = dot(jnp.concatenate(grads, axis=1), weight_ref[...], NT)
        some = term if some is None else some + term

    @pl.when(step == 0)
    def _():
        total[...] = some

    @pl.when(step > 0)
    def _():
        total[...] += some

    @pl.when(step == pl.num_programs(0) - 1)
    def _():
        shift_sums, scale_sums = [], []
        for f in range(frames):
            here = slice(f * patches, (f + 1) * patches)
            x = tok_ref[f].astype(f32)
            centre = x - jnp.mean(x, axis=1, keepdims=True)
            inv = lax.rsqrt(jnp.mean(centre * centre, axis=1, keepdims=True) + norm_eps)
            normed = centre * inv
            back = total[here, :]
            shift_sums.append(column_sum(back))
            scale_sums.append(column_sum(back * normed))
            scaled = back * (1.0 + scale_ref[f : f + 1, :])
            mean_grad = jnp.mean(scaled, axis=1, keepdims=True)
            mean_mix = jnp.mean(scaled * normed, axis=1, keepdims=True)
            grad = after_ref[here, :] + inv * (scaled - mean_grad - normed * mean_mix)
            out_ref[f] = grad.astype(bf16)
        sums = jnp.concatenate(shift_sums + scale_sums, axis=0)
        sums = jnp.concatenate(
            [sums[:, i : i + LANES] for i in range(0, width, LANES)], axis=0
        ).astype(bf16)
        bias = [partbias_ref[:, k * LANES : (k + 1) * LANES] for k in range(3)]
        high = [value.astype(bf16).astype(f32) for value in bias]
        low = [value - upper for value, upper in zip(bias, high)]
        bias = jnp.concatenate(high + low + [jnp.zeros((10, LANES), f32)], axis=0).astype(bf16)
        devices, triple, _ = part_ref.shape
        count = sums.shape[0]
        send_ref[:, count : count + triple, :] = part_ref[...]
        for d in range(devices):
            send_ref[d, :count, :] = sums
            send_ref[d, count + triple :, :] = bias


def finish(first, last, qkv_weight, tokens, scale_one, grad_after, part, part_bias, cols=256):
    frames, patches, width = tokens.shape
    rows = frames * patches
    steps, some = width // cols, cols // LANES

    devices, triple, _ = part.shape
    send_shape = (devices, 2 * frames * (width // LANES) + triple + 16, LANES)

    def column(third):
        return lambda c: (0, third * steps + c)

    return pl.pallas_call(
        finish_kernel,
        out_shape=[
            jax.ShapeDtypeStruct((frames, patches, width), bf16),
            jax.ShapeDtypeStruct(send_shape, bf16),
        ],
        grid=(steps,),
        in_specs=[
            pl.BlockSpec((some,) + first.shape[1:], lambda c: (c, 0, 0)),
            pl.BlockSpec((some,) + last.shape[1:], lambda c: (c, 0, 0)),
        ]
        + [pl.BlockSpec((width, cols), column(part)) for part in range(3)]
        + [whole(tokens.shape), whole(scale_one.shape), whole((rows, width))]
        + [whole(part.shape), whole(part_bias.shape)],
        out_specs=[whole((frames, patches, width)), whole(send_shape)],
        scratch_shapes=[VMEM((rows, width), f32)],
        compiler_params=pltpu.CompilerParams(vmem_limit_bytes=48 * MIB),
        cost_estimate=pl.CostEstimate(
            flops=6 * rows * width * width, bytes_accessed=16 * MIB, transcendentals=0
        ),
        name="finish",
    )(first, last, *[qkv_weight] * 3, tokens, scale_one, grad_after, part, part_bias)


def last_kernel(group, frames, got_ref, member_ref, cols_ref, rows_ref, bias_ref, ada_ref, adasum_ref):
    devices = got_ref.shape[0]
    clips = devices // group
    width = rows_ref.shape[1] // 3
    tiles = width // LANES
    count = 2 * frames * tiles
    share = (got_ref.shape[1] - count - 16) // 3
    for i in range(tiles // 2):
        sums = got_ref[:, i * 4 * frames : (i + 1) * 4 * frames, :]
        sums = sums.reshape(devices * 4 * frames, LANES)
        for j in range(2):
            for kind in range(2):
                level = dot(member_ref[2 * j + kind], sums).astype(bf16)
                at = kind * width + (2 * i + j) * LANES
                ada_ref[:, at : at + LANES] = dot(cols_ref[...], level)
                adasum_ref[:, at : at + LANES] = column_sum(level.astype(f32))
    for p in range(group):
        bias = got_ref[p, count + 3 * share :, :].astype(f32)
        for c in range(1, clips):
            bias = bias + got_ref[c * group + p, count + 3 * share :, :].astype(f32)
        for third in range(3):
            at = third * width + p * LANES
            here = slice(count + third * share, count + (third + 1) * share)
            total = got_ref[p, here, :].astype(f32)
            for c in range(1, clips):
                total = total + got_ref[c * group + p, here, :].astype(f32)
            rows_ref[:, at : at + LANES] = total
            bias_ref[:, at : at + LANES] = bias[third : third + 1, :] + bias[third + 3 : third + 4, :]


def last_sums(got, member, columns, group, frames, width):
    devices = got.shape[0]
    share = width // devices
    return pl.pallas_call(
        functools.partial(last_kernel, group, frames),
        out_shape=[
            jax.ShapeDtypeStruct((share, 3 * width), f32),
            jax.ShapeDtypeStruct((1, 3 * width), f32),
            jax.ShapeDtypeStruct((share, 2 * width), f32),
            jax.ShapeDtypeStruct((1, 2 * width), f32),
        ],
        in_specs=[pl.BlockSpec(memory_space=VMEM)] * 3,
        out_specs=[pl.BlockSpec(memory_space=VMEM)] * 4,
        compiler_params=pltpu.CompilerParams(vmem_limit_bytes=48 * MIB),
        cost_estimate=pl.CostEstimate(flops=0, bytes_accessed=4 * MIB, transcendentals=0),
        name="last_sums",
    )(got, member, columns)


def body(
    tokens,
    out_cotangent,
    level_embed,
    ada_weight,
    ada_bias,
    qkv_weight,
    qkv_bias,
    proj_weight,
    proj_bias,
    up_weight,
    up_bias,
    down_weight,
    down_bias,
    context_count,
    frame_level,
    slot_time,
):
    frames, patches, width = tokens.shape
    rows = frames * patches
    inner = up_weight.shape[1]
    frm_count, sp_count = lax.axis_size("frm"), lax.axis_size("sp")
    devices = frm_count * sp_count
    group = FRAMES // frames * sp_count
    clips = devices // group
    frm, sp = lax.axis_index("frm"), lax.axis_index("sp")
    me = frm * sp_count + sp
    clip = me // group
    clip_groups = [list(range(first, first + group)) for first in range(0, devices, group)]
    across_clips = [list(range(first, devices, group)) for first in range(group)]
    everyone = [list(range(devices))]
    halves = 2
    share = width // devices
    per_dest = inner // devices

    levels_here = level_embed.shape[0]
    embed_all = to_everyone(level_embed, devices).reshape(devices * levels_here, width)

    clip_times = lax.dynamic_slice_in_dim(slot_time, clip * FRAMES, FRAMES)
    clip_levels = lax.dynamic_index_in_dim(frame_level, clip, 0, keepdims=False)
    context = lax.dynamic_index_in_dim(context_count, clip, 0, keepdims=False)
    seen = (clip_times[None, :] <= clip_times[:, None]) | (clip_times[None, :] < context)
    visible = jnp.pad(
        jnp.where(seen, 0.0, masked_out).astype(f32), ((0, 0), (0, LANES - FRAMES))
    )

    def by_blocks(table):
        table = table.reshape(FRAMES // frames, 1, frames, LANES)
        return jnp.broadcast_to(table, (FRAMES // frames, sp_count, frames, LANES)).reshape(
            group * frames, LANES
        )

    visible = by_blocks(visible)
    freq, sign, time_lane, row_lane = rotary_lanes()
    angle_time = clip_times.astype(f32)[:, None] * freq[None, :]
    ctime = by_blocks(jnp.where(time_lane[None, :], jnp.cos(angle_time), 0.0))
    stime = by_blocks(jnp.where(time_lane[None, :], jnp.sin(angle_time) * sign[None, :], 0.0))
    patch_ids = jnp.arange(sp_count * patches, dtype=jnp.int32).reshape(sp_count, patches)
    place = jnp.where(
        row_lane[None, None, :], (patch_ids // GRID)[..., None], (patch_ids % GRID)[..., None]
    )
    angle_patch = place.astype(f32) * freq[None, None, :]
    cpatch = jnp.where(time_lane, 0.0, jnp.cos(angle_patch))
    spatch = jnp.where(time_lane, 0.0, jnp.sin(angle_patch) * sign)
    rotary = [ctime, stime, cpatch, spatch]

    def my_table(time_part, patch_part):
        mine = lax.dynamic_slice_in_dim(time_part, me % group * frames, frames)
        half = lax.dynamic_index_in_dim(patch_part, sp, 0, keepdims=False)
        return (mine[:, None, :] + half[None]).reshape(rows, LANES)

    cosine, sine = my_table(ctime, cpatch), my_table(stime, spatch)

    my_times = lax.dynamic_slice_in_dim(slot_time, frm * frames, frames)
    my_levels = jnp.take(clip_levels, my_times)
    embed_act = jax.nn.silu(embed_all.astype(f32)).astype(bf16)
    level_ids = jnp.arange(devices * levels_here, dtype=jnp.int32)
    pick = (my_levels[:, None] == level_ids[None, :]).astype(bf16)
    my_embed = dot(pick, embed_act).astype(bf16)
    frame_mod = dot(my_embed, ada_weight) + ada_bias.astype(f32)
    frame_mod = lax.reduce_precision(frame_mod, 8, 7)
    shift_one, scale_one, gate_one, shift_two, scale_two, gate_two = [
        frame_mod[:, i * width : (i + 1) * width] for i in range(6)
    ]

    hidden_turned, head_parts = project(
        tokens, shift_one, scale_one, qkv_weight, qkv_bias.astype(f32)[None, :], cosine, sine
    )
    heads = exchange(head_parts, clip_groups)

    grad_branch, grad_act = act_grad(out_cotangent, gate_two, down_weight)
    slot_ids = (jnp.arange(devices * frames, dtype=jnp.int32) // (sp_count * frames)) * frames
    slot_ids = slot_ids + jnp.arange(devices * frames, dtype=jnp.int32) % frames
    slot_levels = frame_level[slot_ids // FRAMES, slot_time[slot_ids]]
    member_of = (level_ids[:, None] == slot_levels[None, :]).astype(bf16)
    my_columns = lax.dynamic_slice_in_dim(embed_act, me * share, share, axis=1)
    which = jnp.arange(4, dtype=jnp.int32)
    member_last = jnp.where(
        (which[:, None] == which[None, :])[:, None, None, :, None],
        member_of.reshape(1, -1, devices, 1, frames),
        jnp.zeros((), bf16),
    ).reshape(4, -1, devices * 4 * frames)
    columns_turned = my_columns.T
    heads, grad_branch, grad_act, member_of, my_columns, member_last, columns_turned = (
        lax.optimization_barrier(
            (heads, grad_branch, grad_act, member_of, my_columns, member_last, columns_turned)
        )
    )
    outs, exts, attended = [], [], []
    for part in range(halves):
        out, ext = attend(heads, visible, patches, part, halves)
        outs.append(out)
        exts.append(ext)
        attended.append(exchange(out, clip_groups))

    hidden_turned, _ = lax.optimization_barrier((hidden_turned, heads))
    hidden_clip = lax.all_gather(hidden_turned, AXES, axis_index_groups=clip_groups)

    attn_low, attn_proj, after_attn, hidden_two = merge_heads(
        attended,
        proj_weight,
        proj_bias.astype(f32)[None, :],
        tokens,
        (gate_one, shift_two, scale_two),
    )
    branch, grad_hidden_two, up_b_grad, joined = feed_forward(
        hidden_two,
        grad_branch,
        grad_act,
        up_weight,
        up_bias.astype(f32)[None, :],
        down_weight,
        group,
        clips,
    )
    grad_after, grad_proj, grad_parts = unmerge_heads(
        grad_hidden_two, after_attn, out_cotangent, gate_one, scale_two, proj_weight
    )
    grads = exchange(grad_parts, clip_groups)
    block_out, early_sums, early_biases = side_sums(
        branch,
        grad_hidden_two,
        after_attn,
        attn_proj,
        out_cotangent,
        gate_two,
        down_bias.astype(f32)[None, :],
        grad_after,
        grad_proj,
        grad_branch,
    )

    joined = proj_weight_grad(attn_low, grad_proj, joined)
    joined, hidden_clip = lax.optimization_barrier((joined, hidden_clip))
    summed = joined
    for groups in (clip_groups, across_clips):
        summed = lax.psum_scatter(
            summed, AXES, scatter_dimension=0, axis_index_groups=groups, tiled=True
        )[0]
    summed = summed.astype(f32)
    quarters = inner // width
    up_w_out = jnp.concatenate([summed[i] for i in range(quarters)], axis=1)
    down_w_out = summed[quarters : 2 * quarters].reshape(per_dest, width)
    proj_w_out = summed[2 * quarters]

    def slot_parts(slot_sums, biases):
        kinds = slot_sums.shape[0] // frames
        sums = slot_sums.reshape(kinds, frames, width).transpose(1, 0, 2).reshape(frames, -1)
        sums = jnp.broadcast_to(sums.astype(bf16)[None], (devices, frames, kinds * width))
        high = biases.astype(bf16)
        low = (biases - high.astype(f32)).astype(bf16)
        both = jnp.concatenate([high, low], axis=1).reshape(devices, frames, -1)
        lanes = -(-both.shape[2] // LANES) * LANES
        both = jnp.pad(both, ((0, 0), (0, 0), (0, lanes - both.shape[2])))
        return jnp.concatenate([sums, both], axis=2)

    def bias_share(got, count, size):
        extra = jnp.sum(got[:, :, count:].astype(f32), axis=0)
        extra = extra[:, : 2 * size // frames].reshape(-1)
        return extra[:size] + extra[size:]

    def level_out(got, count):
        slots = got[:, :, :count].reshape(devices * frames, count)
        level_grad = dot(member_of, slots).astype(bf16)
        return dot(my_columns, level_grad, TN), jnp.sum(level_grad.astype(f32), axis=0)

    early_parts = slot_parts(
        early_sums,
        jnp.concatenate(
            [
                up_b_grad.reshape(devices, per_dest),
                early_biases[0].reshape(devices, share),
                early_biases[1].reshape(devices, share),
            ],
            axis=1,
        ),
    )
    early_parts, _ = lax.optimization_barrier((early_parts, grads))
    early_got = exchange(early_parts, everyone)

    first_grads, carry, mixes = attend_back(
        heads, grads, exts, outs, rotary, None, 0, False, patches
    )
    carry, early_got = lax.optimization_barrier((carry, early_got))
    own_first = exchange(first_grads, clip_groups)
    (last_grads,) = attend_back(
        heads, grads, exts, outs, rotary, (carry, mixes), 1, True, patches
    )
    last_parts, own_first = lax.optimization_barrier((last_grads, own_first))
    own_last = exchange(last_parts, clip_groups)

    early_w, early_b = level_out(early_got, 4 * width)
    early_bias_out = bias_share(early_got, 4 * width, per_dest + 2 * share)
    up_b_out = early_bias_out[:per_dest]
    proj_b_out = early_bias_out[per_dest : per_dest + share]
    down_b_out = early_bias_out[per_dest + share :]

    qkv_part, qkv_b_part = heads_grad(hidden_clip, first_grads, last_grads, devices)
    tokens_grad, last_send = finish(
        own_first, own_last, qkv_weight, tokens, scale_one, grad_after, qkv_part, qkv_b_part
    )
    last_got = exchange(last_send, everyone)
    qkv_w_out, qkv_b_all, late_w, late_b = last_sums(
        last_got, member_last, columns_turned, group, frames, width
    )
    qkv_b_out = lax.dynamic_slice_in_dim(qkv_b_all[0], me * 3 * share, 3 * share)
    ada_w_out = jnp.concatenate([late_w, early_w], axis=1)
    ada_b_all = jnp.concatenate([late_b[0], early_b])
    ada_share = ada_b_all.shape[0] // devices
    ada_b_out = lax.dynamic_slice_in_dim(ada_b_all, me * ada_share, ada_share)
    return (
        block_out,
        tokens_grad,
        ada_w_out,
        ada_b_out,
        qkv_w_out,
        qkv_b_out,
        proj_w_out,
        proj_b_out,
        up_w_out,
        up_b_out,
        down_w_out,
        down_b_out,
    )


def solution(mesh):
    tokens_spec = P("frm", "sp", None)
    rows_spec = P(AXES, None)
    vector_spec = P(AXES)
    return jax.shard_map(
        body,
        mesh=mesh,
        in_specs=(tokens_spec, tokens_spec, rows_spec) + (P(),) * 13,
        out_specs=(tokens_spec, tokens_spec) + (rows_spec, vector_spec) * 5,
        check_vma=False,
    )
```

time: 480 us -> 453 us (0.944)
  blocking collectives: 42.2 us -> 0 us
  local copies, waits for them, and re-layouts: 31.1 us -> 43 us
    all_to_all x1 -> x0, blocking collectives: 42.2 us -> none  [exchange(): return lax.all_to_all(value, AXES, 0, 0, axis_index_groups=groups)]
    pallas_call x3 -> x5, Pallas kernels: 19 us -> 32.5 us  [the longest x1 9.35 us: act_grad(): pl.pallas_call(act_grad_kernel, out_shape=[jax.ShapeDtypeStruct((rows, wi...]
    unnamed x70 -> x74, local copies, waits for them, and re-layouts: 18.1 us -> 27.8 us
    pallas_call x2, Pallas kernels: 113 us -> 104 us  [attend_back(): pl.pallas_call(functools.partial(attend_back_kernel, parts, part, patches...]
  transfers between devices with their start and end apart: 11 -> 12, of which waited for: 5 -> 6; matrix products, arithmetic and copies ran while one was open for 5% -> 6% of each run, Pallas kernels for 50% -> 54%
where the time goes in v3:
time: 453 us; the launch traced here: 445 us
  Pallas kernels  248 us (55%)
  waiting for transfers between devices  76.3 us (17%)
  local copies, waits for them, and re-layouts  43 us (9%)
  starting transfers between devices  41.1 us (9%)
  between operations  14.7 us (3%)
  other arithmetic  14.4 us (3%)
  matrix products  7.55 us (2%)
    pallas_call x2, Pallas kernels, attend_back(): pl.pallas_call(functools.partial(attend_back_kernel, parts, part, patches...  104 us
    all_to_all x9, waiting for transfers between devices, exchange(): return lax.all_to_all(value, AXES, 0, 0, axis_index_groups=groups)  74.7 us
    pallas_call x2, Pallas kernels, attend(): pl.pallas_call(functools.partial(attend_kernel, part, rows_part, patches,...  48.8 us
    all_to_all x9, starting transfers between devices, exchange(): return lax.all_to_all(value, AXES, 0, 0, axis_index_groups=groups)  40.8 us
    pallas_call x1, Pallas kernels, feed_forward(): pl.pallas_call(feed_kernel, out_shape=[jax.ShapeDtypeStruct((rows, width)...  36.3 us
    unnamed x74, local copies, waits for them, and re-layouts  27.8 us
    pallas_call x1, Pallas kernels, finish(): pl.pallas_call(finish_kernel, out_shape=[jax.ShapeDtypeStruct((frames, pa...  10.4 us
    pallas_call x1, Pallas kernels, act_grad(): pl.pallas_call(act_grad_kernel, out_shape=[jax.ShapeDtypeStruct((rows, wi...  9.35 us
  transfers between devices with their start and end apart: 12, of which 6 were waited for; matrix products, arithmetic and copies ran while one was open for 6% of the time, Pallas kernels for 54%

profile of v3, /device:TPU:0, one launch (start us, length us, event | category | flops | bytes accessed | tf_op | source)
XLA Modules:
  0.0 445.1 jit_solution(14893830801550308023)
XLA Ops:
  7.2 1.4 broadcast_in_dim.170
  8.6 7.3 %all-to-all-start = ((bf16[32,2,1024]{2,1,0:T(2,128)(2,1)}), bf16[32,2,1024]{2,1,0:T(2,128)(2,1)S(1)}, u32[]{:S(2)}, u32[]{:S(2)}) async-start(bf16[32,2,1024]{2,1,0:T(2,128)(2,1)} %broadcast_in_dim.170), calls=%async_computation | async-start | bytes 262144 | tf_op jit(solution)/shard_map/all_to_all | solution.py:37
  18.1 1.2 dynamic_slice.46
  19.3 1.4 broadcast_compare_fusion.1
  20.8 0.8 fusion.8
  21.6 1.5 multiply_select_fusion
  25.2 5.8 %fusion = f32[4,6144]{1,0:T(4,128)S(1)} fusion(bf16[1024,6144]{1,0:T(8,128)(2,1)} %param.27, bf16[64,1024]{0,1:T(8,128)(2,1)S(1)} %multiply_convert_fusion, f32[6144]{0:T(1024)S(1)} %convert_element_type.85, s32[4]{0:T(128)S(1)} %and_select_fusion.5), kind=kOutput, calls=%fused_computation.4 | convolution fusion | flops 50909440 | bytes 12836880 | tf_op jit(solution)/shard_map/dot_general | solution.py:33
  31.1 2.8 copy-done.2
  33.8 8.8 %project.1 = (bf16[1024,512]{1,0:T(8,128)(2,1)}, bf16[8,3,512,128]{3,2,1,0:T(8,128)(2,1)S(1)}) custom-call(bf16[4,128,1024]{2,1,0:T(8,128)(2,1)S(1)} %copy-done.3, f32[4,1024]{1,0:T(4,128)S(1)} %get-tuple-element.124.shift_ref, f32[4,1024]{1,0:T(4,128)S(1)} %get-tuple-element.123.scale_ref, bf16[1024,3072]{1,0:T(8,128)(2,1)S(1)} %copy-done.2, ...), custom_call_target="tpu_custom_call" | custom-call | flops 3221225472 | bytes 10485760 | tf_op jit(solution)/shard_map/project/pallas_call | solution.py:114
  42.6 1.6 copy-done.6
  44.2 4.6 %all-to-all-start.1 = ((bf16[8,3,512,128]{3,2,1,0:T(8,128)(2,1)}), bf16[8,3,512,128]{3,2,1,0:T(8,128)(2,1)}, u32[]{:S(2)}, u32[]{:S(2)}) async-start(bf16[8,3,512,128]{3,2,1,0:T(8,128)(2,1)} %copy-done.6), calls=%async_computation.1 | async-start | bytes 6291456 | tf_op jit(solution)/shard_map/all_to_all | solution.py:37
  48.9 1.2 gather_fusion.1
  50.1 1.5 gather_fusion.2
  53.6 9.3 %act_grad.1 = (bf16[512,1024]{1,0:T(8,128)(2,1)S(1)}, f32[512,4096]{1,0:T(8,128)S(1)}) custom-call(bf16[4,128,1024]{2,1,0:T(8,128)(2,1)S(1)} %copy-done.5, f32[4,1024]{1,0:T(4,128)S(1)} %get-tuple-element.122.gate_ref.gate_two_ref, bf16[4096,1024]{1,0:T(8,128)(2,1)} %down_ref.3), custom_call_target="tpu_custom_call" | custom-call | flops 4294967296 | bytes 18874368 | tf_op jit(solution)/shard_map/act_grad/pallas_call | solution.py:395
  63.0 1.0 copy-done.10
  63.9 3.3 copy-done.21
  67.2 19.5 %all-to-all-done.1.qkv_ref.refs_0_ = bf16[8,3,512,128]{3,2,1,0:T(8,128)(2,1)} async-done(((bf16[8,3,512,128]{3,2,1,0:T(8,128)(2,1)}), bf16[8,3,512,128]{3,2,1,0:T(8,128)(2,1)}, u32[]{:S(2)}, u32[]{:S(2)}) %all-to-all-start.1) | async-done | bytes 3145760 | tf_op jit(solution)/shard_map/all_to_all | solution.py:37
  86.8 24.9 %attend.2 = (bf16[8,256,128]{2,1,0:T(8,128)(2,1)}, bf16[2,8,256,128]{3,2,1,0:T(8,128)(2,1)S(1)}) custom-call(bf16[8,3,512,128]{3,2,1,0:T(8,128)(2,1)} %all-to-all-done.1.qkv_ref.refs_0_, f32[32,128]{1,0:T(8,128)S(1)} %bitcast.61), custom_call_target="tpu_custom_call" | custom-call | flops 17179869184 | bytes 4194304 | tf_op jit(solution)/shard_map/attend/pallas_call | solution.py:221
  111.7 1.0 copy-done.22
  112.7 3.9 all-to-all-start.2
  116.7 23.9 %attend.3 = (bf16[8,256,128]{2,1,0:T(8,128)(2,1)S(1)}, bf16[2,8,256,128]{3,2,1,0:T(8,128)(2,1)S(1)}) custom-call(bf16[8,3,512,128]{3,2,1,0:T(8,128)(2,1)} %all-to-all-done.1.qkv_ref.refs_0_, f32[32,128]{1,0:T(8,128)S(1)} %bitcast.62), custom_call_target="tpu_custom_call" | custom-call | flops 17179869184 | bytes 4194304 | tf_op jit(solution)/shard_map/attend/pallas_call | solution.py:221
  140.6 0.8 copy-done.16
  141.4 1.0 copy-done.23
  142.4 4.2 all-to-all-start.3
  147.4 8.9 %all-to-all-done.3.refs_1_ = bf16[8,256,128]{2,1,0:T(8,128)(2,1)S(1)} async-done(((bf16[8,256,128]{2,1,0:T(8,128)(2,1)}), bf16[8,256,128]{2,1,0:T(8,128)(2,1)S(1)}, u32[]{:S(2)}, u32[]{:S(2)}) %all-to-all-start.3) | async-done | bytes 524320 | tf_op jit(solution)/shard_map/all_to_all | solution.py:37
  156.3 5.1 %merge_heads.1 = (bf16[512,1024]{1,0:T(8,128)(2,1)S(1)}, f32[512,1024]{1,0:T(8,128)}, f32[512,1024]{1,0:T(8,128)}, bf16[512,1024]{1,0:T(8,128)(2,1)S(1)}) custom-call(bf16[8,256,128]{2,1,0:T(8,128)(2,1)S(1)} %all-to-all-done.2.refs_0_, bf16[8,256,128]{2,1,0:T(8,128)(2,1)S(1)} %all-to-all-done.3.refs_1_, bf16[1024,1024]{1,0:T(8,128)(2,1)} %weight_ref.1, ...), custom_call_target="tpu_custom_call" | custom-call | flops 1073741824 | bytes 16777216 | tf_op jit(solution)/shard_map/merge_heads/pallas_call | solution.py:591
  161.4 1.0 copy-done.20
  162.3 36.3 %feed_forward.1 = (f32[512,1024]{1,0:T(8,128)}, f32[512,1024]{1,0:T(8,128)}, f32[1,4096]{1,0:T(1,128)}, bf16[8,4,9,32,1024]{4,3,2,1,0:T(8,128)(2,1)}) custom-call(bf16[512,1024]{1,0:T(8,128)(2,1)} %copy-done.20, bf16[512,1024]{1,0:T(8,128)(2,1)} %copy-done.10, f32[512,4096]{1,0:T(8,128)} %copy-done.21, bf16[1024,4096]{1,0:T(8,128)(2,1)} %up_ref.1, ...), custom_call_target="tpu_custom_call" | custom-call | flops 21474836480 | bytes 46137344 | tf_op jit(solution)/shard_map/feed_forward/pallas_call | solution.py:493
  198.6 5.4 %unmerge_heads.1 = (f32[512,1024]{1,0:T(8,128)S(1)}, bf16[512,1024]{1,0:T(8,128)(2,1)S(1)}, bf16[8,512,128]{2,1,0:T(8,128)(2,1)S(1)}) custom-call(f32[512,1024]{1,0:T(8,128)} %get-tuple-element.70.back_ref, f32[512,1024]{1,0:T(8,128)} %get-tuple-element.71.after_ref, bf16[4,128,1024]{2,1,0:T(8,128)(2,1)S(1)} %copy-done.5, ...), custom_call_target="tpu_custom_call" | custom-call | flops 1073741824 | bytes 12582912 | tf_op jit(solution)/shard_map/unmerge_heads/pallas_call | solution.py:641
  204.0 1.3 copy-done.4
  205.3 1.0 copy-done.12
  206.3 2.6 proj_weight_grad.1
  209.7 4.2 all-to-all-start.4
  213.9 1.7 copy-done.7
  215.6 1.5 copy-done.11
  217.1 7.5 %side_sums.1 = (bf16[4,128,1024]{2,1,0:T(8,128)(2,1)}, f32[16,1024]{1,0:T(8,128)S(1)}, f32[2,1024]{1,0:T(2,128)S(1)}) custom-call(f32[512,1024]{1,0:T(8,128)S(1)} %copy-done.7, f32[512,1024]{1,0:T(8,128)} %get-tuple-element.70.back_ref, f32[512,1024]{1,0:T(8,128)} %get-tuple-element.71.after_ref, f32[512,1024]{1,0:T(8,128)} %get-tuple-element.72.proj_ref, ...), custom_call_target="tpu_custom_call" | custom-call | bytes 16777216 | tf_op jit(solution)/shard_map/side_sums/pallas_call | solution.py:687
  225.5 1.5 pad_maximum_fusion
  227.1 2.3 all-to-all-done.4.refs_1_
  229.3 4.4 all-to-all-start.5
  233.7 51.4 %attend_back.2 = (bf16[8,512,128]{2,1,0:T(8,128)(2,1)}, f32[128,4096]{1,0:T(8,128)}, bf16[2,8,512,128]{3,2,1,0:T(8,128)(2,1)}) custom-call(bf16[8,3,512,128]{3,2,1,0:T(8,128)(2,1)} %all-to-all-done.1.qkv_ref.refs_0_, bf16[8,512,128]{2,1,0:T(8,128)(2,1)} %all-to-all-done.4.refs_1_, bf16[2,8,256,128]{3,2,1,0:T(8,128)(2,1)} %copy-done.22, ...), custom_call_target="tpu_custom_call" | custom-call | flops 42949672960 | bytes 8388608 | tf_op jit(solution)/shard_map/attend_back/pallas_call | solution.py:362
  285.2 1.0 copy-done.25
  286.2 4.2 all-to-all-start.6
  290.4 52.4 %attend_back.3.last_ref = bf16[8,1024,128]{2,1,0:T(8,128)(2,1)} custom-call(bf16[8,3,512,128]{3,2,1,0:T(8,128)(2,1)} %all-to-all-done.1.qkv_ref.refs_0_, bf16[8,512,128]{2,1,0:T(8,128)(2,1)} %all-to-all-done.4.refs_1_, bf16[2,8,256,128]{3,2,1,0:T(8,128)(2,1)} %copy-done.22, bf16[2,8,256,128]{3,2,1,0:T(8,128)(2,1)} %copy-done.23, ...), custom_call_target="tpu_custom_call" | custom-call | flops 42949672960 | bytes 8388608 | tf_op jit(solution)/shard_map/attend_back/pallas_call | solution.py:362
  342.7 4.4 all-to-all-start.7
  347.2 1.5 reduce-scatter.3.cloned.1.call-done
  348.7 1.6 copy-done.8
  350.3 3.4 copy-done.19
  353.7 7.0 %heads_grad.1 = (bf16[32,96,128]{2,1,0:T(8,128)(2,1)S(1)}, f32[1,384]{1,0:T(1,128)S(1)}) custom-call(bf16[8,1024,512]{2,1,0:T(8,128)(2,1)S(1)} %bitcast.64, bf16[8,512,128]{2,1,0:T(8,128)(2,1)S(1)} %copy-done.13, bf16[8,1024,128]{2,1,0:T(8,128)(2,1)S(1)} %copy-done.8), custom_call_target="tpu_custom_call" | custom-call | flops 3221225472 | bytes 12582912 | tf_op jit(solution)/shard_map/heads_grad/pallas_call | solution.py:740
  360.7 0.9 copy-done.14
  361.6 12.1 %all-to-all-done.7.last_ref = bf16[8,1024,128]{2,1,0:T(8,128)(2,1)} async-done(((bf16[8,1024,128]{2,1,0:T(8,128)(2,1)}), bf16[8,1024,128]{2,1,0:T(8,128)(2,1)}, u32[]{:S(2)}, u32[]{:S(2)}) %all-to-all-start.7) | async-done | bytes 2097184 | tf_op jit(solution)/shard_map/all_to_all | solution.py:37
  373.8 1.1 copy-done.15
  374.9 10.4 %finish.1 = (bf16[4,128,1024]{2,1,0:T(8,128)(2,1)}, bf16[32,176,128]{2,1,0:T(8,128)(2,1)S(1)}) custom-call(bf16[8,512,128]{2,1,0:T(8,128)(2,1)S(1)} %all-to-all-done.6.first_ref, bf16[8,1024,128]{2,1,0:T(8,128)(2,1)} %all-to-all-done.7.last_ref, bf16[1024,3072]{1,0:T(8,128)(2,1)} %wv_ref.3, bf16[1024,3072]{1,0:T(8,128)(2,1)} %wv_ref.3, ...), custom_call_target="tpu_custom_call" | custom-call | flops 3221225472 | bytes 16777216 | tf_op jit(solution)/shard_map/finish/pallas_call | solution.py:836
  385.3 1.1 copy-done.9
  386.4 3.6 all-to-all-start.8
  390.0 2.4 copy.61
  392.5 1.1 reshape.374
  393.6 0.8 convert_reduce_fusion.1
  395.6 1.5 convert_reduce_fusion
  397.3 31.9 %all-to-all-done.8.got_ref = bf16[32,176,128]{2,1,0:T(8,128)(2,1)S(1)} async-done(((bf16[32,176,128]{2,1,0:T(8,128)(2,1)}), bf16[32,176,128]{2,1,0:T(8,128)(2,1)S(1)}, u32[]{:S(2)}, u32[]{:S(2)}) %all-to-all-start.8) | async-done | bytes 1441824 | tf_op jit(solution)/shard_map/all_to_all | solution.py:37
  429.3 3.3 last_sums.1
  433.8 0.9 pad_maximum_fusion.1
  434.7 1.3 convert_element_type.99
  436.7 0.8 pad_maximum_fusion.2
  437.5 0.8 slice.113
  (129 shorter events, 12.1 us)
Async XLA Ops:
  7.2 9.5 %copy-start = (s32[4,16]{1,0:T(4,128)S(1)}, s32[4,16]{1,0:T(4,128)}, u32[]{:S(2)}) copy-start(s32[4,16]{1,0:T(4,128)} %param.38) | copy-start | bytes 772
  8.6 16.1 %all-to-all-start = ((bf16[32,2,1024]{2,1,0:T(2,128)(2,1)}), bf16[32,2,1024]{2,1,0:T(2,128)(2,1)S(1)}, u32[]{:S(2)}, u32[]{:S(2)}) async-start(bf16[32,2,1024]{2,1,0:T(2,128)(2,1)} %broadcast_in_dim.170), calls=%async_computation | async-start | bytes 262144 | tf_op jit(solution)/shard_map/all_to_all | solution.py:37
  23.1 1.6 copy-start.28
  23.1 1.9 copy-start.27
  23.2 7.8 %copy-start.31 = (f32[4,2,4,128]{3,2,1,0:T(4,128)}, f32[4,2,4,128]{3,2,1,0:T(4,128)S(1)}, u32[]{:S(2)}) copy-start(f32[4,2,4,128]{3,2,1,0:T(4,128)S(1)} %broadcast_in_dim.185) | copy-start | bytes 49156
  23.2 1.5 copy-start.32
  25.2 5.9 %copy-start.3 = (bf16[4,128,1024]{2,1,0:T(8,128)(2,1)S(1)}, bf16[4,128,1024]{2,1,0:T(8,128)(2,1)}, u32[]{:S(2)}) copy-start(bf16[4,128,1024]{2,1,0:T(8,128)(2,1)} %tok_ref.3) | copy-start | bytes 3145732
  31.0 11.6 %copy-start.17 = (f32[4,1024]{1,0:T(4,128)}, f32[4,1024]{1,0:T(4,128)S(1)}, u32[]{:S(2)}) copy-start(f32[4,1024]{1,0:T(4,128)S(1)} %get-tuple-element.123.scale_ref) | copy-start | bytes 49156
  31.0 2.8 copy-start.2
  42.6 1.6 copy-start.6
  44.2 4.7 %copy-start.24 = (s32[64]{0:T(128)S(1)}, s32[64]{0:T(128)}, u32[]{:S(2)}) copy-start(s32[64]{0:T(128)} %param.39) | copy-start | bytes 772
  44.2 9.4 %copy-start.5 = (bf16[4,128,1024]{2,1,0:T(8,128)(2,1)S(1)}, bf16[4,128,1024]{2,1,0:T(8,128)(2,1)}, u32[]{:S(2)}) copy-start(bf16[4,128,1024]{2,1,0:T(8,128)(2,1)} %cot_ref.5) | copy-start | bytes 3145732
  44.2 42.5 %all-to-all-start.1 = ((bf16[8,3,512,128]{3,2,1,0:T(8,128)(2,1)}), bf16[8,3,512,128]{3,2,1,0:T(8,128)(2,1)}, u32[]{:S(2)}, u32[]{:S(2)}) async-start(bf16[8,3,512,128]{3,2,1,0:T(8,128)(2,1)} %copy-done.6), calls=%async_computation.1 | async-start | bytes 6291456 | tf_op jit(solution)/shard_map/all_to_all | solution.py:37
  48.8 160.2 %all-gather.3.cloned.1.call-start = ((), (), s32[]{:S(2)}) async-start(), calls=%async_computation.13 | async-start | bytes 9437184 | tf_op jit(solution)/shard_map/all_gather | solution.py:1025
  63.0 1.0 copy-start.10
  63.9 3.3 copy-start.21
  111.7 1.0 copy-start.22
  112.7 29.7 %all-to-all-start.2 = ((bf16[8,256,128]{2,1,0:T(8,128)(2,1)}), bf16[8,256,128]{2,1,0:T(8,128)(2,1)S(1)}, u32[]{:S(2)}, u32[]{:S(2)}) async-start(bf16[8,256,128]{2,1,0:T(8,128)(2,1)} %get-tuple-element.64.refs_4_), calls=%async_computation.2 | async-start | bytes 1048576 | tf_op jit(solution)/shard_map/all_to_all | solution.py:37
  116.6 30.2 %copy-start.35 = (bf16[1024]{0:T(1024)(128)(2,1)S(1)}, bf16[1024]{0:T(1024)(128)(2,1)}, u32[]{:S(2)}) copy-start(bf16[1024]{0:T(1024)(128)(2,1)} %param.32) | copy-start | bytes 6148
  116.6 30.2 %copy-start.34 = (bf16[4096]{0:T(1024)(128)(2,1)S(1)}, bf16[4096]{0:T(1024)(128)(2,1)}, u32[]{:S(2)}) copy-start(bf16[4096]{0:T(1024)(128)(2,1)} %param.34) | copy-start | bytes 24580
  140.6 0.8 copy-start.16
  141.4 1.0 copy-start.23
  142.4 13.9 %all-to-all-start.3 = ((bf16[8,256,128]{2,1,0:T(8,128)(2,1)}), bf16[8,256,128]{2,1,0:T(8,128)(2,1)S(1)}, u32[]{:S(2)}, u32[]{:S(2)}) async-start(bf16[8,256,128]{2,1,0:T(8,128)(2,1)} %copy-done.16), calls=%async_computation.3 | async-start | bytes 1048576 | tf_op jit(solution)/shard_map/all_to_all | solution.py:37
  146.6 202.1 %reduce-scatter.3.cloned.1.call-start = ((), (), s32[]{:S(2)}) async-start(), calls=%async_computation.11 | async-start | bytes 21233664 | tf_op jit(solution)/shard_map/reduce_scatter | solution.py:1065
  161.4 1.0 copy-start.20
  204.0 1.3 copy-start.4
  205.3 1.0 copy-start.12
  209.0 0.7 copy-start.36
  209.7 19.7 %all-to-all-start.4 = ((bf16[8,512,128]{2,1,0:T(8,128)(2,1)}), bf16[8,512,128]{2,1,0:T(8,128)(2,1)}, u32[]{:S(2)}, u32[]{:S(2)}) async-start(bf16[8,512,128]{2,1,0:T(8,128)(2,1)} %copy-done.12), calls=%async_computation.4 | async-start | bytes 2097152 | tf_op jit(solution)/shard_map/all_to_all | solution.py:37
  213.9 1.7 copy-start.7
  215.6 1.5 copy-start.11
  217.1 7.7 %copy-start.33 = (f32[1,4096]{1,0:T(1,128)S(1)}, f32[1,4096]{1,0:T(1,128)}, u32[]{:S(2)}) copy-start(f32[1,4096]{1,0:T(1,128)} %get-tuple-element.81) | copy-start | bytes 49156
  229.3 55.9 %all-to-all-start.5 = ((bf16[32,4,4224]{2,1,0:T(4,128)(2,1)}), bf16[32,4,4224]{2,1,0:T(4,128)(2,1)S(1)}, u32[]{:S(2)}, u32[]{:S(2)}) async-start(bf16[32,4,4224]{2,1,0:T(4,128)(2,1)} %pad_maximum_fusion), calls=%async_computation.5 | async-start | bytes 2162688 | tf_op jit(solution)/shard_map/all_to_all | solution.py:37
  285.2 1.0 copy-start.25
  286.2 56.6 %all-to-all-start.6 = ((bf16[8,512,128]{2,1,0:T(8,128)(2,1)}), bf16[8,512,128]{2,1,0:T(8,128)(2,1)S(1)}, u32[]{:S(2)}, u32[]{:S(2)}) async-start(bf16[8,512,128]{2,1,0:T(8,128)(2,1)} %get-tuple-element.86.first_ref), calls=%async_computation.6 | async-start | bytes 2097152 | tf_op jit(solution)/shard_map/all_to_all | solution.py:37
  342.7 31.0 %all-to-all-start.7 = ((bf16[8,1024,128]{2,1,0:T(8,128)(2,1)}), bf16[8,1024,128]{2,1,0:T(8,128)(2,1)}, u32[]{:S(2)}, u32[]{:S(2)}) async-start(bf16[8,1024,128]{2,1,0:T(8,128)(2,1)} %attend_back.3.last_ref), calls=%async_computation.7 | async-start | bytes 4194304 | tf_op jit(solution)/shard_map/all_to_all | solution.py:37
  347.1 1.6 copy-start.13
  347.1 87.6 %reduce-scatter.5.cloned.1.call-start = ((), (), s32[]{:S(2)}) async-start(), calls=%async_computation.12 | async-start | bytes 2949120 | tf_op jit(solution)/shard_map/reduce_scatter | solution.py:1065
  348.7 1.6 copy-start.8
  350.3 3.4 copy-start.19
  353.7 20.0 %copy-start.18 = (f32[4,1024]{1,0:T(4,128)S(1)}, f32[4,1024]{1,0:T(4,128)}, u32[]{:S(2)}) copy-start(f32[4,1024]{1,0:T(4,128)} %copy-done.17) | copy-start | bytes 49156
  360.7 0.9 copy-start.14
  373.8 1.1 copy-start.15
  385.3 1.1 copy-start.9
  386.4 42.9 %all-to-all-start.8 = ((bf16[32,176,128]{2,1,0:T(8,128)(2,1)}), bf16[32,176,128]{2,1,0:T(8,128)(2,1)S(1)}, u32[]{:S(2)}, u32[]{:S(2)}) async-start(bf16[32,176,128]{2,1,0:T(8,128)(2,1)} %copy-done.9), calls=%async_computation.8 | async-start | bytes 2883584 | tf_op jit(solution)/shard_map/all_to_all | solution.py:37
  390.0 2.4 slice-start
  390.0 5.5 %copy-start.29 = (bf16[64,128]{1,0:T(8,128)(2,1)S(1)}, bf16[64,128]{1,0:T(8,128)(2,1)}, u32[]{:S(2)}) copy-start(bf16[64,128]{1,0:T(8,128)(2,1)} %fusion.5) | copy-start | bytes 49156
  392.5 4.6 %copy-start.30 = (bf16[64,32]{0,1:T(8,128)(2,1)S(1)}, bf16[64,32]{0,1:T(8,128)(2,1)}, u32[]{:S(2)}) copy-start(bf16[64,32]{0,1:T(8,128)(2,1)} %constant_dynamic-slice_fusion.1) | copy-start | bytes 12292
  434.7 2.8 copy-start.26
  434.7 3.7 copy-start.1
Sparse Core Ops, SparseCore 0:
  86.8 59.4 all-gather.2
  209.1 139.5 reduce-scatter.2
  351.0 51.8 reduce-scatter.4

commit v4 on v3

--- a/solution.py
+++ b/solution.py
@@ -98,6 +98,10 @@
         out_ref[p, 2] = vals[:, lanes]
 
 
+def in_hbm(value):
+    return pltpu.with_memory_space_constraint(value, pltpu.HBM)
+
+
 def whole(shape):
     return pl.BlockSpec(shape, lambda *_: (0,) * len(shape))
 
@@ -114,8 +118,8 @@
     return pl.pallas_call(
         project_kernel,
         out_shape=[
-            jax.ShapeDtypeStruct((width, rows), bf16),
-            jax.ShapeDtypeStruct((pairs, 3, rows, LANES), bf16),
+            pltpu.HBM((width, rows), bf16),
+            pltpu.HBM((pairs, 3, rows, LANES), bf16),
         ],
         grid=(steps,),
         in_specs=[whole(tokens.shape), whole(shift_one.shape), whole(scale_one.shape)]
@@ -132,7 +136,7 @@
             flops=6 * rows * width * width, bytes_accessed=10 * MIB, transcendentals=0
         ),
         name="project",
-    )(tokens, shift_one, scale_one, *[qkv_weight] * 3, *[qkv_bias] * 3, cosine, sine)
+    )(tokens, shift_one, scale_one, *[in_hbm(qkv_weight)] * 3, *[qkv_bias] * 3, cosine, sine)
 
 
 def key_extra(first_frame, rows, patches):
@@ -223,8 +227,8 @@
             attend_kernel, part, rows_part, patches, tile // rows_part, chunk // rows
         ),
         out_shape=[
-            jax.ShapeDtypeStruct((blocks, rows_part, LANES), bf16),
-            jax.ShapeDtypeStruct((2, blocks, rows_part, LANES), bf16),
+            pltpu.HBM((blocks, rows_part, LANES), bf16),
+            pltpu.HBM((2, blocks, rows_part, LANES), bf16),
         ],
         in_specs=[pl.BlockSpec(memory_space=VMEM)] * 2,
         out_specs=[pl.BlockSpec(memory_space=VMEM)] * 2,
@@ -355,7 +359,7 @@
     total = blocks * rows
     operands = [heads, grads, *exts, *outs, *rotary, *(carry or ())]
     kept = 2 * rows_part + (rows if last else 0)
-    out_shape = [jax.ShapeDtypeStruct((blocks, kept, LANES), bf16)]
+    out_shape = [pltpu.HBM((blocks, kept, LANES), bf16)]
     if not last:
         out_shape.append(jax.ShapeDtypeStruct((LANES, total), f32))
         out_shape.append(jax.ShapeDtypeStruct((2, blocks, rows, LANES), bf16))
@@ -396,7 +400,7 @@
         act_grad_kernel,
         out_shape=[
             jax.ShapeDtypeStruct((rows, width), bf16),
-            jax.ShapeDtypeStruct((rows, inner), f32),
+            pltpu.HBM((rows, inner), f32),
         ],
         grid=(inner // cols,),
         in_specs=[
@@ -594,7 +598,7 @@
             jax.ShapeDtypeStruct((rows, width), bf16),
             jax.ShapeDtypeStruct((rows, width), f32),
             jax.ShapeDtypeStruct((rows, width), f32),
-            jax.ShapeDtypeStruct((rows, width), bf16),
+            pltpu.HBM((rows, width), bf16),
         ],
         in_specs=[pl.BlockSpec(memory_space=VMEM)] * len(operands),
         out_specs=[pl.BlockSpec(memory_space=VMEM)] * 4,
@@ -641,9 +645,9 @@
     return pl.pallas_call(
         unmerge_kernel,
         out_shape=[
-            jax.ShapeDtypeStruct((rows, width), f32),
+            pltpu.HBM((rows, width), f32),
             jax.ShapeDtypeStruct((rows, width), bf16),
-            jax.ShapeDtypeStruct((width // LANES, rows, LANES), bf16),
+            pltpu.HBM((width // LANES, rows, LANES), bf16),
         ],
         in_specs=[pl.BlockSpec(memory_space=VMEM)] * len(operands),
         out_specs=[pl.BlockSpec(memory_space=VMEM)] * 3,
@@ -756,11 +760,11 @@
             flops=6 * blocks * rows * width * LANES, bytes_accessed=12 * MIB, transcendentals=0
         ),
         name="heads_grad",
-    )(hidden_clip, first, last)
+    )(in_hbm(hidden_clip), first, last)
 
 
 def finish_kernel(first_ref, last_ref, wq_ref, wk_ref, wv_ref, tok_ref, scale_ref, after_ref,
-                  part_ref, partbias_ref, out_ref, send_ref, total):
+                  partbias_ref, out_ref, send_ref, total):
     frames, patches, width = tok_ref.shape
     rows = frames * patches
     rows_part = first_ref.shape[1] // 2
@@ -814,21 +818,18 @@
         high = [value.astype(bf16).astype(f32) for value in bias]
         low = [value - upper for value, upper in zip(bias, high)]
         bias = jnp.concatenate(high + low + [jnp.zeros((10, LANES), f32)], axis=0).astype(bf16)
-        devices, triple, _ = part_ref.shape
         count = sums.shape[0]
-        send_ref[:, count : count + triple, :] = part_ref[...]
-        for d in range(devices):
+        for d in range(send_ref.shape[0]):
             send_ref[d, :count, :] = sums
-            send_ref[d, count + triple :, :] = bias
-
-
-def finish(first, last, qkv_weight, tokens, scale_one, grad_after, part, part_bias, cols=256):
+            send_ref[d, count:, :] = bias
+
+
+def finish(first, last, qkv_weight, tokens, scale_one, grad_after, part_bias, copies, cols=256):
     frames, patches, width = tokens.shape
     rows = frames * patches
     steps, some = width // cols, cols // LANES
 
-    devices, triple, _ = part.shape
-    send_shape = (devices, 2 * frames * (width // LANES) + triple + 16, LANES)
+    send_shape = (copies, 2 * frames * (width // LANES) + 16, LANES)
 
     def column(third):
         return lambda c: (0, third * steps + c)
@@ -837,7 +838,7 @@
         finish_kernel,
         out_shape=[
             jax.ShapeDtypeStruct((frames, patches, width), bf16),
-            jax.ShapeDtypeStruct(send_shape, bf16),
+            pltpu.HBM(send_shape, bf16),
         ],
         grid=(steps,),
         in_specs=[
@@ -846,7 +847,7 @@
         ]
         + [pl.BlockSpec((width, cols), column(part)) for part in range(3)]
         + [whole(tokens.shape), whole(scale_one.shape), whole((rows, width))]
-        + [whole(part.shape), whole(part_bias.shape)],
+        + [whole(part_bias.shape)],
         out_specs=[whole((frames, patches, width)), whole(send_shape)],
         scratch_shapes=[VMEM((rows, width), f32)],
         compiler_params=pltpu.CompilerParams(vmem_limit_bytes=48 * MIB),
@@ -854,19 +855,27 @@
             flops=6 * rows * width * width, bytes_accessed=16 * MIB, transcendentals=0
         ),
         name="finish",
-    )(first, last, *[qkv_weight] * 3, tokens, scale_one, grad_after, part, part_bias)
-
-
-def last_kernel(group, frames, got_ref, member_ref, cols_ref, rows_ref, bias_ref, ada_ref, adasum_ref):
-    devices = got_ref.shape[0]
-    clips = devices // group
-    width = rows_ref.shape[1] // 3
+    )(first, last, *[qkv_weight] * 3, tokens, scale_one, grad_after, part_bias)
+
+
+def last_kernel(clips, frames, got_ref, member_ref, cols_ref, early_ref, earlysum_ref,
+                rows_ref, bias_ref, ada_ref, adasum_ref):
+    group = got_ref.shape[0]
+    share, width = rows_ref.shape[0], rows_ref.shape[1] // 3
     tiles = width // LANES
     count = 2 * frames * tiles
-    share = (got_ref.shape[1] - count - 16) // 3
+    starts = [3 * share + c * (count + 16) for c in range(clips)]
+    some = 4 * frames
+    ada_ref[:, 2 * width :] = early_ref[...]
+    adasum_ref[:, 2 * width :] = earlysum_ref[...]
     for i in range(tiles // 2):
-        sums = got_ref[:, i * 4 * frames : (i + 1) * 4 * frames, :]
-        sums = sums.reshape(devices * 4 * frames, LANES)
+        sums = jnp.concatenate(
+            [
+                got_ref[:, at + i * some : at + (i + 1) * some, :].reshape(group * some, LANES)
+                for at in starts
+            ],
+            axis=0,
+        )
         for j in range(2):
             for kind in range(2):
                 level = dot(member_ref[2 * j + kind], sums).astype(bf16)
@@ -874,36 +883,33 @@
                 ada_ref[:, at : at + LANES] = dot(cols_ref[...], level)
                 adasum_ref[:, at : at + LANES] = column_sum(level.astype(f32))
     for p in range(group):
-        bias = got_ref[p, count + 3 * share :, :].astype(f32)
-        for c in range(1, clips):
-            bias = bias + got_ref[c * group + p, count + 3 * share :, :].astype(f32)
+        bias = None
+        for at in starts:
+            term = got_ref[p, at + count : at + count + 16, :].astype(f32)
+            bias = term if bias is None else bias + term
         for third in range(3):
             at = third * width + p * LANES
-            here = slice(count + third * share, count + (third + 1) * share)
-            total = got_ref[p, here, :].astype(f32)
-            for c in range(1, clips):
-                total = total + got_ref[c * group + p, here, :].astype(f32)
-            rows_ref[:, at : at + LANES] = total
+            here = slice(third * share, (third + 1) * share)
+            rows_ref[:, at : at + LANES] = got_ref[p, here, :].astype(f32)
             bias_ref[:, at : at + LANES] = bias[third : third + 1, :] + bias[third + 3 : third + 4, :]
 
 
-def last_sums(got, member, columns, group, frames, width):
-    devices = got.shape[0]
-    share = width // devices
+def last_sums(got, member, columns, early, early_sum, clips, frames):
+    share, width = early.shape[0], early.shape[1] // 4
     return pl.pallas_call(
-        functools.partial(last_kernel, group, frames),
+        functools.partial(last_kernel, clips, frames),
         out_shape=[
             jax.ShapeDtypeStruct((share, 3 * width), f32),
             jax.ShapeDtypeStruct((1, 3 * width), f32),
-            jax.ShapeDtypeStruct((share, 2 * width), f32),
-            jax.ShapeDtypeStruct((1, 2 * width), f32),
-        ],
-        in_specs=[pl.BlockSpec(memory_space=VMEM)] * 3,
+            jax.ShapeDtypeStruct((share, 6 * width), f32),
+            jax.ShapeDtypeStruct((1, 6 * width), f32),
+        ],
+        in_specs=[pl.BlockSpec(memory_space=VMEM)] * 5,
         out_specs=[pl.BlockSpec(memory_space=VMEM)] * 4,
         compiler_params=pltpu.CompilerParams(vmem_limit_bytes=48 * MIB),
         cost_estimate=pl.CostEstimate(flops=0, bytes_accessed=4 * MIB, transcendentals=0),
         name="last_sums",
-    )(got, member, columns)
+    )(got, member, columns, early, early_sum)
 
 
 def body(
@@ -1060,16 +1066,9 @@
 
     joined = proj_weight_grad(attn_low, grad_proj, joined)
     joined, hidden_clip = lax.optimization_barrier((joined, hidden_clip))
-    summed = joined
-    for groups in (clip_groups, across_clips):
-        summed = lax.psum_scatter(
-            summed, AXES, scatter_dimension=0, axis_index_groups=groups, tiled=True
-        )[0]
-    summed = summed.astype(f32)
-    quarters = inner // width
-    up_w_out = jnp.concatenate([summed[i] for i in range(quarters)], axis=1)
-    down_w_out = summed[quarters : 2 * quarters].reshape(per_dest, width)
-    proj_w_out = summed[2 * quarters]
+    summed = lax.psum_scatter(
+        joined, AXES, scatter_dimension=0, axis_index_groups=clip_groups, tiled=True
+    )[0]
 
     def slot_parts(slot_sums, biases):
         kinds = slot_sums.shape[0] // frames
@@ -1119,21 +1118,43 @@
 
     early_w, early_b = level_out(early_got, 4 * width)
     early_bias_out = bias_share(early_got, 4 * width, per_dest + 2 * share)
+
+    qkv_part, qkv_b_part = heads_grad(hidden_clip, first_grads, last_grads, devices)
+    qkv_part = qkv_part.reshape(clips, group, 3 * share, LANES)
+    qkv_sum = lax.dynamic_index_in_dim(qkv_part, clip, 0, keepdims=False).astype(f32)
+    for j in range(1, clips):
+        some = lax.dynamic_index_in_dim(qkv_part, clip ^ j, 0, keepdims=False)
+        pairs = [(source, source ^ (j * group)) for source in range(devices)]
+        qkv_sum = qkv_sum + lax.ppermute(some, AXES, pairs).astype(f32)
+    qkv_sum, own_last, summed = lax.optimization_barrier(
+        (qkv_sum.astype(bf16), own_last, summed)
+    )
+
+    summed = lax.psum_scatter(
+        summed, AXES, scatter_dimension=0, axis_index_groups=across_clips, tiled=True
+    )[0].astype(f32)
+    quarters = inner // width
+    up_w_out = jnp.concatenate([summed[i] for i in range(quarters)], axis=1)
+    down_w_out = summed[quarters : 2 * quarters].reshape(per_dest, width)
+    proj_w_out = summed[2 * quarters]
+
+    tokens_grad, last_send = finish(
+        own_first, own_last, qkv_weight, tokens, scale_one, grad_after, qkv_b_part, clips
+    )
+    clip_got = exchange(last_send, across_clips).reshape(1, -1, LANES)
+    clip_got = jnp.broadcast_to(clip_got, (group,) + clip_got.shape[1:])
+    last_got = exchange(jnp.concatenate([qkv_sum, clip_got], axis=1), clip_groups)
+    last_got, early_w, early_b, early_bias_out = lax.optimization_barrier(
+        (last_got, early_w, early_b, early_bias_out)
+    )
     up_b_out = early_bias_out[:per_dest]
     proj_b_out = early_bias_out[per_dest : per_dest + share]
     down_b_out = early_bias_out[per_dest + share :]
-
-    qkv_part, qkv_b_part = heads_grad(hidden_clip, first_grads, last_grads, devices)
-    tokens_grad, last_send = finish(
-        own_first, own_last, qkv_weight, tokens, scale_one, grad_after, qkv_part, qkv_b_part
-    )
-    last_got = exchange(last_send, everyone)
-    qkv_w_out, qkv_b_all, late_w, late_b = last_sums(
-        last_got, member_last, columns_turned, group, frames, width
+    qkv_w_out, qkv_b_all, ada_w_out, ada_b_all = last_sums(
+        last_got, member_last, columns_turned, early_w, early_b[None, :], clips, frames
     )
     qkv_b_out = lax.dynamic_slice_in_dim(qkv_b_all[0], me * 3 * share, 3 * share)
-    ada_w_out = jnp.concatenate([late_w, early_w], axis=1)
-    ada_b_all = jnp.concatenate([late_b[0], early_b])
+    ada_b_all = ada_b_all[0]
     ada_share = ada_b_all.shape[0] // devices
     ada_b_out = lax.dynamic_slice_in_dim(ada_b_all, me * ada_share, ada_share)
     return (

time: 453 us -> 445 us (0.982)
  local copies, waits for them, and re-layouts: 43 us -> 31.7 us
  starting transfers between devices: 41.1 us -> 49.1 us
  waiting for transfers between devices: 76.3 us -> 69.4 us
    all_to_all x9 -> x10, waiting for transfers between devices: 74.7 us -> 50.6 us  [exchange(): return lax.all_to_all(value, AXES, 0, 0, axis_index_groups=groups)]
    ppermute x0 -> x3, waiting for transfers between devices: none -> 16.4 us  [body(): qkv_sum = qkv_sum + lax.ppermute(some, AXES, pairs).astype(f32)]
    unnamed x74 -> x60, local copies, waits for them, and re-layouts: 27.8 us -> 17.6 us
    all_to_all x9 -> x10, starting transfers between devices: 40.8 us -> 44.3 us  [exchange(): return lax.all_to_all(value, AXES, 0, 0, axis_index_groups=groups)]
  transfers between devices with their start and end apart: 12 -> 16, of which waited for: 6 -> 8; matrix products, arithmetic and copies ran while one was open for 6% -> 5% of each run, Pallas kernels for 54% -> 55%
where the time goes in v4:
time: 445 us; the launch traced here: 437 us
  Pallas kernels  252 us (57%)
  waiting for transfers between devices  69.4 us (16%)
  starting transfers between devices  49.1 us (11%)
  local copies, waits for them, and re-layouts  31.7 us (7%)
  between operations  14.7 us (3%)
  other arithmetic  13.8 us (3%)
  matrix products  6.31 us (1%)
    pallas_call x2, Pallas kernels, attend_back(): pl.pallas_call(functools.partial(attend_back_kernel, parts, part, patches...  104 us
    all_to_all x10, waiting for transfers between devices, exchange(): return lax.all_to_all(value, AXES, 0, 0, axis_index_groups=groups)  50.6 us
    pallas_call x2, Pallas kernels, attend(): pl.pallas_call(functools.partial(attend_kernel, part, rows_part, patches,...  50.3 us
    all_to_all x10, starting transfers between devices, exchange(): return lax.all_to_all(value, AXES, 0, 0, axis_index_groups=groups)  44.3 us
    pallas_call x1, Pallas kernels, feed_forward(): pl.pallas_call(feed_kernel, out_shape=[jax.ShapeDtypeStruct((rows, width)...  36.3 us
    unnamed x60, local copies, waits for them, and re-layouts  17.6 us
    ppermute x3, waiting for transfers between devices, body(): qkv_sum = qkv_sum + lax.ppermute(some, AXES, pairs).astype(f32)  16.4 us
    pallas_call x1, Pallas kernels, finish(): pl.pallas_call(finish_kernel, out_shape=[jax.ShapeDtypeStruct((frames, pa...  10.1 us
  transfers between devices with their start and end apart: 16, of which 8 were waited for; matrix products, arithmetic and copies ran while one was open for 5% of the time, Pallas kernels for 55%

profile of v4, /device:TPU:0, one launch (start us, length us, event | category | flops | bytes accessed | tf_op | source)
XLA Modules:
  0.0 437.2 jit_solution(3607751524503957279)
XLA Ops:
  7.2 1.4 broadcast_in_dim.180
  8.6 7.3 %all-to-all-start = ((bf16[32,2,1024]{2,1,0:T(2,128)(2,1)}), bf16[32,2,1024]{2,1,0:T(2,128)(2,1)S(1)}, u32[]{:S(2)}, u32[]{:S(2)}) async-start(bf16[32,2,1024]{2,1,0:T(2,128)(2,1)} %broadcast_in_dim.180), calls=%async_computation | async-start | bytes 262144 | tf_op jit(solution)/shard_map/all_to_all | solution.py:37
  16.0 0.7 compare_select_fusion.2
  17.4 0.7 and_select_fusion.5
  18.1 1.2 dynamic_slice.61
  19.3 1.4 broadcast_compare_fusion.1
  20.8 0.8 fusion.11
  21.6 1.5 multiply_select_fusion
  23.3 0.7 convert_element_type.103
  25.2 5.8 %fusion = f32[4,6144]{1,0:T(4,128)S(1)} fusion(bf16[1024,6144]{1,0:T(8,128)(2,1)} %param.27, bf16[64,1024]{0,1:T(8,128)(2,1)S(1)} %multiply_convert_fusion, f32[6144]{0:T(1024)S(1)} %convert_element_type.103, s32[4]{0:T(128)S(1)} %and_select_fusion.5), kind=kOutput, calls=%fused_computation.4 | convolution fusion | flops 50909440 | bytes 12836880 | tf_op jit(solution)/shard_map/dot_general | solution.py:33
  31.0 9.8 %project.1 = (bf16[1024,512]{1,0:T(8,128)(2,1)}, bf16[8,3,512,128]{3,2,1,0:T(8,128)(2,1)}) custom-call(bf16[4,128,1024]{2,1,0:T(8,128)(2,1)S(1)} %copy-done.2, f32[4,1024]{1,0:T(4,128)S(1)} %get-tuple-element.141.shift_ref, f32[4,1024]{1,0:T(4,128)S(1)} %get-tuple-element.140.scale_ref, bf16[1024,3072]{1,0:T(8,128)(2,1)} %wv_ref.3, ...), custom_call_target="tpu_custom_call" | custom-call | flops 3221225472 | bytes 10485760 | tf_op jit(solution)/shard_map/project/pallas_call | solution.py:118
  40.9 4.6 %all-to-all-start.1 = ((bf16[8,3,512,128]{3,2,1,0:T(8,128)(2,1)}), bf16[8,3,512,128]{3,2,1,0:T(8,128)(2,1)}, u32[]{:S(2)}, u32[]{:S(2)}) async-start(bf16[8,3,512,128]{3,2,1,0:T(8,128)(2,1)} %get-tuple-element.67), calls=%async_computation.1 | async-start | bytes 6291456 | tf_op jit(solution)/shard_map/all_to_all | solution.py:37
  45.5 1.2 gather_fusion.1
  46.8 1.5 gather_fusion.2
  50.3 3.4 copy-done.15
  53.7 8.2 %act_grad.1 = (bf16[512,1024]{1,0:T(8,128)(2,1)S(1)}, f32[512,4096]{1,0:T(8,128)}) custom-call(bf16[4,128,1024]{2,1,0:T(8,128)(2,1)S(1)} %copy-done.4, f32[4,1024]{1,0:T(4,128)S(1)} %get-tuple-element.139.gate_ref.gate_two_ref, bf16[4096,1024]{1,0:T(8,128)(2,1)S(1)} %copy-done.15), custom_call_target="tpu_custom_call" | custom-call | flops 4294967296 | bytes 18874368 | tf_op jit(solution)/shard_map/act_grad/pallas_call | solution.py:399
  61.9 1.0 copy-done.10
  62.9 20.4 %all-to-all-done.1.qkv_ref.refs_0_ = bf16[8,3,512,128]{3,2,1,0:T(8,128)(2,1)} async-done(((bf16[8,3,512,128]{3,2,1,0:T(8,128)(2,1)}), bf16[8,3,512,128]{3,2,1,0:T(8,128)(2,1)}, u32[]{:S(2)}, u32[]{:S(2)}) %all-to-all-start.1) | async-done | bytes 3145760 | tf_op jit(solution)/shard_map/all_to_all | solution.py:37
  83.5 25.3 %attend.2 = (bf16[8,256,128]{2,1,0:T(8,128)(2,1)}, bf16[2,8,256,128]{3,2,1,0:T(8,128)(2,1)}) custom-call(bf16[8,3,512,128]{3,2,1,0:T(8,128)(2,1)} %all-to-all-done.1.qkv_ref.refs_0_, f32[32,128]{1,0:T(8,128)S(1)} %bitcast.76), custom_call_target="tpu_custom_call" | custom-call | flops 17179869184 | bytes 4194304 | tf_op jit(solution)/shard_map/attend/pallas_call | solution.py:225
  108.7 3.9 all-to-all-start.2
  112.7 25.1 %attend.3 = (bf16[8,256,128]{2,1,0:T(8,128)(2,1)}, bf16[2,8,256,128]{3,2,1,0:T(8,128)(2,1)}) custom-call(bf16[8,3,512,128]{3,2,1,0:T(8,128)(2,1)} %all-to-all-done.1.qkv_ref.refs_0_, f32[32,128]{1,0:T(8,128)S(1)} %bitcast.77), custom_call_target="tpu_custom_call" | custom-call | flops 17179869184 | bytes 4194304 | tf_op jit(solution)/shard_map/attend/pallas_call | solution.py:225
  137.8 4.2 all-to-all-start.3
  142.8 8.9 %all-to-all-done.3.refs_1_ = bf16[8,256,128]{2,1,0:T(8,128)(2,1)S(1)} async-done(((bf16[8,256,128]{2,1,0:T(8,128)(2,1)}), bf16[8,256,128]{2,1,0:T(8,128)(2,1)S(1)}, u32[]{:S(2)}, u32[]{:S(2)}) %all-to-all-start.3) | async-done | bytes 524320 | tf_op jit(solution)/shard_map/all_to_all | solution.py:37
  151.7 4.7 %merge_heads.1 = (bf16[512,1024]{1,0:T(8,128)(2,1)S(1)}, f32[512,1024]{1,0:T(8,128)S(1)}, f32[512,1024]{1,0:T(8,128)}, bf16[512,1024]{1,0:T(8,128)(2,1)}) custom-call(bf16[8,256,128]{2,1,0:T(8,128)(2,1)S(1)} %all-to-all-done.2.refs_0_, bf16[8,256,128]{2,1,0:T(8,128)(2,1)S(1)} %all-to-all-done.3.refs_1_, bf16[1024,1024]{1,0:T(8,128)(2,1)} %weight_ref.1, ...), custom_call_target="tpu_custom_call" | custom-call | flops 1073741824 | bytes 16777216 | tf_op jit(solution)/shard_map/merge_heads/pallas_call | solution.py:595
  156.4 1.3 copy-done.7
  157.8 36.3 %feed_forward.1 = (f32[512,1024]{1,0:T(8,128)}, f32[512,1024]{1,0:T(8,128)}, f32[1,4096]{1,0:T(1,128)}, bf16[8,4,9,32,1024]{4,3,2,1,0:T(8,128)(2,1)}) custom-call(bf16[512,1024]{1,0:T(8,128)(2,1)} %get-tuple-element.73.hid_ref, bf16[512,1024]{1,0:T(8,128)(2,1)} %copy-done.10, f32[512,4096]{1,0:T(8,128)} %get-tuple-element.75.actgrad_ref, ...), custom_call_target="tpu_custom_call" | custom-call | flops 21474836480 | bytes 46137344 | tf_op jit(solution)/shard_map/feed_forward/pallas_call | solution.py:497
  194.1 1.6 copy-done.3
  195.7 6.0 %unmerge_heads.1 = (f32[512,1024]{1,0:T(8,128)}, bf16[512,1024]{1,0:T(8,128)(2,1)S(1)}, bf16[8,512,128]{2,1,0:T(8,128)(2,1)}) custom-call(f32[512,1024]{1,0:T(8,128)S(1)} %copy-done.3, f32[512,1024]{1,0:T(8,128)} %get-tuple-element.78.after_ref, bf16[4,128,1024]{2,1,0:T(8,128)(2,1)S(1)} %copy-done.4, f32[4,1024]{1,0:T(4,128)S(1)} %get-tuple-element.138.refs_5_.gate_one_ref, ...), custom_call_target="tpu_custom_call" | custom-call | flops 1073741824 | bytes 12582912 | tf_op jit(solution)/shard_map/unmerge_heads/pallas_call | solution.py:645
  201.6 2.6 proj_weight_grad.1
  205.0 4.2 all-to-all-start.4
  209.2 1.7 copy-done.8
  210.9 1.5 copy-done.11
  212.4 7.5 %side_sums.1 = (bf16[4,128,1024]{2,1,0:T(8,128)(2,1)}, f32[16,1024]{1,0:T(8,128)S(1)}, f32[2,1024]{1,0:T(2,128)S(1)}) custom-call(f32[512,1024]{1,0:T(8,128)S(1)} %copy-done.8, f32[512,1024]{1,0:T(8,128)} %get-tuple-element.77.back_ref, f32[512,1024]{1,0:T(8,128)} %get-tuple-element.78.after_ref, f32[512,1024]{1,0:T(8,128)} %copy-done.7, ...), custom_call_target="tpu_custom_call" | custom-call | bytes 16777216 | tf_op jit(solution)/shard_map/side_sums/pallas_call | solution.py:691
  220.8 1.5 pad_maximum_fusion
  222.3 2.3 all-to-all-done.4.refs_1_
  224.6 4.4 %all-to-all-start.5 = ((bf16[32,4,4224]{2,1,0:T(4,128)(2,1)}), bf16[32,4,4224]{2,1,0:T(4,128)(2,1)S(1)}, u32[]{:S(2)}, u32[]{:S(2)}) async-start(bf16[32,4,4224]{2,1,0:T(4,128)(2,1)} %pad_maximum_fusion), calls=%async_computation.5 | async-start | bytes 2162688 | tf_op jit(solution)/shard_map/all_to_all | solution.py:37
  229.1 51.4 %attend_back.2 = (bf16[8,512,128]{2,1,0:T(8,128)(2,1)}, f32[128,4096]{1,0:T(8,128)}, bf16[2,8,512,128]{3,2,1,0:T(8,128)(2,1)}) custom-call(bf16[8,3,512,128]{3,2,1,0:T(8,128)(2,1)} %all-to-all-done.1.qkv_ref.refs_0_, bf16[8,512,128]{2,1,0:T(8,128)(2,1)} %all-to-all-done.4.refs_1_, bf16[2,8,256,128]{3,2,1,0:T(8,128)(2,1)} %get-tuple-element.84.refs_2_, ...), custom_call_target="tpu_custom_call" | custom-call | flops 42949672960 | bytes 8388608 | tf_op jit(solution)/shard_map/attend_back/pallas_call | solution.py:366
  280.5 1.0 copy-done.17
  281.5 4.2 all-to-all-start.6
  285.6 52.4 %attend_back.3.last_ref = bf16[8,1024,128]{2,1,0:T(8,128)(2,1)} custom-call(bf16[8,3,512,128]{3,2,1,0:T(8,128)(2,1)} %all-to-all-done.1.qkv_ref.refs_0_, bf16[8,512,128]{2,1,0:T(8,128)(2,1)} %all-to-all-done.4.refs_1_, bf16[2,8,256,128]{3,2,1,0:T(8,128)(2,1)} %get-tuple-element.84.refs_2_, bf16[2,8,256,128]{3,2,1,0:T(8,128)(2,1)} %get-tuple-element.85.refs_3_, ...), custom_call_target="tpu_custom_call" | custom-call | flops 42949672960 | bytes 8388608 | tf_op jit(solution)/shard_map/attend_back/pallas_call | solution.py:366
  338.0 1.0 copy-done.5
  339.0 3.9 all-to-all-start.7
  343.0 1.7 copy-done.9
  344.7 1.2 copy-done.12
  345.9 9.5 %heads_grad.1 = (bf16[32,96,128]{2,1,0:T(8,128)(2,1)S(1)}, f32[1,384]{1,0:T(1,128)S(1)}) custom-call(bf16[8,1024,512]{2,1,0:T(8,128)(2,1)} %bitcast.93, bf16[8,512,128]{2,1,0:T(8,128)(2,1)S(1)} %copy-done.12, bf16[8,1024,128]{2,1,0:T(8,128)(2,1)S(1)} %copy-done.9), custom_call_target="tpu_custom_call" | custom-call | flops 3221225472 | bytes 12582912 | tf_op jit(solution)/shard_map/heads_grad/pallas_call | solution.py:744
  355.5 3.4 collective-permute-start.2
  358.9 1.0 collective-permute-start
  360.0 5.3 %collective-permute-done.2 = bf16[8,96,128]{2,1,0:T(8,128)(2,1)S(1)} collective-permute-done((bf16[8,96,128]{2,1,0:T(8,128)(2,1)S(1)}, bf16[8,96,128]{2,1,0:T(8,128)(2,1)S(1)}, u32[]{:S(2)}, u32[]{:S(2)}) %collective-permute-start.2) | collective-permute-done | bytes 196640 | tf_op jit(solution)/shard_map/ppermute | solution.py:1128
  365.3 11.1 %collective-permute-done.1 = bf16[8,96,128]{2,1,0:T(8,128)(2,1)S(1)} collective-permute-done((bf16[8,96,128]{2,1,0:T(8,128)(2,1)S(1)}, bf16[8,96,128]{2,1,0:T(8,128)(2,1)S(1)}, u32[]{:S(2)}, u32[]{:S(2)}) %collective-permute-start.1) | collective-permute-done | bytes 196640 | tf_op jit(solution)/shard_map/ppermute | solution.py:1128
  376.3 0.8 fusion.3
  377.2 1.2 copy-done.6
  378.4 10.1 %finish.1 = (bf16[4,128,1024]{2,1,0:T(8,128)(2,1)}, bf16[4,80,128]{2,1,0:T(8,128)(2,1)}) custom-call(bf16[8,512,128]{2,1,0:T(8,128)(2,1)S(1)} %copy-done.6, bf16[8,1024,128]{2,1,0:T(8,128)(2,1)S(1)} %all-to-all-done.7.last_ref, bf16[1024,3072]{1,0:T(8,128)(2,1)} %wv_ref.3, bf16[1024,3072]{1,0:T(8,128)(2,1)} %wv_ref.3, bf16[1024,3072]{1,0:T(8,128)(2,1)} %wv_ref.3, ...), custom_call_target="tpu_custom_call" | custom-call | flops 3221225472 | bytes 16777216 | tf_op jit(solution)/shard_map/finish/pallas_call | solution.py:837
  388.5 3.6 all-to-all-start.8
  392.1 1.3 copy.61
  393.4 6.9 %all-to-all-done.8 = bf16[4,80,128]{2,1,0:T(8,128)(2,1)S(1)} async-done(((bf16[4,80,128]{2,1,0:T(8,128)(2,1)}), bf16[4,80,128]{2,1,0:T(8,128)(2,1)S(1)}, u32[]{:S(2)}, u32[]{:S(2)}) %all-to-all-start.8) | async-done | bytes 81952 | tf_op jit(solution)/shard_map/all_to_all | solution.py:37
  400.4 1.0 pad_maximum_fusion.1
  401.4 4.0 all-to-all-start.9
  406.6 12.0 %all-to-all-done.9.got_ref = bf16[8,416,128]{2,1,0:T(8,128)(2,1)S(1)} async-done(((bf16[8,416,128]{2,1,0:T(8,128)(2,1)}), bf16[8,416,128]{2,1,0:T(8,128)(2,1)S(1)}, u32[]{:S(2)}, u32[]{:S(2)}) %all-to-all-start.9) | async-done | bytes 852000 | tf_op jit(solution)/shard_map/all_to_all | solution.py:37
  419.2 3.4 last_sums.1
  424.4 2.4 reduce-scatter.5.cloned.1.call-done
  426.8 1.3 convert_element_type.124
  428.0 0.7 slice_bitcast_fusion.3
  428.8 0.8 pad_maximum_fusion.2
  429.6 0.8 slice.113
  (126 shorter events, 10.3 us)
Async XLA Ops:
  7.2 9.5 %copy-start = (s32[4,16]{1,0:T(4,128)S(1)}, s32[4,16]{1,0:T(4,128)}, u32[]{:S(2)}) copy-start(s32[4,16]{1,0:T(4,128)} %param.38) | copy-start | bytes 772
  8.6 16.1 %all-to-all-start = ((bf16[32,2,1024]{2,1,0:T(2,128)(2,1)}), bf16[32,2,1024]{2,1,0:T(2,128)(2,1)S(1)}, u32[]{:S(2)}, u32[]{:S(2)}) async-start(bf16[32,2,1024]{2,1,0:T(2,128)(2,1)} %broadcast_in_dim.180), calls=%async_computation | async-start | bytes 262144 | tf_op jit(solution)/shard_map/all_to_all | solution.py:37
  23.1 1.9 copy-start.20
  23.1 1.9 copy-start.21
  23.2 7.8 %copy-start.24 = (f32[4,2,4,128]{3,2,1,0:T(4,128)}, f32[4,2,4,128]{3,2,1,0:T(4,128)S(1)}, u32[]{:S(2)}) copy-start(f32[4,2,4,128]{3,2,1,0:T(4,128)S(1)} %broadcast_in_dim.195) | copy-start | bytes 49156
  23.2 1.8 copy-start.25
  25.2 5.9 %copy-start.2 = (bf16[4,128,1024]{2,1,0:T(8,128)(2,1)S(1)}, bf16[4,128,1024]{2,1,0:T(8,128)(2,1)}, u32[]{:S(2)}) copy-start(bf16[4,128,1024]{2,1,0:T(8,128)(2,1)} %tok_ref.3) | copy-start | bytes 3145732
  31.0 9.8 %copy-start.13 = (f32[4,1024]{1,0:T(4,128)}, f32[4,1024]{1,0:T(4,128)S(1)}, u32[]{:S(2)}) copy-start(f32[4,1024]{1,0:T(4,128)S(1)} %get-tuple-element.140.scale_ref) | copy-start | bytes 49156
  40.9 4.7 %copy-start.16 = (s32[64]{0:T(128)S(1)}, s32[64]{0:T(128)}, u32[]{:S(2)}) copy-start(s32[64]{0:T(128)} %param.39) | copy-start | bytes 772
  40.9 9.4 %copy-start.4 = (bf16[4,128,1024]{2,1,0:T(8,128)(2,1)S(1)}, bf16[4,128,1024]{2,1,0:T(8,128)(2,1)}, u32[]{:S(2)}) copy-start(bf16[4,128,1024]{2,1,0:T(8,128)(2,1)} %cot_ref.5) | copy-start | bytes 3145732
  40.9 42.5 %all-to-all-start.1 = ((bf16[8,3,512,128]{3,2,1,0:T(8,128)(2,1)}), bf16[8,3,512,128]{3,2,1,0:T(8,128)(2,1)}, u32[]{:S(2)}, u32[]{:S(2)}) async-start(bf16[8,3,512,128]{3,2,1,0:T(8,128)(2,1)} %get-tuple-element.67), calls=%async_computation.1 | async-start | bytes 6291456 | tf_op jit(solution)/shard_map/all_to_all | solution.py:37
  45.5 158.8 %all-gather.3.cloned.1.call-start = ((), (), s32[]{:S(2)}) async-start(), calls=%async_computation.14 | async-start | bytes 9437184 | tf_op jit(solution)/shard_map/all_gather | solution.py:1031
  50.3 3.4 copy-start.15
  61.9 1.0 copy-start.10
  108.7 29.0 %all-to-all-start.2 = ((bf16[8,256,128]{2,1,0:T(8,128)(2,1)}), bf16[8,256,128]{2,1,0:T(8,128)(2,1)S(1)}, u32[]{:S(2)}, u32[]{:S(2)}) async-start(bf16[8,256,128]{2,1,0:T(8,128)(2,1)} %get-tuple-element.71.refs_4_), calls=%async_computation.2 | async-start | bytes 1048576 | tf_op jit(solution)/shard_map/all_to_all | solution.py:37
  112.7 29.5 %copy-start.28 = (bf16[1024]{0:T(1024)(128)(2,1)S(1)}, bf16[1024]{0:T(1024)(128)(2,1)}, u32[]{:S(2)}) copy-start(bf16[1024]{0:T(1024)(128)(2,1)} %param.32) | copy-start | bytes 6148
  112.7 29.5 %copy-start.27 = (bf16[4096]{0:T(1024)(128)(2,1)S(1)}, bf16[4096]{0:T(1024)(128)(2,1)}, u32[]{:S(2)}) copy-start(bf16[4096]{0:T(1024)(128)(2,1)} %param.34) | copy-start | bytes 24580
  137.8 13.9 %all-to-all-start.3 = ((bf16[8,256,128]{2,1,0:T(8,128)(2,1)}), bf16[8,256,128]{2,1,0:T(8,128)(2,1)S(1)}, u32[]{:S(2)}, u32[]{:S(2)}) async-start(bf16[8,256,128]{2,1,0:T(8,128)(2,1)} %get-tuple-element.72.refs_5_), calls=%async_computation.3 | async-start | bytes 1048576 | tf_op jit(solution)/shard_map/all_to_all | solution.py:37
  141.9 235.2 %reduce-scatter.3.cloned.1.call-start = ((), (), s32[]{:S(2)}) async-start(), calls=%async_computation.12 | async-start | bytes 21233664 | tf_op jit(solution)/shard_map/reduce_scatter | solution.py:1069
  156.4 1.4 copy-start.7
  194.1 1.6 copy-start.3
  204.3 0.7 copy-start.29
  205.0 19.7 %all-to-all-start.4 = ((bf16[8,512,128]{2,1,0:T(8,128)(2,1)}), bf16[8,512,128]{2,1,0:T(8,128)(2,1)}, u32[]{:S(2)}, u32[]{:S(2)}) async-start(bf16[8,512,128]{2,1,0:T(8,128)(2,1)} %get-tuple-element.83), calls=%async_computation.4 | async-start | bytes 2097152 | tf_op jit(solution)/shard_map/all_to_all | solution.py:37
  209.2 1.7 copy-start.8
  210.9 1.5 copy-start.11
  212.4 7.7 %copy-start.26 = (f32[1,4096]{1,0:T(1,128)S(1)}, f32[1,4096]{1,0:T(1,128)}, u32[]{:S(2)}) copy-start(f32[1,4096]{1,0:T(1,128)} %get-tuple-element.88) | copy-start | bytes 49156
  224.6 55.8 %all-to-all-start.5 = ((bf16[32,4,4224]{2,1,0:T(4,128)(2,1)}), bf16[32,4,4224]{2,1,0:T(4,128)(2,1)S(1)}, u32[]{:S(2)}, u32[]{:S(2)}) async-start(bf16[32,4,4224]{2,1,0:T(4,128)(2,1)} %pad_maximum_fusion), calls=%async_computation.5 | async-start | bytes 2162688 | tf_op jit(solution)/shard_map/all_to_all | solution.py:37
  280.5 1.0 copy-start.17
  281.5 56.6 %all-to-all-start.6 = ((bf16[8,512,128]{2,1,0:T(8,128)(2,1)}), bf16[8,512,128]{2,1,0:T(8,128)(2,1)S(1)}, u32[]{:S(2)}, u32[]{:S(2)}) async-start(bf16[8,512,128]{2,1,0:T(8,128)(2,1)} %get-tuple-element.93.first_ref), calls=%async_computation.6 | async-start | bytes 2097152 | tf_op jit(solution)/shard_map/all_to_all | solution.py:37
  338.0 1.0 copy-start.5
  339.0 38.1 %all-to-all-start.7 = ((bf16[8,1024,128]{2,1,0:T(8,128)(2,1)}), bf16[8,1024,128]{2,1,0:T(8,128)(2,1)S(1)}, u32[]{:S(2)}, u32[]{:S(2)}) async-start(bf16[8,1024,128]{2,1,0:T(8,128)(2,1)} %attend_back.3.last_ref), calls=%async_computation.7 | async-start | bytes 4194304 | tf_op jit(solution)/shard_map/all_to_all | solution.py:37
  343.0 83.8 %reduce-scatter.5.cloned.1.call-start = ((), (), s32[]{:S(2)}) async-start(), calls=%async_computation.13 | async-start | bytes 2949120 | tf_op jit(solution)/shard_map/reduce_scatter | solution.py:1133
  343.0 1.7 copy-start.9
  344.7 1.2 copy-start.12
  355.4 21.7 %copy-start.14 = (f32[4,1024]{1,0:T(4,128)S(1)}, f32[4,1024]{1,0:T(4,128)}, u32[]{:S(2)}) copy-start(f32[4,1024]{1,0:T(4,128)} %copy-done.13) | copy-start | bytes 49156
  355.5 9.7 %collective-permute-start.2 = (bf16[8,96,128]{2,1,0:T(8,128)(2,1)S(1)}, bf16[8,96,128]{2,1,0:T(8,128)(2,1)S(1)}, u32[]{:S(2)}, u32[]{:S(2)}) collective-permute-start(bf16[8,96,128]{2,1,0:T(8,128)(2,1)S(1)} %get-tuple-element.134), channel_id=1, source_target_pairs={{0,24},{1,25},{2,26},{3,27},{4,28},{5,29},{6,30},{7,31},{8,16},{9,... | collective-permute-start | bytes 589832 | tf_op jit(solution)/shard_map/ppermute | solution.py:1128
  358.9 17.4 %collective-permute-start.1 = (bf16[8,96,128]{2,1,0:T(8,128)(2,1)S(1)}, bf16[8,96,128]{2,1,0:T(8,128)(2,1)S(1)}, u32[]{:S(2)}, u32[]{:S(2)}) collective-permute-start(bf16[8,96,128]{2,1,0:T(8,128)(2,1)S(1)} %get-tuple-element.135), channel_id=1, source_target_pairs={{0,16},{1,17},{2,18},{3,19},{4,20},{5,21},{6,22},{7,23},{8,24},{9,... | collective-permute-start | bytes 589832 | tf_op jit(solution)/shard_map/ppermute | solution.py:1128
  358.9 17.4 %collective-permute-start = (bf16[8,96,128]{2,1,0:T(8,128)(2,1)S(1)}, bf16[8,96,128]{2,1,0:T(8,128)(2,1)S(1)}, u32[]{:S(2)}, u32[]{:S(2)}) collective-permute-start(bf16[8,96,128]{2,1,0:T(8,128)(2,1)S(1)} %get-tuple-element.133), channel_id=1, source_target_pairs={{0,8},{1,9},{2,10},{3,11},{4,12},{5,13},{6,14},{7,15},{8,0},{9,1},... | collective-permute-start | bytes 589832 | tf_op jit(solution)/shard_map/ppermute | solution.py:1128
  377.2 1.2 copy-start.6
  388.5 12.0 %copy-start.19 = (bf16[8,96,128]{2,1,0:T(8,128)(2,1)S(1)}, bf16[8,96,128]{2,1,0:T(8,128)(2,1)}, u32[]{:S(2)}) copy-start(bf16[8,96,128]{2,1,0:T(8,128)(2,1)} %fusion.3) | copy-start | bytes 589828
  388.5 11.9 %all-to-all-start.8 = ((bf16[4,80,128]{2,1,0:T(8,128)(2,1)}), bf16[4,80,128]{2,1,0:T(8,128)(2,1)S(1)}, u32[]{:S(2)}, u32[]{:S(2)}) async-start(bf16[4,80,128]{2,1,0:T(8,128)(2,1)} %get-tuple-element.107), calls=%async_computation.9 | async-start | bytes 163840 | tf_op jit(solution)/shard_map/all_to_all | solution.py:37
  401.4 4.0 slice-start
  401.4 17.3 %all-to-all-start.9 = ((bf16[8,416,128]{2,1,0:T(8,128)(2,1)}), bf16[8,416,128]{2,1,0:T(8,128)(2,1)S(1)}, u32[]{:S(2)}, u32[]{:S(2)}) async-start(bf16[8,416,128]{2,1,0:T(8,128)(2,1)} %pad_maximum_fusion.1), calls=%async_computation.10 | async-start | bytes 1703936 | tf_op jit(solution)/shard_map/all_to_all | solution.py:37
  405.4 0.7 copy-start.22
  405.4 1.0 copy-start.23
  426.8 2.8 copy-start.18
  426.8 3.7 copy-start.1
Sparse Core Ops, SparseCore 0:
  83.5 59.4 all-gather.2
  204.4 139.5 reduce-scatter.2
  377.3 49.4 reduce-scatter.4

commit v5 on v4

--- a/solution.py
+++ b/solution.py
@@ -153,12 +153,12 @@
     return high, mid, rest - mid
 
 
-def attend_kernel(part, rows_part, patches, joined, joined_keys, qkv_ref, vis_ref, o_ref, ext_ref):
+def attend_kernel(first, rows_part, patches, joined, joined_keys, qkv_ref, vis_ref, o_ref, ext_ref):
     blocks, _, rows, _ = qkv_ref.shape
     frames, frames_part = rows // patches, rows_part // patches
     tile, chunk = joined * rows_part, joined_keys * rows
     lane = lax.broadcasted_iota(jnp.int32, (tile, LANES), 1)
-    mine_rows = slice(part * rows_part, (part + 1) * rows_part)
+    mine_rows = slice(first * patches, first * patches + rows_part)
     ones = jnp.full((chunk, LANES), 1.0, bf16)
 
     def step(t, carry):
@@ -169,7 +169,7 @@
         seen = jnp.concatenate(
             [
                 jnp.broadcast_to(
-                    vis_ref[pl.ds((t * joined + i) * frames + part * frames_part + f, 1), :],
+                    vis_ref[pl.ds((t * joined + i) * frames + first + f, 1), :],
                     (patches, LANES),
                 )
                 for i in range(joined)
@@ -218,13 +218,16 @@
     lax.fori_loop(0, blocks // joined, step, 0)
 
 
-def attend(heads, visible, patches, part, parts, tile=1024, chunk=1024):
+def attend(heads, visible, patches, first, frames_part, tile=1024, chunk=1024):
     blocks, _, rows, _ = heads.shape
-    rows_part = rows // parts
+    rows_part = frames_part * patches
     keys = blocks * rows
+    joined = blocks
+    while joined * rows_part > tile:
+        joined //= 2
     return pl.pallas_call(
         functools.partial(
-            attend_kernel, part, rows_part, patches, tile // rows_part, chunk // rows
+            attend_kernel, first, rows_part, patches, joined, chunk // rows
         ),
         out_shape=[
             pltpu.HBM((blocks, rows_part, LANES), bf16),
@@ -242,7 +245,7 @@
     )(heads, visible)
 
 
-def attend_back_kernel(parts, part, patches, joined, together, carried, last, *refs):
+def attend_back_kernel(parts, query_parts, part, patches, joined, together, carried, last, *refs):
     at = 0
 
     def take(count):
@@ -252,7 +255,7 @@
         return found
 
     (qkv_ref, do_ref) = take(2)
-    ext_refs, o_refs = take(parts), take(parts)
+    ext_refs, o_refs = take(query_parts), take(query_parts)
     ctime_ref, stime_ref, cpatch_ref, spatch_ref = take(4)
     if carried:
         carry_ref, mix_ref = take(2)
@@ -264,15 +267,18 @@
     blocks, _, rows, _ = qkv_ref.shape
     rows_part = rows // parts
     frames, frames_part = rows // patches, rows_part // patches
-    lane = lax.broadcasted_iota(jnp.int32, (rows_part, LANES), 1)
     if carried:
         dq_turned[...] = carry_ref[...]
     else:
         dq_turned[...] = jnp.zeros_like(dq_turned)
         for b in range(blocks):
-            for i in range(parts):
-                there = slice(i * rows_part, (i + 1) * rows_part)
-                mixed = do_ref[b, there, :].astype(f32) * o_refs[i][b].astype(f32)
+            at = 0
+            for o_ref in o_refs:
+                size = o_ref.shape[1]
+                there = slice(at, at + size)
+                at += size
+                lane = lax.broadcasted_iota(jnp.int32, (size, LANES), 1)
+                mixed = do_ref[b, there, :].astype(f32) * o_ref[b].astype(f32)
                 for h in range(2):
                     mine = jnp.where((lane >= HDIM) == (h == 1), mixed, 0.0)
                     high, mid, low = split_three(-jnp.sum(mine, axis=1, keepdims=True))
@@ -318,7 +324,7 @@
             query = jnp.concatenate([qkv_ref[b, 0] for b in some], axis=0)
             grad = jnp.concatenate([do_ref[b] for b in some], axis=0)
             for h in range(2):
-                ext = jnp.concatenate([ext_refs[i][h, b] for b in some for i in range(parts)], axis=0)
+                ext = jnp.concatenate([ext_ref[h, b] for b in some for ext_ref in ext_refs], axis=0)
                 mix = jnp.concatenate([mix_ref[h, b] for b in some], axis=0)
                 probs = jnp.exp(dot(key_tiles[h], jnp.concatenate([query, ext], axis=1), NT))
                 dv[h] = dv[h] + dot(probs.astype(bf16), grad)
@@ -352,8 +358,8 @@
         carry_out[...] = dq_turned[...]
 
 
-def attend_back(heads, grads, exts, outs, rotary, carry, part, last, patches, chunk=2048, together=2):
-    parts = len(exts)
+def attend_back(heads, grads, exts, outs, rotary, carry, part, parts, patches, chunk=2048, together=2):
+    last = part == parts - 1
     blocks, _, rows, _ = heads.shape
     rows_part = rows // parts
     total = blocks * rows
@@ -365,7 +371,15 @@
         out_shape.append(jax.ShapeDtypeStruct((2, blocks, rows, LANES), bf16))
     return pl.pallas_call(
         functools.partial(
-            attend_back_kernel, parts, part, patches, chunk // rows, together, carry is not None, last
+            attend_back_kernel,
+            parts,
+            len(exts),
+            part,
+            patches,
+            chunk // rows,
+            together,
+            carry is not None,
+            last,
         ),
         out_shape=out_shape,
         in_specs=[pl.BlockSpec(memory_space=VMEM)] * len(operands),
@@ -567,15 +581,17 @@
     (weight_ref, bias_ref, tok_ref, gate_one_ref, shift_ref, scale_ref,
      low_ref, proj_ref, after_ref, hid_ref) = refs[parts:]
     frames, patches, width = tok_ref.shape
-    pairs, rows_part, _ = att_refs[0].shape
-    for i, att_ref in enumerate(att_refs):
+    pairs = att_refs[0].shape[0]
+    at = 0
+    for att_ref in att_refs:
         low = jnp.concatenate([att_ref[p] for p in range(pairs)], axis=1)
-        there = slice(i * rows_part, (i + 1) * rows_part)
+        rows_part = att_ref.shape[1]
+        there = slice(at, at + rows_part)
         low_ref[there, :] = low
         proj = dot(low, weight_ref[...]) + bias_ref[...]
         proj_ref[there, :] = proj
         for j in range(rows_part // patches):
-            f = i * (rows_part // patches) + j
+            f = at // patches + j
             here = slice(f * patches, (f + 1) * patches)
             row = slice(f, f + 1)
             after = tok_ref[f].astype(f32) + gate_one_ref[row, :] * proj[
@@ -586,6 +602,7 @@
             inv = lax.rsqrt(jnp.mean(centre * centre, axis=1, keepdims=True) + norm_eps)
             hid = centre * inv * (1.0 + scale_ref[row, :]) + shift_ref[row, :]
             hid_ref[here, :] = hid.astype(bf16)
+        at += rows_part
 
 
 def merge_heads(attended, proj_weight, proj_bias, tokens, mods):
@@ -661,33 +678,32 @@
 
 def side_kernel(branch_ref, back_ref, after_ref, proj_ref, cot_ref, gate_two_ref, bias_ref,
                 grad_ref, gproj_ref, gbranch_ref, out_ref, sums_ref, biases_ref):
-    frames, patches, width = cot_ref.shape
-    proj_sum = jnp.zeros((1, width), f32)
-    down_sum = jnp.zeros((1, width), f32)
-    for f in range(frames):
-        here = slice(f * patches, (f + 1) * patches)
-        cot = cot_ref[f].astype(f32)
-        after = after_ref[here, :]
-        branch = branch_ref[here, :] + bias_ref[...]
-        out_ref[f] = (after + gate_two_ref[f : f + 1, :] * branch).astype(bf16)
-        centre = after - jnp.mean(after, axis=1, keepdims=True)
-        inv = lax.rsqrt(jnp.mean(centre * centre, axis=1, keepdims=True) + norm_eps)
-        back = back_ref[here, :]
-        for kind, term in enumerate(
-            (grad_ref[here, :] * proj_ref[here, :], back, back * (centre * inv), cot * branch)
-        ):
-            sums_ref[kind * frames + f : kind * frames + f + 1, :] = column_sum(term)
-        down_sum += column_sum(gbranch_ref[here, :].astype(f32))
-        proj_sum += column_sum(gproj_ref[here, :].astype(f32))
-    biases_ref[0:1, :] = proj_sum
-    biases_ref[1:2, :] = down_sum
+    f, frames = pl.program_id(0), pl.num_programs(0)
+    cot = cot_ref[0].astype(f32)
+    after = after_ref[...]
+    branch = branch_ref[...] + bias_ref[...]
+    out_ref[0] = (after + gate_two_ref[pl.ds(f, 1), :] * branch).astype(bf16)
+    centre = after - jnp.mean(after, axis=1, keepdims=True)
+    inv = lax.rsqrt(jnp.mean(centre * centre, axis=1, keepdims=True) + norm_eps)
+    back = back_ref[...]
+    for kind, term in enumerate(
+        (grad_ref[...] * proj_ref[...], back, back * (centre * inv), cot * branch)
+    ):
+        sums_ref[pl.ds(kind * frames + f, 1), :] = column_sum(term)
+
+    @pl.when(f == 0)
+    def _():
+        biases_ref[...] = jnp.zeros_like(biases_ref)
+
+    biases_ref[0:1, :] += column_sum(gproj_ref[...].astype(f32))
+    biases_ref[1:2, :] += column_sum(gbranch_ref[...].astype(f32))
 
 
 def side_sums(branch, back, after, proj, cotangent, gate_two, down_bias, grad_after, grad_proj,
               grad_branch):
     frames, patches, width = cotangent.shape
-    operands = [branch, back, after, proj, cotangent, gate_two, down_bias, grad_after, grad_proj,
-                grad_branch]
+    rows = pl.BlockSpec((patches, width), lambda f: (f, 0))
+    slot = pl.BlockSpec((1, patches, width), lambda f: (f, 0, 0))
     return pl.pallas_call(
         side_kernel,
         out_shape=[
@@ -695,12 +711,25 @@
             jax.ShapeDtypeStruct((4 * frames, width), f32),
             jax.ShapeDtypeStruct((2, width), f32),
         ],
-        in_specs=[pl.BlockSpec(memory_space=VMEM)] * len(operands),
-        out_specs=[pl.BlockSpec(memory_space=VMEM)] * 3,
+        grid=(frames,),
+        in_specs=[rows, rows, rows, rows, slot, whole(gate_two.shape), whole(down_bias.shape), rows,
+                  rows, rows],
+        out_specs=[slot, whole((4 * frames, width)), whole((2, width))],
         compiler_params=pltpu.CompilerParams(vmem_limit_bytes=48 * MIB),
         cost_estimate=pl.CostEstimate(flops=0, bytes_accessed=16 * MIB, transcendentals=0),
         name="side_sums",
-    )(*operands)
+    )(
+        in_hbm(branch),
+        in_hbm(back),
+        in_hbm(after),
+        in_hbm(proj),
+        cotangent,
+        gate_two,
+        down_bias,
+        grad_after,
+        grad_proj,
+        in_hbm(grad_branch),
+    )
 
 
 def heads_grad_kernel(hid_ref, first_ref, last_ref, out_ref, bias_ref, total):
@@ -856,6 +885,31 @@
         ),
         name="finish",
     )(first, last, *[qkv_weight] * 3, tokens, scale_one, grad_after, part_bias)
+
+
+def unpack_kernel(summed_ref, up_ref, down_ref, proj_ref):
+    entries, share, width = summed_ref.shape
+    quarters = entries // 2
+    for i in range(quarters):
+        up_ref[:, i * width : (i + 1) * width] = summed_ref[i].astype(f32)
+        down_ref[i * share : (i + 1) * share, :] = summed_ref[quarters + i].astype(f32)
+    proj_ref[...] = summed_ref[2 * quarters].astype(f32)
+
+
+def unpack(summed):
+    entries, share, width = summed.shape
+    quarters = entries // 2
+    return pl.pallas_call(
+        unpack_kernel,
+        out_shape=[
+            jax.ShapeDtypeStruct((share, quarters * width), f32),
+            jax.ShapeDtypeStruct((quarters * share, width), f32),
+            jax.ShapeDtypeStruct((share, width), f32),
+        ],
+        in_specs=[pl.BlockSpec(memory_space=VMEM)],
+        out_specs=[pl.BlockSpec(memory_space=VMEM)] * 3,
+        name="unpack",
+    )(summed)
 
 
 def last_kernel(clips, frames, got_ref, member_ref, cols_ref, early_ref, earlysum_ref,
@@ -991,17 +1045,22 @@
     level_ids = jnp.arange(devices * levels_here, dtype=jnp.int32)
     pick = (my_levels[:, None] == level_ids[None, :]).astype(bf16)
     my_embed = dot(pick, embed_act).astype(bf16)
-    frame_mod = dot(my_embed, ada_weight) + ada_bias.astype(f32)
-    frame_mod = lax.reduce_precision(frame_mod, 8, 7)
-    shift_one, scale_one, gate_one, shift_two, scale_two, gate_two = [
-        frame_mod[:, i * width : (i + 1) * width] for i in range(6)
-    ]
+
+    def modulation(embeds, first, count):
+        here = slice(first * width, (first + count) * width)
+        rows_mod = dot(embeds, ada_weight[:, here]) + ada_bias[here].astype(f32)
+        rows_mod = lax.reduce_precision(rows_mod, 8, 7)
+        return [rows_mod[:, i * width : (i + 1) * width] for i in range(count)]
+
+    shift_one, scale_one = modulation(my_embed, 0, 2)
 
     hidden_turned, head_parts = project(
         tokens, shift_one, scale_one, qkv_weight, qkv_bias.astype(f32)[None, :], cosine, sine
     )
+
+    my_embed, head_parts = lax.optimization_barrier((my_embed, head_parts))
+    gate_one, shift_two, scale_two, gate_two = modulation(my_embed, 2, 4)
     heads = exchange(head_parts, clip_groups)
-
     grad_branch, grad_act = act_grad(out_cotangent, gate_two, down_weight)
     slot_ids = (jnp.arange(devices * frames, dtype=jnp.int32) // (sp_count * frames)) * frames
     slot_ids = slot_ids + jnp.arange(devices * frames, dtype=jnp.int32) % frames
@@ -1021,8 +1080,9 @@
         )
     )
     outs, exts, attended = [], [], []
-    for part in range(halves):
-        out, ext = attend(heads, visible, patches, part, halves)
+    for first, frames_part in ((0, frames - frames // 4), (frames - frames // 4, frames // 4)):
+        out, ext = attend(heads, visible, patches, first, frames_part)
+        visible, out = lax.optimization_barrier((visible, out))
         outs.append(out)
         exts.append(ext)
         attended.append(exchange(out, clip_groups))
@@ -1106,12 +1166,12 @@
     early_got = exchange(early_parts, everyone)
 
     first_grads, carry, mixes = attend_back(
-        heads, grads, exts, outs, rotary, None, 0, False, patches
+        heads, grads, exts, outs, rotary, None, 0, halves, patches
     )
     carry, early_got = lax.optimization_barrier((carry, early_got))
     own_first = exchange(first_grads, clip_groups)
     (last_grads,) = attend_back(
-        heads, grads, exts, outs, rotary, (carry, mixes), 1, True, patches
+        heads, grads, exts, outs, rotary, (carry, mixes), 1, halves, patches
     )
     last_parts, own_first = lax.optimization_barrier((last_grads, own_first))
     own_last = exchange(last_parts, clip_groups)
@@ -1132,11 +1192,8 @@
 
     summed = lax.psum_scatter(
         summed, AXES, scatter_dimension=0, axis_index_groups=across_clips, tiled=True
-    )[0].astype(f32)
-    quarters = inner // width
-    up_w_out = jnp.concatenate([summed[i] for i in range(quarters)], axis=1)
-    down_w_out = summed[quarters : 2 * quarters].reshape(per_dest, width)
-    proj_w_out = summed[2 * quarters]
+    )[0]
+    up_w_out, down_w_out, proj_w_out = unpack(summed)
 
     tokens_grad, last_send = finish(
         own_first, own_last, qkv_weight, tokens, scale_one, grad_after, qkv_b_part, clips

time: 445 us -> 449 us (level)
  blocking collectives: 0 us -> 10.3 us
  starting transfers between devices: 49.1 us -> 44.2 us
    all_to_all x0 -> x1, blocking collectives: none -> 10.3 us  [exchange(): return lax.all_to_all(value, AXES, 0, 0, axis_index_groups=groups)]
    all_to_all x10 -> x9, starting transfers between devices: 44.3 us -> 39.3 us  [exchange(): return lax.all_to_all(value, AXES, 0, 0, axis_index_groups=groups)]
    pallas_call x4 -> x5, Pallas kernels: 154 us -> 156 us  [the longest x2 104 us: attend_back(): pl.pallas_call(functools.partial(attend_back_kernel, parts, len(exts), pa...]
    unnamed x60 -> x66, local copies, waits for them, and re-layouts: 17.6 us -> 18.5 us
    all_to_all x10 -> x9, waiting for transfers between devices: 50.6 us -> 50 us  [exchange(): return lax.all_to_all(value, AXES, 0, 0, axis_index_groups=groups)]
  transfers between devices with their start and end apart: 16 -> 15, of which waited for: 8 -> 9; matrix products, arithmetic and copies ran while one was open for 5% -> 6% of each run, Pallas kernels for 55% -> 55%
where the time goes in v5:
time: 449 us; the launch traced here: 443 us
  Pallas kernels  255 us (57%)
  waiting for transfers between devices  68.9 us (15%)
  starting transfers between devices  44.2 us (10%)
  local copies, waits for them, and re-layouts  30.3 us (7%)
  between operations  14.6 us (3%)
  other arithmetic  11.7 us (3%)
  blocking collectives  10.3 us (2%)
  matrix products  8.33 us (2%)
    pallas_call x2, Pallas kernels, attend_back(): pl.pallas_call(functools.partial(attend_back_kernel, parts, len(exts), pa...  104 us
    pallas_call x2, Pallas kernels, attend(): pl.pallas_call(functools.partial(attend_kernel, first, rows_part, patches...  50.6 us
    all_to_all x9, waiting for transfers between devices, exchange(): return lax.all_to_all(value, AXES, 0, 0, axis_index_groups=groups)  50 us
    all_to_all x9, starting transfers between devices, exchange(): return lax.all_to_all(value, AXES, 0, 0, axis_index_groups=groups)  39.3 us
    pallas_call x1, Pallas kernels, feed_forward(): pl.pallas_call(feed_kernel, out_shape=[jax.ShapeDtypeStruct((rows, width)...  36.3 us
    unnamed x66, local copies, waits for them, and re-layouts  18.5 us
    ppermute x3, waiting for transfers between devices, body(): qkv_sum = qkv_sum + lax.ppermute(some, AXES, pairs).astype(f32)  16.4 us
    all_to_all x1, blocking collectives, exchange(): return lax.all_to_all(value, AXES, 0, 0, axis_index_groups=groups)  10.3 us
  transfers between devices with their start and end apart: 15, of which 9 were waited for; matrix products, arithmetic and copies ran while one was open for 6% of the time, Pallas kernels for 55%

profile of v5, /device:TPU:0, one launch (start us, length us, event | category | flops | bytes accessed | tf_op | source)
XLA Modules:
  0.0 443.1 jit_solution(12881162997336842545)
XLA Ops:
  7.2 1.4 broadcast_in_dim.185
  8.6 7.3 %all-to-all-start = ((bf16[32,2,1024]{2,1,0:T(2,128)(2,1)}), bf16[32,2,1024]{2,1,0:T(2,128)(2,1)S(1)}, u32[]{:S(2)}, u32[]{:S(2)}) async-start(bf16[32,2,1024]{2,1,0:T(2,128)(2,1)} %broadcast_in_dim.185), calls=%async_computation | async-start | bytes 262144 | tf_op jit(solution)/shard_map/all_to_all | solution.py:37
  16.0 0.7 fusion.40
  16.7 0.7 compare_select_fusion.2
  18.1 0.7 and_select_fusion.5
  18.8 0.7 slice_convert_fusion.1
  19.6 0.8 fusion.26
  20.4 1.5 multiply_select_fusion
  22.6 0.7 broadcast_in_dim.218
  23.4 0.8 all-to-all-done
  24.8 3.0 fusion.13
  27.8 9.8 %project.1 = (bf16[1024,512]{1,0:T(8,128)(2,1)}, bf16[8,3,512,128]{3,2,1,0:T(8,128)(2,1)}) custom-call(bf16[4,128,1024]{2,1,0:T(8,128)(2,1)S(1)} %copy-done.2, f32[4,1024]{1,0:T(4,128)S(1)} %get-tuple-element.152.shift_ref, f32[4,1024]{1,0:T(4,128)S(1)} %get-tuple-element.151.scale_ref, bf16[1024,3072]{1,0:T(8,128)(2,1)} %wv_ref.3, ...), custom_call_target="tpu_custom_call" | custom-call | flops 3221225472 | bytes 10485760 | tf_op jit(solution)/shard_map/project/pallas_call | solution.py:118
  37.6 4.6 %all-to-all-start.1 = ((bf16[8,3,512,128]{3,2,1,0:T(8,128)(2,1)}), bf16[8,3,512,128]{3,2,1,0:T(8,128)(2,1)}, u32[]{:S(2)}, u32[]{:S(2)}) async-start(bf16[8,3,512,128]{3,2,1,0:T(8,128)(2,1)} %get-tuple-element.76), calls=%async_computation.1 | async-start | bytes 6291456 | tf_op jit(solution)/shard_map/all_to_all | solution.py:37
  42.4 1.2 gather_fusion.1
  43.7 1.5 gather_fusion.2
  47.2 4.7 %fusion.5 = f32[4,4096]{1,0:T(4,128)S(1)} fusion(bf16[4,1024]{1,0:T(4,128)(2,1)S(1)} %convolution_convert_fusion.1, bf16[1024,6144]{1,0:T(8,128)(2,1)} %param.27, f32[4096]{0:T(1024)S(1)} %slice_convert_fusion), kind=kOutput, calls=%fused_computation.7 | convolution fusion | flops 33587200 | bytes 8478720 | tf_op jit(solution)/shard_map/dot_general | solution.py:33
  51.9 3.4 copy-done.17
  55.3 8.3 %act_grad.1 = (bf16[512,1024]{1,0:T(8,128)(2,1)S(1)}, f32[512,4096]{1,0:T(8,128)}) custom-call(bf16[4,128,1024]{2,1,0:T(8,128)(2,1)S(1)} %copy-done.5, f32[4,1024]{1,0:T(4,128)S(1)} %get-tuple-element.150.gate_ref.gate_two_ref, bf16[4096,1024]{1,0:T(8,128)(2,1)S(1)} %copy-done.17), custom_call_target="tpu_custom_call" | custom-call | flops 4294967296 | bytes 18874368 | tf_op jit(solution)/shard_map/act_grad/pallas_call | solution.py:413
  63.5 1.0 copy-done.13
  64.5 15.5 %all-to-all-done.1.qkv_ref.refs_0_ = bf16[8,3,512,128]{3,2,1,0:T(8,128)(2,1)} async-done(((bf16[8,3,512,128]{3,2,1,0:T(8,128)(2,1)}), bf16[8,3,512,128]{3,2,1,0:T(8,128)(2,1)}, u32[]{:S(2)}, u32[]{:S(2)}) %all-to-all-start.1) | async-done | bytes 3145760 | tf_op jit(solution)/shard_map/all_to_all | solution.py:37
  81.4 36.8 %attend.2 = (bf16[8,384,128]{2,1,0:T(8,128)(2,1)}, bf16[2,8,384,128]{3,2,1,0:T(8,128)(2,1)}) custom-call(bf16[8,3,512,128]{3,2,1,0:T(8,128)(2,1)} %all-to-all-done.1.qkv_ref.refs_0_, f32[32,128]{1,0:T(8,128)S(1)} %bitcast.67), custom_call_target="tpu_custom_call" | custom-call | flops 25769803776 | bytes 4194304 | tf_op jit(solution)/shard_map/attend/pallas_call | solution.py:228
  118.2 13.8 %attend.3 = (bf16[8,128,128]{2,1,0:T(8,128)(2,1)}, bf16[2,8,128,128]{3,2,1,0:T(8,128)(2,1)}) custom-call(bf16[8,3,512,128]{3,2,1,0:T(8,128)(2,1)} %all-to-all-done.1.qkv_ref.refs_0_, f32[32,128]{1,0:T(8,128)S(1)} %bitcast.68), custom_call_target="tpu_custom_call" | custom-call | flops 8589934592 | bytes 4194304 | tf_op jit(solution)/shard_map/attend/pallas_call | solution.py:228
  132.0 10.3 %all_to_all.50.refs_1_ = bf16[8,128,128]{2,1,0:T(8,128)(2,1)S(1)} all-to-all(bf16[8,128,128]{2,1,0:T(8,128)(2,1)} %get-tuple-element.85.refs_5_), channel_id=1, replica_groups={{0,1,2,3,4,5,6,7},{8,9,10,11,12,13,14,15},{16,17,18,19,20,21,22,23},{24..., dimensions={0} | all-to-all | bytes 524288 | tf_op jit(solution)/shard_map/all_to_all | solution.py:37
  142.3 3.5 all-to-all-start.2
  146.7 11.7 %all-to-all-done.2.refs_0_ = bf16[8,384,128]{2,1,0:T(8,128)(2,1)S(1)} async-done(((bf16[8,384,128]{2,1,0:T(8,128)(2,1)}), bf16[8,384,128]{2,1,0:T(8,128)(2,1)S(1)}, u32[]{:S(2)}, u32[]{:S(2)}) %all-to-all-start.2) | async-done | bytes 786464 | tf_op jit(solution)/shard_map/all_to_all | solution.py:37
  158.4 4.9 %merge_heads.1 = (bf16[512,1024]{1,0:T(8,128)(2,1)S(1)}, f32[512,1024]{1,0:T(8,128)S(1)}, f32[512,1024]{1,0:T(8,128)}, bf16[512,1024]{1,0:T(8,128)(2,1)}) custom-call(bf16[8,384,128]{2,1,0:T(8,128)(2,1)S(1)} %all-to-all-done.2.refs_0_, bf16[8,128,128]{2,1,0:T(8,128)(2,1)S(1)} %all_to_all.50.refs_1_, bf16[1024,1024]{1,0:T(8,128)(2,1)} %weight_ref.1, ...), custom_call_target="tpu_custom_call" | custom-call | flops 1073741824 | bytes 16777216 | tf_op jit(solution)/shard_map/merge_heads/pallas_call | solution.py:612
  163.2 1.4 copy-done.11
  164.6 36.3 %feed_forward.1 = (f32[512,1024]{1,0:T(8,128)}, f32[512,1024]{1,0:T(8,128)}, f32[1,4096]{1,0:T(1,128)}, bf16[8,4,9,32,1024]{4,3,2,1,0:T(8,128)(2,1)}) custom-call(bf16[512,1024]{1,0:T(8,128)(2,1)} %get-tuple-element.86.hid_ref, bf16[512,1024]{1,0:T(8,128)(2,1)} %copy-done.13, f32[512,4096]{1,0:T(8,128)} %get-tuple-element.88.actgrad_ref, ...), custom_call_target="tpu_custom_call" | custom-call | flops 21474836480 | bytes 46137344 | tf_op jit(solution)/shard_map/feed_forward/pallas_call | solution.py:511
  200.9 1.6 copy-done.4
  202.5 6.0 %unmerge_heads.1 = (f32[512,1024]{1,0:T(8,128)}, bf16[512,1024]{1,0:T(8,128)(2,1)S(1)}, bf16[8,512,128]{2,1,0:T(8,128)(2,1)}) custom-call(f32[512,1024]{1,0:T(8,128)S(1)} %copy-done.4, f32[512,1024]{1,0:T(8,128)} %get-tuple-element.91.after_ref, bf16[4,128,1024]{2,1,0:T(8,128)(2,1)S(1)} %copy-done.5, f32[4,1024]{1,0:T(4,128)S(1)} %get-tuple-element.149.refs_5_.gate_one_ref, ...), custom_call_target="tpu_custom_call" | custom-call | flops 1073741824 | bytes 12582912 | tf_op jit(solution)/shard_map/unmerge_heads/pallas_call | solution.py:662
  208.5 2.7 proj_weight_grad.1
  211.2 1.0 copy-done.7
  212.8 4.4 all-to-all-start.4
  217.2 1.2 copy-done.6
  218.5 1.4 copy-done.8
  219.9 7.3 %side_sums.1 = (bf16[4,128,1024]{2,1,0:T(8,128)(2,1)}, f32[16,1024]{1,0:T(8,128)S(1)}, f32[2,1024]{1,0:T(2,128)S(1)}) custom-call(f32[512,1024]{1,0:T(8,128)} %get-tuple-element.89.branch_ref, f32[512,1024]{1,0:T(8,128)} %get-tuple-element.90.back_ref, f32[512,1024]{1,0:T(8,128)} %get-tuple-element.91.after_ref, f32[512,1024]{1,0:T(8,128)} %copy-done.11, ...), custom_call_target="tpu_custom_call" | custom-call | bytes 16777216 | tf_op jit(solution)/shard_map/side_sums/pallas_call | solution.py:707
  228.1 1.5 pad_maximum_fusion
  229.6 3.0 all-to-all-done.4.refs_1_
  232.6 3.5 all-to-all-start.5
  236.1 51.5 %attend_back.2 = (bf16[8,512,128]{2,1,0:T(8,128)(2,1)}, f32[128,4096]{1,0:T(8,128)}, bf16[2,8,512,128]{3,2,1,0:T(8,128)(2,1)}) custom-call(bf16[8,3,512,128]{3,2,1,0:T(8,128)(2,1)} %all-to-all-done.1.qkv_ref.refs_0_, bf16[8,512,128]{2,1,0:T(8,128)(2,1)} %all-to-all-done.4.refs_1_, bf16[2,8,384,128]{3,2,1,0:T(8,128)(2,1)} %get-tuple-element.97.refs_2_, ...), custom_call_target="tpu_custom_call" | custom-call | flops 42949672960 | bytes 8388608 | tf_op jit(solution)/shard_map/attend_back/pallas_call | solution.py:372
  287.6 1.0 copy-done.19
  288.6 4.4 %all-to-all-start.6 = ((bf16[8,512,128]{2,1,0:T(8,128)(2,1)}), bf16[8,512,128]{2,1,0:T(8,128)(2,1)S(1)}, u32[]{:S(2)}, u32[]{:S(2)}) async-start(bf16[8,512,128]{2,1,0:T(8,128)(2,1)} %get-tuple-element.106.first_ref), calls=%async_computation.6 | async-start | bytes 2097152 | tf_op jit(solution)/shard_map/all_to_all | solution.py:37
  293.1 52.3 %attend_back.3.last_ref = bf16[8,1024,128]{2,1,0:T(8,128)(2,1)} custom-call(bf16[8,3,512,128]{3,2,1,0:T(8,128)(2,1)} %all-to-all-done.1.qkv_ref.refs_0_, bf16[8,512,128]{2,1,0:T(8,128)(2,1)} %all-to-all-done.4.refs_1_, bf16[2,8,384,128]{3,2,1,0:T(8,128)(2,1)} %get-tuple-element.97.refs_2_, bf16[2,8,128,128]{3,2,1,0:T(8,128)(2,1)} %get-tuple-element.98.refs_3_, ...), custom_call_target="tpu_custom_call" | custom-call | flops 42949672960 | bytes 8388608 | tf_op jit(solution)/shard_map/attend_back/pallas_call | solution.py:372
  345.4 1.0 copy-done.9
  346.4 4.0 all-to-all-start.7
  350.4 1.6 copy-done.12
  352.1 1.2 copy-done.14
  353.3 9.5 %heads_grad.1 = (bf16[32,96,128]{2,1,0:T(8,128)(2,1)S(1)}, f32[1,384]{1,0:T(1,128)S(1)}) custom-call(bf16[8,1024,512]{2,1,0:T(8,128)(2,1)} %bitcast.84, bf16[8,512,128]{2,1,0:T(8,128)(2,1)S(1)} %copy-done.14, bf16[8,1024,128]{2,1,0:T(8,128)(2,1)S(1)} %copy-done.12), custom_call_target="tpu_custom_call" | custom-call | flops 3221225472 | bytes 12582912 | tf_op jit(solution)/shard_map/heads_grad/pallas_call | solution.py:773
  362.9 3.4 collective-permute-start.2
  366.3 1.1 collective-permute-start
  367.4 5.3 %collective-permute-done.2 = bf16[8,96,128]{2,1,0:T(8,128)(2,1)S(1)} collective-permute-done((bf16[8,96,128]{2,1,0:T(8,128)(2,1)S(1)}, bf16[8,96,128]{2,1,0:T(8,128)(2,1)S(1)}, u32[]{:S(2)}, u32[]{:S(2)}) %collective-permute-start.2) | collective-permute-done | bytes 196640 | tf_op jit(solution)/shard_map/ppermute | solution.py:1188
  372.7 11.2 %collective-permute-done.1 = bf16[8,96,128]{2,1,0:T(8,128)(2,1)S(1)} collective-permute-done((bf16[8,96,128]{2,1,0:T(8,128)(2,1)S(1)}, bf16[8,96,128]{2,1,0:T(8,128)(2,1)S(1)}, u32[]{:S(2)}, u32[]{:S(2)}) %collective-permute-start.1) | collective-permute-done | bytes 196640 | tf_op jit(solution)/shard_map/ppermute | solution.py:1188
  383.8 0.8 fusion.18
  384.6 1.2 copy-done.10
  385.9 10.0 %finish.1 = (bf16[4,128,1024]{2,1,0:T(8,128)(2,1)}, bf16[4,80,128]{2,1,0:T(8,128)(2,1)}) custom-call(bf16[8,512,128]{2,1,0:T(8,128)(2,1)S(1)} %copy-done.10, bf16[8,1024,128]{2,1,0:T(8,128)(2,1)S(1)} %all-to-all-done.7.last_ref, bf16[1024,3072]{1,0:T(8,128)(2,1)} %wv_ref.3, bf16[1024,3072]{1,0:T(8,128)(2,1)} %wv_ref.3, bf16[1024,3072]{1,0:T(8,128)(2,1)} %wv_ref.3, ...), custom_call_target="tpu_custom_call" | custom-call | flops 3221225472 | bytes 16777216 | tf_op jit(solution)/shard_map/finish/pallas_call | solution.py:866
  395.9 3.6 all-to-all-start.8
  399.5 1.3 copy.61
  400.9 6.9 %all-to-all-done.8 = bf16[4,80,128]{2,1,0:T(8,128)(2,1)S(1)} async-done(((bf16[4,80,128]{2,1,0:T(8,128)(2,1)}), bf16[4,80,128]{2,1,0:T(8,128)(2,1)S(1)}, u32[]{:S(2)}, u32[]{:S(2)}) %all-to-all-start.8) | async-done | bytes 81952 | tf_op jit(solution)/shard_map/all_to_all | solution.py:37
  407.9 1.0 pad_maximum_fusion.1
  408.9 3.9 all-to-all-start.9
  414.0 12.1 %all-to-all-done.9.got_ref = bf16[8,416,128]{2,1,0:T(8,128)(2,1)S(1)} async-done(((bf16[8,416,128]{2,1,0:T(8,128)(2,1)}), bf16[8,416,128]{2,1,0:T(8,128)(2,1)S(1)}, u32[]{:S(2)}, u32[]{:S(2)}) %all-to-all-start.9) | async-done | bytes 852000 | tf_op jit(solution)/shard_map/all_to_all | solution.py:37
  426.6 3.4 last_sums.1
  431.8 2.4 reduce-scatter.5.cloned.1.call-done
  434.2 2.1 unpack.1
  (132 shorter events, 11.7 us)
Async XLA Ops:
  7.2 10.3 %copy-start = (s32[4,16]{1,0:T(4,128)S(1)}, s32[4,16]{1,0:T(4,128)}, u32[]{:S(2)}) copy-start(s32[4,16]{1,0:T(4,128)} %param.38) | copy-start | bytes 772
  8.6 15.5 %all-to-all-start = ((bf16[32,2,1024]{2,1,0:T(2,128)(2,1)}), bf16[32,2,1024]{2,1,0:T(2,128)(2,1)S(1)}, u32[]{:S(2)}, u32[]{:S(2)}) async-start(bf16[32,2,1024]{2,1,0:T(2,128)(2,1)} %broadcast_in_dim.185), calls=%async_computation | async-start | bytes 262144 | tf_op jit(solution)/shard_map/all_to_all | solution.py:37
  21.9 0.7 copy-start.22
  21.9 2.6 copy-start.21
  22.0 5.7 %copy-start.25 = (f32[4,2,4,128]{3,2,1,0:T(4,128)}, f32[4,2,4,128]{3,2,1,0:T(4,128)S(1)}, u32[]{:S(2)}) copy-start(f32[4,2,4,128]{3,2,1,0:T(4,128)S(1)} %broadcast_in_dim.200) | copy-start | bytes 49156
  22.0 5.7 %copy-start.26 = (f32[4,2,4,128]{3,2,1,0:T(4,128)}, f32[4,2,4,128]{3,2,1,0:T(4,128)S(1)}, u32[]{:S(2)}) copy-start(f32[4,2,4,128]{3,2,1,0:T(4,128)S(1)} %broadcast_in_dim.191) | copy-start | bytes 49156
  24.7 3.0 copy-start.2
  27.7 9.8 %copy-start.15 = (f32[4,1024]{1,0:T(4,128)}, f32[4,1024]{1,0:T(4,128)S(1)}, u32[]{:S(2)}) copy-start(f32[4,1024]{1,0:T(4,128)S(1)} %get-tuple-element.151.scale_ref) | copy-start | bytes 49156
  37.5 4.9 %copy-start.18 = (s32[64]{0:T(128)S(1)}, s32[64]{0:T(128)}, u32[]{:S(2)}) copy-start(s32[64]{0:T(128)} %param.39) | copy-start | bytes 772
  37.5 9.0 %copy-start.28 = (bf16[6144]{0:T(1024)(128)(2,1)S(1)}, bf16[6144]{0:T(1024)(128)(2,1)}, u32[]{:S(2)}) copy-start(bf16[6144]{0:T(1024)(128)(2,1)} %param.28) | copy-start | bytes 36868
  37.6 42.5 %all-to-all-start.1 = ((bf16[8,3,512,128]{3,2,1,0:T(8,128)(2,1)}), bf16[8,3,512,128]{3,2,1,0:T(8,128)(2,1)}, u32[]{:S(2)}, u32[]{:S(2)}) async-start(bf16[8,3,512,128]{3,2,1,0:T(8,128)(2,1)} %get-tuple-element.76), calls=%async_computation.1 | async-start | bytes 6291456 | tf_op jit(solution)/shard_map/all_to_all | solution.py:37
  42.1 170.0 %all-gather.3.cloned.1.call-start = ((), (), s32[]{:S(2)}) async-start(), calls=%async_computation.14 | async-start | bytes 9437184 | tf_op jit(solution)/shard_map/all_gather | solution.py:1091
  47.2 4.7 %copy-start.5 = (bf16[4,128,1024]{2,1,0:T(8,128)(2,1)S(1)}, bf16[4,128,1024]{2,1,0:T(8,128)(2,1)}, u32[]{:S(2)}) copy-start(bf16[4,128,1024]{2,1,0:T(8,128)(2,1)} %cot_ref.5) | copy-start | bytes 3145732
  51.9 3.4 copy-start.17
  55.3 24.8 %copy-start.32 = (s32[4]{0:T(128)S(1)}, s32[4]{0:T(128)}, u32[]{:S(2)}) copy-start(s32[4]{0:T(128)} %param.37) | copy-start | bytes 52
  63.5 1.0 copy-start.13
  118.2 27.8 %copy-start.30 = (bf16[1024]{0:T(1024)(128)(2,1)S(1)}, bf16[1024]{0:T(1024)(128)(2,1)}, u32[]{:S(2)}) copy-start(bf16[1024]{0:T(1024)(128)(2,1)} %param.32) | copy-start | bytes 6148
  118.2 27.9 %copy-start.29 = (bf16[4096]{0:T(1024)(128)(2,1)S(1)}, bf16[4096]{0:T(1024)(128)(2,1)}, u32[]{:S(2)}) copy-start(bf16[4096]{0:T(1024)(128)(2,1)} %param.34) | copy-start | bytes 24580
  142.3 16.1 %all-to-all-start.2 = ((bf16[8,384,128]{2,1,0:T(8,128)(2,1)}), bf16[8,384,128]{2,1,0:T(8,128)(2,1)S(1)}, u32[]{:S(2)}, u32[]{:S(2)}) async-start(bf16[8,384,128]{2,1,0:T(8,128)(2,1)} %get-tuple-element.82.refs_4_), calls=%async_computation.2 | async-start | bytes 1572864 | tf_op jit(solution)/shard_map/all_to_all | solution.py:37
  145.8 238.8 %reduce-scatter.3.cloned.1.call-start = ((), (), s32[]{:S(2)}) async-start(), calls=%async_computation.12 | async-start | bytes 21233664 | tf_op jit(solution)/shard_map/reduce_scatter | solution.py:1129
  163.2 1.4 copy-start.11
  200.9 1.6 copy-start.4
  211.2 1.0 copy-start.7
  212.2 0.7 copy-start.31
  212.8 4.4 copy-start.3
  212.8 19.8 %all-to-all-start.4 = ((bf16[8,512,128]{2,1,0:T(8,128)(2,1)}), bf16[8,512,128]{2,1,0:T(8,128)(2,1)}, u32[]{:S(2)}, u32[]{:S(2)}) async-start(bf16[8,512,128]{2,1,0:T(8,128)(2,1)} %get-tuple-element.96), calls=%async_computation.4 | async-start | bytes 2097152 | tf_op jit(solution)/shard_map/all_to_all | solution.py:37
  217.2 1.2 copy-start.6
  218.5 1.4 copy-start.8
  219.9 7.5 %copy-start.27 = (f32[1,4096]{1,0:T(1,128)S(1)}, f32[1,4096]{1,0:T(1,128)}, u32[]{:S(2)}) copy-start(f32[1,4096]{1,0:T(1,128)} %get-tuple-element.101) | copy-start | bytes 49156
  232.6 55.0 %all-to-all-start.5 = ((bf16[32,4,4224]{2,1,0:T(4,128)(2,1)}), bf16[32,4,4224]{2,1,0:T(4,128)(2,1)S(1)}, u32[]{:S(2)}, u32[]{:S(2)}) async-start(bf16[32,4,4224]{2,1,0:T(4,128)(2,1)} %pad_maximum_fusion), calls=%async_computation.5 | async-start | bytes 2162688 | tf_op jit(solution)/shard_map/all_to_all | solution.py:37
  287.6 1.0 copy-start.19
  288.6 56.8 %all-to-all-start.6 = ((bf16[8,512,128]{2,1,0:T(8,128)(2,1)}), bf16[8,512,128]{2,1,0:T(8,128)(2,1)S(1)}, u32[]{:S(2)}, u32[]{:S(2)}) async-start(bf16[8,512,128]{2,1,0:T(8,128)(2,1)} %get-tuple-element.106.first_ref), calls=%async_computation.6 | async-start | bytes 2097152 | tf_op jit(solution)/shard_map/all_to_all | solution.py:37
  345.4 1.0 copy-start.9
  346.4 38.2 %all-to-all-start.7 = ((bf16[8,1024,128]{2,1,0:T(8,128)(2,1)}), bf16[8,1024,128]{2,1,0:T(8,128)(2,1)S(1)}, u32[]{:S(2)}, u32[]{:S(2)}) async-start(bf16[8,1024,128]{2,1,0:T(8,128)(2,1)} %attend_back.3.last_ref), calls=%async_computation.7 | async-start | bytes 4194304 | tf_op jit(solution)/shard_map/all_to_all | solution.py:37
  350.4 83.9 %reduce-scatter.5.cloned.1.call-start = ((), (), s32[]{:S(2)}) async-start(), calls=%async_computation.13 | async-start | bytes 2949120 | tf_op jit(solution)/shard_map/reduce_scatter | solution.py:1193
  350.4 1.7 copy-start.12
  352.1 1.2 copy-start.14
  362.9 21.8 %copy-start.16 = (f32[4,1024]{1,0:T(4,128)S(1)}, f32[4,1024]{1,0:T(4,128)}, u32[]{:S(2)}) copy-start(f32[4,1024]{1,0:T(4,128)} %copy-done.15) | copy-start | bytes 49156
  362.9 9.7 %collective-permute-start.2 = (bf16[8,96,128]{2,1,0:T(8,128)(2,1)S(1)}, bf16[8,96,128]{2,1,0:T(8,128)(2,1)S(1)}, u32[]{:S(2)}, u32[]{:S(2)}) collective-permute-start(bf16[8,96,128]{2,1,0:T(8,128)(2,1)S(1)} %get-tuple-element.145), channel_id=1, source_target_pairs={{0,24},{1,25},{2,26},{3,27},{4,28},{5,29},{6,30},{7,31},{8,16},{9,... | collective-permute-start | bytes 589832 | tf_op jit(solution)/shard_map/ppermute | solution.py:1188
  366.3 17.5 %collective-permute-start.1 = (bf16[8,96,128]{2,1,0:T(8,128)(2,1)S(1)}, bf16[8,96,128]{2,1,0:T(8,128)(2,1)S(1)}, u32[]{:S(2)}, u32[]{:S(2)}) collective-permute-start(bf16[8,96,128]{2,1,0:T(8,128)(2,1)S(1)} %get-tuple-element.146), channel_id=1, source_target_pairs={{0,16},{1,17},{2,18},{3,19},{4,20},{5,21},{6,22},{7,23},{8,24},{9,... | collective-permute-start | bytes 589832 | tf_op jit(solution)/shard_map/ppermute | solution.py:1188
  366.3 17.5 %collective-permute-start = (bf16[8,96,128]{2,1,0:T(8,128)(2,1)S(1)}, bf16[8,96,128]{2,1,0:T(8,128)(2,1)S(1)}, u32[]{:S(2)}, u32[]{:S(2)}) collective-permute-start(bf16[8,96,128]{2,1,0:T(8,128)(2,1)S(1)} %get-tuple-element.144), channel_id=1, source_target_pairs={{0,8},{1,9},{2,10},{3,11},{4,12},{5,13},{6,14},{7,15},{8,0},{9,1},... | collective-permute-start | bytes 589832 | tf_op jit(solution)/shard_map/ppermute | solution.py:1188
  384.6 1.2 copy-start.10
  395.9 12.0 %copy-start.20 = (bf16[8,96,128]{2,1,0:T(8,128)(2,1)S(1)}, bf16[8,96,128]{2,1,0:T(8,128)(2,1)}, u32[]{:S(2)}) copy-start(bf16[8,96,128]{2,1,0:T(8,128)(2,1)} %fusion.18) | copy-start | bytes 589828
  395.9 11.9 %all-to-all-start.8 = ((bf16[4,80,128]{2,1,0:T(8,128)(2,1)}), bf16[4,80,128]{2,1,0:T(8,128)(2,1)S(1)}, u32[]{:S(2)}, u32[]{:S(2)}) async-start(bf16[4,80,128]{2,1,0:T(8,128)(2,1)} %get-tuple-element.120), calls=%async_computation.9 | async-start | bytes 163840 | tf_op jit(solution)/shard_map/all_to_all | solution.py:37
  408.9 3.9 slice-start
  408.9 17.2 %all-to-all-start.9 = ((bf16[8,416,128]{2,1,0:T(8,128)(2,1)}), bf16[8,416,128]{2,1,0:T(8,128)(2,1)S(1)}, u32[]{:S(2)}, u32[]{:S(2)}) async-start(bf16[8,416,128]{2,1,0:T(8,128)(2,1)} %pad_maximum_fusion.1), calls=%async_computation.10 | async-start | bytes 1703936 | tf_op jit(solution)/shard_map/all_to_all | solution.py:37
  412.8 0.7 copy-start.23
  412.8 1.0 copy-start.24
  413.1 23.2 %copy-start.1 = (s32[4,16]{1,0:T(4,128)S(1)}, s32[4,16]{1,0:T(4,128)}, u32[]{:S(2)}) copy-start(s32[4,16]{1,0:T(4,128)} %param.38) | copy-start | bytes 772
Sparse Core Ops, SparseCore 0:
  80.2 53.0 all-gather.2
  212.3 138.7 reduce-scatter.2
  384.7 49.4 reduce-scatter.4

commit v6 on v5

--- a/solution.py
+++ b/solution.py
@@ -1083,9 +1083,12 @@
     for first, frames_part in ((0, frames - frames // 4), (frames - frames // 4, frames // 4)):
         out, ext = attend(heads, visible, patches, first, frames_part)
         visible, out = lax.optimization_barrier((visible, out))
+        sent = out
+        if attended:
+            sent, attended[0] = lax.optimization_barrier((sent, attended[0]))
         outs.append(out)
         exts.append(ext)
-        attended.append(exchange(out, clip_groups))
+        attended.append(exchange(sent, clip_groups))
 
     hidden_turned, _ = lax.optimization_barrier((hidden_turned, heads))
     hidden_clip = lax.all_gather(hidden_turned, AXES, axis_index_groups=clip_groups)

time: 449 us -> 442 us (0.984)
  blocking collectives: 10.3 us -> 0 us
    all_to_all x1 -> x0, blocking collectives: 10.3 us -> none  [exchange(): return lax.all_to_all(value, AXES, 0, 0, axis_index_groups=groups)]
    all_to_all x9 -> x10, starting transfers between devices: 39.3 us -> 43.6 us  [exchange(): return lax.all_to_all(value, AXES, 0, 0, axis_index_groups=groups)]
    all_to_all x9 -> x10, waiting for transfers between devices: 50 us -> 48.9 us  [exchange(): return lax.all_to_all(value, AXES, 0, 0, axis_index_groups=groups)]
  transfers between devices with their start and end apart: 15 -> 16, of which waited for: 9 -> 10; matrix products, arithmetic and copies ran while one was open for 6% -> 6% of each run, Pallas kernels for 55% -> 56%
where the time goes in v6:
time: 442 us; the launch traced here: 435 us
  Pallas kernels  254 us (57%)
  waiting for transfers between devices  67.8 us (15%)
  starting transfers between devices  48.5 us (11%)
  local copies, waits for them, and re-layouts  30 us (7%)
  between operations  14.7 us (3%)
  other arithmetic  11.7 us (3%)
  matrix products  8.33 us (2%)
    pallas_call x2, Pallas kernels, attend_back(): pl.pallas_call(functools.partial(attend_back_kernel, parts, len(exts), pa...  104 us
    pallas_call x2, Pallas kernels, attend(): pl.pallas_call(functools.partial(attend_kernel, first, rows_part, patches...  50.4 us
    all_to_all x10, waiting for transfers between devices, exchange(): return lax.all_to_all(value, AXES, 0, 0, axis_index_groups=groups)  48.9 us
    all_to_all x10, starting transfers between devices, exchange(): return lax.all_to_all(value, AXES, 0, 0, axis_index_groups=groups)  43.6 us
    pallas_call x1, Pallas kernels, feed_forward(): pl.pallas_call(feed_kernel, out_shape=[jax.ShapeDtypeStruct((rows, width)...  36.4 us
    unnamed x66, local copies, waits for them, and re-layouts  18.1 us
    ppermute x3, waiting for transfers between devices, body(): qkv_sum = qkv_sum + lax.ppermute(some, AXES, pairs).astype(f32)  16.4 us
    pallas_call x1, Pallas kernels, finish(): pl.pallas_call(finish_kernel, out_shape=[jax.ShapeDtypeStruct((frames, pa...  10.1 us
  transfers between devices with their start and end apart: 16, of which 10 were waited for; matrix products, arithmetic and copies ran while one was open for 6% of the time, Pallas kernels for 56%

profile of v6, /device:TPU:0, one launch (start us, length us, event | category | flops | bytes accessed | tf_op | source)
XLA Modules:
  0.0 435.4 jit_solution(86923519125138817)
XLA Ops:
  7.2 1.4 broadcast_in_dim.185
  8.6 7.3 %all-to-all-start = ((bf16[32,2,1024]{2,1,0:T(2,128)(2,1)}), bf16[32,2,1024]{2,1,0:T(2,128)(2,1)S(1)}, u32[]{:S(2)}, u32[]{:S(2)}) async-start(bf16[32,2,1024]{2,1,0:T(2,128)(2,1)} %broadcast_in_dim.185), calls=%async_computation | async-start | bytes 262144 | tf_op jit(solution)/shard_map/all_to_all | solution.py:37
  16.0 0.7 fusion.40
  16.7 0.7 compare_select_fusion.2
  18.1 0.7 and_select_fusion.5
  19.6 0.8 fusion.26
  20.4 1.5 multiply_select_fusion
  22.1 0.7 broadcast_in_dim.218
  22.8 1.3 all-to-all-done
  24.7 3.0 fusion.13
  27.8 9.7 %project.1 = (bf16[1024,512]{1,0:T(8,128)(2,1)}, bf16[8,3,512,128]{3,2,1,0:T(8,128)(2,1)}) custom-call(bf16[4,128,1024]{2,1,0:T(8,128)(2,1)S(1)} %copy-done.2, f32[4,1024]{1,0:T(4,128)S(1)} %get-tuple-element.156.shift_ref, f32[4,1024]{1,0:T(4,128)S(1)} %get-tuple-element.155.scale_ref, bf16[1024,3072]{1,0:T(8,128)(2,1)} %wv_ref.3, ...), custom_call_target="tpu_custom_call" | custom-call | flops 3221225472 | bytes 10485760 | tf_op jit(solution)/shard_map/project/pallas_call | solution.py:118
  37.5 4.6 %all-to-all-start.1 = ((bf16[8,3,512,128]{3,2,1,0:T(8,128)(2,1)}), bf16[8,3,512,128]{3,2,1,0:T(8,128)(2,1)}, u32[]{:S(2)}, u32[]{:S(2)}) async-start(bf16[8,3,512,128]{3,2,1,0:T(8,128)(2,1)} %get-tuple-element.78), calls=%async_computation.1 | async-start | bytes 6291456 | tf_op jit(solution)/shard_map/all_to_all | solution.py:37
  42.4 1.2 gather_fusion.1
  43.7 1.5 gather_fusion.2
  47.1 4.7 %fusion.5 = f32[4,4096]{1,0:T(4,128)S(1)} fusion(bf16[4,1024]{1,0:T(4,128)(2,1)S(1)} %convolution_convert_fusion.1, bf16[1024,6144]{1,0:T(8,128)(2,1)} %param.27, f32[4096]{0:T(1024)S(1)} %slice_convert_fusion), kind=kOutput, calls=%fused_computation.7 | convolution fusion | flops 33587200 | bytes 8478720 | tf_op jit(solution)/shard_map/dot_general | solution.py:33
  51.9 3.4 copy-done.17
  55.2 8.2 %act_grad.1 = (bf16[512,1024]{1,0:T(8,128)(2,1)S(1)}, f32[512,4096]{1,0:T(8,128)}) custom-call(bf16[4,128,1024]{2,1,0:T(8,128)(2,1)S(1)} %copy-done.5, f32[4,1024]{1,0:T(4,128)S(1)} %get-tuple-element.154.gate_ref.gate_two_ref, bf16[4096,1024]{1,0:T(8,128)(2,1)S(1)} %copy-done.17), custom_call_target="tpu_custom_call" | custom-call | flops 4294967296 | bytes 18874368 | tf_op jit(solution)/shard_map/act_grad/pallas_call | solution.py:413
  63.4 1.0 copy-done.13
  64.4 15.6 %all-to-all-done.1.qkv_ref.refs_0_ = bf16[8,3,512,128]{3,2,1,0:T(8,128)(2,1)} async-done(((bf16[8,3,512,128]{3,2,1,0:T(8,128)(2,1)}), bf16[8,3,512,128]{3,2,1,0:T(8,128)(2,1)}, u32[]{:S(2)}, u32[]{:S(2)}) %all-to-all-start.1) | async-done | bytes 3145760 | tf_op jit(solution)/shard_map/all_to_all | solution.py:37
  81.4 36.6 %attend.2 = (bf16[8,384,128]{2,1,0:T(8,128)(2,1)}, bf16[2,8,384,128]{3,2,1,0:T(8,128)(2,1)}) custom-call(bf16[8,3,512,128]{3,2,1,0:T(8,128)(2,1)} %all-to-all-done.1.qkv_ref.refs_0_, f32[32,128]{1,0:T(8,128)S(1)} %bitcast.67), custom_call_target="tpu_custom_call" | custom-call | flops 25769803776 | bytes 4194304 | tf_op jit(solution)/shard_map/attend/pallas_call | solution.py:228
  118.0 4.0 all-to-all-start.2
  122.0 13.8 %attend.3 = (bf16[8,128,128]{2,1,0:T(8,128)(2,1)}, bf16[2,8,128,128]{3,2,1,0:T(8,128)(2,1)}) custom-call(bf16[8,3,512,128]{3,2,1,0:T(8,128)(2,1)} %all-to-all-done.1.qkv_ref.refs_0_, f32[32,128]{1,0:T(8,128)S(1)} %bitcast.68), custom_call_target="tpu_custom_call" | custom-call | flops 8589934592 | bytes 4194304 | tf_op jit(solution)/shard_map/attend/pallas_call | solution.py:228
  135.9 4.2 all-to-all-done.2.refs_0_
  140.0 3.4 all-to-all-start.3
  144.3 6.0 %all-to-all-done.3.refs_1_ = bf16[8,128,128]{2,1,0:T(8,128)(2,1)S(1)} async-done(((bf16[8,128,128]{2,1,0:T(8,128)(2,1)}), bf16[8,128,128]{2,1,0:T(8,128)(2,1)S(1)}, u32[]{:S(2)}, u32[]{:S(2)}) %all-to-all-start.3) | async-done | bytes 262176 | tf_op jit(solution)/shard_map/all_to_all | solution.py:37
  150.3 4.8 %merge_heads.1 = (bf16[512,1024]{1,0:T(8,128)(2,1)S(1)}, f32[512,1024]{1,0:T(8,128)S(1)}, f32[512,1024]{1,0:T(8,128)}, bf16[512,1024]{1,0:T(8,128)(2,1)}) custom-call(bf16[8,384,128]{2,1,0:T(8,128)(2,1)S(1)} %all-to-all-done.2.refs_0_, bf16[8,128,128]{2,1,0:T(8,128)(2,1)S(1)} %all-to-all-done.3.refs_1_, bf16[1024,1024]{1,0:T(8,128)(2,1)} %weight_ref.1, ...), custom_call_target="tpu_custom_call" | custom-call | flops 1073741824 | bytes 16777216 | tf_op jit(solution)/shard_map/merge_heads/pallas_call | solution.py:612
  155.2 1.3 copy-done.11
  156.5 36.4 %feed_forward.1 = (f32[512,1024]{1,0:T(8,128)}, f32[512,1024]{1,0:T(8,128)}, f32[1,4096]{1,0:T(1,128)}, bf16[8,4,9,32,1024]{4,3,2,1,0:T(8,128)(2,1)}) custom-call(bf16[512,1024]{1,0:T(8,128)(2,1)} %get-tuple-element.90.hid_ref, bf16[512,1024]{1,0:T(8,128)(2,1)} %copy-done.13, f32[512,4096]{1,0:T(8,128)} %get-tuple-element.92.actgrad_ref, ...), custom_call_target="tpu_custom_call" | custom-call | flops 21474836480 | bytes 46137344 | tf_op jit(solution)/shard_map/feed_forward/pallas_call | solution.py:511
  192.9 1.6 copy-done.4
  194.5 6.0 %unmerge_heads.1 = (f32[512,1024]{1,0:T(8,128)}, bf16[512,1024]{1,0:T(8,128)(2,1)S(1)}, bf16[8,512,128]{2,1,0:T(8,128)(2,1)}) custom-call(f32[512,1024]{1,0:T(8,128)S(1)} %copy-done.4, f32[512,1024]{1,0:T(8,128)} %get-tuple-element.95.after_ref, bf16[4,128,1024]{2,1,0:T(8,128)(2,1)S(1)} %copy-done.5, f32[4,1024]{1,0:T(4,128)S(1)} %get-tuple-element.153.refs_5_.gate_one_ref, ...), custom_call_target="tpu_custom_call" | custom-call | flops 1073741824 | bytes 12582912 | tf_op jit(solution)/shard_map/unmerge_heads/pallas_call | solution.py:662
  200.5 2.7 proj_weight_grad.1
  203.1 1.0 copy-done.7
  204.8 4.4 %all-to-all-start.4 = ((bf16[8,512,128]{2,1,0:T(8,128)(2,1)}), bf16[8,512,128]{2,1,0:T(8,128)(2,1)}, u32[]{:S(2)}, u32[]{:S(2)}) async-start(bf16[8,512,128]{2,1,0:T(8,128)(2,1)} %get-tuple-element.100), calls=%async_computation.4 | async-start | bytes 2097152 | tf_op jit(solution)/shard_map/all_to_all | solution.py:37
  209.2 1.2 copy-done.6
  210.4 1.5 copy-done.8
  211.9 7.4 %side_sums.1 = (bf16[4,128,1024]{2,1,0:T(8,128)(2,1)}, f32[16,1024]{1,0:T(8,128)S(1)}, f32[2,1024]{1,0:T(2,128)S(1)}) custom-call(f32[512,1024]{1,0:T(8,128)} %get-tuple-element.93.branch_ref, f32[512,1024]{1,0:T(8,128)} %get-tuple-element.94.back_ref, f32[512,1024]{1,0:T(8,128)} %get-tuple-element.95.after_ref, f32[512,1024]{1,0:T(8,128)} %copy-done.11, ...), custom_call_target="tpu_custom_call" | custom-call | bytes 16777216 | tf_op jit(solution)/shard_map/side_sums/pallas_call | solution.py:707
  220.2 1.5 pad_maximum_fusion
  221.7 2.8 all-to-all-done.4.refs_1_
  224.6 3.9 all-to-all-start.5
  228.5 51.4 %attend_back.2 = (bf16[8,512,128]{2,1,0:T(8,128)(2,1)}, f32[128,4096]{1,0:T(8,128)}, bf16[2,8,512,128]{3,2,1,0:T(8,128)(2,1)}) custom-call(bf16[8,3,512,128]{3,2,1,0:T(8,128)(2,1)} %all-to-all-done.1.qkv_ref.refs_0_, bf16[8,512,128]{2,1,0:T(8,128)(2,1)} %all-to-all-done.4.refs_1_, bf16[2,8,384,128]{3,2,1,0:T(8,128)(2,1)} %get-tuple-element.101.refs_2_, ...), custom_call_target="tpu_custom_call" | custom-call | flops 42949672960 | bytes 8388608 | tf_op jit(solution)/shard_map/attend_back/pallas_call | solution.py:372
  280.0 1.0 copy-done.19
  280.9 4.4 %all-to-all-start.6 = ((bf16[8,512,128]{2,1,0:T(8,128)(2,1)}), bf16[8,512,128]{2,1,0:T(8,128)(2,1)S(1)}, u32[]{:S(2)}, u32[]{:S(2)}) async-start(bf16[8,512,128]{2,1,0:T(8,128)(2,1)} %get-tuple-element.110.first_ref), calls=%async_computation.6 | async-start | bytes 2097152 | tf_op jit(solution)/shard_map/all_to_all | solution.py:37
  285.4 52.3 %attend_back.3.last_ref = bf16[8,1024,128]{2,1,0:T(8,128)(2,1)} custom-call(bf16[8,3,512,128]{3,2,1,0:T(8,128)(2,1)} %all-to-all-done.1.qkv_ref.refs_0_, bf16[8,512,128]{2,1,0:T(8,128)(2,1)} %all-to-all-done.4.refs_1_, bf16[2,8,384,128]{3,2,1,0:T(8,128)(2,1)} %get-tuple-element.101.refs_2_, bf16[2,8,128,128]{3,2,1,0:T(8,128)(2,1)} %get-tuple-element.102.refs_3_, ...), custom_call_target="tpu_custom_call" | custom-call | flops 42949672960 | bytes 8388608 | tf_op jit(solution)/shard_map/attend_back/pallas_call | solution.py:372
  337.7 1.0 copy-done.9
  338.7 4.0 all-to-all-start.7
  342.8 1.7 copy-done.12
  344.4 1.2 copy-done.14
  345.7 9.5 %heads_grad.1 = (bf16[32,96,128]{2,1,0:T(8,128)(2,1)S(1)}, f32[1,384]{1,0:T(1,128)S(1)}) custom-call(bf16[8,1024,512]{2,1,0:T(8,128)(2,1)} %bitcast.84, bf16[8,512,128]{2,1,0:T(8,128)(2,1)S(1)} %copy-done.14, bf16[8,1024,128]{2,1,0:T(8,128)(2,1)S(1)} %copy-done.12), custom_call_target="tpu_custom_call" | custom-call | flops 3221225472 | bytes 12582912 | tf_op jit(solution)/shard_map/heads_grad/pallas_call | solution.py:773
  355.3 3.4 collective-permute-start.2
  358.7 1.1 collective-permute-start
  359.7 5.3 %collective-permute-done.2 = bf16[8,96,128]{2,1,0:T(8,128)(2,1)S(1)} collective-permute-done((bf16[8,96,128]{2,1,0:T(8,128)(2,1)S(1)}, bf16[8,96,128]{2,1,0:T(8,128)(2,1)S(1)}, u32[]{:S(2)}, u32[]{:S(2)}) %collective-permute-start.2) | collective-permute-done | bytes 196640 | tf_op jit(solution)/shard_map/ppermute | solution.py:1191
  365.0 11.1 %collective-permute-done.1 = bf16[8,96,128]{2,1,0:T(8,128)(2,1)S(1)} collective-permute-done((bf16[8,96,128]{2,1,0:T(8,128)(2,1)S(1)}, bf16[8,96,128]{2,1,0:T(8,128)(2,1)S(1)}, u32[]{:S(2)}, u32[]{:S(2)}) %collective-permute-start.1) | collective-permute-done | bytes 196640 | tf_op jit(solution)/shard_map/ppermute | solution.py:1191
  376.1 0.8 fusion.18
  377.0 1.2 copy-done.10
  378.2 10.1 %finish.1 = (bf16[4,128,1024]{2,1,0:T(8,128)(2,1)}, bf16[4,80,128]{2,1,0:T(8,128)(2,1)}) custom-call(bf16[8,512,128]{2,1,0:T(8,128)(2,1)S(1)} %copy-done.10, bf16[8,1024,128]{2,1,0:T(8,128)(2,1)S(1)} %all-to-all-done.7.last_ref, bf16[1024,3072]{1,0:T(8,128)(2,1)} %wv_ref.3, bf16[1024,3072]{1,0:T(8,128)(2,1)} %wv_ref.3, bf16[1024,3072]{1,0:T(8,128)(2,1)} %wv_ref.3, ...), custom_call_target="tpu_custom_call" | custom-call | flops 3221225472 | bytes 16777216 | tf_op jit(solution)/shard_map/finish/pallas_call | solution.py:866
  388.3 3.6 all-to-all-start.8
  391.9 1.3 copy.61
  393.2 6.9 %all-to-all-done.8 = bf16[4,80,128]{2,1,0:T(8,128)(2,1)S(1)} async-done(((bf16[4,80,128]{2,1,0:T(8,128)(2,1)}), bf16[4,80,128]{2,1,0:T(8,128)(2,1)S(1)}, u32[]{:S(2)}, u32[]{:S(2)}) %all-to-all-start.8) | async-done | bytes 81952 | tf_op jit(solution)/shard_map/all_to_all | solution.py:37
  400.3 0.9 pad_maximum_fusion.1
  401.2 3.9 all-to-all-start.9
  406.4 12.1 %all-to-all-done.9.got_ref = bf16[8,416,128]{2,1,0:T(8,128)(2,1)S(1)} async-done(((bf16[8,416,128]{2,1,0:T(8,128)(2,1)}), bf16[8,416,128]{2,1,0:T(8,128)(2,1)S(1)}, u32[]{:S(2)}, u32[]{:S(2)}) %all-to-all-start.9) | async-done | bytes 852000 | tf_op jit(solution)/shard_map/all_to_all | solution.py:37
  418.9 3.4 last_sums.1
  424.2 2.4 reduce-scatter.5.cloned.1.call-done
  426.6 2.1 unpack.1
  (133 shorter events, 11.9 us)
Async XLA Ops:
  7.2 10.3 %copy-start = (s32[4,16]{1,0:T(4,128)S(1)}, s32[4,16]{1,0:T(4,128)}, u32[]{:S(2)}) copy-start(s32[4,16]{1,0:T(4,128)} %param.38) | copy-start | bytes 772
  8.6 15.5 %all-to-all-start = ((bf16[32,2,1024]{2,1,0:T(2,128)(2,1)}), bf16[32,2,1024]{2,1,0:T(2,128)(2,1)S(1)}, u32[]{:S(2)}, u32[]{:S(2)}) async-start(bf16[32,2,1024]{2,1,0:T(2,128)(2,1)} %broadcast_in_dim.185), calls=%async_computation | async-start | bytes 262144 | tf_op jit(solution)/shard_map/all_to_all | solution.py:37
  21.9 2.2 copy-start.21
  21.9 2.2 copy-start.22
  22.0 5.7 %copy-start.25 = (f32[4,2,4,128]{3,2,1,0:T(4,128)}, f32[4,2,4,128]{3,2,1,0:T(4,128)S(1)}, u32[]{:S(2)}) copy-start(f32[4,2,4,128]{3,2,1,0:T(4,128)S(1)} %broadcast_in_dim.200) | copy-start | bytes 49156
  22.0 5.7 %copy-start.26 = (f32[4,2,4,128]{3,2,1,0:T(4,128)}, f32[4,2,4,128]{3,2,1,0:T(4,128)S(1)}, u32[]{:S(2)}) copy-start(f32[4,2,4,128]{3,2,1,0:T(4,128)S(1)} %broadcast_in_dim.191) | copy-start | bytes 49156
  24.7 3.0 copy-start.2
  27.7 9.8 %copy-start.15 = (f32[4,1024]{1,0:T(4,128)}, f32[4,1024]{1,0:T(4,128)S(1)}, u32[]{:S(2)}) copy-start(f32[4,1024]{1,0:T(4,128)S(1)} %get-tuple-element.155.scale_ref) | copy-start | bytes 49156
  37.5 4.9 %copy-start.18 = (s32[64]{0:T(128)S(1)}, s32[64]{0:T(128)}, u32[]{:S(2)}) copy-start(s32[64]{0:T(128)} %param.39) | copy-start | bytes 772
  37.5 9.0 %copy-start.28 = (bf16[6144]{0:T(1024)(128)(2,1)S(1)}, bf16[6144]{0:T(1024)(128)(2,1)}, u32[]{:S(2)}) copy-start(bf16[6144]{0:T(1024)(128)(2,1)} %param.28) | copy-start | bytes 36868
  37.5 42.5 %all-to-all-start.1 = ((bf16[8,3,512,128]{3,2,1,0:T(8,128)(2,1)}), bf16[8,3,512,128]{3,2,1,0:T(8,128)(2,1)}, u32[]{:S(2)}, u32[]{:S(2)}) async-start(bf16[8,3,512,128]{3,2,1,0:T(8,128)(2,1)} %get-tuple-element.78), calls=%async_computation.1 | async-start | bytes 6291456 | tf_op jit(solution)/shard_map/all_to_all | solution.py:37
  42.1 162.0 %all-gather.3.cloned.1.call-start = ((), (), s32[]{:S(2)}) async-start(), calls=%async_computation.14 | async-start | bytes 9437184 | tf_op jit(solution)/shard_map/all_gather | solution.py:1094
  47.1 4.7 %copy-start.5 = (bf16[4,128,1024]{2,1,0:T(8,128)(2,1)S(1)}, bf16[4,128,1024]{2,1,0:T(8,128)(2,1)}, u32[]{:S(2)}) copy-start(bf16[4,128,1024]{2,1,0:T(8,128)(2,1)} %cot_ref.5) | copy-start | bytes 3145732
  51.8 3.4 copy-start.17
  55.2 24.8 %copy-start.32 = (s32[4]{0:T(128)S(1)}, s32[4]{0:T(128)}, u32[]{:S(2)}) copy-start(s32[4]{0:T(128)} %param.37) | copy-start | bytes 52
  63.4 1.0 copy-start.13
  118.0 22.0 %all-to-all-start.2 = ((bf16[8,384,128]{2,1,0:T(8,128)(2,1)}), bf16[8,384,128]{2,1,0:T(8,128)(2,1)S(1)}, u32[]{:S(2)}, u32[]{:S(2)}) async-start(bf16[8,384,128]{2,1,0:T(8,128)(2,1)} %get-tuple-element.87.refs_4_), calls=%async_computation.2 | async-start | bytes 1572864 | tf_op jit(solution)/shard_map/all_to_all | solution.py:37
  122.0 21.7 %copy-start.30 = (bf16[1024]{0:T(1024)(128)(2,1)S(1)}, bf16[1024]{0:T(1024)(128)(2,1)}, u32[]{:S(2)}) copy-start(bf16[1024]{0:T(1024)(128)(2,1)} %param.32) | copy-start | bytes 6148
  122.0 21.7 %copy-start.29 = (bf16[4096]{0:T(1024)(128)(2,1)S(1)}, bf16[4096]{0:T(1024)(128)(2,1)}, u32[]{:S(2)}) copy-start(bf16[4096]{0:T(1024)(128)(2,1)} %param.34) | copy-start | bytes 24580
  140.0 10.3 %all-to-all-start.3 = ((bf16[8,128,128]{2,1,0:T(8,128)(2,1)}), bf16[8,128,128]{2,1,0:T(8,128)(2,1)S(1)}, u32[]{:S(2)}, u32[]{:S(2)}) async-start(bf16[8,128,128]{2,1,0:T(8,128)(2,1)} %get-tuple-element.89.refs_5_), calls=%async_computation.3 | async-start | bytes 524288 | tf_op jit(solution)/shard_map/all_to_all | solution.py:37
  143.4 233.5 %reduce-scatter.3.cloned.1.call-start = ((), (), s32[]{:S(2)}) async-start(), calls=%async_computation.12 | async-start | bytes 21233664 | tf_op jit(solution)/shard_map/reduce_scatter | solution.py:1132
  155.1 1.3 copy-start.11
  192.9 1.6 copy-start.4
  203.1 1.0 copy-start.7
  204.1 0.7 copy-start.31
  204.8 4.4 %copy-start.3 = (f32[512,1024]{1,0:T(8,128)S(1)}, f32[512,1024]{1,0:T(8,128)}, u32[]{:S(2)}) copy-start(f32[512,1024]{1,0:T(8,128)} %get-tuple-element.97.grad_ref.after_ref) | copy-start | bytes 6291460
  204.8 19.8 %all-to-all-start.4 = ((bf16[8,512,128]{2,1,0:T(8,128)(2,1)}), bf16[8,512,128]{2,1,0:T(8,128)(2,1)}, u32[]{:S(2)}, u32[]{:S(2)}) async-start(bf16[8,512,128]{2,1,0:T(8,128)(2,1)} %get-tuple-element.100), calls=%async_computation.4 | async-start | bytes 2097152 | tf_op jit(solution)/shard_map/all_to_all | solution.py:37
  209.2 1.3 copy-start.6
  210.4 1.5 copy-start.8
  211.9 7.5 %copy-start.27 = (f32[1,4096]{1,0:T(1,128)S(1)}, f32[1,4096]{1,0:T(1,128)}, u32[]{:S(2)}) copy-start(f32[1,4096]{1,0:T(1,128)} %get-tuple-element.105) | copy-start | bytes 49156
  224.6 55.4 %all-to-all-start.5 = ((bf16[32,4,4224]{2,1,0:T(4,128)(2,1)}), bf16[32,4,4224]{2,1,0:T(4,128)(2,1)S(1)}, u32[]{:S(2)}, u32[]{:S(2)}) async-start(bf16[32,4,4224]{2,1,0:T(4,128)(2,1)} %pad_maximum_fusion), calls=%async_computation.5 | async-start | bytes 2162688 | tf_op jit(solution)/shard_map/all_to_all | solution.py:37
  280.0 1.0 copy-start.19
  280.9 56.8 %all-to-all-start.6 = ((bf16[8,512,128]{2,1,0:T(8,128)(2,1)}), bf16[8,512,128]{2,1,0:T(8,128)(2,1)S(1)}, u32[]{:S(2)}, u32[]{:S(2)}) async-start(bf16[8,512,128]{2,1,0:T(8,128)(2,1)} %get-tuple-element.110.first_ref), calls=%async_computation.6 | async-start | bytes 2097152 | tf_op jit(solution)/shard_map/all_to_all | solution.py:37
  337.7 1.0 copy-start.9
  338.7 38.2 %all-to-all-start.7 = ((bf16[8,1024,128]{2,1,0:T(8,128)(2,1)}), bf16[8,1024,128]{2,1,0:T(8,128)(2,1)S(1)}, u32[]{:S(2)}, u32[]{:S(2)}) async-start(bf16[8,1024,128]{2,1,0:T(8,128)(2,1)} %attend_back.3.last_ref), calls=%async_computation.7 | async-start | bytes 4194304 | tf_op jit(solution)/shard_map/all_to_all | solution.py:37
  342.7 83.9 %reduce-scatter.5.cloned.1.call-start = ((), (), s32[]{:S(2)}) async-start(), calls=%async_computation.13 | async-start | bytes 2949120 | tf_op jit(solution)/shard_map/reduce_scatter | solution.py:1196
  342.8 1.7 copy-start.12
  344.4 1.2 copy-start.14
  355.2 21.7 %copy-start.16 = (f32[4,1024]{1,0:T(4,128)S(1)}, f32[4,1024]{1,0:T(4,128)}, u32[]{:S(2)}) copy-start(f32[4,1024]{1,0:T(4,128)} %copy-done.15) | copy-start | bytes 49156
  355.3 9.7 %collective-permute-start.2 = (bf16[8,96,128]{2,1,0:T(8,128)(2,1)S(1)}, bf16[8,96,128]{2,1,0:T(8,128)(2,1)S(1)}, u32[]{:S(2)}, u32[]{:S(2)}) collective-permute-start(bf16[8,96,128]{2,1,0:T(8,128)(2,1)S(1)} %get-tuple-element.149), channel_id=1, source_target_pairs={{0,24},{1,25},{2,26},{3,27},{4,28},{5,29},{6,30},{7,31},{8,16},{9,... | collective-permute-start | bytes 589832 | tf_op jit(solution)/shard_map/ppermute | solution.py:1191
  358.7 17.5 %collective-permute-start.1 = (bf16[8,96,128]{2,1,0:T(8,128)(2,1)S(1)}, bf16[8,96,128]{2,1,0:T(8,128)(2,1)S(1)}, u32[]{:S(2)}, u32[]{:S(2)}) collective-permute-start(bf16[8,96,128]{2,1,0:T(8,128)(2,1)S(1)} %get-tuple-element.150), channel_id=1, source_target_pairs={{0,16},{1,17},{2,18},{3,19},{4,20},{5,21},{6,22},{7,23},{8,24},{9,... | collective-permute-start | bytes 589832 | tf_op jit(solution)/shard_map/ppermute | solution.py:1191
  358.7 17.5 %collective-permute-start = (bf16[8,96,128]{2,1,0:T(8,128)(2,1)S(1)}, bf16[8,96,128]{2,1,0:T(8,128)(2,1)S(1)}, u32[]{:S(2)}, u32[]{:S(2)}) collective-permute-start(bf16[8,96,128]{2,1,0:T(8,128)(2,1)S(1)} %get-tuple-element.148), channel_id=1, source_target_pairs={{0,8},{1,9},{2,10},{3,11},{4,12},{5,13},{6,14},{7,15},{8,0},{9,1},... | collective-permute-start | bytes 589832 | tf_op jit(solution)/shard_map/ppermute | solution.py:1191
  377.0 1.2 copy-start.10
  388.3 12.0 %copy-start.20 = (bf16[8,96,128]{2,1,0:T(8,128)(2,1)S(1)}, bf16[8,96,128]{2,1,0:T(8,128)(2,1)}, u32[]{:S(2)}) copy-start(bf16[8,96,128]{2,1,0:T(8,128)(2,1)} %fusion.18) | copy-start | bytes 589828
  388.3 11.9 %all-to-all-start.8 = ((bf16[4,80,128]{2,1,0:T(8,128)(2,1)}), bf16[4,80,128]{2,1,0:T(8,128)(2,1)S(1)}, u32[]{:S(2)}, u32[]{:S(2)}) async-start(bf16[4,80,128]{2,1,0:T(8,128)(2,1)} %get-tuple-element.124), calls=%async_computation.9 | async-start | bytes 163840 | tf_op jit(solution)/shard_map/all_to_all | solution.py:37
  401.2 3.9 slice-start
  401.2 17.2 %all-to-all-start.9 = ((bf16[8,416,128]{2,1,0:T(8,128)(2,1)}), bf16[8,416,128]{2,1,0:T(8,128)(2,1)S(1)}, u32[]{:S(2)}, u32[]{:S(2)}) async-start(bf16[8,416,128]{2,1,0:T(8,128)(2,1)} %pad_maximum_fusion.1), calls=%async_computation.10 | async-start | bytes 1703936 | tf_op jit(solution)/shard_map/all_to_all | solution.py:37
  405.1 0.7 copy-start.23
  405.2 1.0 copy-start.24
  405.5 23.2 %copy-start.1 = (s32[4,16]{1,0:T(4,128)S(1)}, s32[4,16]{1,0:T(4,128)}, u32[]{:S(2)}) copy-start(s32[4,16]{1,0:T(4,128)} %param.38) | copy-start | bytes 772
Sparse Core Ops, SparseCore 0:
  80.1 58.8 all-gather.2
  204.2 139.2 reduce-scatter.2
  377.1 49.4 reduce-scatter.4

commit v7 on v6

--- a/solution.py
+++ b/solution.py
@@ -789,7 +789,7 @@
             flops=6 * blocks * rows * width * LANES, bytes_accessed=12 * MIB, transcendentals=0
         ),
         name="heads_grad",
-    )(in_hbm(hidden_clip), first, last)
+    )(in_hbm(hidden_clip), in_hbm(first), in_hbm(last))
 
 
 def finish_kernel(first_ref, last_ref, wq_ref, wk_ref, wv_ref, tok_ref, scale_ref, after_ref,

time: 442 us -> 439 us (level)
    unnamed x66 -> x62, local copies, waits for them, and re-layouts: 18.1 us -> 15.2 us
where the time goes in v7:
time: 439 us; the launch traced here: 433 us
  Pallas kernels  255 us (58%)
  waiting for transfers between devices  67.6 us (15%)
  starting transfers between devices  48.6 us (11%)
  local copies, waits for them, and re-layouts  27.1 us (6%)
  between operations  14.6 us (3%)
  other arithmetic  11.7 us (3%)
  matrix products  8.33 us (2%)
    pallas_call x2, Pallas kernels, attend_back(): pl.pallas_call(functools.partial(attend_back_kernel, parts, len(exts), pa...  104 us
    pallas_call x2, Pallas kernels, attend(): pl.pallas_call(functools.partial(attend_kernel, first, rows_part, patches...  50.4 us
    all_to_all x10, waiting for transfers between devices, exchange(): return lax.all_to_all(value, AXES, 0, 0, axis_index_groups=groups)  48.8 us
    all_to_all x10, starting transfers between devices, exchange(): return lax.all_to_all(value, AXES, 0, 0, axis_index_groups=groups)  43.6 us
    pallas_call x1, Pallas kernels, feed_forward(): pl.pallas_call(feed_kernel, out_shape=[jax.ShapeDtypeStruct((rows, width)...  36.3 us
    ppermute x3, waiting for transfers between devices, body(): qkv_sum = qkv_sum + lax.ppermute(some, AXES, pairs).astype(f32)  16.3 us
    unnamed x62, local copies, waits for them, and re-layouts  15.2 us
    pallas_call x1, Pallas kernels, finish(): pl.pallas_call(finish_kernel, out_shape=[jax.ShapeDtypeStruct((frames, pa...  10.1 us
  transfers between devices with their start and end apart: 16, of which 10 were waited for; matrix products, arithmetic and copies ran while one was open for 6% of the time, Pallas kernels for 56%

profile of v7, /device:TPU:0, one launch (start us, length us, event | category | flops | bytes accessed | tf_op | source)
XLA Modules:
  0.0 433.0 jit_solution(15783039538706312845)
XLA Ops:
  7.2 1.4 broadcast_in_dim.185
  8.6 7.3 %all-to-all-start = ((bf16[32,2,1024]{2,1,0:T(2,128)(2,1)}), bf16[32,2,1024]{2,1,0:T(2,128)(2,1)S(1)}, u32[]{:S(2)}, u32[]{:S(2)}) async-start(bf16[32,2,1024]{2,1,0:T(2,128)(2,1)} %broadcast_in_dim.185), calls=%async_computation | async-start | bytes 262144 | tf_op jit(solution)/shard_map/all_to_all | solution.py:37
  16.0 0.7 fusion.40
  16.7 0.7 compare_select_fusion.2
  18.1 0.7 and_select_fusion.5
  18.8 0.7 slice_convert_fusion.1
  19.6 0.8 fusion.26
  20.4 1.5 multiply_select_fusion
  22.1 0.7 broadcast_in_dim.218
  22.8 1.3 all-to-all-done
  24.7 3.0 fusion.13
  27.8 9.7 %project.1 = (bf16[1024,512]{1,0:T(8,128)(2,1)}, bf16[8,3,512,128]{3,2,1,0:T(8,128)(2,1)}) custom-call(bf16[4,128,1024]{2,1,0:T(8,128)(2,1)S(1)} %copy-done.2, f32[4,1024]{1,0:T(4,128)S(1)} %get-tuple-element.156.shift_ref, f32[4,1024]{1,0:T(4,128)S(1)} %get-tuple-element.155.scale_ref, bf16[1024,3072]{1,0:T(8,128)(2,1)} %wv_ref.3, ...), custom_call_target="tpu_custom_call" | custom-call | flops 3221225472 | bytes 10485760 | tf_op jit(solution)/shard_map/project/pallas_call | solution.py:118
  37.5 4.6 %all-to-all-start.1 = ((bf16[8,3,512,128]{3,2,1,0:T(8,128)(2,1)}), bf16[8,3,512,128]{3,2,1,0:T(8,128)(2,1)}, u32[]{:S(2)}, u32[]{:S(2)}) async-start(bf16[8,3,512,128]{3,2,1,0:T(8,128)(2,1)} %get-tuple-element.78), calls=%async_computation.1 | async-start | bytes 6291456 | tf_op jit(solution)/shard_map/all_to_all | solution.py:37
  42.4 1.2 gather_fusion.1
  43.7 1.5 gather_fusion.2
  47.1 4.7 %fusion.5 = f32[4,4096]{1,0:T(4,128)S(1)} fusion(bf16[4,1024]{1,0:T(4,128)(2,1)S(1)} %convolution_convert_fusion.1, bf16[1024,6144]{1,0:T(8,128)(2,1)} %param.27, f32[4096]{0:T(1024)S(1)} %slice_convert_fusion), kind=kOutput, calls=%fused_computation.7 | convolution fusion | flops 33587200 | bytes 8478720 | tf_op jit(solution)/shard_map/dot_general | solution.py:33
  51.8 3.4 copy-done.15
  55.2 8.3 %act_grad.1 = (bf16[512,1024]{1,0:T(8,128)(2,1)S(1)}, f32[512,4096]{1,0:T(8,128)}) custom-call(bf16[4,128,1024]{2,1,0:T(8,128)(2,1)S(1)} %copy-done.5, f32[4,1024]{1,0:T(4,128)S(1)} %get-tuple-element.154.gate_ref.gate_two_ref, bf16[4096,1024]{1,0:T(8,128)(2,1)S(1)} %copy-done.15), custom_call_target="tpu_custom_call" | custom-call | flops 4294967296 | bytes 18874368 | tf_op jit(solution)/shard_map/act_grad/pallas_call | solution.py:413
  63.5 1.0 copy-done.12
  64.5 15.5 %all-to-all-done.1.qkv_ref.refs_0_ = bf16[8,3,512,128]{3,2,1,0:T(8,128)(2,1)} async-done(((bf16[8,3,512,128]{3,2,1,0:T(8,128)(2,1)}), bf16[8,3,512,128]{3,2,1,0:T(8,128)(2,1)}, u32[]{:S(2)}, u32[]{:S(2)}) %all-to-all-start.1) | async-done | bytes 3145760 | tf_op jit(solution)/shard_map/all_to_all | solution.py:37
  81.4 36.6 %attend.2 = (bf16[8,384,128]{2,1,0:T(8,128)(2,1)}, bf16[2,8,384,128]{3,2,1,0:T(8,128)(2,1)}) custom-call(bf16[8,3,512,128]{3,2,1,0:T(8,128)(2,1)} %all-to-all-done.1.qkv_ref.refs_0_, f32[32,128]{1,0:T(8,128)S(1)} %bitcast.67), custom_call_target="tpu_custom_call" | custom-call | flops 25769803776 | bytes 4194304 | tf_op jit(solution)/shard_map/attend/pallas_call | solution.py:228
  118.0 4.0 all-to-all-start.2
  122.0 13.8 %attend.3 = (bf16[8,128,128]{2,1,0:T(8,128)(2,1)}, bf16[2,8,128,128]{3,2,1,0:T(8,128)(2,1)}) custom-call(bf16[8,3,512,128]{3,2,1,0:T(8,128)(2,1)} %all-to-all-done.1.qkv_ref.refs_0_, f32[32,128]{1,0:T(8,128)S(1)} %bitcast.68), custom_call_target="tpu_custom_call" | custom-call | flops 8589934592 | bytes 4194304 | tf_op jit(solution)/shard_map/attend/pallas_call | solution.py:228
  135.8 4.2 all-to-all-done.2.refs_0_
  140.0 3.4 all-to-all-start.3
  144.3 6.0 %all-to-all-done.3.refs_1_ = bf16[8,128,128]{2,1,0:T(8,128)(2,1)S(1)} async-done(((bf16[8,128,128]{2,1,0:T(8,128)(2,1)}), bf16[8,128,128]{2,1,0:T(8,128)(2,1)S(1)}, u32[]{:S(2)}, u32[]{:S(2)}) %all-to-all-start.3) | async-done | bytes 262176 | tf_op jit(solution)/shard_map/all_to_all | solution.py:37
  150.3 4.8 %merge_heads.1 = (bf16[512,1024]{1,0:T(8,128)(2,1)S(1)}, f32[512,1024]{1,0:T(8,128)S(1)}, f32[512,1024]{1,0:T(8,128)}, bf16[512,1024]{1,0:T(8,128)(2,1)}) custom-call(bf16[8,384,128]{2,1,0:T(8,128)(2,1)S(1)} %all-to-all-done.2.refs_0_, bf16[8,128,128]{2,1,0:T(8,128)(2,1)S(1)} %all-to-all-done.3.refs_1_, bf16[1024,1024]{1,0:T(8,128)(2,1)} %weight_ref.1, ...), custom_call_target="tpu_custom_call" | custom-call | flops 1073741824 | bytes 16777216 | tf_op jit(solution)/shard_map/merge_heads/pallas_call | solution.py:612
  155.1 1.4 copy-done.11
  156.5 36.3 %feed_forward.1 = (f32[512,1024]{1,0:T(8,128)}, f32[512,1024]{1,0:T(8,128)}, f32[1,4096]{1,0:T(1,128)}, bf16[8,4,9,32,1024]{4,3,2,1,0:T(8,128)(2,1)}) custom-call(bf16[512,1024]{1,0:T(8,128)(2,1)} %get-tuple-element.90.hid_ref, bf16[512,1024]{1,0:T(8,128)(2,1)} %copy-done.12, f32[512,4096]{1,0:T(8,128)} %get-tuple-element.92.actgrad_ref, ...), custom_call_target="tpu_custom_call" | custom-call | flops 21474836480 | bytes 46137344 | tf_op jit(solution)/shard_map/feed_forward/pallas_call | solution.py:511
  192.8 1.6 copy-done.4
  194.4 6.0 %unmerge_heads.1 = (f32[512,1024]{1,0:T(8,128)}, bf16[512,1024]{1,0:T(8,128)(2,1)S(1)}, bf16[8,512,128]{2,1,0:T(8,128)(2,1)}) custom-call(f32[512,1024]{1,0:T(8,128)S(1)} %copy-done.4, f32[512,1024]{1,0:T(8,128)} %get-tuple-element.95.after_ref, bf16[4,128,1024]{2,1,0:T(8,128)(2,1)S(1)} %copy-done.5, f32[4,1024]{1,0:T(4,128)S(1)} %get-tuple-element.153.refs_5_.gate_one_ref, ...), custom_call_target="tpu_custom_call" | custom-call | flops 1073741824 | bytes 12582912 | tf_op jit(solution)/shard_map/unmerge_heads/pallas_call | solution.py:662
  200.4 2.7 proj_weight_grad.1
  203.1 1.0 copy-done.7
  204.1 0.7 copy-done.29
  204.8 4.4 %all-to-all-start.4 = ((bf16[8,512,128]{2,1,0:T(8,128)(2,1)}), bf16[8,512,128]{2,1,0:T(8,128)(2,1)}, u32[]{:S(2)}, u32[]{:S(2)}) async-start(bf16[8,512,128]{2,1,0:T(8,128)(2,1)} %get-tuple-element.100), calls=%async_computation.4 | async-start | bytes 2097152 | tf_op jit(solution)/shard_map/all_to_all | solution.py:37
  209.2 1.2 copy-done.6
  210.4 1.5 copy-done.8
  211.9 7.4 %side_sums.1 = (bf16[4,128,1024]{2,1,0:T(8,128)(2,1)}, f32[16,1024]{1,0:T(8,128)S(1)}, f32[2,1024]{1,0:T(2,128)S(1)}) custom-call(f32[512,1024]{1,0:T(8,128)} %get-tuple-element.93.branch_ref, f32[512,1024]{1,0:T(8,128)} %get-tuple-element.94.back_ref, f32[512,1024]{1,0:T(8,128)} %get-tuple-element.95.after_ref, f32[512,1024]{1,0:T(8,128)} %copy-done.11, ...), custom_call_target="tpu_custom_call" | custom-call | bytes 16777216 | tf_op jit(solution)/shard_map/side_sums/pallas_call | solution.py:707
  220.2 1.5 pad_maximum_fusion
  221.7 2.8 all-to-all-done.4.refs_1_
  224.6 3.9 all-to-all-start.5
  228.5 51.4 %attend_back.2 = (bf16[8,512,128]{2,1,0:T(8,128)(2,1)}, f32[128,4096]{1,0:T(8,128)}, bf16[2,8,512,128]{3,2,1,0:T(8,128)(2,1)}) custom-call(bf16[8,3,512,128]{3,2,1,0:T(8,128)(2,1)} %all-to-all-done.1.qkv_ref.refs_0_, bf16[8,512,128]{2,1,0:T(8,128)(2,1)} %all-to-all-done.4.refs_1_, bf16[2,8,384,128]{3,2,1,0:T(8,128)(2,1)} %get-tuple-element.101.refs_2_, ...), custom_call_target="tpu_custom_call" | custom-call | flops 42949672960 | bytes 8388608 | tf_op jit(solution)/shard_map/attend_back/pallas_call | solution.py:372
  280.0 1.0 copy-done.17
  280.9 4.4 %all-to-all-start.6 = ((bf16[8,512,128]{2,1,0:T(8,128)(2,1)}), bf16[8,512,128]{2,1,0:T(8,128)(2,1)S(1)}, u32[]{:S(2)}, u32[]{:S(2)}) async-start(bf16[8,512,128]{2,1,0:T(8,128)(2,1)} %get-tuple-element.110.first_ref), calls=%async_computation.6 | async-start | bytes 2097152 | tf_op jit(solution)/shard_map/all_to_all | solution.py:37
  285.4 52.3 %attend_back.3.last_ref = bf16[8,1024,128]{2,1,0:T(8,128)(2,1)} custom-call(bf16[8,3,512,128]{3,2,1,0:T(8,128)(2,1)} %all-to-all-done.1.qkv_ref.refs_0_, bf16[8,512,128]{2,1,0:T(8,128)(2,1)} %all-to-all-done.4.refs_1_, bf16[2,8,384,128]{3,2,1,0:T(8,128)(2,1)} %get-tuple-element.101.refs_2_, bf16[2,8,128,128]{3,2,1,0:T(8,128)(2,1)} %get-tuple-element.102.refs_3_, ...), custom_call_target="tpu_custom_call" | custom-call | flops 42949672960 | bytes 8388608 | tf_op jit(solution)/shard_map/attend_back/pallas_call | solution.py:372
  337.7 1.0 copy-done.9
  338.7 4.0 all-to-all-start.7
  342.8 10.0 %heads_grad.1 = (bf16[32,96,128]{2,1,0:T(8,128)(2,1)S(1)}, f32[1,384]{1,0:T(1,128)S(1)}) custom-call(bf16[8,1024,512]{2,1,0:T(8,128)(2,1)} %bitcast.84, bf16[8,512,128]{2,1,0:T(8,128)(2,1)} %get-tuple-element.110.first_ref, bf16[8,1024,128]{2,1,0:T(8,128)(2,1)} %attend_back.3.last_ref), custom_call_target="tpu_custom_call" | custom-call | flops 3221225472 | bytes 12582912 | tf_op jit(solution)/shard_map/heads_grad/pallas_call | solution.py:773
  352.9 3.4 collective-permute-start.2
  356.3 1.1 collective-permute-start
  357.4 5.3 %collective-permute-done.2 = bf16[8,96,128]{2,1,0:T(8,128)(2,1)S(1)} collective-permute-done((bf16[8,96,128]{2,1,0:T(8,128)(2,1)S(1)}, bf16[8,96,128]{2,1,0:T(8,128)(2,1)S(1)}, u32[]{:S(2)}, u32[]{:S(2)}) %collective-permute-start.2) | collective-permute-done | bytes 196640 | tf_op jit(solution)/shard_map/ppermute | solution.py:1191
  362.6 11.1 %collective-permute-done.1 = bf16[8,96,128]{2,1,0:T(8,128)(2,1)S(1)} collective-permute-done((bf16[8,96,128]{2,1,0:T(8,128)(2,1)S(1)}, bf16[8,96,128]{2,1,0:T(8,128)(2,1)S(1)}, u32[]{:S(2)}, u32[]{:S(2)}) %collective-permute-start.1) | collective-permute-done | bytes 196640 | tf_op jit(solution)/shard_map/ppermute | solution.py:1191
  373.7 0.8 fusion.18
  374.5 1.2 copy-done.10
  375.7 10.1 %finish.1 = (bf16[4,128,1024]{2,1,0:T(8,128)(2,1)}, bf16[4,80,128]{2,1,0:T(8,128)(2,1)}) custom-call(bf16[8,512,128]{2,1,0:T(8,128)(2,1)S(1)} %copy-done.10, bf16[8,1024,128]{2,1,0:T(8,128)(2,1)S(1)} %all-to-all-done.7.last_ref, bf16[1024,3072]{1,0:T(8,128)(2,1)} %wv_ref.3, bf16[1024,3072]{1,0:T(8,128)(2,1)} %wv_ref.3, bf16[1024,3072]{1,0:T(8,128)(2,1)} %wv_ref.3, ...), custom_call_target="tpu_custom_call" | custom-call | flops 3221225472 | bytes 16777216 | tf_op jit(solution)/shard_map/finish/pallas_call | solution.py:866
  385.8 3.6 all-to-all-start.8
  389.4 1.3 copy.61
  390.8 6.9 %all-to-all-done.8 = bf16[4,80,128]{2,1,0:T(8,128)(2,1)S(1)} async-done(((bf16[4,80,128]{2,1,0:T(8,128)(2,1)}), bf16[4,80,128]{2,1,0:T(8,128)(2,1)S(1)}, u32[]{:S(2)}, u32[]{:S(2)}) %all-to-all-start.8) | async-done | bytes 81952 | tf_op jit(solution)/shard_map/all_to_all | solution.py:37
  397.8 1.0 pad_maximum_fusion.1
  398.7 4.0 all-to-all-start.9
  403.9 12.1 %all-to-all-done.9.got_ref = bf16[8,416,128]{2,1,0:T(8,128)(2,1)S(1)} async-done(((bf16[8,416,128]{2,1,0:T(8,128)(2,1)}), bf16[8,416,128]{2,1,0:T(8,128)(2,1)S(1)}, u32[]{:S(2)}, u32[]{:S(2)}) %all-to-all-start.9) | async-done | bytes 852000 | tf_op jit(solution)/shard_map/all_to_all | solution.py:37
  416.5 3.4 last_sums.1
  421.8 2.4 reduce-scatter.5.cloned.1.call-done
  424.2 2.1 unpack.1
  (129 shorter events, 10.5 us)
Async XLA Ops:
  7.2 10.3 %copy-start = (s32[4,16]{1,0:T(4,128)S(1)}, s32[4,16]{1,0:T(4,128)}, u32[]{:S(2)}) copy-start(s32[4,16]{1,0:T(4,128)} %param.38) | copy-start | bytes 772
  8.6 15.5 %all-to-all-start = ((bf16[32,2,1024]{2,1,0:T(2,128)(2,1)}), bf16[32,2,1024]{2,1,0:T(2,128)(2,1)S(1)}, u32[]{:S(2)}, u32[]{:S(2)}) async-start(bf16[32,2,1024]{2,1,0:T(2,128)(2,1)} %broadcast_in_dim.185), calls=%async_computation | async-start | bytes 262144 | tf_op jit(solution)/shard_map/all_to_all | solution.py:37
  21.9 2.2 copy-start.19
  21.9 2.2 copy-start.20
  22.0 5.7 %copy-start.23 = (f32[4,2,4,128]{3,2,1,0:T(4,128)}, f32[4,2,4,128]{3,2,1,0:T(4,128)S(1)}, u32[]{:S(2)}) copy-start(f32[4,2,4,128]{3,2,1,0:T(4,128)S(1)} %broadcast_in_dim.200) | copy-start | bytes 49156
  22.0 5.7 %copy-start.24 = (f32[4,2,4,128]{3,2,1,0:T(4,128)}, f32[4,2,4,128]{3,2,1,0:T(4,128)S(1)}, u32[]{:S(2)}) copy-start(f32[4,2,4,128]{3,2,1,0:T(4,128)S(1)} %broadcast_in_dim.191) | copy-start | bytes 49156
  24.7 3.0 copy-start.2
  27.7 9.8 %copy-start.13 = (f32[4,1024]{1,0:T(4,128)}, f32[4,1024]{1,0:T(4,128)S(1)}, u32[]{:S(2)}) copy-start(f32[4,1024]{1,0:T(4,128)S(1)} %get-tuple-element.155.scale_ref) | copy-start | bytes 49156
  37.5 4.9 %copy-start.16 = (s32[64]{0:T(128)S(1)}, s32[64]{0:T(128)}, u32[]{:S(2)}) copy-start(s32[64]{0:T(128)} %param.39) | copy-start | bytes 772
  37.5 9.0 %copy-start.26 = (bf16[6144]{0:T(1024)(128)(2,1)S(1)}, bf16[6144]{0:T(1024)(128)(2,1)}, u32[]{:S(2)}) copy-start(bf16[6144]{0:T(1024)(128)(2,1)} %param.28) | copy-start | bytes 36868
  37.5 42.5 %all-to-all-start.1 = ((bf16[8,3,512,128]{3,2,1,0:T(8,128)(2,1)}), bf16[8,3,512,128]{3,2,1,0:T(8,128)(2,1)}, u32[]{:S(2)}, u32[]{:S(2)}) async-start(bf16[8,3,512,128]{3,2,1,0:T(8,128)(2,1)} %get-tuple-element.78), calls=%async_computation.1 | async-start | bytes 6291456 | tf_op jit(solution)/shard_map/all_to_all | solution.py:37
  42.1 162.0 %all-gather.3.cloned.1.call-start = ((), (), s32[]{:S(2)}) async-start(), calls=%async_computation.14 | async-start | bytes 9437184 | tf_op jit(solution)/shard_map/all_gather | solution.py:1094
  47.1 4.7 %copy-start.5 = (bf16[4,128,1024]{2,1,0:T(8,128)(2,1)S(1)}, bf16[4,128,1024]{2,1,0:T(8,128)(2,1)}, u32[]{:S(2)}) copy-start(bf16[4,128,1024]{2,1,0:T(8,128)(2,1)} %cot_ref.5) | copy-start | bytes 3145732
  51.8 3.4 copy-start.15
  55.2 24.8 %copy-start.30 = (s32[4]{0:T(128)S(1)}, s32[4]{0:T(128)}, u32[]{:S(2)}) copy-start(s32[4]{0:T(128)} %param.37) | copy-start | bytes 52
  63.5 1.0 copy-start.12
  118.0 22.0 %all-to-all-start.2 = ((bf16[8,384,128]{2,1,0:T(8,128)(2,1)}), bf16[8,384,128]{2,1,0:T(8,128)(2,1)S(1)}, u32[]{:S(2)}, u32[]{:S(2)}) async-start(bf16[8,384,128]{2,1,0:T(8,128)(2,1)} %get-tuple-element.87.refs_4_), calls=%async_computation.2 | async-start | bytes 1572864 | tf_op jit(solution)/shard_map/all_to_all | solution.py:37
  122.0 21.7 %copy-start.28 = (bf16[1024]{0:T(1024)(128)(2,1)S(1)}, bf16[1024]{0:T(1024)(128)(2,1)}, u32[]{:S(2)}) copy-start(bf16[1024]{0:T(1024)(128)(2,1)} %param.32) | copy-start | bytes 6148
  122.0 21.7 %copy-start.27 = (bf16[4096]{0:T(1024)(128)(2,1)S(1)}, bf16[4096]{0:T(1024)(128)(2,1)}, u32[]{:S(2)}) copy-start(bf16[4096]{0:T(1024)(128)(2,1)} %param.34) | copy-start | bytes 24580
  140.0 10.3 %all-to-all-start.3 = ((bf16[8,128,128]{2,1,0:T(8,128)(2,1)}), bf16[8,128,128]{2,1,0:T(8,128)(2,1)S(1)}, u32[]{:S(2)}, u32[]{:S(2)}) async-start(bf16[8,128,128]{2,1,0:T(8,128)(2,1)} %get-tuple-element.89.refs_5_), calls=%async_computation.3 | async-start | bytes 524288 | tf_op jit(solution)/shard_map/all_to_all | solution.py:37
  143.4 231.1 %reduce-scatter.3.cloned.1.call-start = ((), (), s32[]{:S(2)}) async-start(), calls=%async_computation.12 | async-start | bytes 21233664 | tf_op jit(solution)/shard_map/reduce_scatter | solution.py:1132
  155.1 1.4 copy-start.11
  192.8 1.6 copy-start.4
  203.1 1.0 copy-start.7
  204.1 0.7 copy-start.29
  204.8 4.4 %copy-start.3 = (f32[512,1024]{1,0:T(8,128)S(1)}, f32[512,1024]{1,0:T(8,128)}, u32[]{:S(2)}) copy-start(f32[512,1024]{1,0:T(8,128)} %get-tuple-element.97.grad_ref.after_ref) | copy-start | bytes 6291460
  204.8 19.8 %all-to-all-start.4 = ((bf16[8,512,128]{2,1,0:T(8,128)(2,1)}), bf16[8,512,128]{2,1,0:T(8,128)(2,1)}, u32[]{:S(2)}, u32[]{:S(2)}) async-start(bf16[8,512,128]{2,1,0:T(8,128)(2,1)} %get-tuple-element.100), calls=%async_computation.4 | async-start | bytes 2097152 | tf_op jit(solution)/shard_map/all_to_all | solution.py:37
  209.2 1.3 copy-start.6
  210.4 1.5 copy-start.8
  211.9 7.5 %copy-start.25 = (f32[1,4096]{1,0:T(1,128)S(1)}, f32[1,4096]{1,0:T(1,128)}, u32[]{:S(2)}) copy-start(f32[1,4096]{1,0:T(1,128)} %get-tuple-element.105) | copy-start | bytes 49156
  224.6 55.4 %all-to-all-start.5 = ((bf16[32,4,4224]{2,1,0:T(4,128)(2,1)}), bf16[32,4,4224]{2,1,0:T(4,128)(2,1)S(1)}, u32[]{:S(2)}, u32[]{:S(2)}) async-start(bf16[32,4,4224]{2,1,0:T(4,128)(2,1)} %pad_maximum_fusion), calls=%async_computation.5 | async-start | bytes 2162688 | tf_op jit(solution)/shard_map/all_to_all | solution.py:37
  280.0 1.0 copy-start.17
  280.9 56.8 %all-to-all-start.6 = ((bf16[8,512,128]{2,1,0:T(8,128)(2,1)}), bf16[8,512,128]{2,1,0:T(8,128)(2,1)S(1)}, u32[]{:S(2)}, u32[]{:S(2)}) async-start(bf16[8,512,128]{2,1,0:T(8,128)(2,1)} %get-tuple-element.110.first_ref), calls=%async_computation.6 | async-start | bytes 2097152 | tf_op jit(solution)/shard_map/all_to_all | solution.py:37
  337.7 1.0 copy-start.9
  338.7 35.8 %all-to-all-start.7 = ((bf16[8,1024,128]{2,1,0:T(8,128)(2,1)}), bf16[8,1024,128]{2,1,0:T(8,128)(2,1)S(1)}, u32[]{:S(2)}, u32[]{:S(2)}) async-start(bf16[8,1024,128]{2,1,0:T(8,128)(2,1)} %attend_back.3.last_ref), calls=%async_computation.7 | async-start | bytes 4194304 | tf_op jit(solution)/shard_map/all_to_all | solution.py:37
  342.7 81.4 %reduce-scatter.5.cloned.1.call-start = ((), (), s32[]{:S(2)}) async-start(), calls=%async_computation.13 | async-start | bytes 2949120 | tf_op jit(solution)/shard_map/reduce_scatter | solution.py:1196
  352.8 21.7 %copy-start.14 = (f32[4,1024]{1,0:T(4,128)S(1)}, f32[4,1024]{1,0:T(4,128)}, u32[]{:S(2)}) copy-start(f32[4,1024]{1,0:T(4,128)} %copy-done.13) | copy-start | bytes 49156
  352.9 9.7 %collective-permute-start.2 = (bf16[8,96,128]{2,1,0:T(8,128)(2,1)S(1)}, bf16[8,96,128]{2,1,0:T(8,128)(2,1)S(1)}, u32[]{:S(2)}, u32[]{:S(2)}) collective-permute-start(bf16[8,96,128]{2,1,0:T(8,128)(2,1)S(1)} %get-tuple-element.149), channel_id=1, source_target_pairs={{0,24},{1,25},{2,26},{3,27},{4,28},{5,29},{6,30},{7,31},{8,16},{9,... | collective-permute-start | bytes 589832 | tf_op jit(solution)/shard_map/ppermute | solution.py:1191
  356.3 17.4 %collective-permute-start.1 = (bf16[8,96,128]{2,1,0:T(8,128)(2,1)S(1)}, bf16[8,96,128]{2,1,0:T(8,128)(2,1)S(1)}, u32[]{:S(2)}, u32[]{:S(2)}) collective-permute-start(bf16[8,96,128]{2,1,0:T(8,128)(2,1)S(1)} %get-tuple-element.150), channel_id=1, source_target_pairs={{0,16},{1,17},{2,18},{3,19},{4,20},{5,21},{6,22},{7,23},{8,24},{9,... | collective-permute-start | bytes 589832 | tf_op jit(solution)/shard_map/ppermute | solution.py:1191
  356.3 17.4 %collective-permute-start = (bf16[8,96,128]{2,1,0:T(8,128)(2,1)S(1)}, bf16[8,96,128]{2,1,0:T(8,128)(2,1)S(1)}, u32[]{:S(2)}, u32[]{:S(2)}) collective-permute-start(bf16[8,96,128]{2,1,0:T(8,128)(2,1)S(1)} %get-tuple-element.148), channel_id=1, source_target_pairs={{0,8},{1,9},{2,10},{3,11},{4,12},{5,13},{6,14},{7,15},{8,0},{9,1},... | collective-permute-start | bytes 589832 | tf_op jit(solution)/shard_map/ppermute | solution.py:1191
  374.5 1.2 copy-start.10
  385.8 12.0 %copy-start.18 = (bf16[8,96,128]{2,1,0:T(8,128)(2,1)S(1)}, bf16[8,96,128]{2,1,0:T(8,128)(2,1)}, u32[]{:S(2)}) copy-start(bf16[8,96,128]{2,1,0:T(8,128)(2,1)} %fusion.18) | copy-start | bytes 589828
  385.8 11.9 %all-to-all-start.8 = ((bf16[4,80,128]{2,1,0:T(8,128)(2,1)}), bf16[4,80,128]{2,1,0:T(8,128)(2,1)S(1)}, u32[]{:S(2)}, u32[]{:S(2)}) async-start(bf16[4,80,128]{2,1,0:T(8,128)(2,1)} %get-tuple-element.124), calls=%async_computation.9 | async-start | bytes 163840 | tf_op jit(solution)/shard_map/all_to_all | solution.py:37
  398.7 4.0 slice-start
  398.7 17.3 %all-to-all-start.9 = ((bf16[8,416,128]{2,1,0:T(8,128)(2,1)}), bf16[8,416,128]{2,1,0:T(8,128)(2,1)S(1)}, u32[]{:S(2)}, u32[]{:S(2)}) async-start(bf16[8,416,128]{2,1,0:T(8,128)(2,1)} %pad_maximum_fusion.1), calls=%async_computation.10 | async-start | bytes 1703936 | tf_op jit(solution)/shard_map/all_to_all | solution.py:37
  402.7 0.7 copy-start.21
  402.7 1.0 copy-start.22
  403.0 23.2 %copy-start.1 = (s32[4,16]{1,0:T(4,128)S(1)}, s32[4,16]{1,0:T(4,128)}, u32[]{:S(2)}) copy-start(s32[4,16]{1,0:T(4,128)} %param.38) | copy-start | bytes 772
Sparse Core Ops, SparseCore 0:
  80.1 58.8 all-gather.2
  204.2 139.2 reduce-scatter.2
  374.6 49.4 reduce-scatter.4
